TPU v7x, 512 devices: a whole 4x8x8 slice. The times are simulated.
512 devices in a mesh: group: 2 (over y_hi), dp: 64 (over y_lo, z, core), tensor: 4 (over x).
Axes of the slice: x: 4, y: 8 (y_hi: 2, y_lo: 4; y = y_hi * 4 + y_lo), z: 8, core: 2. Of those that a mesh axis runs over, the one named last changes fastest.
Arguments:
- teacher_clips: bfloat16 [128, 256, 1024], P(('group', 'dp')), may hold values from -6 to 6
- teacher_gain: float32 [1024], replicated, may hold values from 0.5 to 2
- teacher_qkv: bfloat16 [1024, 3072], P('dp', 'tensor'), may hold values from -0.25 to 0.25
- teacher_out_t: bfloat16 [1024, 1024], P('dp', 'tensor'), may hold values from -0.75 to 0.75
- event_tokens: bfloat16 [128, 256, 768], P(('group', 'dp')), may hold values from -6 to 6
- valid_counts: int32 [128], P(('group', 'dp')), may hold values from 32 to 256, as said below
- alignment: int32 [128, 2], P(('group', 'dp')), may hold values from 0 to 1
- student_qkv: bfloat16 [768, 2304], P(None, 'tensor'), may hold values from -0.3125 to 0.3125
- student_out: bfloat16 [768, 768], P('tensor'), may hold values from -0.75 to 0.75
- projector: bfloat16 [768, 1024], P(None, 'tensor'), may hold values from -0.21875 to 0.21875
Outputs:
- clip_loss: float32 [128], P(('group', 'dp'))
- grad_qkv: float32 [768, 2304], P(('group', 'dp'), 'tensor')
- grad_out: float32 [768, 768], P('tensor', ('group', 'dp'))
- grad_projector: float32 [768, 1024], P(('group', 'dp'), 'tensor')
Inputs may be any that keep to these rules, and one draw needn't show every extreme that they name: `valid_counts`: some clip has all 256 event tokens valid.
All inputs are finite; a program needn't handle non-finite values.
Results may differ from a plain program's by a relative error of at most 0.018.
Values may be sent and summed in bfloat16 or wider, within the bound.
No kernel may reach another device: no remote copies, remote signals or barrier semaphores. Data moves between devices by JAX's collectives and lax.ppermute only.
A program may use at most 64 MiB of HBM per device.

v0:
```python
import jax
import jax.numpy as jnp
from jax import lax
from jax.sharding import PartitionSpec as P

HEAD = 64
BLOCK = 128


def norm_rows(rows):
    rows = rows.astype(jnp.float32)
    centre = rows - jnp.mean(rows, -1, keepdims=True)
    spread = jnp.mean(centre * centre, -1, keepdims=True)
    return centre * lax.rsqrt(spread + 1e-05)


def attend(normed, weight, count):
    length = normed.shape[0]
    head_size = HEAD
    heads = weight.shape[1] // (3 * head_size)
    packed = jnp.dot(normed, weight, preferred_element_type=jnp.float32).astype(jnp.bfloat16)
    packed = packed.reshape(length, heads, 3, head_size)
    query = packed[:, :, 0]
    keys = packed[:, :, 1]
    values = packed[:, :, 2]
    scores = jnp.einsum(
        "qhd,khd->hqk", query, keys, preferred_element_type=jnp.float32
    ) * head_size ** (-0.5)
    usable = jnp.arange(length) < count
    scores = jnp.where(usable[None, None, :], scores, -1e30)
    top = jnp.max(scores, -1, keepdims=True)
    weights = jnp.exp(scores - top)
    weights = (weights / jnp.sum(weights, -1, keepdims=True)).astype(jnp.bfloat16)
    mixed = jnp.einsum("hqk,khd->qhd", weights, values, preferred_element_type=jnp.float32).astype(
        jnp.bfloat16
    )
    return mixed.reshape(length, heads * head_size)


def student_heads(normed, weight_qkv, weight_out, count):
    mixed = attend(normed, weight_qkv.astype(jnp.bfloat16), count)
    return jnp.dot(mixed, weight_out.astype(jnp.bfloat16), preferred_element_type=jnp.float32)


def teacher_side(teacher_clips, teacher_gain, teacher_qkv, teacher_out_t, start, columns):
    tokens = teacher_clips[0]
    full_qkv, full_out = (
        lax.all_gather(teacher_qkv, "dp", axis=0, tiled=True),
        lax.all_gather(teacher_out_t, "dp", axis=0, tiled=True),
    )
    normed = (norm_rows(tokens) * teacher_gain).astype(jnp.bfloat16)
    mixed = attend(normed, full_qkv, tokens.shape[0])
    part = lax.dot_general(
        mixed, full_out, (((1,), (1,)), ((), ())), preferred_element_type=jnp.float32
    )
    own_tokens = lax.dynamic_slice_in_dim(tokens, start, columns, 1)
    whole = lax.psum(part.astype(jnp.bfloat16), "tensor").astype(jnp.float32)
    branch = lax.dynamic_slice_in_dim(whole, start, columns, 1)
    return (own_tokens.astype(jnp.float32) + branch).astype(jnp.bfloat16)


def student_side(event_tokens, count, student_qkv, student_out):
    events = event_tokens[0]
    normed = norm_rows(events).astype(jnp.bfloat16)
    weight_q = student_qkv.astype(jnp.float32)
    weight_o = student_out.astype(jnp.float32)
    part, back = jax.vjp(
        lambda first, second: student_heads(normed, first, second, count), weight_q, weight_o
    )
    branch = lax.psum(part.astype(jnp.bfloat16), "tensor").astype(jnp.float32)
    student_feat = (events.astype(jnp.float32) + branch).astype(jnp.bfloat16)
    return (student_feat, back)


def on_device(
    teacher_clips,
    teacher_gain,
    teacher_qkv,
    teacher_out_t,
    event_tokens,
    valid_counts,
    alignment,
    student_qkv,
    student_out,
    projector,
):
    count = valid_counts[0]
    columns = projector.shape[1]
    start = lax.axis_index("tensor") * columns
    teacher_feat = teacher_side(
        teacher_clips, teacher_gain, teacher_qkv, teacher_out_t, start, columns
    )
    student_feat, back = student_side(event_tokens, count, student_qkv, student_out)
    length = student_feat.shape[0]
    teach_len = teacher_feat.shape[0]
    width_all = teacher_clips.shape[2]
    block_rows = teacher_feat.reshape(teach_len // BLOCK, BLOCK, columns)
    target = jnp.take(block_rows, alignment[0], axis=0).reshape(length, columns)
    pred = jnp.dot(student_feat, projector, preferred_element_type=jnp.float32)
    live = (jnp.arange(length) < count)[:, None]
    diff = jnp.where(live, pred - target.astype(jnp.float32), 0.0)
    scale = count.astype(jnp.float32) * width_all
    clip_total = lax.axis_size("group") * lax.axis_size("dp")
    dpred = (diff * (2.0 / (scale * clip_total))).astype(jnp.bfloat16)
    grad_proj = lax.dot_general(
        student_feat, dpred, (((0,), (0,)), ((), ())), preferred_element_type=jnp.float32
    )
    feat_part = lax.dot_general(
        dpred, projector, (((1,), (1,)), ((), ())), preferred_element_type=jnp.float32
    )
    dfeat, squares = lax.psum((feat_part, jnp.sum(diff * diff)), "tensor")
    clip_loss = jnp.reshape(squares / scale, (1,))
    grad_q, grad_o = back(dfeat)
    shares = (
        lax.psum_scatter(grad_q, ("group", "dp"), scatter_dimension=0, tiled=True),
        lax.psum_scatter(grad_o, ("group", "dp"), scatter_dimension=1, tiled=True),
        lax.psum_scatter(grad_proj, ("group", "dp"), scatter_dimension=0, tiled=True),
    )
    return (clip_loss, shares[0], shares[1], shares[2])


def solution(mesh):
    in_specs = (
        P(("group", "dp"), None, None),
        P(),
        P("dp", "tensor"),
        P("dp", "tensor"),
        P(("group", "dp"), None, None),
        P(("group", "dp")),
        P(("group", "dp"), None),
        P(None, "tensor"),
        P("tensor", None),
        P(None, "tensor"),
    )
    out_specs = (
        P(("group", "dp")),
        P(("group", "dp"), "tensor"),
        P("tensor", ("group", "dp")),
        P(("group", "dp"), "tensor"),
    )
    return jax.shard_map(
        on_device, mesh=mesh, in_specs=in_specs, out_specs=out_specs, check_vma=False
    )
```

profile of v0, /device:TPU:1, one launch (start us, length us, event | category | flops | bytes accessed | tf_op | source)
XLA Modules:
  0.0 682.5 jit_solution(17576674818471033548)
XLA Ops:
  17.0 88.6 %all_gather.7 = bf16[1024,256]{1,0:T(8,128)(2,1)S(1)} all-gather(bf16[16,256]{1,0:T(8,128)(2,1)S(1)} %copy-done.15), channel_id=1, replica_groups=mesh['group'=2,'dp'=64,'tensor'=4] {'dp'}, dimensions={0}, use_global_device_ids=true | all-gather | bytes 532480 | tf_op jit(solution)/shard_map/all_gather | solution.py:49
  105.5 27.4 %all-gather.2.cloned.1.call-done = bf16[1024,768]{1,0:T(8,128)(2,1)} async-done(((bf16[16,768]{1,0:T(8,128)(2,1)}), bf16[1024,768]{1,0:T(8,128)(2,1)}) %all-gather.2.cloned.1.call-update) | async-done | bytes 1572880 | tf_op jit(solution)/shard_map/all_gather | solution.py:48
  143.7 52.8 %all-reduce.17.cloned.1.call-done = (bf16[256,1024]{1,0:T(8,128)(2,1)}, bf16[256,768]{1,0:T(8,128)(2,1)}) async-done(((bf16[256,1024]{1,0:T(8,128)(2,1)}, bf16[256,768]{1,0:T(8,128)(2,1)}), (bf16[256,1024]{1,0:T(8,128)(2,1)}, bf16[256,768]{1,0:T(8,128)(2,1)})) %all-reduce.17.cloned.1.call-update) | async-done | bytes 917520 | tf_op jit(solution)/shard_map/psum | solution.py:57
  201.7 22.4 %all-reduce.18 = (f32[]{:T(128)}, bf16[256,768]{1,0:T(8,128)(2,1)}) all-reduce(f32[]{:T(128)} %get-tuple-element.21, f32[256,768]{1,0:T(8,128)} %fusion.53), channel_id=1, replica_groups=mesh['group'=2,'dp'=64,'tensor'=4] {'tensor'}, use_global_device_ids=true, to_apply=%region_11.12 | all-reduce | flops 196609 | bytes 1179656 | tf_op jit(solution)/shard_map/psum | solution.py:111
  230.4 261.2 %fusion.62 = (f32[192,8]{0,1:T(8,128)S(1)}, f32[8,256]{1,0:T(8,128)S(1)}) fusion(f32[192,768]{0,1:T(8,128)S(1)} %fusion.9, f32[768,256]{1,0:T(8,128)S(1)} %fusion.50), kind=kCustom, calls=%all-reduce-scatter.2 | all-reduce-scatter fusion | flops 458753 | bytes 1392640
  493.0 8.3 %collective-permute-start.30 = (f32[192,8]{0,1:T(8,128)S(1)}, f32[192,8]{0,1:T(8,128)S(1)}, u32[]{:S(2)}, u32[]{:S(2)}) collective-permute-start(f32[192,8]{0,1:T(8,128)S(1)} %get-tuple-element.10), channel_id=1, source_target_pairs={{0,124},{4,128},{8,132},{12,136},{16,140},{20,144},{24,148},{28,15... | collective-permute-start | bytes 18440
  512.7 15.9 %collective-permute-start.22 = (f32[192,8]{0,1:T(8,128)S(1)}, f32[192,8]{0,1:T(8,128)S(1)}, u32[]{:S(2)}, u32[]{:S(2)}) collective-permute-start(f32[192,8]{0,1:T(8,128)S(1)} %get-tuple-element.10), channel_id=1, source_target_pairs={{0,92},{4,96},{8,100},{12,104},{16,108},{20,112},{24,116},{28,120}... | collective-permute-start | bytes 18440
  542.8 3.7 collective-permute-start.13
  546.5 2.8 collective-permute-start.12
  551.9 3.1 collective-permute-start.10
  555.0 4.3 collective-permute-start.9
  559.4 3.1 collective-permute-start.8
  562.4 3.7 collective-permute-start.7
  566.1 4.1 collective-permute-start.6
  570.3 3.1 collective-permute-start.5
  573.4 3.3 collective-permute-start.4
  578.0 2.8 collective-permute-start.3
  580.9 3.4 collective-permute-start.2
  597.8 3.3 collective-permute-start.55
  601.1 3.3 collective-permute-start.54
  613.6 2.8 collective-permute-start.48
  619.1 3.2 collective-permute-start.45
  622.3 2.8 collective-permute-start.44
  627.4 3.8 collective-permute-start.42
  631.2 4.1 collective-permute-start.41
  635.3 3.3 collective-permute-start.40
  638.7 3.5 collective-permute-start.39
  642.2 4.7 collective-permute-start.38
  651.9 2.9 concatenate
  654.9 3.6 collective-permute-start.36
  660.7 3.8 collective-permute-start.34
  669.9 2.9 concatenate.1
  (207 shorter events, 101.4 us)
Async XLA Ops:
  7.2 125.7 %all-gather.2.cloned.1.call-start = ((), (), s32[]{:S(2)}) async-start(), calls=%async_computation | async-start | bytes 1597440 | tf_op jit(solution)/shard_map/all_gather | solution.py:48
  7.9 188.6 %all-reduce.17.cloned.1.call-start = ((), (), s32[]{:S(2)}) async-start(), calls=%async_computation.2 | async-start | bytes 1835008 | tf_op jit(solution)/shard_map/psum | solution.py:57
  143.5 530.0 %all-reduce.15.cloned.1.call-start = ((), (), s32[]{:S(2)}) async-start(), calls=%async_computation.1 | async-start | bytes 3932160
  491.7 15.8 %collective-permute-start.63 = (f32[6,256]{1,0:T(8,128)S(1)}, f32[6,256]{1,0:T(8,128)S(1)}, u32[]{:S(2)}, u32[]{:S(2)}) collective-permute-start(f32[6,256]{1,0:T(8,128)S(1)} %slice.33), channel_id=1, source_target_pairs={{0,128},{4,132},{8,136},{12,140},{16,144},{20,148},{24,152},{28,15... | collective-permute-start | bytes 18440
  493.0 15.8 %collective-permute-start.30 = (f32[192,8]{0,1:T(8,128)S(1)}, f32[192,8]{0,1:T(8,128)S(1)}, u32[]{:S(2)}, u32[]{:S(2)}) collective-permute-start(f32[192,8]{0,1:T(8,128)S(1)} %get-tuple-element.10), channel_id=1, source_target_pairs={{0,124},{4,128},{8,132},{12,136},{16,140},{20,144},{24,148},{28,15... | collective-permute-start | bytes 18440
  507.5 21.2 %collective-permute-start.26 = (f32[192,8]{0,1:T(8,128)S(1)}, f32[192,8]{0,1:T(8,128)S(1)}, u32[]{:S(2)}, u32[]{:S(2)}) collective-permute-start(f32[192,8]{0,1:T(8,128)S(1)} %get-tuple-element.10), channel_id=1, source_target_pairs={{0,108},{4,112},{8,116},{12,120},{16,124},{20,128},{24,132},{28,13... | collective-permute-start | bytes 18440
  508.8 22.2 %collective-permute-start.25 = (f32[192,8]{0,1:T(8,128)S(1)}, f32[192,8]{0,1:T(8,128)S(1)}, u32[]{:S(2)}, u32[]{:S(2)}) collective-permute-start(f32[192,8]{0,1:T(8,128)S(1)} %get-tuple-element.10), channel_id=1, source_target_pairs={{0,104},{4,108},{8,112},{12,116},{16,120},{20,124},{24,128},{28,13... | collective-permute-start | bytes 18440
  510.1 22.2 %collective-permute-start.24 = (f32[192,8]{0,1:T(8,128)S(1)}, f32[192,8]{0,1:T(8,128)S(1)}, u32[]{:S(2)}, u32[]{:S(2)}) collective-permute-start(f32[192,8]{0,1:T(8,128)S(1)} %get-tuple-element.10), channel_id=1, source_target_pairs={{0,100},{4,104},{8,108},{12,112},{16,116},{20,120},{24,124},{28,12... | collective-permute-start | bytes 18440
  511.4 22.9 %collective-permute-start.23 = (f32[192,8]{0,1:T(8,128)S(1)}, f32[192,8]{0,1:T(8,128)S(1)}, u32[]{:S(2)}, u32[]{:S(2)}) collective-permute-start(f32[192,8]{0,1:T(8,128)S(1)} %get-tuple-element.10), channel_id=1, source_target_pairs={{0,96},{4,100},{8,104},{12,108},{16,112},{20,116},{24,120},{28,124... | collective-permute-start | bytes 18440
  512.7 23.1 %collective-permute-start.22 = (f32[192,8]{0,1:T(8,128)S(1)}, f32[192,8]{0,1:T(8,128)S(1)}, u32[]{:S(2)}, u32[]{:S(2)}) collective-permute-start(f32[192,8]{0,1:T(8,128)S(1)} %get-tuple-element.10), channel_id=1, source_target_pairs={{0,92},{4,96},{8,100},{12,104},{16,108},{20,112},{24,116},{28,120}... | collective-permute-start | bytes 18440
  540.5 14.5 %collective-permute-start.14 = (f32[192,8]{0,1:T(8,128)S(1)}, f32[192,8]{0,1:T(8,128)S(1)}, u32[]{:S(2)}, u32[]{:S(2)}) collective-permute-start(f32[192,8]{0,1:T(8,128)S(1)} %get-tuple-element.10), channel_id=1, source_target_pairs={{0,60},{4,64},{8,68},{12,72},{16,76},{20,80},{24,84},{28,88},{32,9... | collective-permute-start | bytes 18440
  542.8 16.6 %collective-permute-start.13 = (f32[192,8]{0,1:T(8,128)S(1)}, f32[192,8]{0,1:T(8,128)S(1)}, u32[]{:S(2)}, u32[]{:S(2)}) collective-permute-start(f32[192,8]{0,1:T(8,128)S(1)} %get-tuple-element.10), channel_id=1, source_target_pairs={{0,56},{4,60},{8,64},{12,68},{16,72},{20,76},{24,80},{28,84},{32,8... | collective-permute-start | bytes 18440
  546.5 16.0 %collective-permute-start.12 = (f32[192,8]{0,1:T(8,128)S(1)}, f32[192,8]{0,1:T(8,128)S(1)}, u32[]{:S(2)}, u32[]{:S(2)}) collective-permute-start(f32[192,8]{0,1:T(8,128)S(1)} %get-tuple-element.10), channel_id=1, source_target_pairs={{0,52},{4,56},{8,60},{12,64},{16,68},{20,72},{24,76},{28,80},{32,8... | collective-permute-start | bytes 18440
  549.3 16.8 %collective-permute-start.11 = (f32[192,8]{0,1:T(8,128)S(1)}, f32[192,8]{0,1:T(8,128)S(1)}, u32[]{:S(2)}, u32[]{:S(2)}) collective-permute-start(f32[192,8]{0,1:T(8,128)S(1)} %get-tuple-element.10), channel_id=1, source_target_pairs={{0,48},{4,52},{8,56},{12,60},{16,64},{20,68},{24,72},{28,76},{32,8... | collective-permute-start | bytes 18440
  551.9 18.3 %collective-permute-start.10 = (f32[192,8]{0,1:T(8,128)S(1)}, f32[192,8]{0,1:T(8,128)S(1)}, u32[]{:S(2)}, u32[]{:S(2)}) collective-permute-start(f32[192,8]{0,1:T(8,128)S(1)} %get-tuple-element.10), channel_id=1, source_target_pairs={{0,44},{4,48},{8,52},{12,56},{16,60},{20,64},{24,68},{28,72},{32,7... | collective-permute-start | bytes 18440
  555.0 18.3 %collective-permute-start.9 = (f32[192,8]{0,1:T(8,128)S(1)}, f32[192,8]{0,1:T(8,128)S(1)}, u32[]{:S(2)}, u32[]{:S(2)}) collective-permute-start(f32[192,8]{0,1:T(8,128)S(1)} %get-tuple-element.10), channel_id=1, source_target_pairs={{0,40},{4,44},{8,48},{12,52},{16,56},{20,60},{24,64},{28,68},{32,7... | collective-permute-start | bytes 18440
  559.4 17.4 %collective-permute-start.8 = (f32[192,8]{0,1:T(8,128)S(1)}, f32[192,8]{0,1:T(8,128)S(1)}, u32[]{:S(2)}, u32[]{:S(2)}) collective-permute-start(f32[192,8]{0,1:T(8,128)S(1)} %get-tuple-element.10), channel_id=1, source_target_pairs={{0,36},{4,40},{8,44},{12,48},{16,52},{20,56},{24,60},{28,64},{32,6... | collective-permute-start | bytes 18440
  562.4 15.6 %collective-permute-start.7 = (f32[192,8]{0,1:T(8,128)S(1)}, f32[192,8]{0,1:T(8,128)S(1)}, u32[]{:S(2)}, u32[]{:S(2)}) collective-permute-start(f32[192,8]{0,1:T(8,128)S(1)} %get-tuple-element.10), channel_id=1, source_target_pairs={{0,32},{4,36},{8,40},{12,44},{16,48},{20,52},{24,56},{28,60},{32,6... | collective-permute-start | bytes 18440
  566.1 14.7 %collective-permute-start.6 = (f32[192,8]{0,1:T(8,128)S(1)}, f32[192,8]{0,1:T(8,128)S(1)}, u32[]{:S(2)}, u32[]{:S(2)}) collective-permute-start(f32[192,8]{0,1:T(8,128)S(1)} %get-tuple-element.10), channel_id=1, source_target_pairs={{0,28},{4,32},{8,36},{12,40},{16,44},{20,48},{24,52},{28,56},{32,6... | collective-permute-start | bytes 18440
  570.3 14.1 %collective-permute-start.5 = (f32[192,8]{0,1:T(8,128)S(1)}, f32[192,8]{0,1:T(8,128)S(1)}, u32[]{:S(2)}, u32[]{:S(2)}) collective-permute-start(f32[192,8]{0,1:T(8,128)S(1)} %get-tuple-element.10), channel_id=1, source_target_pairs={{0,24},{4,28},{8,32},{12,36},{16,40},{20,44},{24,48},{28,52},{32,5... | collective-permute-start | bytes 18440
  573.4 13.7 %collective-permute-start.4 = (f32[192,8]{0,1:T(8,128)S(1)}, f32[192,8]{0,1:T(8,128)S(1)}, u32[]{:S(2)}, u32[]{:S(2)}) collective-permute-start(f32[192,8]{0,1:T(8,128)S(1)} %get-tuple-element.10), channel_id=1, source_target_pairs={{0,20},{4,24},{8,28},{12,32},{16,36},{20,40},{24,44},{28,48},{32,5... | collective-permute-start | bytes 18440
  576.7 18.3 %collective-permute-start.62 = (f32[8,256]{1,0:T(8,128)S(1)}, f32[8,256]{1,0:T(8,128)S(1)}, u32[]{:S(2)}, u32[]{:S(2)}) collective-permute-start(f32[8,256]{1,0:T(8,128)S(1)} %get-tuple-element.11), channel_id=1, source_target_pairs={{0,124},{4,128},{8,132},{12,136},{16,140},{20,144},{24,148},{28,15... | collective-permute-start | bytes 24584
  619.1 16.2 %collective-permute-start.45 = (f32[8,256]{1,0:T(8,128)S(1)}, f32[8,256]{1,0:T(8,128)S(1)}, u32[]{:S(2)}, u32[]{:S(2)}) collective-permute-start(f32[8,256]{1,0:T(8,128)S(1)} %get-tuple-element.11), channel_id=1, source_target_pairs={{0,56},{4,60},{8,64},{12,68},{16,72},{20,76},{24,80},{28,84},{32,8... | collective-permute-start | bytes 24584
  622.3 16.3 %collective-permute-start.44 = (f32[8,256]{1,0:T(8,128)S(1)}, f32[8,256]{1,0:T(8,128)S(1)}, u32[]{:S(2)}, u32[]{:S(2)}) collective-permute-start(f32[8,256]{1,0:T(8,128)S(1)} %get-tuple-element.11), channel_id=1, source_target_pairs={{0,52},{4,56},{8,60},{12,64},{16,68},{20,72},{24,76},{28,80},{32,8... | collective-permute-start | bytes 24584
  625.2 17.0 %collective-permute-start.43 = (f32[8,256]{1,0:T(8,128)S(1)}, f32[8,256]{1,0:T(8,128)S(1)}, u32[]{:S(2)}, u32[]{:S(2)}) collective-permute-start(f32[8,256]{1,0:T(8,128)S(1)} %get-tuple-element.11), channel_id=1, source_target_pairs={{0,48},{4,52},{8,56},{12,60},{16,64},{20,68},{24,72},{28,76},{32,8... | collective-permute-start | bytes 24584
  627.4 19.5 %collective-permute-start.42 = (f32[8,256]{1,0:T(8,128)S(1)}, f32[8,256]{1,0:T(8,128)S(1)}, u32[]{:S(2)}, u32[]{:S(2)}) collective-permute-start(f32[8,256]{1,0:T(8,128)S(1)} %get-tuple-element.11), channel_id=1, source_target_pairs={{0,44},{4,48},{8,52},{12,56},{16,60},{20,64},{24,68},{28,72},{32,7... | collective-permute-start | bytes 24584
  631.2 23.7 %collective-permute-start.41 = (f32[8,256]{1,0:T(8,128)S(1)}, f32[8,256]{1,0:T(8,128)S(1)}, u32[]{:S(2)}, u32[]{:S(2)}) collective-permute-start(f32[8,256]{1,0:T(8,128)S(1)} %get-tuple-element.11), channel_id=1, source_target_pairs={{0,40},{4,44},{8,48},{12,52},{16,56},{20,60},{24,64},{28,68},{32,7... | collective-permute-start | bytes 24584
  635.3 23.1 %collective-permute-start.40 = (f32[8,256]{1,0:T(8,128)S(1)}, f32[8,256]{1,0:T(8,128)S(1)}, u32[]{:S(2)}, u32[]{:S(2)}) collective-permute-start(f32[8,256]{1,0:T(8,128)S(1)} %get-tuple-element.11), channel_id=1, source_target_pairs={{0,36},{4,40},{8,44},{12,48},{16,52},{20,56},{24,60},{28,64},{32,6... | collective-permute-start | bytes 24584
  638.7 22.0 %collective-permute-start.39 = (f32[8,256]{1,0:T(8,128)S(1)}, f32[8,256]{1,0:T(8,128)S(1)}, u32[]{:S(2)}, u32[]{:S(2)}) collective-permute-start(f32[8,256]{1,0:T(8,128)S(1)} %get-tuple-element.11), channel_id=1, source_target_pairs={{0,32},{4,36},{8,40},{12,44},{16,48},{20,52},{24,56},{28,60},{32,6... | collective-permute-start | bytes 24584
  642.2 22.3 %collective-permute-start.38 = (f32[8,256]{1,0:T(8,128)S(1)}, f32[8,256]{1,0:T(8,128)S(1)}, u32[]{:S(2)}, u32[]{:S(2)}) collective-permute-start(f32[8,256]{1,0:T(8,128)S(1)} %get-tuple-element.11), channel_id=1, source_target_pairs={{0,28},{4,32},{8,36},{12,40},{16,44},{20,48},{24,52},{28,56},{32,6... | collective-permute-start | bytes 24584
  647.0 19.9 %collective-permute-start.37 = (f32[8,256]{1,0:T(8,128)S(1)}, f32[8,256]{1,0:T(8,128)S(1)}, u32[]{:S(2)}, u32[]{:S(2)}) collective-permute-start(f32[8,256]{1,0:T(8,128)S(1)} %get-tuple-element.11), channel_id=1, source_target_pairs={{0,24},{4,28},{8,32},{12,36},{16,40},{20,44},{24,48},{28,52},{32,5... | collective-permute-start | bytes 24584
  654.9 14.8 %collective-permute-start.36 = (f32[8,256]{1,0:T(8,128)S(1)}, f32[8,256]{1,0:T(8,128)S(1)}, u32[]{:S(2)}, u32[]{:S(2)}) collective-permute-start(f32[8,256]{1,0:T(8,128)S(1)} %get-tuple-element.11), channel_id=1, source_target_pairs={{0,20},{4,24},{8,28},{12,32},{16,36},{20,40},{24,44},{28,48},{32,5... | collective-permute-start | bytes 24584
  (58 other events, 1284.4 us)
Sparse Core Ops, SparseCore 0:
  10.2 122.7 all-gather.1
  143.6 52.8 all-reduce.16
  230.2 204.7 all-reduce.14
where the time goes:
time: 685 us; the launch traced here: 683 us
  blocking collectives  372 us (54%)
  starting transfers between devices  171 us (25%)
  waiting for transfers between devices  81.3 us (12%)
  matrix products  21.8 us (3%)
  between operations  19 us (3%)
  local copies, waits for them, and re-layouts  11 us (2%)
    unnamed x1, blocking collectives  261 us
    unnamed x65, starting transfers between devices  171 us
    all_gather x1, blocking collectives, teacher_side(): lax.all_gather(teacher_out_t, 'dp', axis=0, tiled=True)  88.6 us
    psum x1, waiting for transfers between devices, teacher_side(): whole = lax.psum(part.astype(jnp.bfloat16), 'tensor').astype(jnp.float32)  52.8 us
    all_gather x1, waiting for transfers between devices, teacher_side(): lax.all_gather(teacher_qkv, 'dp', axis=0, tiled=True)  27.4 us
    psum x1, blocking collectives, on_device(): dfeat, squares = lax.psum((feat_part, jnp.sum(diff * diff)), 'tensor')  22.4 us
  transfers between devices with their start and end apart: 67, of which 3 were waited for; matrix products, arithmetic and copies ran while one was open for 41% of the time, Pallas kernels for 0%

commit v1 on v0

v1 whole, which is shorter than its diff:
```python
import jax
import jax.numpy as jnp
from jax import lax
from jax.experimental import pallas as pl
from jax.experimental.pallas import tpu as pltpu
from jax.sharding import Mesh, PartitionSpec as P

HEAD = 64
BLOCK = 128
F32 = jnp.float32
BF16 = jnp.bfloat16
CLIP = ("g", "yl", "z", "c")
VMEM = pl.BlockSpec(memory_space=pltpu.VMEM)
SMEM = pl.BlockSpec(memory_space=pltpu.SMEM)
PARAMS = pltpu.CompilerParams(vmem_limit_bytes=40 * 1024 * 1024)


def shape(dims, dtype):
    return jax.ShapeDtypeStruct(dims, dtype)


def nn(a, b):
    return lax.dot_general(a, b, (((1,), (0,)), ((), ())), preferred_element_type=F32)


def nt(a, b):
    return lax.dot_general(a, b, (((1,), (1,)), ((), ())), preferred_element_type=F32)


def tn(a, b):
    return lax.dot_general(a, b, (((0,), (0,)), ((), ())), preferred_element_type=F32)


def norm_rows(rows):
    rows = rows.astype(F32)
    centre = rows - jnp.mean(rows, -1, keepdims=True)
    spread = jnp.mean(centre * centre, -1, keepdims=True)
    return centre * lax.rsqrt(spread + 1e-05)


def split_head(packed, head):
    first = head * 3 * HEAD
    return [packed[:, first + i * HEAD : first + (i + 1) * HEAD].astype(BF16) for i in range(3)]


def softmax(scores):
    top = jnp.max(scores, -1, keepdims=True)
    weights = jnp.exp(scores - top)
    return weights / jnp.sum(weights, -1, keepdims=True)


def student_kernel(
    count_ref, events_ref, qkv_ref, out_ref, clip_ref, gain_ref,
    part_ref, normed_ref, packed_ref, mixed_ref, weights_ref, teacher_ref,
):
    length = events_ref.shape[0]
    heads = out_ref.shape[0] // HEAD
    normed = norm_rows(events_ref[...]).astype(BF16)
    normed_ref[...] = normed
    packed = nn(normed, qkv_ref[...])
    packed_ref[...] = packed.astype(BF16)
    usable = lax.broadcasted_iota(jnp.int32, (length, length), 1) < count_ref[0]
    mixed = []
    for head in range(heads):
        query, keys, values = split_head(packed, head)
        scores = jnp.where(usable, nt(query, keys) * HEAD ** (-0.5), -1e30)
        weights = softmax(scores)
        weights_ref[head] = weights
        mixed.append(nn(weights.astype(BF16), values))
    mixed = jnp.concatenate(mixed, axis=1).astype(BF16)
    mixed_ref[...] = mixed
    part_ref[...] = nn(mixed, out_ref[...]).astype(BF16)
    teacher_ref[...] = (norm_rows(clip_ref[...]) * gain_ref[...]).astype(BF16)


def teacher_kernel(
    place_ref, align_ref, normed_ref, own_ref, near_ref, swap_ref, far_ref, fars_ref,
    part_ref, full_ref, mixed_ref,
):
    rows = own_ref.shape[0]
    for i, piece in enumerate((own_ref, near_ref, swap_ref, far_ref, fars_ref)):
        size = piece.shape[0]
        full_ref[pl.ds(pl.multiple_of(place_ref[i], BLOCK), size), :] = piece[...]
    width = full_ref.shape[1]
    heads = width // (4 * HEAD)
    packed = nn(normed_ref[...], full_ref[:, : heads * 3 * HEAD])
    mixed = []
    for head in range(heads):
        query, keys, values = split_head(packed, head)
        weights = softmax(nt(query, keys) * HEAD ** (-0.5))
        mixed.append(nn(weights.astype(BF16), values))
    mixed_ref[...] = jnp.concatenate(mixed, axis=1)
    for i in range(align_ref.shape[0]):
        first = pl.multiple_of(align_ref[i] * BLOCK, BLOCK)
        chosen = mixed_ref[pl.ds(first, BLOCK), :].astype(BF16)
        part_ref[i * BLOCK : (i + 1) * BLOCK, :] = nt(
            chosen, full_ref[:, heads * 3 * HEAD :]
        ).astype(BF16)


def diff_kernel(clips, count_ref, start_ref, parts_ref, tokens_ref, feat_ref, proj_ref, out_ref):
    rows, width = tokens_ref.shape
    ways = proj_ref.shape[0]
    columns = proj_ref.shape[2]
    branch = parts_ref[0].astype(F32)
    for i in range(1, ways):
        branch = branch + parts_ref[i].astype(F32)
    target = (tokens_ref[...].astype(F32) + branch).astype(BF16).astype(F32)
    count = count_ref[0]
    live = lax.broadcasted_iota(jnp.int32, (rows, 1), 0) + start_ref[0] < count
    scale = jnp.full((1, 1), count, jnp.int32).astype(F32) * width
    factor = 2.0 / (scale * clips)
    feat = feat_ref[...]
    features = proj_ref.shape[1]
    dfeat = jnp.zeros((rows, features), F32)
    squares = jnp.zeros((rows, 1), F32)
    for i in range(ways):
        pred = nn(feat, proj_ref[i])
        diff = jnp.where(live, pred - target[:, i * columns : (i + 1) * columns], 0.0)
        squares = squares + jnp.sum(diff * diff, -1, keepdims=True)
        dpred = (diff * factor).astype(BF16)
        out_ref[i, :, features : features + columns] = dpred
        dfeat = dfeat + nt(dpred, proj_ref[i])
    dfeat = dfeat.astype(BF16)
    squares = squares / scale
    high = squares.astype(BF16)
    rest = squares - high.astype(F32)
    middle = rest.astype(BF16)
    low = (rest - middle.astype(F32)).astype(BF16)
    lane = lax.broadcasted_iota(jnp.int32, (rows, BLOCK), 1)
    tail = jnp.where(lane == 0, high.astype(F32), jnp.where(lane == 1, middle.astype(F32), 0.0))
    tail = jnp.where(lane == 2, low.astype(F32), tail).astype(BF16)
    for i in range(ways):
        out_ref[i, :, :features] = dfeat
        out_ref[i, :, features + columns :] = tail


def backward_kernel(
    back_ref, packed_ref, weights_ref, mixed_ref, out_ref, pick_ref, normed_ref, feat_ref,
    keep_ref, send_ref, loss_ref,
):
    features = out_ref.shape[1]
    heads = out_ref.shape[0] // HEAD
    dfeat = back_ref[:, :features]
    columns = back_ref.shape[1] - features - BLOCK
    dpred = back_ref[:, features : features + columns]
    tail = back_ref[:, features + columns :].astype(F32)
    loss_ref[...] = jnp.sum(jnp.sum(tail, 0, keepdims=True), 1, keepdims=True)
    dmixed = nt(dfeat, out_ref[...])
    packed = packed_ref[...].astype(F32)
    pieces = []
    for head in range(heads):
        query, keys, values = split_head(packed, head)
        weights = weights_ref[head]
        cot = dmixed[:, head * HEAD : (head + 1) * HEAD].astype(BF16)
        dvalues = tn(weights.astype(BF16), cot)
        dweights = nt(cot, values)
        inner = jnp.sum(dweights * weights, -1, keepdims=True)
        dscores = (weights * (dweights - inner) * HEAD ** (-0.5)).astype(BF16)
        pieces += [nn(dscores, keys), tn(dscores, query), dvalues]
    dpacked = jnp.concatenate(pieces, axis=1)
    used = dpacked.shape[1]
    length = dpacked.shape[0]
    right = jnp.concatenate([dpacked, jnp.zeros((length, features - used), F32)], 1).astype(BF16)
    tailed = features - columns
    mixed = jnp.concatenate(
        [jnp.zeros((length, used - tailed), F32), mixed_ref[...].astype(F32)], 1
    ).astype(BF16)
    for half, into in enumerate((keep_ref, send_ref)):
        dfeat_rows = nt(pick_ref[half], dfeat).astype(BF16)
        normed_rows = normed_ref[half]
        for b in range(features // columns):
            block = slice(b * columns, (b + 1) * columns)
            total = nn(normed_rows, right[:, block]) + nn(feat_ref[half, b], dpred)
            if b == features // columns - 1:
                total = total + nn(dfeat_rows, mixed)
            into[:, block] = total.astype(BF16)


def gather_rows(shard, own_c, own_yl):
    spread = lax.axis_size("z") * lax.axis_size("c")
    rows, width = shard.shape
    run = lax.all_to_all(
        jnp.broadcast_to(shard[None], (spread, rows, width)), ("z", "c"), 0, 0
    ).reshape(spread * rows, width)
    ring = lax.axis_size("g") * lax.axis_size("yl")
    near, far = [], []
    for y in range(ring):
        for c, sign in ((0, -1), (1, 1)):
            near.append((y * 2 + c, (y + sign) % ring * 2 + c))
            far.append((y * 2 + c, (y + 2 * sign) % ring * 2 + c))
    half = spread * rows // 2
    first = lax.ppermute(run, ("g", "yl", "c"), near)
    second = lax.ppermute(lax.dynamic_slice_in_dim(run, own_c * half, half, 0), ("g", "yl", "c"), far)
    swap = [(0, 1), (1, 0)]
    first_other = lax.ppermute(first, "c", swap)
    second_other = lax.ppermute(second, "c", swap)
    ways = lax.axis_size("yl")
    step = 1 - 2 * own_c
    size = spread * rows
    opposite = (own_yl + 2) % ways * size
    place = jnp.stack([
        own_yl * size,
        (own_yl + step + ways) % ways * size,
        (own_yl - step + ways) % ways * size,
        opposite + own_c * half,
        opposite + (1 - own_c) * half,
    ]).astype(jnp.int32)
    return place, (run, first, first_other, second, second_other)


def pick_rows(rows, own_c, shares, columns):
    each = rows // shares
    extra = each * columns // rows
    block = each + extra
    place = jnp.arange(shares // 2 * block)
    chip, row = place // block, place % block
    source = jnp.arange(rows)
    picks, extras = [], []
    for core in (own_c, 1 - own_c):
        base = (chip * 2 + core) * each
        picks.append((source[None] == (base + row)[:, None]) & (row < each)[:, None])
        extras.append(jnp.stack([
            (source[None] == (base + (row - each) * (rows // columns) + b)[:, None]) & (row >= each)[:, None]
            for b in range(rows // columns)
        ]))
    return jnp.stack(picks).astype(BF16), jnp.stack(extras).astype(BF16)


def on_device(
    teacher_clips, teacher_gain, teacher_qkv, teacher_out_t, event_tokens, valid_counts, alignment,
    student_qkv, student_out, projector,
):
    clip, events, align = teacher_clips[0], event_tokens[0], alignment[0]
    length, width = clip.shape
    features = events.shape[1]
    columns = projector.shape[1]
    ways = lax.axis_size("x")
    rows = length // ways
    own_c, own_yl, own_x = lax.axis_index("c"), lax.axis_index("yl"), lax.axis_index("x")
    shares = 1
    for axis in CLIP:
        shares = shares * lax.axis_size(axis)

    place, pieces = gather_rows(jnp.concatenate([teacher_qkv, teacher_out_t], 1), own_c, own_yl)

    heads = student_out.shape[0] // HEAD
    part, normed, packed, mixed, weights, teacher_normed = pl.pallas_call(
        student_kernel,
        out_shape=(
            shape((length, features), BF16),
            shape((length, features), BF16),
            shape((length, 3 * HEAD * heads), BF16),
            shape((length, HEAD * heads), BF16),
            shape((heads, length, length), F32),
            shape((length, width), BF16),
        ),
        in_specs=[SMEM] + [VMEM] * 5,
        out_specs=(VMEM,) * 6,
        compiler_params=PARAMS,
        name="student_forward",
    )(valid_counts, events, student_qkv, student_out, clip, teacher_gain.reshape(1, width))

    whole_proj = lax.all_gather(projector, "x", axis=0, tiled=False)
    parts = lax.all_to_all(part.reshape(ways, rows, features), "x", 0, 0)
    own_events = lax.dynamic_slice_in_dim(events, own_x * rows, rows, 0)
    feat_rows = (own_events.astype(F32) + jnp.sum(parts.astype(F32), 0)).astype(BF16)
    feat = lax.all_gather(feat_rows, "x", axis=0, tiled=True)

    pick, extra = pick_rows(features, own_c, shares, columns)
    normed_rows = jnp.einsum("hpf,tf->hpt", pick, normed, preferred_element_type=F32).astype(BF16)
    feat_extra = jnp.einsum("hbpf,tf->hbpt", extra, feat, preferred_element_type=F32).astype(BF16)

    teacher_part = pl.pallas_call(
        teacher_kernel,
        out_shape=shape((length, width), BF16),
        in_specs=[SMEM] * 2 + [VMEM] * 6,
        out_specs=VMEM,
        scratch_shapes=[
            pltpu.VMEM((width, teacher_qkv.shape[1] + teacher_out_t.shape[1]), BF16),
            pltpu.VMEM((length, teacher_out_t.shape[1]), F32),
        ],
        compiler_params=PARAMS,
        name="teacher",
    )(place, align, teacher_normed, *pieces)

    teacher_parts = lax.all_to_all(teacher_part.reshape(ways, rows, width), "x", 0, 0)
    per_block = BLOCK // rows
    source = align[own_x // per_block] * BLOCK + own_x % per_block * rows
    own_tokens = lax.dynamic_slice_in_dim(clip, source, rows, 0)
    message = pl.pallas_call(
        lambda *refs: diff_kernel(shares, *refs),
        out_shape=shape((ways, rows, features + columns + BLOCK), BF16),
        in_specs=[SMEM] * 2 + [VMEM] * 4,
        out_specs=VMEM,
        compiler_params=PARAMS,
        name="difference",
    )(
        valid_counts, (own_x * rows).astype(jnp.int32).reshape(1), teacher_parts, own_tokens,
        feat_rows, whole_proj,
    )
    back = lax.all_to_all(message, "x", 0, 0).reshape(length, features + columns + BLOCK)

    half = pick.shape[1]
    keep, send, loss = pl.pallas_call(
        backward_kernel,
        out_shape=(shape((half, features), BF16), shape((half, features), BF16), shape((1, 1), F32)),
        in_specs=[VMEM] * 8,
        out_specs=(VMEM,) * 3,
        compiler_params=PARAMS,
        name="student_backward",
    )(back, packed, weights, mixed, student_out, pick, normed_rows, feat_extra)

    chips = shares // 2
    both = (keep.astype(F32) + lax.ppermute(send, "c", [(0, 1), (1, 0)]).astype(F32)).astype(BF16)
    spread = lax.all_to_all(both.reshape(chips, half // chips, features), ("g", "yl", "z"), 0, 0)
    total = jnp.sum(spread.astype(F32), 0)
    each = features // shares
    used = 3 * HEAD * heads
    grad_q = total[:each, :used]
    grad_o = total[:each, used:].T
    grad_p = total[each:].reshape(each, columns)
    return loss.reshape(1), grad_q, grad_o, grad_p


def solution(mesh):
    sizes = mesh.devices.shape
    fine = Mesh(mesh.devices.reshape(sizes[0], 4, sizes[1] // 8, 2, sizes[2]), (*CLIP, "x"))
    dp = CLIP[1:]
    in_specs = (
        P(CLIP, None, None), P(), P(dp, "x"), P(dp, "x"), P(CLIP, None, None), P(CLIP), P(CLIP, None),
        P(None, "x"), P("x", None), P(None, "x"),
    )
    out_specs = (P(CLIP), P(CLIP, "x"), P("x", CLIP), P(CLIP, "x"))
    return jax.shard_map(
        on_device, mesh=fine, in_specs=in_specs, out_specs=out_specs, check_vma=False
    )
```

time: 685 us -> 169 us (0.25)
  the two profiles are of different devices: /device:TPU:1 before, /device:TPU:16 now
where the time goes in v1:
time: 169 us; the launch traced here: 168 us
  blocking collectives  52 us (31%)
  starting transfers between devices  37.1 us (22%)
  waiting for transfers between devices  19.2 us (11%)
  between operations  15.8 us (9%)
  local copies, waits for them, and re-layouts  13.1 us (8%)
  other arithmetic  12 us (7%)
  Pallas kernels  11.6 us (7%)
  matrix products  7.04 us (4%)
    all_to_all x1, blocking collectives, on_device(): lax.all_to_all(both.reshape(chips, half // chips, features), ('g', 'yl',...  34.5 us
    all_gather x1, blocking collectives, on_device(): feat = lax.all_gather(feat_rows, 'x', axis=0, tiled=True)  17.5 us
    all_to_all x1, starting transfers between devices, gather_rows(): lax.all_to_all(jnp.broadcast_to(shard[None], (spread, rows, width)), ('z'...  10.4 us
    unnamed x45, local copies, waits for them, and re-layouts  10.2 us
    all_to_all x1, waiting for transfers between devices, on_device(): lax.all_to_all(teacher_part.reshape(ways, rows, width), 'x', 0, 0)  8.99 us
    ppermute x1, starting transfers between devices, gather_rows(): lax.ppermute(lax.dynamic_slice_in_dim(run, own_c * half, half, 0), ('g',...  5.26 us
    all_to_all x1, starting transfers between devices, on_device(): lax.all_to_all(teacher_part.reshape(ways, rows, width), 'x', 0, 0)  4.8 us
    pallas_call x1, Pallas kernels, on_device(): pl.pallas_call(teacher_kernel, out_shape=shape((length, width), BF16), in...  4.54 us
  transfers between devices with their start and end apart: 10, of which 5 were waited for; matrix products, arithmetic and copies ran while one was open for 12% of the time, Pallas kernels for 4%

profile of v1, /device:TPU:16, one launch (start us, length us, event | category | flops | bytes accessed | tf_op | source)
XLA Modules:
  0.0 167.7 jit_solution(2612597117752411503)
XLA Ops:
  8.8 10.4 %all-to-all-start = ((bf16[16,16,1024]{2,1,0:T(8,128)(2,1)}), bf16[16,16,1024]{2,1,0:T(8,128)(2,1)S(1)}, u32[]{:S(2)}, u32[]{:S(2)}) async-start(bf16[16,16,1024]{2,1,0:T(8,128)(2,1)} %broadcast_in_dim.2), calls=%async_computation | async-start | bytes 1048576 | tf_op jit(solution)/shard_map/all_to_all | solution.py:183
  20.1 3.4 %fusion.9 = (pred[1,512,768]{2,1,0:T(32,128)(4,1)}, pred[1,512,768]{2,1,0:T(32,128)(4,1)}, pred[1,512,768]{2,1,0:T(32,128)(4,1)}, pred[1,512,768]{2,1,0:T(32,128...) fusion(s32[512]{0:T(512)S(1)} %get-tuple-element.30, pred[512]{0:T(512)(128)(4,1)S(1)} %broadcast_compare_fusion, ...), kind=kLoop, calls=%fused_computation.20 | loop fusion | flops 4718592 | bytes 2372096 | tf_op jit(solution)/shard_map/and | solution.py:224
  24.2 1.5 copy.14.qkv_ref
  25.7 1.7 student_forward.1
  31.2 2.4 %add_bitcast_fusion = pred[1,3,512,768]{3,2,1,0:T(32,128)(4,1)} fusion(pred[1,512,768]{2,1,0:T(32,128)(4,1)} %get-tuple-element.24, pred[1,512,768]{2,1,0:T(32,128)(4,1)} %get-tuple-element.23, pred[1,512,768]{2,1,0:T(32,128)(4,1)} %get-tuple-element.22), kind=kLoop, calls=%fused_computation.4 | loop fusion | flops 2359296 | bytes 2359296 | tf_op jit(solution)/shard_map/stack | solution.py:227
  33.6 1.6 all-to-all-done
  35.2 4.3 %all-to-all-start.2 = ((bf16[4,64,768]{2,1,0:T(8,128)(2,1)}), bf16[4,64,768]{2,1,0:T(8,128)(2,1)}, u32[]{:S(2)}, u32[]{:S(2)}) async-start(bf16[4,64,768]{2,1,0:T(8,128)(2,1)} %bitcast.45), calls=%async_computation.2 | async-start | bytes 786432 | tf_op jit(solution)/shard_map/all_to_all | solution.py:265
  39.5 2.3 %collective-permute-start = (bf16[256,1024]{1,0:T(8,128)(2,1)S(1)}, bf16[256,1024]{1,0:T(8,128)(2,1)}, u32[]{:S(2)}, u32[]{:S(2)}) collective-permute-start(bf16[256,1024]{1,0:T(8,128)(2,1)S(1)} %bitcast.38), channel_id=1, source_target_pairs={{0,448},{4,68},{64,0},{68,132},{128,64},{132,196},{192,128},{196,2... | collective-permute-start | bytes 1572872 | tf_op jit(solution)/shard_map/ppermute | solution.py:193
  41.9 2.1 %add_bitcast_fusion.1 = pred[1,3,512,768]{3,2,1,0:T(32,128)(4,1)} fusion(pred[1,512,768]{2,1,0:T(32,128)(4,1)} %get-tuple-element.27, pred[1,512,768]{2,1,0:T(32,128)(4,1)S(1)} %copy-done.21, pred[1,512,768]{2,1,0:T(32,128)(4,1)S(1)} %copy-done.20), kind=kLoop, calls=%fused_computation.5 | loop fusion | flops 2359296 | bytes 2359296 | tf_op jit(solution)/shard_map/stack | solution.py:227
  44.1 5.3 %collective-permute-start.2 = (bf16[128,1024]{1,0:T(8,128)(2,1)S(1)}, bf16[128,1024]{1,0:T(8,128)(2,1)}, u32[]{:S(2)}, u32[]{:S(2)}) collective-permute-start(bf16[128,1024]{1,0:T(8,128)(2,1)S(1)} %constant_dynamic-slice_fusion.1), channel_id=1, source_target_pairs={{0,384},{4,132},{64,448},{68,196},{128,0},{132,260},{192,64},{196,... | collective-permute-start | bytes 786440 | tf_op jit(solution)/shard_map/ppermute | solution.py:194
  49.4 1.4 collective-permute-done.near_ref
  50.7 2.6 %collective-permute-start.1 = (bf16[256,1024]{1,0:T(8,128)(2,1)}, bf16[256,1024]{1,0:T(8,128)(2,1)}, u32[]{:S(2)}, u32[]{:S(2)}) collective-permute-start(bf16[256,1024]{1,0:T(8,128)(2,1)} %collective-permute-done.near_ref), channel_id=1, source_target_pairs={{0,4},{4,0},{1,5},{5,1},{2,6},{6,2},{3,7},{7,3},{8,12},{12,8},{9,1... | collective-permute-start | bytes 1572872 | tf_op jit(solution)/shard_map/ppermute | solution.py:196
  53.3 0.9 fusion.7
  54.3 4.3 %collective-permute-done.2.far_ref = bf16[128,1024]{1,0:T(8,128)(2,1)} collective-permute-done((bf16[128,1024]{1,0:T(8,128)(2,1)S(1)}, bf16[128,1024]{1,0:T(8,128)(2,1)}, u32[]{:S(2)}, u32[]{:S(2)}) %collective-permute-start.2) | collective-permute-done | bytes 262176 | tf_op jit(solution)/shard_map/ppermute | solution.py:194
  58.6 1.9 %collective-permute-start.3 = (bf16[128,1024]{1,0:T(8,128)(2,1)}, bf16[128,1024]{1,0:T(8,128)(2,1)}, u32[]{:S(2)}, u32[]{:S(2)}) collective-permute-start(bf16[128,1024]{1,0:T(8,128)(2,1)} %collective-permute-done.2.far_ref), channel_id=1, source_target_pairs={{0,4},{4,0},{1,5},{5,1},{2,6},{6,2},{3,7},{7,3},{8,12},{12,8},{9,1... | collective-permute-start | bytes 786440 | tf_op jit(solution)/shard_map/ppermute | solution.py:197
  62.2 2.7 %convolution_convert_fusion.normed_ref = bf16[2,512,256]{2,1,0:T(8,128)(2,1)} fusion(pred[1,512,768]{2,1,0:T(32,128)(4,1)} %copy-done.19, pred[1,512,768]{2,1,0:T(32,128)(4,1)} %copy-done.18, bf16[256,768]{1,0:T(8,128)(2,1)} %copy-done.17), kind=kOutput, calls=%fused_computation.26 | convolution fusion | flops 403701760 | bytes 1703936 | tf_op jit(solution)/shard_map/hpf,tf->hpt/dot_general | solution.py:271
  64.9 4.5 %teacher.1 = bf16[256,1024]{1,0:T(8,128)(2,1)} custom-call(s32[5]{0:T(128)S(1)} %stack.49.place_ref, s32[2]{0:T(128)S(1)} %bitcast.47, bf16[256,1024]{1,0:T(8,128)(2,1)S(1)} %copy-done.8, bf16[256,1024]{1,0:T(8,128)(2,1)S(1)} %bitcast.40, bf16[256,1024]{1,0:T(8,128)(2,1)} %collective-permute-done.near_ref, ...), custom_call_target="tpu_custom_call" | custom-call | tf_op jit(solution)/shard_map/teacher/pallas_call | solution.py:274
  69.5 4.8 %all-to-all-start.1 = ((bf16[4,64,1024]{2,1,0:T(8,128)(2,1)}), bf16[4,64,1024]{2,1,0:T(8,128)(2,1)S(1)}, u32[]{:S(2)}, u32[]{:S(2)}) async-start(bf16[4,64,1024]{2,1,0:T(8,128)(2,1)} %bitcast.11), calls=%async_computation.1 | async-start | bytes 1048576 | tf_op jit(solution)/shard_map/all_to_all | solution.py:287
  74.3 1.1 convert_reduce_fusion.1
  75.4 9.0 %all-to-all-done.1.refs_2_ = bf16[4,64,1024]{2,1,0:T(8,128)(2,1)S(1)} async-done(((bf16[4,64,1024]{2,1,0:T(8,128)(2,1)}), bf16[4,64,1024]{2,1,0:T(8,128)(2,1)S(1)}, u32[]{:S(2)}, u32[]{:S(2)}) %all-to-all-start.1) | async-done | bytes 524320 | tf_op jit(solution)/shard_map/all_to_all | solution.py:287
  84.4 1.4 copy-done
  85.8 1.9 %difference.1 = bf16[4,64,1152]{2,1,0:T(8,128)(2,1)} custom-call(s32[1]{0:T(128)S(6)} %copy.38.count_ref.refs_0_, s32[1]{0:T(128)} %bitcast.refs_1_, bf16[4,64,1024]{2,1,0:T(8,128)(2,1)S(1)} %all-to-all-done.1.refs_2_, bf16[64,1024]{1,0:T(8,128)(2,1)S(1)} %dynamic-slice_bitcast_fusion.refs_3_, bf16[64,768]{1,0:T(8,128)(2,1)S(1)} %fusion.19.refs_4_, ...), custom_call_target="tpu_custom_call" | custom-call | tf_op jit(solution)/shard_map/difference/pallas_call | solution.py:291
  87.7 3.5 %all-to-all-start.3 = ((bf16[4,64,1152]{2,1,0:T(8,128)(2,1)}), bf16[4,64,1152]{2,1,0:T(8,128)(2,1)S(1)}, u32[]{:S(2)}, u32[]{:S(2)}) async-start(bf16[4,64,1152]{2,1,0:T(8,128)(2,1)} %difference.1), calls=%async_computation.3 | async-start | bytes 1179648 | tf_op jit(solution)/shard_map/all_to_all | solution.py:302
  91.2 17.5 %all_gather.11 = bf16[256,768]{1,0:T(8,128)(2,1)S(1)} all-gather(bf16[64,768]{1,0:T(8,128)(2,1)S(1)} %fusion.19.refs_4_), channel_id=1, replica_groups=mesh['g'=2,'yl'=4,'z'=8,'c'=2,'x'=4] {'x'}, dimensions={0}, use_global_device_ids=true | all-gather | bytes 491520 | tf_op jit(solution)/shard_map/all_gather | solution.py:268
  108.7 4.3 %fusion.4.feat_ref = bf16[2,3,512,256]{3,2,1,0:T(8,128)(2,1)} fusion(pred[1,3,512,768]{3,2,1,0:T(32,128)(4,1)} %add_bitcast_fusion.1, pred[1,3,512,768]{3,2,1,0:T(32,128)(4,1)} %add_bitcast_fusion, bf16[256,768]{1,0:T(8,128)(2,1)S(1)} %all_gather.11), kind=kOutput, calls=%fused_computation.7 | convolution fusion | flops 1211105280 | bytes 4325376 | tf_op jit(solution)/shard_map/hbpf,tf->hbpt/dot_general | solution.py:272
  113.1 1.4 copy-done.1
  114.5 1.0 copy-done.9
  115.5 1.0 copy-done.12
  116.5 3.5 %student_backward.1 = (bf16[512,768]{1,0:T(8,128)(2,1)S(1)}, bf16[512,768]{1,0:T(8,128)(2,1)S(1)}, f32[1,1]{1,0:T(1,128)}) custom-call(bf16[256,1152]{1,0:T(8,128)(2,1)S(1)} %bitcast.41, bf16[256,576]{1,0:T(8,128)(2,1)S(1)} %copy-done.12, f32[3,256,256]{2,1,0:T(8,128)S(1)} %copy-done.5, bf16[256,192]{1,0:T(8,128)(2,1)S(1)} %copy-done.14, ...), custom_call_target="tpu_custom_call" | custom-call | tf_op jit(solution)/shard_map/student_backward/pallas_call | solution.py:305
  120.0 1.9 %collective-permute-start.4 = (bf16[512,768]{1,0:T(8,128)(2,1)S(1)}, bf16[512,768]{1,0:T(8,128)(2,1)S(1)}, u32[]{:S(2)}, u32[]{:S(2)}) collective-permute-start(bf16[512,768]{1,0:T(8,128)(2,1)S(1)} %get-tuple-element.21), channel_id=1, source_target_pairs={{0,4},{4,0},{1,5},{5,1},{2,6},{6,2},{3,7},{7,3},{8,12},{12,8},{9,1... | collective-permute-start | bytes 2359304 | tf_op jit(solution)/shard_map/ppermute | solution.py:315
  121.9 2.3 %collective-permute-done.4 = bf16[512,768]{1,0:T(8,128)(2,1)S(1)} collective-permute-done((bf16[512,768]{1,0:T(8,128)(2,1)S(1)}, bf16[512,768]{1,0:T(8,128)(2,1)S(1)}, u32[]{:S(2)}, u32[]{:S(2)}) %collective-permute-start.4) | collective-permute-done | bytes 786464 | tf_op jit(solution)/shard_map/ppermute | solution.py:315
  124.4 34.5 %all_to_all.25 = bf16[64,8,768]{2,1,0:T(8,128)(2,1)S(1)} all-to-all(bf16[64,8,768]{2,1,0:T(8,128)(2,1)S(1)} %fusion.16), channel_id=1, replica_groups=mesh['g'=2,'yl'=4,'z'=8,'c'=2,'x'=4] {'g','yl','z'}, dimensions={0} | all-to-all | bytes 1572864 | tf_op jit(solution)/shard_map/all_to_all | solution.py:316
  (67 shorter events, 9.5 us)
Async XLA Ops:
  8.8 26.5 %all-to-all-start = ((bf16[16,16,1024]{2,1,0:T(8,128)(2,1)}), bf16[16,16,1024]{2,1,0:T(8,128)(2,1)S(1)}, u32[]{:S(2)}, u32[]{:S(2)}) async-start(bf16[16,16,1024]{2,1,0:T(8,128)(2,1)} %broadcast_in_dim.2), calls=%async_computation | async-start | bytes 1048576 | tf_op jit(solution)/shard_map/all_to_all | solution.py:183
  19.2 56.2 %all-gather.3.cloned.1.call-start = ((), (), s32[]{:S(2)}) async-start(), calls=%async_computation.5 | async-start | bytes 1966080 | tf_op jit(solution)/shard_map/all_gather | solution.py:264
  20.0 5.7 %copy-start.2 = (bf16[192,768]{1,0:T(8,128)(2,1)S(1)}, bf16[192,768]{1,0:T(8,128)(2,1)}, u32[]{:S(2)}) copy-start(bf16[192,768]{1,0:T(8,128)(2,1)} %out_ref.3) | copy-start | bytes 884740
  20.0 5.7 %copy-start.3 = (bf16[1,256,1024]{2,1,0:T(8,128)(2,1)S(1)}, bf16[1,256,1024]{2,1,0:T(8,128)(2,1)}, u32[]{:S(2)}) copy-start(bf16[1,256,1024]{2,1,0:T(8,128)(2,1)} %param.10) | copy-start | bytes 1572868
  20.1 5.7 %copy-start.6 = (bf16[1,256,768]{2,1,0:T(8,128)(2,1)S(1)}, bf16[1,256,768]{2,1,0:T(8,128)(2,1)}, u32[]{:S(2)}) copy-start(bf16[1,256,768]{2,1,0:T(8,128)(2,1)} %param.14) | copy-start | bytes 1179652
  20.1 5.7 %copy-start.15 = (f32[1024]{0:T(1024)S(1)}, f32[1024]{0:T(1024)}, u32[]{:S(2)}) copy-start(f32[1024]{0:T(1024)} %param.11) | copy-start | bytes 12292
  27.4 0.9 copy-start.4
  28.3 0.7 copy-start.11
  29.0 0.7 copy-start.13
  29.7 0.8 copy-start.17
  30.5 0.8 copy-start.10
  30.5 4.8 %copy-start.7 = (bf16[256,1024]{1,0:T(8,128)(2,1)}, bf16[256,1024]{1,0:T(8,128)(2,1)S(1)}, u32[]{:S(2)}) copy-start(bf16[256,1024]{1,0:T(8,128)(2,1)S(1)} %get-tuple-element.13.normed_ref) | copy-start | bytes 1572868
  31.2 10.7 %copy-start.20 = (pred[1,512,768]{2,1,0:T(32,128)(4,1)S(1)}, pred[1,512,768]{2,1,0:T(32,128)(4,1)}, u32[]{:S(2)}) copy-start(pred[1,512,768]{2,1,0:T(32,128)(4,1)} %get-tuple-element.25) | copy-start | bytes 1179652
  31.2 10.7 %copy-start.21 = (pred[1,512,768]{2,1,0:T(32,128)(4,1)S(1)}, pred[1,512,768]{2,1,0:T(32,128)(4,1)}, u32[]{:S(2)}) copy-start(pred[1,512,768]{2,1,0:T(32,128)(4,1)} %get-tuple-element.26) | copy-start | bytes 1179652
  35.2 34.2 %all-to-all-start.2 = ((bf16[4,64,768]{2,1,0:T(8,128)(2,1)}), bf16[4,64,768]{2,1,0:T(8,128)(2,1)}, u32[]{:S(2)}, u32[]{:S(2)}) async-start(bf16[4,64,768]{2,1,0:T(8,128)(2,1)} %bitcast.45), calls=%async_computation.2 | async-start | bytes 786432 | tf_op jit(solution)/shard_map/all_to_all | solution.py:265
  39.5 11.2 %collective-permute-start = (bf16[256,1024]{1,0:T(8,128)(2,1)S(1)}, bf16[256,1024]{1,0:T(8,128)(2,1)}, u32[]{:S(2)}, u32[]{:S(2)}) collective-permute-start(bf16[256,1024]{1,0:T(8,128)(2,1)S(1)} %bitcast.38), channel_id=1, source_target_pairs={{0,448},{4,68},{64,0},{68,132},{128,64},{132,196},{192,128},{196,2... | collective-permute-start | bytes 1572872 | tf_op jit(solution)/shard_map/ppermute | solution.py:193
  44.1 14.5 %collective-permute-start.2 = (bf16[128,1024]{1,0:T(8,128)(2,1)S(1)}, bf16[128,1024]{1,0:T(8,128)(2,1)}, u32[]{:S(2)}, u32[]{:S(2)}) collective-permute-start(bf16[128,1024]{1,0:T(8,128)(2,1)S(1)} %constant_dynamic-slice_fusion.1), channel_id=1, source_target_pairs={{0,384},{4,132},{64,448},{68,196},{128,0},{132,260},{192,64},{196,... | collective-permute-start | bytes 786440 | tf_op jit(solution)/shard_map/ppermute | solution.py:194
  50.7 14.2 %collective-permute-start.1 = (bf16[256,1024]{1,0:T(8,128)(2,1)}, bf16[256,1024]{1,0:T(8,128)(2,1)}, u32[]{:S(2)}, u32[]{:S(2)}) collective-permute-start(bf16[256,1024]{1,0:T(8,128)(2,1)} %collective-permute-done.near_ref), channel_id=1, source_target_pairs={{0,4},{4,0},{1,5},{5,1},{2,6},{6,2},{3,7},{7,3},{8,12},{12,8},{9,1... | collective-permute-start | bytes 1572872 | tf_op jit(solution)/shard_map/ppermute | solution.py:196
  53.3 7.5 %copy-start.16 = (s32[1,2]{1,0:T(1,128)S(1)}, s32[1,2]{1,0:T(1,128)}, u32[]{:S(2)}) copy-start(s32[1,2]{1,0:T(1,128)} %param.16) | copy-start | bytes 28
  54.3 6.2 %copy-start.18 = (pred[1,512,768]{2,1,0:T(32,128)(4,1)}, pred[1,512,768]{2,1,0:T(32,128)(4,1)S(1)}, u32[]{:S(2)}) copy-start(pred[1,512,768]{2,1,0:T(32,128)(4,1)S(1)} %get-tuple-element.28) | copy-start | bytes 1179652
  54.3 6.2 %copy-start.19 = (pred[1,512,768]{2,1,0:T(32,128)(4,1)}, pred[1,512,768]{2,1,0:T(32,128)(4,1)S(1)}, u32[]{:S(2)}) copy-start(pred[1,512,768]{2,1,0:T(32,128)(4,1)S(1)} %get-tuple-element.29) | copy-start | bytes 1179652
  58.6 6.4 %collective-permute-start.3 = (bf16[128,1024]{1,0:T(8,128)(2,1)}, bf16[128,1024]{1,0:T(8,128)(2,1)}, u32[]{:S(2)}, u32[]{:S(2)}) collective-permute-start(bf16[128,1024]{1,0:T(8,128)(2,1)} %collective-permute-done.2.far_ref), channel_id=1, source_target_pairs={{0,4},{4,0},{1,5},{5,1},{2,6},{6,2},{3,7},{7,3},{8,12},{12,8},{9,1... | collective-permute-start | bytes 786440 | tf_op jit(solution)/shard_map/ppermute | solution.py:197
  62.2 2.7 %copy-start.8 = (bf16[256,1024]{1,0:T(8,128)(2,1)S(1)}, bf16[256,1024]{1,0:T(8,128)(2,1)}, u32[]{:S(2)}) copy-start(bf16[256,1024]{1,0:T(8,128)(2,1)} %copy-done.7) | copy-start | bytes 1572868
  69.5 14.9 %all-to-all-start.1 = ((bf16[4,64,1024]{2,1,0:T(8,128)(2,1)}), bf16[4,64,1024]{2,1,0:T(8,128)(2,1)S(1)}, u32[]{:S(2)}, u32[]{:S(2)}) async-start(bf16[4,64,1024]{2,1,0:T(8,128)(2,1)} %bitcast.11), calls=%async_computation.1 | async-start | bytes 1048576 | tf_op jit(solution)/shard_map/all_to_all | solution.py:287
  84.4 1.4 copy-start
  87.7 25.3 %all-to-all-start.3 = ((bf16[4,64,1152]{2,1,0:T(8,128)(2,1)}), bf16[4,64,1152]{2,1,0:T(8,128)(2,1)S(1)}, u32[]{:S(2)}, u32[]{:S(2)}) async-start(bf16[4,64,1152]{2,1,0:T(8,128)(2,1)} %difference.1), calls=%async_computation.3 | async-start | bytes 1179648 | tf_op jit(solution)/shard_map/all_to_all | solution.py:302
  108.7 4.3 %copy-start.5 = (f32[3,256,256]{2,1,0:T(8,128)S(1)}, f32[3,256,256]{2,1,0:T(8,128)}, u32[]{:S(2)}) copy-start(f32[3,256,256]{2,1,0:T(8,128)} %copy-done.4) | copy-start | bytes 2359300
  108.7 4.3 %copy-start.14 = (bf16[256,192]{1,0:T(8,128)(2,1)S(1)}, bf16[256,192]{1,0:T(8,128)(2,1)}, u32[]{:S(2)}) copy-start(bf16[256,192]{1,0:T(8,128)(2,1)} %copy-done.13) | copy-start | bytes 294916
  113.1 1.4 copy-start.1
  114.5 1.0 copy-start.9
  115.5 1.0 copy-start.12
  120.0 4.2 %collective-permute-start.4 = (bf16[512,768]{1,0:T(8,128)(2,1)S(1)}, bf16[512,768]{1,0:T(8,128)(2,1)S(1)}, u32[]{:S(2)}, u32[]{:S(2)}) collective-permute-start(bf16[512,768]{1,0:T(8,128)(2,1)S(1)} %get-tuple-element.21), channel_id=1, source_target_pairs={{0,4},{4,0},{1,5},{5,1},{2,6},{6,2},{3,7},{7,3},{8,12},{12,8},{9,1... | collective-permute-start | bytes 2359304 | tf_op jit(solution)/shard_map/ppermute | solution.py:315
Sparse Core Ops, SparseCore 0:
  22.2 37.3 all-gather.2

commit v2 on v1

--- a/solution.py
+++ b/solution.py
@@ -12,7 +12,11 @@
 CLIP = ("g", "yl", "z", "c")
 VMEM = pl.BlockSpec(memory_space=pltpu.VMEM)
 SMEM = pl.BlockSpec(memory_space=pltpu.SMEM)
-PARAMS = pltpu.CompilerParams(vmem_limit_bytes=40 * 1024 * 1024)
+PARAMS = pltpu.CompilerParams(vmem_limit_bytes=20 * 1024 * 1024)
+
+
+def cost(microseconds):
+    return pl.CostEstimate(flops=microseconds * 10**9, bytes_accessed=10**6, transcendentals=0)
 
 
 def shape(dims, dtype):
@@ -49,15 +53,32 @@
     return weights / jnp.sum(weights, -1, keepdims=True)
 
 
+def pick_rows(rows, shares, columns, core, extra):
+    each = rows // shares
+    block = each + each * columns // rows
+    place = lax.broadcasted_iota(jnp.int32, (shares // 2 * block, 1), 0)
+    chip, row = place // block, place % block
+    base = (chip * 2 + core) * each
+    if extra is None:
+        wanted = jnp.where(row < each, base + row, -1)
+    else:
+        wanted = jnp.where(row >= each, base + (row - each) * (rows // columns) + extra, -1)
+    source = lax.broadcasted_iota(jnp.int32, (shares // 2 * block, rows), 1)
+    return jnp.where(source == wanted, 1.0, 0.0).astype(BF16)
+
+
 def student_kernel(
-    count_ref, events_ref, qkv_ref, out_ref, clip_ref, gain_ref,
-    part_ref, normed_ref, packed_ref, mixed_ref, weights_ref, teacher_ref,
-):
-    length = events_ref.shape[0]
+    shares, count_ref, core_ref, events_ref, qkv_ref, out_ref, clip_ref, gain_ref,
+    part_ref, normed_ref, packed_ref, mixed_ref, weights_ref, teacher_ref, pick_ref,
+):
+    length, features = events_ref.shape
     heads = out_ref.shape[0] // HEAD
     normed = norm_rows(events_ref[...]).astype(BF16)
-    normed_ref[...] = normed
-    packed = nn(normed, qkv_ref[...])
+    for half in range(2):
+        core = core_ref[0] if half == 0 else 1 - core_ref[0]
+        pick_ref[half] = pick_rows(features, shares, clip_ref.shape[1] // 4, core, None)
+        normed_ref[half] = nt(pick_ref[half], normed).astype(BF16)
+    packed = nt(normed, qkv_ref[...])
     packed_ref[...] = packed.astype(BF16)
     usable = lax.broadcasted_iota(jnp.int32, (length, length), 1) < count_ref[0]
     mixed = []
@@ -98,31 +119,43 @@
         ).astype(BF16)
 
 
-def diff_kernel(clips, count_ref, start_ref, parts_ref, tokens_ref, feat_ref, proj_ref, out_ref):
+def feature_kernel(shares, ways, place_ref, *refs):
+    feat_refs = refs[:ways]
+    proj_ref, after_ref, extra_ref, pred_ref, feat_ref = refs[ways:]
+    features, columns = proj_ref.shape[1:]
+    rows = feat_refs[0].shape[0]
+    for k in range(ways):
+        source = place_ref[1 + k]
+        feat_ref[pl.ds(pl.multiple_of(source * rows, rows), rows), :] = feat_refs[k][...]
+        pred_ref[:, k * columns : (k + 1) * columns] = nn(feat_refs[0][...], proj_ref[k])
+    feat = feat_ref[...]
+    for half in range(2):
+        core = place_ref[0] if half == 0 else 1 - place_ref[0]
+        for b in range(features // columns):
+            pick = pick_rows(features, shares, columns, core, b)
+            extra_ref[half, b] = nt(pick, feat).astype(BF16)
+
+
+def diff_kernel(
+    clips, count_ref, place_ref, parts_ref, tokens_ref, pred_ref, proj_ref, out_ref
+):
     rows, width = tokens_ref.shape
-    ways = proj_ref.shape[0]
-    columns = proj_ref.shape[2]
+    ways, features, columns = proj_ref.shape
     branch = parts_ref[0].astype(F32)
     for i in range(1, ways):
         branch = branch + parts_ref[i].astype(F32)
     target = (tokens_ref[...].astype(F32) + branch).astype(BF16).astype(F32)
     count = count_ref[0]
-    live = lax.broadcasted_iota(jnp.int32, (rows, 1), 0) + start_ref[0] < count
+    live = lax.broadcasted_iota(jnp.int32, (rows, 1), 0) + place_ref[1] * rows < count
     scale = jnp.full((1, 1), count, jnp.int32).astype(F32) * width
     factor = 2.0 / (scale * clips)
-    feat = feat_ref[...]
-    features = proj_ref.shape[1]
+    diff = jnp.where(live, pred_ref[...] - target, 0.0)
+    squares = jnp.sum(diff * diff, -1, keepdims=True) / scale
+    dpred = (diff * factor).astype(BF16)
     dfeat = jnp.zeros((rows, features), F32)
-    squares = jnp.zeros((rows, 1), F32)
-    for i in range(ways):
-        pred = nn(feat, proj_ref[i])
-        diff = jnp.where(live, pred - target[:, i * columns : (i + 1) * columns], 0.0)
-        squares = squares + jnp.sum(diff * diff, -1, keepdims=True)
-        dpred = (diff * factor).astype(BF16)
-        out_ref[i, :, features : features + columns] = dpred
-        dfeat = dfeat + nt(dpred, proj_ref[i])
+    for k in range(ways):
+        dfeat = dfeat + nt(dpred[:, k * columns : (k + 1) * columns], proj_ref[k])
     dfeat = dfeat.astype(BF16)
-    squares = squares / scale
     high = squares.astype(BF16)
     rest = squares - high.astype(F32)
     middle = rest.astype(BF16)
@@ -132,6 +165,7 @@
     tail = jnp.where(lane == 2, low.astype(F32), tail).astype(BF16)
     for i in range(ways):
         out_ref[i, :, :features] = dfeat
+        out_ref[i, :, features : features + columns] = dpred[:, i * columns : (i + 1) * columns]
         out_ref[i, :, features + columns :] = tail
 
 
@@ -177,19 +211,22 @@
             into[:, block] = total.astype(BF16)
 
 
-def gather_rows(shard, own_c, own_yl):
+def gather_run(shard):
     spread = lax.axis_size("z") * lax.axis_size("c")
-    rows, width = shard.shape
-    run = lax.all_to_all(
-        jnp.broadcast_to(shard[None], (spread, rows, width)), ("z", "c"), 0, 0
-    ).reshape(spread * rows, width)
+    return lax.all_to_all(
+        jnp.broadcast_to(shard[None], (spread, *shard.shape)), ("z", "c"), 0, 0
+    ).reshape(spread * shard.shape[0], shard.shape[1])
+
+
+def gather_runs(run, own_c, own_yl):
+    size = run.shape[0]
+    half = size // 2
     ring = lax.axis_size("g") * lax.axis_size("yl")
     near, far = [], []
     for y in range(ring):
         for c, sign in ((0, -1), (1, 1)):
             near.append((y * 2 + c, (y + sign) % ring * 2 + c))
             far.append((y * 2 + c, (y + 2 * sign) % ring * 2 + c))
-    half = spread * rows // 2
     first = lax.ppermute(run, ("g", "yl", "c"), near)
     second = lax.ppermute(lax.dynamic_slice_in_dim(run, own_c * half, half, 0), ("g", "yl", "c"), far)
     swap = [(0, 1), (1, 0)]
@@ -197,7 +234,6 @@
     second_other = lax.ppermute(second, "c", swap)
     ways = lax.axis_size("yl")
     step = 1 - 2 * own_c
-    size = spread * rows
     opposite = (own_yl + 2) % ways * size
     place = jnp.stack([
         own_yl * size,
@@ -209,22 +245,24 @@
     return place, (run, first, first_other, second, second_other)
 
 
-def pick_rows(rows, own_c, shares, columns):
-    each = rows // shares
-    extra = each * columns // rows
-    block = each + extra
-    place = jnp.arange(shares // 2 * block)
-    chip, row = place // block, place % block
-    source = jnp.arange(rows)
-    picks, extras = [], []
-    for core in (own_c, 1 - own_c):
-        base = (chip * 2 + core) * each
-        picks.append((source[None] == (base + row)[:, None]) & (row < each)[:, None])
-        extras.append(jnp.stack([
-            (source[None] == (base + (row - each) * (rows // columns) + b)[:, None]) & (row >= each)[:, None]
-            for b in range(rows // columns)
-        ]))
-    return jnp.stack(picks).astype(BF16), jnp.stack(extras).astype(BF16)
+def from_peers(rows, axis):
+    ways = lax.axis_size(axis)
+    return [
+        lax.ppermute(rows(k), axis, [(i, (i + k) % ways) for i in range(ways)])
+        for k in range(1, ways)
+    ]
+
+
+def result_kernel(parts_ref, q_ref, o_ref, p_ref):
+    each, used = q_ref.shape
+    columns = p_ref.shape[1]
+    total = jnp.sum(parts_ref[...].astype(F32), 0)
+    q_ref[...] = total[:each, :used]
+    o_ref[...] = total[:each, used:]
+    for i in range(total.shape[0] - each):
+        for b in range(total.shape[1] // columns):
+            row = i * (total.shape[1] // columns) + b
+            p_ref[row : row + 1] = total[each + i : each + i + 1, b * columns : (b + 1) * columns]
 
 
 def on_device(
@@ -242,34 +280,39 @@
     for axis in CLIP:
         shares = shares * lax.axis_size(axis)
 
-    place, pieces = gather_rows(jnp.concatenate([teacher_qkv, teacher_out_t], 1), own_c, own_yl)
+    run = gather_run(jnp.concatenate([teacher_qkv, teacher_out_t], 1))
 
     heads = student_out.shape[0] // HEAD
-    part, normed, packed, mixed, weights, teacher_normed = pl.pallas_call(
-        student_kernel,
+    each = features // shares
+    half = shares // 2 * (each + each * columns // features)
+    core = own_c.astype(jnp.int32).reshape(1)
+    part, normed_rows, packed, mixed, weights, teacher_normed, pick = pl.pallas_call(
+        lambda *refs: student_kernel(shares, *refs),
         out_shape=(
             shape((length, features), BF16),
-            shape((length, features), BF16),
+            shape((2, half, length), BF16),
             shape((length, 3 * HEAD * heads), BF16),
             shape((length, HEAD * heads), BF16),
             shape((heads, length, length), F32),
             shape((length, width), BF16),
+            shape((2, half, features), BF16),
         ),
-        in_specs=[SMEM] + [VMEM] * 5,
-        out_specs=(VMEM,) * 6,
-        compiler_params=PARAMS,
+        in_specs=[SMEM] * 2 + [VMEM] * 5,
+        out_specs=(VMEM,) * 7,
+        compiler_params=PARAMS,
+        cost_estimate=cost(4),
         name="student_forward",
-    )(valid_counts, events, student_qkv, student_out, clip, teacher_gain.reshape(1, width))
+    )(valid_counts, core, events, student_qkv.T, student_out, clip, teacher_gain.reshape(1, width))
 
     whole_proj = lax.all_gather(projector, "x", axis=0, tiled=False)
-    parts = lax.all_to_all(part.reshape(ways, rows, features), "x", 0, 0)
-    own_events = lax.dynamic_slice_in_dim(events, own_x * rows, rows, 0)
-    feat_rows = (own_events.astype(F32) + jnp.sum(parts.astype(F32), 0)).astype(BF16)
-    feat = lax.all_gather(feat_rows, "x", axis=0, tiled=True)
-
-    pick, extra = pick_rows(features, own_c, shares, columns)
-    normed_rows = jnp.einsum("hpf,tf->hpt", pick, normed, preferred_element_type=F32).astype(BF16)
-    feat_extra = jnp.einsum("hbpf,tf->hbpt", extra, feat, preferred_element_type=F32).astype(BF16)
+    own_rows = lambda array, place: lax.dynamic_slice_in_dim(array, place * rows, rows, 0)
+    branch = own_rows(part, own_x).astype(F32)
+    for received in from_peers(lambda k: own_rows(part, (own_x + k) % ways), "x"):
+        branch = branch + received.astype(F32)
+    feat_rows = (own_rows(events, own_x).astype(F32) + branch).astype(BF16)
+    run, feat_rows = lax.optimization_barrier((run, feat_rows))
+    place, pieces = gather_runs(run, own_c, own_yl)
+    feats = [feat_rows] + from_peers(lambda k: feat_rows, "x")
 
     teacher_part = pl.pallas_call(
         teacher_kernel,
@@ -281,6 +324,7 @@
             pltpu.VMEM((length, teacher_out_t.shape[1]), F32),
         ],
         compiler_params=PARAMS,
+        cost_estimate=cost(5),
         name="teacher",
     )(place, align, teacher_normed, *pieces)
 
@@ -288,39 +332,56 @@
     per_block = BLOCK // rows
     source = align[own_x // per_block] * BLOCK + own_x % per_block * rows
     own_tokens = lax.dynamic_slice_in_dim(clip, source, rows, 0)
+    places = jnp.stack([own_c] + [(own_x - k + ways) % ways for k in range(ways)]).astype(jnp.int32)
+    feat_extra, pred = pl.pallas_call(
+        lambda *refs: feature_kernel(shares, ways, *refs),
+        out_shape=(
+            shape((2, features // columns, half, length), BF16), shape((rows, width), F32),
+        ),
+        in_specs=[SMEM] + [VMEM] * (ways + 1) + [pl.BlockSpec(memory_space=pl.ANY)],
+        out_specs=(VMEM,) * 2,
+        scratch_shapes=[pltpu.VMEM((length, features), BF16)],
+        compiler_params=PARAMS,
+        cost_estimate=cost(4),
+        name="student_features",
+    )(places, *feats, whole_proj, teacher_part)
     message = pl.pallas_call(
         lambda *refs: diff_kernel(shares, *refs),
         out_shape=shape((ways, rows, features + columns + BLOCK), BF16),
         in_specs=[SMEM] * 2 + [VMEM] * 4,
         out_specs=VMEM,
         compiler_params=PARAMS,
+        cost_estimate=cost(2),
         name="difference",
-    )(
-        valid_counts, (own_x * rows).astype(jnp.int32).reshape(1), teacher_parts, own_tokens,
-        feat_rows, whole_proj,
-    )
+    )(valid_counts, places, teacher_parts, own_tokens, pred, whole_proj)
     back = lax.all_to_all(message, "x", 0, 0).reshape(length, features + columns + BLOCK)
 
-    half = pick.shape[1]
     keep, send, loss = pl.pallas_call(
         backward_kernel,
         out_shape=(shape((half, features), BF16), shape((half, features), BF16), shape((1, 1), F32)),
         in_specs=[VMEM] * 8,
         out_specs=(VMEM,) * 3,
         compiler_params=PARAMS,
+        cost_estimate=cost(4),
         name="student_backward",
     )(back, packed, weights, mixed, student_out, pick, normed_rows, feat_extra)
 
     chips = shares // 2
     both = (keep.astype(F32) + lax.ppermute(send, "c", [(0, 1), (1, 0)]).astype(F32)).astype(BF16)
     spread = lax.all_to_all(both.reshape(chips, half // chips, features), ("g", "yl", "z"), 0, 0)
-    total = jnp.sum(spread.astype(F32), 0)
-    each = features // shares
     used = 3 * HEAD * heads
-    grad_q = total[:each, :used]
-    grad_o = total[:each, used:].T
-    grad_p = total[each:].reshape(each, columns)
-    return loss.reshape(1), grad_q, grad_o, grad_p
+    grad_q, grad_o, grad_p = pl.pallas_call(
+        result_kernel,
+        out_shape=(
+            shape((each, used), F32), shape((each, HEAD * heads), F32), shape((each, columns), F32),
+        ),
+        in_specs=[VMEM],
+        out_specs=(VMEM,) * 3,
+        compiler_params=PARAMS,
+        cost_estimate=cost(1),
+        name="gradient_rows",
+    )(spread)
+    return loss.reshape(1), grad_q, grad_o.T, grad_p
 
 
 def solution(mesh):

time: 169 us -> 161 us (0.953)
  starting transfers between devices: 37.1 us -> 48.9 us
  other arithmetic: 12 us -> 1.7 us
  matrix products: 7.04 us -> 0 us
  blocking collectives: 52 us -> 48 us
  local copies, waits for them, and re-layouts: 13.1 us -> 9.11 us
  waiting for transfers between devices: 19.2 us -> 22.3 us
  Pallas kernels: 11.6 us -> 14.1 us
    ppermute x4 -> x10, starting transfers between devices: 12.1 us -> 33.1 us  [the longest x6 21.6 us: from_peers(): lax.ppermute(rows(k), axis, [(i, (i + k) % ways) for i in range(ways)])]
    all_gather x1 -> x0, blocking collectives: 17.5 us -> none  [on_device(): feat = lax.all_gather(feat_rows, 'x', axis=0, tiled=True)]
    all_to_all x0 -> x1, blocking collectives: none -> 12.2 us  [on_device(): lax.all_to_all(message, 'x', 0, 0)]
    ppermute x4 -> x10, waiting for transfers between devices: 5.65 us -> 14.5 us  [the longest x1 5.93 us: gather_runs(): lax.ppermute(lax.dynamic_slice_in_dim(run, own_c * half, half, 0), ('g',...]
    all_to_all x3 -> x1, starting transfers between devices: 18.2 us -> 10.4 us  [gather_run(): lax.all_to_all(jnp.broadcast_to(shard[None], (spread, *shard.shape)), ('z...]
    dot_general x2 -> x0, matrix products: 7.04 us -> none  [the longest x1 4.33 us: on_device(): jnp.einsum('hbpf,tf->hbpt', extra, feat, preferred_element_type=F32)]
    another operation x2 -> x0, other arithmetic: 4.54 us -> none  [pick_rows(): return (jnp.stack(picks).astype(BF16), jnp.stack(extras).astype(BF16))]
    and x2 -> x0, other arithmetic: 4.33 us -> none  [the longest x1 3.42 us: pick_rows(): (source[None] == (base + (row - each) * (rows // columns) + b)[:, None])...]
  transfers between devices with their start and end apart: 10 -> 14, of which waited for: 5 -> 6; matrix products, arithmetic and copies ran while one was open for 12% -> 1% of each run, Pallas kernels for 4% -> 5%
where the time goes in v2:
time: 161 us; the launch traced here: 160 us
  starting transfers between devices  48.9 us (30%)
  blocking collectives  48 us (30%)
  waiting for transfers between devices  22.3 us (14%)
  between operations  15.8 us (10%)
  Pallas kernels  14.1 us (9%)
  local copies, waits for them, and re-layouts  9.11 us (6%)
  other arithmetic  1.7 us (1%)
    all_to_all x1, blocking collectives, on_device(): lax.all_to_all(both.reshape(chips, half // chips, features), ('g', 'yl',...  35.8 us
    ppermute x6, starting transfers between devices, from_peers(): lax.ppermute(rows(k), axis, [(i, (i + k) % ways) for i in range(ways)])  21.6 us
    all_to_all x1, blocking collectives, on_device(): lax.all_to_all(message, 'x', 0, 0)  12.2 us
    all_to_all x1, starting transfers between devices, gather_run(): lax.all_to_all(jnp.broadcast_to(shard[None], (spread, *shard.shape)), ('z...  10.4 us
    unnamed x40, local copies, waits for them, and re-layouts  8.01 us
    ppermute x1, waiting for transfers between devices, gather_runs(): lax.ppermute(lax.dynamic_slice_in_dim(run, own_c * half, half, 0), ('g',...  5.93 us
    ppermute x1, starting transfers between devices, gather_runs(): lax.ppermute(lax.dynamic_slice_in_dim(run, own_c * half, half, 0), ('g',...  5.33 us
    ppermute x6, waiting for transfers between devices, from_peers(): lax.ppermute(rows(k), axis, [(i, (i + k) % ways) for i in range(ways)])  5.2 us
  transfers between devices with their start and end apart: 14, of which 6 were waited for; matrix products, arithmetic and copies ran while one was open for 1% of the time, Pallas kernels for 5%

profile of v2, /device:TPU:16, one launch (start us, length us, event | category | flops | bytes accessed | tf_op | source)
XLA Modules:
  0.0 159.9 jit_solution(12110241167384692282)
XLA Ops:
  7.2 0.9 pad_maximum_fusion
  8.1 0.9 broadcast_in_dim.2
  9.0 10.4 %all-to-all-start = ((bf16[16,16,1024]{2,1,0:T(8,128)(2,1)}), bf16[16,16,1024]{2,1,0:T(8,128)(2,1)S(1)}, u32[]{:S(2)}, u32[]{:S(2)}) async-start(bf16[16,16,1024]{2,1,0:T(8,128)(2,1)} %broadcast_in_dim.2), calls=%async_computation | async-start | bytes 1048576 | tf_op jit(solution)/shard_map/all_to_all | solution.py:216
  20.9 2.7 %student_forward.1 = (bf16[256,768]{1,0:T(8,128)(2,1)S(1)}, bf16[2,512,256]{2,1,0:T(8,128)(2,1)S(1)}, bf16[256,576]{1,0:T(8,128)(2,1)S(1)}, bf16[256,192]{1,0:T(...) custom-call(s32[1]{0:T(128)S(6)} %copy.14.refs_0_, ...), custom_call_target="tpu_custom_call" | custom-call | flops 4000000000 | bytes 1000000 | tf_op jit(solution)/shard_map/student_forward/pallas_call | solution.py:289
  23.6 1.2 copy-done.8
  24.7 0.9 copy-done.12
  28.0 3.4 %collective-permute-start = (bf16[64,768]{1,0:T(8,128)(2,1)S(1)}, bf16[64,768]{1,0:T(8,128)(2,1)S(1)}, u32[]{:S(2)}, u32[]{:S(2)}) collective-permute-start(bf16[64,768]{1,0:T(8,128)(2,1)S(1)} %get-tuple-element.38), channel_id=1, source_target_pairs={{0,1},{1,2},{2,3},{3,0},{4,5},{5,6},{6,7},{7,4},{8,9},{9,10},{10,1... | collective-permute-start | bytes 294920 | tf_op jit(solution)/shard_map/ppermute | solution.py:251
  31.4 4.6 %collective-permute-start.1 = (bf16[64,768]{1,0:T(8,128)(2,1)S(1)}, bf16[64,768]{1,0:T(8,128)(2,1)S(1)}, u32[]{:S(2)}, u32[]{:S(2)}) collective-permute-start(bf16[64,768]{1,0:T(8,128)(2,1)S(1)} %get-tuple-element.40), channel_id=1, source_target_pairs={{0,2},{1,3},{2,0},{3,1},{4,6},{5,7},{6,4},{7,5},{8,10},{9,11},{10,... | collective-permute-start | bytes 294920 | tf_op jit(solution)/shard_map/ppermute | solution.py:251
  36.1 3.3 %collective-permute-start.2 = (bf16[64,768]{1,0:T(8,128)(2,1)S(1)}, bf16[64,768]{1,0:T(8,128)(2,1)S(1)}, u32[]{:S(2)}, u32[]{:S(2)}) collective-permute-start(bf16[64,768]{1,0:T(8,128)(2,1)S(1)} %get-tuple-element.39), channel_id=1, source_target_pairs={{0,3},{1,0},{2,1},{3,2},{4,7},{5,4},{6,5},{7,6},{8,11},{9,8},{10,9... | collective-permute-start | bytes 294920 | tf_op jit(solution)/shard_map/ppermute | solution.py:251
  39.7 5.0 %collective-permute-done.2 = bf16[64,768]{1,0:T(8,128)(2,1)S(1)} collective-permute-done((bf16[64,768]{1,0:T(8,128)(2,1)S(1)}, bf16[64,768]{1,0:T(8,128)(2,1)S(1)}, u32[]{:S(2)}, u32[]{:S(2)}) %collective-permute-start.2) | collective-permute-done | bytes 98336 | tf_op jit(solution)/shard_map/ppermute | solution.py:251
  44.7 2.4 %collective-permute-start.3 = (bf16[256,1024]{1,0:T(8,128)(2,1)S(1)}, bf16[256,1024]{1,0:T(8,128)(2,1)S(1)}, u32[]{:S(2)}, u32[]{:S(2)}) collective-permute-start(bf16[256,1024]{1,0:T(8,128)(2,1)S(1)} %bitcast.29), channel_id=1, source_target_pairs={{0,448},{4,68},{64,0},{68,132},{128,64},{132,196},{192,128},{196,2... | collective-permute-start | bytes 1572872 | tf_op jit(solution)/shard_map/ppermute | solution.py:230
  47.1 5.3 %collective-permute-start.5 = (bf16[128,1024]{1,0:T(8,128)(2,1)S(1)}, bf16[128,1024]{1,0:T(8,128)(2,1)S(1)}, u32[]{:S(2)}, u32[]{:S(2)}) collective-permute-start(bf16[128,1024]{1,0:T(8,128)(2,1)S(1)} %constant_dynamic-slice_fusion.1), channel_id=1, source_target_pairs={{0,384},{4,132},{64,448},{68,196},{128,0},{132,260},{192,64},{196,... | collective-permute-start | bytes 786440 | tf_op jit(solution)/shard_map/ppermute | solution.py:231
  52.4 3.3 %collective-permute-done.3.near_ref = bf16[256,1024]{1,0:T(8,128)(2,1)S(1)} collective-permute-done((bf16[256,1024]{1,0:T(8,128)(2,1)S(1)}, bf16[256,1024]{1,0:T(8,128)(2,1)S(1)}, u32[]{:S(2)}, u32[]{:S(2)}) %collective-permute-start.3) | collective-permute-done | bytes 524320 | tf_op jit(solution)/shard_map/ppermute | solution.py:230
  55.8 1.9 %collective-permute-start.4 = (bf16[256,1024]{1,0:T(8,128)(2,1)S(1)}, bf16[256,1024]{1,0:T(8,128)(2,1)S(1)}, u32[]{:S(2)}, u32[]{:S(2)}) collective-permute-start(bf16[256,1024]{1,0:T(8,128)(2,1)S(1)} %collective-permute-done.3.near_ref), channel_id=1, source_target_pairs={{0,4},{4,0},{1,5},{5,1},{2,6},{6,2},{3,7},{7,3},{8,12},{12,8},{9,1... | collective-permute-start | bytes 1572872 | tf_op jit(solution)/shard_map/ppermute | solution.py:233
  57.7 5.9 %collective-permute-done.5.far_ref = bf16[128,1024]{1,0:T(8,128)(2,1)S(1)} collective-permute-done((bf16[128,1024]{1,0:T(8,128)(2,1)S(1)}, bf16[128,1024]{1,0:T(8,128)(2,1)S(1)}, u32[]{:S(2)}, u32[]{:S(2)}) %collective-permute-start.5) | collective-permute-done | bytes 262176 | tf_op jit(solution)/shard_map/ppermute | solution.py:231
  63.6 1.9 %collective-permute-start.6 = (bf16[128,1024]{1,0:T(8,128)(2,1)S(1)}, bf16[128,1024]{1,0:T(8,128)(2,1)S(1)}, u32[]{:S(2)}, u32[]{:S(2)}) collective-permute-start(bf16[128,1024]{1,0:T(8,128)(2,1)S(1)} %collective-permute-done.5.far_ref), channel_id=1, source_target_pairs={{0,4},{4,0},{1,5},{5,1},{2,6},{6,2},{3,7},{7,3},{8,12},{12,8},{9,1... | collective-permute-start | bytes 786440 | tf_op jit(solution)/shard_map/ppermute | solution.py:234
  66.8 1.9 %collective-permute-start.7 = (bf16[64,768]{1,0:T(8,128)(2,1)S(1)}, bf16[64,768]{1,0:T(8,128)(2,1)S(1)}, u32[]{:S(2)}, u32[]{:S(2)}) collective-permute-start(bf16[64,768]{1,0:T(8,128)(2,1)S(1)} %fusion.1.refs_1_), channel_id=1, source_target_pairs={{0,1},{1,2},{2,3},{3,0},{4,5},{5,6},{6,7},{7,4},{8,9},{9,10},{10,1... | collective-permute-start | bytes 294920 | tf_op jit(solution)/shard_map/ppermute | solution.py:251
  68.8 6.4 %collective-permute-start.8 = (bf16[64,768]{1,0:T(8,128)(2,1)S(1)}, bf16[64,768]{1,0:T(8,128)(2,1)S(1)}, u32[]{:S(2)}, u32[]{:S(2)}) collective-permute-start(bf16[64,768]{1,0:T(8,128)(2,1)S(1)} %fusion.1.refs_1_), channel_id=1, source_target_pairs={{0,2},{1,3},{2,0},{3,1},{4,6},{5,7},{6,4},{7,5},{8,10},{9,11},{10,... | collective-permute-start | bytes 294920 | tf_op jit(solution)/shard_map/ppermute | solution.py:251
  75.2 1.9 %collective-permute-start.9 = (bf16[64,768]{1,0:T(8,128)(2,1)S(1)}, bf16[64,768]{1,0:T(8,128)(2,1)S(1)}, u32[]{:S(2)}, u32[]{:S(2)}) collective-permute-start(bf16[64,768]{1,0:T(8,128)(2,1)S(1)} %fusion.1.refs_1_), channel_id=1, source_target_pairs={{0,3},{1,0},{2,1},{3,2},{4,7},{5,4},{6,5},{7,6},{8,11},{9,8},{10,9... | collective-permute-start | bytes 294920 | tf_op jit(solution)/shard_map/ppermute | solution.py:251
  77.1 1.0 copy-done.19
  78.1 3.7 %teacher.1.refs_6_ = bf16[256,1024]{1,0:T(8,128)(2,1)} custom-call(s32[5]{0:T(128)S(1)} %stack.47.place_ref, s32[2]{0:T(128)S(1)} %bitcast.39, bf16[256,1024]{1,0:T(8,128)(2,1)S(1)} %copy-done.19, bf16[256,1024]{1,0:T(8,128)(2,1)S(1)} %bitcast.31, bf16[256,1024]{1,0:T(8,128)(2,1)S(1)} %collective-permute-done.3.near_ref, ...), custom_call_target="tpu_custom_call" | custom-call | flops 5000000000 | bytes 1000000 | tf_op jit(solution)/shard_map/teacher/pallas_call | solution.py:317
  81.9 3.5 %all-to-all-start.1 = ((bf16[4,64,1024]{2,1,0:T(8,128)(2,1)}), bf16[4,64,1024]{2,1,0:T(8,128)(2,1)S(1)}, u32[]{:S(2)}, u32[]{:S(2)}) async-start(bf16[4,64,1024]{2,1,0:T(8,128)(2,1)} %bitcast.17), calls=%async_computation.1 | async-start | bytes 1048576 | tf_op jit(solution)/shard_map/all_to_all | solution.py:331
  85.5 1.4 copy-done.2
  86.9 2.3 %student_features.1 = (bf16[2,3,512,256]{3,2,1,0:T(8,128)(2,1)S(1)}, f32[64,1024]{1,0:T(8,128)S(1)}) custom-call(s32[5]{0:T(128)S(1)} %stack.41.refs_0_.refs_1_, bf16[64,768]{1,0:T(8,128)(2,1)S(1)} %fusion.1.refs_1_, bf16[64,768]{1,0:T(8,128)(2,1)S(1)} %collective-permute-done.7.refs_2_, bf16[64,768]{1,0:T(8,128)(2,1)S(1)} %collective-permute-done.8.refs_3_, ...), custom_call_target="tpu_custom_call" | custom-call | flops 4000000000 | bytes 1000000 | tf_op jit(solution)/shard_map/student_features/pallas_call | solution.py:336
  89.2 1.1 copy-done.10
  90.3 4.8 %all-to-all-done.1.refs_2_ = bf16[4,64,1024]{2,1,0:T(8,128)(2,1)S(1)} async-done(((bf16[4,64,1024]{2,1,0:T(8,128)(2,1)}), bf16[4,64,1024]{2,1,0:T(8,128)(2,1)S(1)}, u32[]{:S(2)}, u32[]{:S(2)}) %all-to-all-start.1) | async-done | bytes 524320 | tf_op jit(solution)/shard_map/all_to_all | solution.py:331
  95.2 1.1 difference.1
  96.4 12.2 %all_to_all.20 = bf16[4,64,1152]{2,1,0:T(8,128)(2,1)S(1)} all-to-all(bf16[4,64,1152]{2,1,0:T(8,128)(2,1)S(1)} %difference.1), channel_id=1, replica_groups=mesh['g'=2,'yl'=4,'z'=8,'c'=2,'x'=4] {'x'}, dimensions={0} | all-to-all | bytes 1179648 | tf_op jit(solution)/shard_map/all_to_all | solution.py:357
  108.6 3.5 %student_backward.1 = (bf16[512,768]{1,0:T(8,128)(2,1)S(1)}, bf16[512,768]{1,0:T(8,128)(2,1)S(1)}, f32[1,1]{1,0:T(1,128)}) custom-call(bf16[256,1152]{1,0:T(8,128)(2,1)S(1)} %bitcast.32, bf16[256,576]{1,0:T(8,128)(2,1)S(1)} %copy-done.17, f32[3,256,256]{2,1,0:T(8,128)S(1)} %copy-done.13, bf16[256,192]{1,0:T(8,128)(2,1)S(1)} %get-tuple-element.28.mixed_ref, ...), custom_call_target="tpu_custom_call" | custom-call | flops 4000000000 | bytes 1000000 | tf_op jit(solution)/shard_map/student_backward/pallas_call | solution.py:359
  112.1 1.9 %collective-permute-start.10 = (bf16[512,768]{1,0:T(8,128)(2,1)S(1)}, bf16[512,768]{1,0:T(8,128)(2,1)S(1)}, u32[]{:S(2)}, u32[]{:S(2)}) collective-permute-start(bf16[512,768]{1,0:T(8,128)(2,1)S(1)} %get-tuple-element.34), channel_id=1, source_target_pairs={{0,4},{4,0},{1,5},{5,1},{2,6},{6,2},{3,7},{7,3},{8,12},{12,8},{9,1... | collective-permute-start | bytes 2359304 | tf_op jit(solution)/shard_map/ppermute | solution.py:370
  114.0 2.3 %collective-permute-done.10 = bf16[512,768]{1,0:T(8,128)(2,1)S(1)} collective-permute-done((bf16[512,768]{1,0:T(8,128)(2,1)S(1)}, bf16[512,768]{1,0:T(8,128)(2,1)S(1)}, u32[]{:S(2)}, u32[]{:S(2)}) %collective-permute-start.10) | collective-permute-done | bytes 786464 | tf_op jit(solution)/shard_map/ppermute | solution.py:370
  116.5 35.8 %all_to_all.21.parts_ref = bf16[64,8,768]{2,1,0:T(8,128)(2,1)S(1)} all-to-all(bf16[64,8,768]{2,1,0:T(8,128)(2,1)S(1)} %fusion), channel_id=1, replica_groups=mesh['g'=2,'yl'=4,'z'=8,'c'=2,'x'=4] {'g','yl','z'}, dimensions={0} | all-to-all | bytes 1572864 | tf_op jit(solution)/shard_map/all_to_all | solution.py:371
  (55 shorter events, 5.2 us)
Async XLA Ops:
  7.2 13.7 %copy-start.1 = (bf16[1,256,768]{2,1,0:T(8,128)(2,1)S(1)}, bf16[1,256,768]{2,1,0:T(8,128)(2,1)}, u32[]{:S(2)}) copy-start(bf16[1,256,768]{2,1,0:T(8,128)(2,1)} %param.14) | copy-start | bytes 1179652
  7.2 13.7 %copy-start.4 = (bf16[768,576]{0,1:T(8,128)(2,1)S(1)}, bf16[768,576]{0,1:T(8,128)(2,1)}, u32[]{:S(2)}) copy-start(bf16[768,576]{0,1:T(8,128)(2,1)} %param.17) | copy-start | bytes 2654212
  7.2 13.7 %copy-start = (bf16[1,256,1024]{2,1,0:T(8,128)(2,1)S(1)}, bf16[1,256,1024]{2,1,0:T(8,128)(2,1)}, u32[]{:S(2)}) copy-start(bf16[1,256,1024]{2,1,0:T(8,128)(2,1)} %param.10) | copy-start | bytes 1572868
  7.2 13.7 %copy-start.6 = (f32[1024]{0:T(1024)S(1)}, f32[1024]{0:T(1024)}, u32[]{:S(2)}) copy-start(f32[1024]{0:T(1024)} %param.11) | copy-start | bytes 12292
  7.2 13.7 %copy-start.5 = (bf16[192,768]{1,0:T(8,128)(2,1)S(1)}, bf16[192,768]{1,0:T(8,128)(2,1)}, u32[]{:S(2)}) copy-start(bf16[192,768]{1,0:T(8,128)(2,1)} %out_ref.1) | copy-start | bytes 884740
  9.0 35.7 %all-to-all-start = ((bf16[16,16,1024]{2,1,0:T(8,128)(2,1)}), bf16[16,16,1024]{2,1,0:T(8,128)(2,1)S(1)}, u32[]{:S(2)}, u32[]{:S(2)}) async-start(bf16[16,16,1024]{2,1,0:T(8,128)(2,1)} %broadcast_in_dim.2), calls=%async_computation | async-start | bytes 1048576 | tf_op jit(solution)/shard_map/all_to_all | solution.py:216
  19.4 66.1 %all-gather.3.cloned.1.call-start = ((), (), s32[]{:S(2)}) async-start(), calls=%async_computation.4 | async-start | bytes 1966080 | tf_op jit(solution)/shard_map/all_gather | solution.py:307
  23.6 1.2 copy-start.8
  24.7 0.9 copy-start.12
  25.7 0.8 copy-start.14
  28.0 37.6 %copy-start.7 = (s32[1,2]{1,0:T(1,128)S(1)}, s32[1,2]{1,0:T(1,128)}, u32[]{:S(2)}) copy-start(s32[1,2]{1,0:T(1,128)} %param.16) | copy-start | bytes 28
  28.0 11.4 %collective-permute-start = (bf16[64,768]{1,0:T(8,128)(2,1)S(1)}, bf16[64,768]{1,0:T(8,128)(2,1)S(1)}, u32[]{:S(2)}, u32[]{:S(2)}) collective-permute-start(bf16[64,768]{1,0:T(8,128)(2,1)S(1)} %get-tuple-element.38), channel_id=1, source_target_pairs={{0,1},{1,2},{2,3},{3,0},{4,5},{5,6},{6,7},{7,4},{8,9},{9,10},{10,1... | collective-permute-start | bytes 294920 | tf_op jit(solution)/shard_map/ppermute | solution.py:251
  31.4 8.2 %collective-permute-start.1 = (bf16[64,768]{1,0:T(8,128)(2,1)S(1)}, bf16[64,768]{1,0:T(8,128)(2,1)S(1)}, u32[]{:S(2)}, u32[]{:S(2)}) collective-permute-start(bf16[64,768]{1,0:T(8,128)(2,1)S(1)} %get-tuple-element.40), channel_id=1, source_target_pairs={{0,2},{1,3},{2,0},{3,1},{4,6},{5,7},{6,4},{7,5},{8,10},{9,11},{10,... | collective-permute-start | bytes 294920 | tf_op jit(solution)/shard_map/ppermute | solution.py:251
  36.1 8.6 %collective-permute-start.2 = (bf16[64,768]{1,0:T(8,128)(2,1)S(1)}, bf16[64,768]{1,0:T(8,128)(2,1)S(1)}, u32[]{:S(2)}, u32[]{:S(2)}) collective-permute-start(bf16[64,768]{1,0:T(8,128)(2,1)S(1)} %get-tuple-element.39), channel_id=1, source_target_pairs={{0,3},{1,0},{2,1},{3,2},{4,7},{5,4},{6,5},{7,6},{8,11},{9,8},{10,9... | collective-permute-start | bytes 294920 | tf_op jit(solution)/shard_map/ppermute | solution.py:251
  44.7 11.1 %collective-permute-start.3 = (bf16[256,1024]{1,0:T(8,128)(2,1)S(1)}, bf16[256,1024]{1,0:T(8,128)(2,1)S(1)}, u32[]{:S(2)}, u32[]{:S(2)}) collective-permute-start(bf16[256,1024]{1,0:T(8,128)(2,1)S(1)} %bitcast.29), channel_id=1, source_target_pairs={{0,448},{4,68},{64,0},{68,132},{128,64},{132,196},{192,128},{196,2... | collective-permute-start | bytes 1572872 | tf_op jit(solution)/shard_map/ppermute | solution.py:230
  47.1 16.5 %collective-permute-start.5 = (bf16[128,1024]{1,0:T(8,128)(2,1)S(1)}, bf16[128,1024]{1,0:T(8,128)(2,1)S(1)}, u32[]{:S(2)}, u32[]{:S(2)}) collective-permute-start(bf16[128,1024]{1,0:T(8,128)(2,1)S(1)} %constant_dynamic-slice_fusion.1), channel_id=1, source_target_pairs={{0,384},{4,132},{64,448},{68,196},{128,0},{132,260},{192,64},{196,... | collective-permute-start | bytes 786440 | tf_op jit(solution)/shard_map/ppermute | solution.py:231
  55.8 21.3 %collective-permute-start.4 = (bf16[256,1024]{1,0:T(8,128)(2,1)S(1)}, bf16[256,1024]{1,0:T(8,128)(2,1)S(1)}, u32[]{:S(2)}, u32[]{:S(2)}) collective-permute-start(bf16[256,1024]{1,0:T(8,128)(2,1)S(1)} %collective-permute-done.3.near_ref), channel_id=1, source_target_pairs={{0,4},{4,0},{1,5},{5,1},{2,6},{6,2},{3,7},{7,3},{8,12},{12,8},{9,1... | collective-permute-start | bytes 1572872 | tf_op jit(solution)/shard_map/ppermute | solution.py:233
  63.6 13.5 %collective-permute-start.6 = (bf16[128,1024]{1,0:T(8,128)(2,1)S(1)}, bf16[128,1024]{1,0:T(8,128)(2,1)S(1)}, u32[]{:S(2)}, u32[]{:S(2)}) collective-permute-start(bf16[128,1024]{1,0:T(8,128)(2,1)S(1)} %collective-permute-done.5.far_ref), channel_id=1, source_target_pairs={{0,4},{4,0},{1,5},{5,1},{2,6},{6,2},{3,7},{7,3},{8,12},{12,8},{9,1... | collective-permute-start | bytes 786440 | tf_op jit(solution)/shard_map/ppermute | solution.py:234
  66.8 18.7 %collective-permute-start.7 = (bf16[64,768]{1,0:T(8,128)(2,1)S(1)}, bf16[64,768]{1,0:T(8,128)(2,1)S(1)}, u32[]{:S(2)}, u32[]{:S(2)}) collective-permute-start(bf16[64,768]{1,0:T(8,128)(2,1)S(1)} %fusion.1.refs_1_), channel_id=1, source_target_pairs={{0,1},{1,2},{2,3},{3,0},{4,5},{5,6},{6,7},{7,4},{8,9},{9,10},{10,1... | collective-permute-start | bytes 294920 | tf_op jit(solution)/shard_map/ppermute | solution.py:251
  68.8 16.7 %collective-permute-start.8 = (bf16[64,768]{1,0:T(8,128)(2,1)S(1)}, bf16[64,768]{1,0:T(8,128)(2,1)S(1)}, u32[]{:S(2)}, u32[]{:S(2)}) collective-permute-start(bf16[64,768]{1,0:T(8,128)(2,1)S(1)} %fusion.1.refs_1_), channel_id=1, source_target_pairs={{0,2},{1,3},{2,0},{3,1},{4,6},{5,7},{6,4},{7,5},{8,10},{9,11},{10,... | collective-permute-start | bytes 294920 | tf_op jit(solution)/shard_map/ppermute | solution.py:251
  75.2 10.3 %collective-permute-start.9 = (bf16[64,768]{1,0:T(8,128)(2,1)S(1)}, bf16[64,768]{1,0:T(8,128)(2,1)S(1)}, u32[]{:S(2)}, u32[]{:S(2)}) collective-permute-start(bf16[64,768]{1,0:T(8,128)(2,1)S(1)} %fusion.1.refs_1_), channel_id=1, source_target_pairs={{0,3},{1,0},{2,1},{3,2},{4,7},{5,4},{6,5},{7,6},{8,11},{9,8},{10,9... | collective-permute-start | bytes 294920 | tf_op jit(solution)/shard_map/ppermute | solution.py:251
  77.1 1.0 copy-start.19
  81.9 13.3 %all-to-all-start.1 = ((bf16[4,64,1024]{2,1,0:T(8,128)(2,1)}), bf16[4,64,1024]{2,1,0:T(8,128)(2,1)S(1)}, u32[]{:S(2)}, u32[]{:S(2)}) async-start(bf16[4,64,1024]{2,1,0:T(8,128)(2,1)} %bitcast.17), calls=%async_computation.1 | async-start | bytes 1048576 | tf_op jit(solution)/shard_map/all_to_all | solution.py:331
  85.5 1.4 copy-start.2
  86.9 8.2 %copy-start.3 = (bf16[3072,256]{1,0:T(8,128)(2,1)S(1)}, bf16[3072,256]{1,0:T(8,128)(2,1)}, u32[]{:S(2)}) copy-start(bf16[3072,256]{1,0:T(8,128)(2,1)} %all-gather.3.cloned.1.call-done) | copy-start | bytes 4718596
  89.2 1.1 copy-start.10
  95.2 13.4 %copy-start.9 = (bf16[2,512,768]{2,1,0:T(8,128)(2,1)S(1)}, bf16[2,512,768]{2,1,0:T(8,128)(2,1)}, u32[]{:S(2)}) copy-start(bf16[2,512,768]{2,1,0:T(8,128)(2,1)} %copy-done.8) | copy-start | bytes 4718596
  95.2 13.4 %copy-start.11 = (bf16[2,3,512,256]{3,2,1,0:T(8,128)(2,1)S(1)}, bf16[2,3,512,256]{3,2,1,0:T(8,128)(2,1)}, u32[]{:S(2)}) copy-start(bf16[2,3,512,256]{3,2,1,0:T(8,128)(2,1)} %copy-done.10) | copy-start | bytes 4718596
  95.2 13.4 %copy-start.13 = (f32[3,256,256]{2,1,0:T(8,128)S(1)}, f32[3,256,256]{2,1,0:T(8,128)}, u32[]{:S(2)}) copy-start(f32[3,256,256]{2,1,0:T(8,128)} %copy-done.12) | copy-start | bytes 2359300
  95.2 13.4 %copy-start.15 = (bf16[2,512,256]{2,1,0:T(8,128)(2,1)S(1)}, bf16[2,512,256]{2,1,0:T(8,128)(2,1)}, u32[]{:S(2)}) copy-start(bf16[2,512,256]{2,1,0:T(8,128)(2,1)} %copy-done.14) | copy-start | bytes 1572868
  95.2 13.4 %copy-start.17 = (bf16[256,576]{1,0:T(8,128)(2,1)S(1)}, bf16[256,576]{1,0:T(8,128)(2,1)}, u32[]{:S(2)}) copy-start(bf16[256,576]{1,0:T(8,128)(2,1)} %copy-done.16) | copy-start | bytes 884740
  112.1 4.2 %collective-permute-start.10 = (bf16[512,768]{1,0:T(8,128)(2,1)S(1)}, bf16[512,768]{1,0:T(8,128)(2,1)S(1)}, u32[]{:S(2)}, u32[]{:S(2)}) collective-permute-start(bf16[512,768]{1,0:T(8,128)(2,1)S(1)} %get-tuple-element.34), channel_id=1, source_target_pairs={{0,4},{4,0},{1,5},{5,1},{2,6},{6,2},{3,7},{7,3},{8,12},{12,8},{9,1... | collective-permute-start | bytes 2359304 | tf_op jit(solution)/shard_map/ppermute | solution.py:370
  (2 other events, 1.5 us)
Sparse Core Ops, SparseCore 0:
  22.3 33.1 all-gather.2

commit v3 on v2

--- a/solution.py
+++ b/solution.py
@@ -9,7 +9,10 @@
 BLOCK = 128
 F32 = jnp.float32
 BF16 = jnp.bfloat16
-CLIP = ("g", "yl", "z", "c")
+CLIP = ("g", "yh", "y0", "zh", "z0", "c")
+Y, Z = CLIP[:3], CLIP[3:5]
+FAR = ("g", "yh", "zh")
+ANY = pl.BlockSpec(memory_space=pl.ANY)
 VMEM = pl.BlockSpec(memory_space=pltpu.VMEM)
 SMEM = pl.BlockSpec(memory_space=pltpu.SMEM)
 PARAMS = pltpu.CompilerParams(vmem_limit_bytes=20 * 1024 * 1024)
@@ -53,11 +56,15 @@
     return weights / jnp.sum(weights, -1, keepdims=True)
 
 
-def pick_rows(rows, shares, columns, core, extra):
+def pick_rows(rows, shares, run, columns, core, extra):
     each = rows // shares
     block = each + each * columns // rows
     place = lax.broadcasted_iota(jnp.int32, (shares // 2 * block, 1), 0)
-    chip, row = place // block, place % block
+    order, row = place // block, place % block
+    others = shares // 8
+    first, second, rest = order // (2 * others), order // others % 2, order % others
+    low_y, low_z = first + core * (second - first), second + core * (first - second)
+    chip = (rest // (run // 2) * 2 + low_y) * run + rest % (run // 2) * 2 + low_z
     base = (chip * 2 + core) * each
     if extra is None:
         wanted = jnp.where(row < each, base + row, -1)
@@ -68,15 +75,15 @@
 
 
 def student_kernel(
-    shares, count_ref, core_ref, events_ref, qkv_ref, out_ref, clip_ref, gain_ref,
-    part_ref, normed_ref, packed_ref, mixed_ref, weights_ref, teacher_ref, pick_ref,
+    shares, run, columns, count_ref, core_ref, events_ref, qkv_ref, out_ref,
+    part_ref, normed_ref, packed_ref, mixed_ref, weights_ref, pick_ref,
 ):
     length, features = events_ref.shape
     heads = out_ref.shape[0] // HEAD
     normed = norm_rows(events_ref[...]).astype(BF16)
     for half in range(2):
         core = core_ref[0] if half == 0 else 1 - core_ref[0]
-        pick_ref[half] = pick_rows(features, shares, clip_ref.shape[1] // 4, core, None)
+        pick_ref[half] = pick_rows(features, shares, run, columns, core, None)
         normed_ref[half] = nt(pick_ref[half], normed).astype(BF16)
     packed = nt(normed, qkv_ref[...])
     packed_ref[...] = packed.astype(BF16)
@@ -91,7 +98,10 @@
     mixed = jnp.concatenate(mixed, axis=1).astype(BF16)
     mixed_ref[...] = mixed
     part_ref[...] = nn(mixed, out_ref[...]).astype(BF16)
-    teacher_ref[...] = (norm_rows(clip_ref[...]) * gain_ref[...]).astype(BF16)
+
+
+def teacher_norm_kernel(clip_ref, gain_ref, after_ref, normed_ref):
+    normed_ref[...] = (norm_rows(clip_ref[...]) * gain_ref[...]).astype(BF16)
 
 
 def teacher_kernel(
@@ -119,20 +129,17 @@
         ).astype(BF16)
 
 
-def feature_kernel(shares, ways, place_ref, *refs):
-    feat_refs = refs[:ways]
-    proj_ref, after_ref, extra_ref, pred_ref, feat_ref = refs[ways:]
-    features, columns = proj_ref.shape[1:]
-    rows = feat_refs[0].shape[0]
+def feature_kernel(
+    shares, run, place_ref, feat_ref, rows_ref, proj_ref, after_ref, extra_ref, pred_ref
+):
+    ways, features, columns = proj_ref.shape
     for k in range(ways):
-        source = place_ref[1 + k]
-        feat_ref[pl.ds(pl.multiple_of(source * rows, rows), rows), :] = feat_refs[k][...]
-        pred_ref[:, k * columns : (k + 1) * columns] = nn(feat_refs[0][...], proj_ref[k])
+        pred_ref[:, k * columns : (k + 1) * columns] = nn(rows_ref[...], proj_ref[k])
     feat = feat_ref[...]
     for half in range(2):
         core = place_ref[0] if half == 0 else 1 - place_ref[0]
         for b in range(features // columns):
-            pick = pick_rows(features, shares, columns, core, b)
+            pick = pick_rows(features, shares, run, columns, core, b)
             extra_ref[half, b] = nt(pick, feat).astype(BF16)
 
 
@@ -211,28 +218,39 @@
             into[:, block] = total.astype(BF16)
 
 
+def axes_size(axes):
+    size = 1
+    for axis in axes:
+        size = size * lax.axis_size(axis)
+    return size
+
+
+def share(rows, axes):
+    return lax.all_to_all(
+        jnp.broadcast_to(rows[None], (axes_size(axes), *rows.shape)), axes, 0, 0
+    )
+
+
 def gather_run(shard):
-    spread = lax.axis_size("z") * lax.axis_size("c")
-    return lax.all_to_all(
-        jnp.broadcast_to(shard[None], (spread, *shard.shape)), ("z", "c"), 0, 0
-    ).reshape(spread * shard.shape[0], shard.shape[1])
+    runs = share(shard, (*Z, "c"))
+    return runs.reshape(runs.shape[0] * runs.shape[1], runs.shape[2])
 
 
 def gather_runs(run, own_c, own_yl):
     size = run.shape[0]
     half = size // 2
-    ring = lax.axis_size("g") * lax.axis_size("yl")
+    ring = axes_size(Y)
     near, far = [], []
     for y in range(ring):
         for c, sign in ((0, -1), (1, 1)):
             near.append((y * 2 + c, (y + sign) % ring * 2 + c))
             far.append((y * 2 + c, (y + 2 * sign) % ring * 2 + c))
-    first = lax.ppermute(run, ("g", "yl", "c"), near)
-    second = lax.ppermute(lax.dynamic_slice_in_dim(run, own_c * half, half, 0), ("g", "yl", "c"), far)
+    first = lax.ppermute(run, (*Y, "c"), near)
+    second = lax.ppermute(lax.dynamic_slice_in_dim(run, own_c * half, half, 0), (*Y, "c"), far)
     swap = [(0, 1), (1, 0)]
     first_other = lax.ppermute(first, "c", swap)
     second_other = lax.ppermute(second, "c", swap)
-    ways = lax.axis_size("yl")
+    ways = axes_size(Y[1:])
     step = 1 - 2 * own_c
     opposite = (own_yl + 2) % ways * size
     place = jnp.stack([
@@ -253,6 +271,10 @@
     ]
 
 
+def add(a, b):
+    return a.astype(F32) + b.astype(F32)
+
+
 def result_kernel(parts_ref, q_ref, o_ref, p_ref):
     each, used = q_ref.shape
     columns = p_ref.shape[1]
@@ -275,10 +297,10 @@
     columns = projector.shape[1]
     ways = lax.axis_size("x")
     rows = length // ways
-    own_c, own_yl, own_x = lax.axis_index("c"), lax.axis_index("yl"), lax.axis_index("x")
-    shares = 1
-    for axis in CLIP:
-        shares = shares * lax.axis_size(axis)
+    own_c, own_x = lax.axis_index("c"), lax.axis_index("x")
+    own_y, own_z = lax.axis_index("y0"), lax.axis_index("z0")
+    own_yl = lax.axis_index("yh") * 2 + own_y
+    shares, along_z = axes_size(CLIP), axes_size(Z)
 
     run = gather_run(jnp.concatenate([teacher_qkv, teacher_out_t], 1))
 
@@ -286,33 +308,42 @@
     each = features // shares
     half = shares // 2 * (each + each * columns // features)
     core = own_c.astype(jnp.int32).reshape(1)
-    part, normed_rows, packed, mixed, weights, teacher_normed, pick = pl.pallas_call(
-        lambda *refs: student_kernel(shares, *refs),
+    part, normed_rows, packed, mixed, weights, pick = pl.pallas_call(
+        lambda *refs: student_kernel(shares, along_z, columns, *refs),
         out_shape=(
             shape((length, features), BF16),
-            shape((2, half, length), BF16),
-            shape((length, 3 * HEAD * heads), BF16),
-            shape((length, HEAD * heads), BF16),
-            shape((heads, length, length), F32),
-            shape((length, width), BF16),
-            shape((2, half, features), BF16),
+            pltpu.HBM((2, half, length), BF16),
+            pltpu.HBM((length, 3 * HEAD * heads), BF16),
+            pltpu.HBM((length, HEAD * heads), BF16),
+            pltpu.HBM((heads, length, length), F32),
+            pltpu.HBM((2, half, features), BF16),
         ),
-        in_specs=[SMEM] * 2 + [VMEM] * 5,
-        out_specs=(VMEM,) * 7,
+        in_specs=[SMEM] * 2 + [VMEM] * 3,
+        out_specs=(VMEM,) + (pl.BlockSpec(),) * 5,
         compiler_params=PARAMS,
         cost_estimate=cost(4),
         name="student_forward",
-    )(valid_counts, core, events, student_qkv.T, student_out, clip, teacher_gain.reshape(1, width))
+    )(valid_counts, core, events, student_qkv.T, student_out)
 
     whole_proj = lax.all_gather(projector, "x", axis=0, tiled=False)
     own_rows = lambda array, place: lax.dynamic_slice_in_dim(array, place * rows, rows, 0)
     branch = own_rows(part, own_x).astype(F32)
-    for received in from_peers(lambda k: own_rows(part, (own_x + k) % ways), "x"):
-        branch = branch + received.astype(F32)
+    received = from_peers(lambda k: own_rows(part, (own_x + k) % ways), "x")
+    run, received = lax.optimization_barrier((run, received))
+    for other in received:
+        branch = branch + other.astype(F32)
     feat_rows = (own_rows(events, own_x).astype(F32) + branch).astype(BF16)
-    run, feat_rows = lax.optimization_barrier((run, feat_rows))
     place, pieces = gather_runs(run, own_c, own_yl)
-    feats = [feat_rows] + from_peers(lambda k: feat_rows, "x")
+    feat = share(feat_rows, "x").reshape(length, features)
+    teacher_normed = pl.pallas_call(
+        teacher_norm_kernel,
+        out_shape=shape((length, width), BF16),
+        in_specs=[VMEM] * 2 + [ANY],
+        out_specs=VMEM,
+        compiler_params=PARAMS,
+        cost_estimate=cost(1),
+        name="teacher_norm",
+    )(clip, teacher_gain.reshape(1, width), pieces[1])
 
     teacher_part = pl.pallas_call(
         teacher_kernel,
@@ -332,19 +363,18 @@
     per_block = BLOCK // rows
     source = align[own_x // per_block] * BLOCK + own_x % per_block * rows
     own_tokens = lax.dynamic_slice_in_dim(clip, source, rows, 0)
-    places = jnp.stack([own_c] + [(own_x - k + ways) % ways for k in range(ways)]).astype(jnp.int32)
+    places = jnp.stack([own_c, own_x]).astype(jnp.int32)
     feat_extra, pred = pl.pallas_call(
-        lambda *refs: feature_kernel(shares, ways, *refs),
+        lambda *refs: feature_kernel(shares, along_z, *refs),
         out_shape=(
-            shape((2, features // columns, half, length), BF16), shape((rows, width), F32),
+            pltpu.HBM((2, features // columns, half, length), BF16), shape((rows, width), F32),
         ),
-        in_specs=[SMEM] + [VMEM] * (ways + 1) + [pl.BlockSpec(memory_space=pl.ANY)],
-        out_specs=(VMEM,) * 2,
-        scratch_shapes=[pltpu.VMEM((length, features), BF16)],
+        in_specs=[SMEM] + [VMEM] * 3 + [ANY],
+        out_specs=(pl.BlockSpec(), VMEM),
         compiler_params=PARAMS,
         cost_estimate=cost(4),
         name="student_features",
-    )(places, *feats, whole_proj, teacher_part)
+    )(places, feat, feat_rows, whole_proj, teacher_part)
     message = pl.pallas_call(
         lambda *refs: diff_kernel(shares, *refs),
         out_shape=shape((ways, rows, features + columns + BLOCK), BF16),
@@ -366,9 +396,22 @@
         name="student_backward",
     )(back, packed, weights, mixed, student_out, pick, normed_rows, feat_extra)
 
-    chips = shares // 2
-    both = (keep.astype(F32) + lax.ppermute(send, "c", [(0, 1), (1, 0)]).astype(F32)).astype(BF16)
-    spread = lax.all_to_all(both.reshape(chips, half // chips, features), ("g", "yl", "z"), 0, 0)
+    total = add(keep, lax.ppermute(send, "c", [(0, 1), (1, 0)]))
+    for step in range(2):
+        bit = jnp.where(own_c == step, own_y, own_z)
+        parts = total.reshape(2, total.shape[0] // 2, features)
+        partners = []
+        for y in range(2):
+            for z in range(2):
+                for c in range(2):
+                    other = (1 - y, z) if c == step else (y, 1 - z)
+                    partners.append(((y * 2 + z) * 2 + c, (other[0] * 2 + other[1]) * 2 + c))
+        away = lax.dynamic_index_in_dim(parts, 1 - bit, 0, False).astype(BF16)
+        stay = lax.dynamic_index_in_dim(parts, bit, 0, False)
+        total = add(stay, lax.ppermute(away, ("y0", "z0", "c"), partners))
+    far = axes_size(FAR)
+    total = total.astype(BF16).reshape(far, total.shape[0] // far, features)
+    spread = lax.all_to_all(total, FAR, 0, 0)
     used = 3 * HEAD * heads
     grad_q, grad_o, grad_p = pl.pallas_call(
         result_kernel,
@@ -385,8 +428,9 @@
 
 
 def solution(mesh):
-    sizes = mesh.devices.shape
-    fine = Mesh(mesh.devices.reshape(sizes[0], 4, sizes[1] // 8, 2, sizes[2]), (*CLIP, "x"))
+    group, dp, tensor = mesh.devices.shape
+    devices = mesh.devices.reshape(group, 2, 2, dp // 16, 2, 2, tensor)
+    fine = Mesh(devices, (*CLIP, "x"))
     dp = CLIP[1:]
     in_specs = (
         P(CLIP, None, None), P(), P(dp, "x"), P(dp, "x"), P(CLIP, None, None), P(CLIP), P(CLIP, None),

time: 161 us -> 156 us (0.969)
  the two profiles are of different devices: /device:TPU:16 before, /device:TPU:2 now
where the time goes in v3:
time: 156 us; the launch traced here: 155 us
  starting transfers between devices  52 us (33%)
  blocking collectives  34.9 us (22%)
  waiting for transfers between devices  27.9 us (18%)
  Pallas kernels  17.9 us (11%)
  between operations  15.8 us (10%)
  local copies, waits for them, and re-layouts  4.02 us (3%)
  other arithmetic  2.81 us (2%)
    all_to_all x1, blocking collectives, on_device(): spread = lax.all_to_all(total, FAR, 0, 0)  23.5 us
    all_to_all x2, starting transfers between devices, share(): lax.all_to_all(jnp.broadcast_to(rows[None], (axes_size(axes), *rows.shape...  15.7 us
    ppermute x2, waiting for transfers between devices, on_device(): total = add(stay, lax.ppermute(away, ('y0', 'z0', 'c'), partners))  11.5 us
    all_to_all x1, blocking collectives, on_device(): lax.all_to_all(message, 'x', 0, 0)  11.3 us
    ppermute x3, starting transfers between devices, from_peers(): lax.ppermute(rows(k), axis, [(i, (i + k) % ways) for i in range(ways)])  10.5 us
    ppermute x2, starting transfers between devices, on_device(): total = add(stay, lax.ppermute(away, ('y0', 'z0', 'c'), partners))  5.75 us
    ppermute x1, starting transfers between devices, gather_runs(): first = lax.ppermute(run, (*Y, 'c'), near)  5.36 us
    all_to_all x1, starting transfers between devices, on_device(): lax.all_to_all(teacher_part.reshape(ways, rows, width), 'x', 0, 0)  4.9 us
  transfers between devices with their start and end apart: 14, of which 9 were waited for; matrix products, arithmetic and copies ran while one was open for 2% of the time, Pallas kernels for 8%

profile of v3, /device:TPU:2, one launch (start us, length us, event | category | flops | bytes accessed | tf_op | source)
XLA Modules:
  0.0 155.3 jit_solution(1280400491190148805)
XLA Ops:
  7.2 0.9 pad_maximum_fusion
  8.9 10.4 %all-to-all-start = ((bf16[16,16,1024]{2,1,0:T(8,128)(2,1)}), bf16[16,16,1024]{2,1,0:T(8,128)(2,1)S(1)}, u32[]{:S(2)}, u32[]{:S(2)}) async-start(bf16[16,16,1024]{2,1,0:T(8,128)(2,1)} %broadcast_in_dim.4), calls=%async_computation | async-start | bytes 1048576 | tf_op jit(solution)/shard_map/all_to_all | solution.py:229
  20.8 4.3 %student_forward.1 = (bf16[256,768]{1,0:T(8,128)(2,1)S(1)}, bf16[2,512,256]{2,1,0:T(8,128)(2,1)}, bf16[256,576]{1,0:T(8,128)(2,1)}, bf16[256,192]{1,0:T(8,128)(2...) custom-call(s32[1]{0:T(128)S(6)} %copy.14.refs_0_, s32[1]{0:T(128)} %bitcast.refs_1_, ...), custom_call_target="tpu_custom_call" | custom-call | flops 4000000000 | bytes 1000000 | tf_op jit(solution)/shard_map/student_forward/pallas_call | solution.py:311
  25.1 3.4 %collective-permute-start = (bf16[64,768]{1,0:T(8,128)(2,1)S(1)}, bf16[64,768]{1,0:T(8,128)(2,1)S(1)}, u32[]{:S(2)}, u32[]{:S(2)}) collective-permute-start(bf16[64,768]{1,0:T(8,128)(2,1)S(1)} %get-tuple-element.42), channel_id=1, source_target_pairs={{0,1},{1,2},{2,3},{3,0},{4,5},{5,6},{6,7},{7,4},{8,9},{9,10},{10,1... | collective-permute-start | bytes 294920 | tf_op jit(solution)/shard_map/ppermute | solution.py:269
  28.5 3.0 %collective-permute-start.1 = (bf16[64,768]{1,0:T(8,128)(2,1)S(1)}, bf16[64,768]{1,0:T(8,128)(2,1)S(1)}, u32[]{:S(2)}, u32[]{:S(2)}) collective-permute-start(bf16[64,768]{1,0:T(8,128)(2,1)S(1)} %get-tuple-element.41), channel_id=1, source_target_pairs={{0,2},{1,3},{2,0},{3,1},{4,6},{5,7},{6,4},{7,5},{8,10},{9,11},{10,... | collective-permute-start | bytes 294920 | tf_op jit(solution)/shard_map/ppermute | solution.py:269
  31.6 4.1 %collective-permute-start.2 = (bf16[64,768]{1,0:T(8,128)(2,1)S(1)}, bf16[64,768]{1,0:T(8,128)(2,1)S(1)}, u32[]{:S(2)}, u32[]{:S(2)}) collective-permute-start(bf16[64,768]{1,0:T(8,128)(2,1)S(1)} %get-tuple-element.40), channel_id=1, source_target_pairs={{0,3},{1,0},{2,1},{3,2},{4,7},{5,4},{6,5},{7,6},{8,11},{9,8},{10,9... | collective-permute-start | bytes 294920 | tf_op jit(solution)/shard_map/ppermute | solution.py:269
  35.6 1.3 collective-permute-done.1
  36.9 1.9 %collective-permute-done.2 = bf16[64,768]{1,0:T(8,128)(2,1)S(1)} collective-permute-done((bf16[64,768]{1,0:T(8,128)(2,1)S(1)}, bf16[64,768]{1,0:T(8,128)(2,1)S(1)}, u32[]{:S(2)}, u32[]{:S(2)}) %collective-permute-start.2) | collective-permute-done | bytes 98336 | tf_op jit(solution)/shard_map/ppermute | solution.py:269
  38.9 5.4 %collective-permute-start.3 = (bf16[256,1024]{1,0:T(8,128)(2,1)S(1)}, bf16[256,1024]{1,0:T(8,128)(2,1)S(1)}, u32[]{:S(2)}, u32[]{:S(2)}) collective-permute-start(bf16[256,1024]{1,0:T(8,128)(2,1)S(1)} %bitcast.41), channel_id=1, source_target_pairs={{0,448},{4,68},{64,0},{68,132},{128,64},{132,196},{192,128},{196,2... | collective-permute-start | bytes 1572872 | tf_op jit(solution)/shard_map/ppermute | solution.py:248
  45.0 4.0 %collective-permute-start.5 = (bf16[128,1024]{1,0:T(8,128)(2,1)}, bf16[128,1024]{1,0:T(8,128)(2,1)}, u32[]{:S(2)}, u32[]{:S(2)}) collective-permute-start(bf16[128,1024]{1,0:T(8,128)(2,1)} %constant_dynamic-slice_fusion.1), channel_id=1, source_target_pairs={{0,384},{4,132},{64,448},{68,196},{128,0},{132,260},{192,64},{196,... | collective-permute-start | bytes 786440 | tf_op jit(solution)/shard_map/ppermute | solution.py:249
  49.0 2.2 %collective-permute-done.3.after_ref.near_ref = bf16[256,1024]{1,0:T(8,128)(2,1)S(1)} collective-permute-done((bf16[256,1024]{1,0:T(8,128)(2,1)S(1)}, bf16[256,1024]{1,0:T(8,128)(2,1)S(1)}, u32[]{:S(2)}, u32[]{:S(2)}) %collective-permute-start.3) | collective-permute-done | bytes 524320 | tf_op jit(solution)/shard_map/ppermute | solution.py:248
  51.2 1.9 %collective-permute-start.4 = (bf16[256,1024]{1,0:T(8,128)(2,1)S(1)}, bf16[256,1024]{1,0:T(8,128)(2,1)S(1)}, u32[]{:S(2)}, u32[]{:S(2)}) collective-permute-start(bf16[256,1024]{1,0:T(8,128)(2,1)S(1)} %collective-permute-done.3.after_ref.near_ref), channel_id=1, source_target_pairs={{0,4},{4,0},{1,5},{5,1},{2,6},{6,2},{3,7},{7,3},{8,12},{12,8},{9,1... | collective-permute-start | bytes 1572872 | tf_op jit(solution)/shard_map/ppermute | solution.py:251
  54.6 2.7 %collective-permute-done.5.far_ref = bf16[128,1024]{1,0:T(8,128)(2,1)} collective-permute-done((bf16[128,1024]{1,0:T(8,128)(2,1)}, bf16[128,1024]{1,0:T(8,128)(2,1)}, u32[]{:S(2)}, u32[]{:S(2)}) %collective-permute-start.5) | collective-permute-done | bytes 262176 | tf_op jit(solution)/shard_map/ppermute | solution.py:249
  57.3 1.9 %collective-permute-start.6 = (bf16[128,1024]{1,0:T(8,128)(2,1)}, bf16[128,1024]{1,0:T(8,128)(2,1)}, u32[]{:S(2)}, u32[]{:S(2)}) collective-permute-start(bf16[128,1024]{1,0:T(8,128)(2,1)} %collective-permute-done.5.far_ref), channel_id=1, source_target_pairs={{0,4},{4,0},{1,5},{5,1},{2,6},{6,2},{3,7},{7,3},{8,12},{12,8},{9,1... | collective-permute-start | bytes 786440 | tf_op jit(solution)/shard_map/ppermute | solution.py:252
  59.2 1.0 fusion.4.refs_2_
  61.0 5.2 %all-to-all-start.2 = ((bf16[4,64,768]{2,1,0:T(8,128)(2,1)}), bf16[4,64,768]{2,1,0:T(8,128)(2,1)S(1)}, u32[]{:S(2)}, u32[]{:S(2)}) async-start(bf16[4,64,768]{2,1,0:T(8,128)(2,1)} %broadcast_in_dim.5), calls=%async_computation.2 | async-start | bytes 786432 | tf_op jit(solution)/shard_map/all_to_all | solution.py:229
  66.7 4.2 %teacher.1.refs_4_ = bf16[256,1024]{1,0:T(8,128)(2,1)} custom-call(s32[5]{0:T(128)S(1)} %stack.35.place_ref, s32[2]{0:T(128)S(1)} %bitcast.52, bf16[256,1024]{1,0:T(8,128)(2,1)S(1)} %teacher_norm.1.normed_ref, bf16[256,1024]{1,0:T(8,128)(2,1)S(1)} %bitcast.43, bf16[256,1024]{1,0:T(8,128)(2,1)S(1)} %collective-permute-done.3.after_ref.near_ref, ...), custom_call_target="tpu_custom_call" | custom-call | flops 5000000000 | bytes 1000000 | tf_op jit(solution)/shard_map/teacher/pallas_call | solution.py:348
  70.9 2.7 %all-to-all-done.2 = bf16[4,64,768]{2,1,0:T(8,128)(2,1)S(1)} async-done(((bf16[4,64,768]{2,1,0:T(8,128)(2,1)}), bf16[4,64,768]{2,1,0:T(8,128)(2,1)S(1)}, u32[]{:S(2)}, u32[]{:S(2)}) %all-to-all-start.2) | async-done | bytes 393248 | tf_op jit(solution)/shard_map/all_to_all | solution.py:229
  73.6 4.9 %all-to-all-start.1 = ((bf16[4,64,1024]{2,1,0:T(8,128)(2,1)}), bf16[4,64,1024]{2,1,0:T(8,128)(2,1)S(1)}, u32[]{:S(2)}, u32[]{:S(2)}) async-start(bf16[4,64,1024]{2,1,0:T(8,128)(2,1)} %bitcast.13), calls=%async_computation.1 | async-start | bytes 1048576 | tf_op jit(solution)/shard_map/all_to_all | solution.py:362
  78.5 1.4 copy-done.2
  80.0 3.7 %student_features.1 = (bf16[2,3,512,256]{3,2,1,0:T(8,128)(2,1)}, f32[64,1024]{1,0:T(8,128)S(1)}) custom-call(s32[2]{0:T(128)S(1)} %pad_add_fusion.refs_0_.refs_1_, bf16[256,768]{1,0:T(8,128)(2,1)S(1)} %bitcast.45, bf16[64,768]{1,0:T(8,128)(2,1)S(1)} %fusion.4.refs_2_, bf16[4,768,256]{2,1,0:T(8,128)(2,1)S(1)} %bitcast.48, bf16[256,1024]{1,0:T(8,128)(2,1)} %teacher.1.refs_4_), custom_call_target="tpu_custom_call" | custom-call | flops 4000000000 | bytes 1000000 | tf_op jit(solution)/shard_map/student_features/pallas_call | solution.py:367
  83.6 2.7 %all-to-all-done.1.refs_2_ = bf16[4,64,1024]{2,1,0:T(8,128)(2,1)S(1)} async-done(((bf16[4,64,1024]{2,1,0:T(8,128)(2,1)}), bf16[4,64,1024]{2,1,0:T(8,128)(2,1)S(1)}, u32[]{:S(2)}, u32[]{:S(2)}) %all-to-all-start.1) | async-done | bytes 524320 | tf_op jit(solution)/shard_map/all_to_all | solution.py:362
  86.4 1.1 difference.1
  87.5 11.3 %all_to_all.25 = bf16[4,64,1152]{2,1,0:T(8,128)(2,1)S(1)} all-to-all(bf16[4,64,1152]{2,1,0:T(8,128)(2,1)S(1)} %difference.1), channel_id=1, replica_groups=mesh['g'=2,'yh'=2,'y0'=2,'zh'=4,'z0'=2,'c'=2,'x'=4] {'x'}, dimensions={0} | all-to-all | bytes 1179648 | tf_op jit(solution)/shard_map/all_to_all | solution.py:387
  98.9 3.5 %student_backward.1 = (bf16[512,768]{1,0:T(8,128)(2,1)S(1)}, bf16[512,768]{1,0:T(8,128)(2,1)S(1)}, f32[1,1]{1,0:T(1,128)}) custom-call(bf16[256,1152]{1,0:T(8,128)(2,1)S(1)} %bitcast.44, bf16[256,576]{1,0:T(8,128)(2,1)S(1)} %copy-done.12, f32[3,256,256]{2,1,0:T(8,128)S(1)} %copy-done.10, bf16[256,192]{1,0:T(8,128)(2,1)S(1)} %copy-done.13, ...), custom_call_target="tpu_custom_call" | custom-call | flops 4000000000 | bytes 1000000 | tf_op jit(solution)/shard_map/student_backward/pallas_call | solution.py:389
  102.4 1.9 %collective-permute-start.7 = (bf16[512,768]{1,0:T(8,128)(2,1)S(1)}, bf16[512,768]{1,0:T(8,128)(2,1)S(1)}, u32[]{:S(2)}, u32[]{:S(2)}) collective-permute-start(bf16[512,768]{1,0:T(8,128)(2,1)S(1)} %get-tuple-element.36), channel_id=1, source_target_pairs={{0,4},{4,0},{1,5},{5,1},{2,6},{6,2},{3,7},{7,3},{8,12},{12,8},{9,1... | collective-permute-start | bytes 2359304 | tf_op jit(solution)/shard_map/ppermute | solution.py:399
  104.3 2.2 %collective-permute-done.7 = bf16[512,768]{1,0:T(8,128)(2,1)S(1)} collective-permute-done((bf16[512,768]{1,0:T(8,128)(2,1)S(1)}, bf16[512,768]{1,0:T(8,128)(2,1)S(1)}, u32[]{:S(2)}, u32[]{:S(2)}) %collective-permute-start.7) | collective-permute-done | bytes 786464 | tf_op jit(solution)/shard_map/ppermute | solution.py:399
  106.8 1.9 %collective-permute-start.8 = (bf16[256,768]{1,0:T(8,128)(2,1)S(1)}, bf16[256,768]{1,0:T(8,128)(2,1)S(1)}, u32[]{:S(2)}, u32[]{:S(2)}) collective-permute-start(bf16[256,768]{1,0:T(8,128)(2,1)S(1)} %fusion), channel_id=1, source_target_pairs={{0,64},{4,12},{8,72},{12,4},{64,0},{68,76},{72,8},{76,68},{1,65},{... | collective-permute-start | bytes 1179656 | tf_op jit(solution)/shard_map/ppermute | solution.py:411
  108.7 7.7 %collective-permute-done.8 = bf16[256,768]{1,0:T(8,128)(2,1)S(1)} collective-permute-done((bf16[256,768]{1,0:T(8,128)(2,1)S(1)}, bf16[256,768]{1,0:T(8,128)(2,1)S(1)}, u32[]{:S(2)}, u32[]{:S(2)}) %collective-permute-start.8) | collective-permute-done | bytes 393248 | tf_op jit(solution)/shard_map/ppermute | solution.py:411
  116.6 3.8 %collective-permute-start.9 = (bf16[128,768]{1,0:T(8,128)(2,1)S(1)}, bf16[128,768]{1,0:T(8,128)(2,1)S(1)}, u32[]{:S(2)}, u32[]{:S(2)}) collective-permute-start(bf16[128,768]{1,0:T(8,128)(2,1)S(1)} %fusion.2), channel_id=1, source_target_pairs={{0,8},{4,68},{8,0},{12,76},{64,72},{68,4},{72,64},{76,12},{1,9},{5... | collective-permute-start | bytes 589832 | tf_op jit(solution)/shard_map/ppermute | solution.py:411
  120.4 3.7 %collective-permute-done.9 = bf16[128,768]{1,0:T(8,128)(2,1)S(1)} collective-permute-done((bf16[128,768]{1,0:T(8,128)(2,1)S(1)}, bf16[128,768]{1,0:T(8,128)(2,1)S(1)}, u32[]{:S(2)}, u32[]{:S(2)}) %collective-permute-start.9) | collective-permute-done | bytes 196640 | tf_op jit(solution)/shard_map/ppermute | solution.py:411
  124.2 23.5 %all_to_all.26.parts_ref = bf16[16,8,768]{2,1,0:T(8,128)(2,1)S(1)} all-to-all(bf16[16,8,768]{2,1,0:T(8,128)(2,1)S(1)} %fusion.3), channel_id=1, replica_groups=mesh['g'=2,'yh'=2,'y0'=2,'zh'=4,'z0'=2,'c'=2,'x'=4] {'g','yh','zh'}, dimensions={0} | all-to-all | bytes 393216 | tf_op jit(solution)/shard_map/all_to_all | solution.py:414
  (53 shorter events, 5.3 us)
Async XLA Ops:
  7.2 13.6 %copy-start.1 = (bf16[1,256,768]{2,1,0:T(8,128)(2,1)S(1)}, bf16[1,256,768]{2,1,0:T(8,128)(2,1)}, u32[]{:S(2)}) copy-start(bf16[1,256,768]{2,1,0:T(8,128)(2,1)} %param.14) | copy-start | bytes 1179652
  7.2 13.6 %copy-start.4 = (bf16[768,576]{0,1:T(8,128)(2,1)S(1)}, bf16[768,576]{0,1:T(8,128)(2,1)}, u32[]{:S(2)}) copy-start(bf16[768,576]{0,1:T(8,128)(2,1)} %param.17) | copy-start | bytes 2654212
  7.2 13.6 %copy-start.5 = (bf16[192,768]{1,0:T(8,128)(2,1)S(1)}, bf16[192,768]{1,0:T(8,128)(2,1)}, u32[]{:S(2)}) copy-start(bf16[192,768]{1,0:T(8,128)(2,1)} %out_ref.1) | copy-start | bytes 884740
  8.9 30.0 %all-to-all-start = ((bf16[16,16,1024]{2,1,0:T(8,128)(2,1)}), bf16[16,16,1024]{2,1,0:T(8,128)(2,1)S(1)}, u32[]{:S(2)}, u32[]{:S(2)}) async-start(bf16[16,16,1024]{2,1,0:T(8,128)(2,1)} %broadcast_in_dim.4), calls=%async_computation | async-start | bytes 1048576 | tf_op jit(solution)/shard_map/all_to_all | solution.py:229
  19.3 59.2 %all-gather.3.cloned.1.call-start = ((), (), s32[]{:S(2)}) async-start(), calls=%async_computation.5 | async-start | bytes 1966080 | tf_op jit(solution)/shard_map/all_gather | solution.py:328
  20.8 32.4 %copy-start.7 = (s32[1,2]{1,0:T(1,128)S(1)}, s32[1,2]{1,0:T(1,128)}, u32[]{:S(2)}) copy-start(s32[1,2]{1,0:T(1,128)} %param.16) | copy-start | bytes 28
  20.8 33.7 %copy-start = (bf16[1,256,1024]{2,1,0:T(8,128)(2,1)S(1)}, bf16[1,256,1024]{2,1,0:T(8,128)(2,1)}, u32[]{:S(2)}) copy-start(bf16[1,256,1024]{2,1,0:T(8,128)(2,1)} %param.10) | copy-start | bytes 1572868
  25.1 41.2 %copy-start.6 = (f32[1024]{0:T(1024)S(1)}, f32[1024]{0:T(1024)}, u32[]{:S(2)}) copy-start(f32[1024]{0:T(1024)} %param.11) | copy-start | bytes 12292
  25.1 10.5 %collective-permute-start = (bf16[64,768]{1,0:T(8,128)(2,1)S(1)}, bf16[64,768]{1,0:T(8,128)(2,1)S(1)}, u32[]{:S(2)}, u32[]{:S(2)}) collective-permute-start(bf16[64,768]{1,0:T(8,128)(2,1)S(1)} %get-tuple-element.42), channel_id=1, source_target_pairs={{0,1},{1,2},{2,3},{3,0},{4,5},{5,6},{6,7},{7,4},{8,9},{9,10},{10,1... | collective-permute-start | bytes 294920 | tf_op jit(solution)/shard_map/ppermute | solution.py:269
  28.5 8.4 %collective-permute-start.1 = (bf16[64,768]{1,0:T(8,128)(2,1)S(1)}, bf16[64,768]{1,0:T(8,128)(2,1)S(1)}, u32[]{:S(2)}, u32[]{:S(2)}) collective-permute-start(bf16[64,768]{1,0:T(8,128)(2,1)S(1)} %get-tuple-element.41), channel_id=1, source_target_pairs={{0,2},{1,3},{2,0},{3,1},{4,6},{5,7},{6,4},{7,5},{8,10},{9,11},{10,... | collective-permute-start | bytes 294920 | tf_op jit(solution)/shard_map/ppermute | solution.py:269
  31.6 7.3 %collective-permute-start.2 = (bf16[64,768]{1,0:T(8,128)(2,1)S(1)}, bf16[64,768]{1,0:T(8,128)(2,1)S(1)}, u32[]{:S(2)}, u32[]{:S(2)}) collective-permute-start(bf16[64,768]{1,0:T(8,128)(2,1)S(1)} %get-tuple-element.40), channel_id=1, source_target_pairs={{0,3},{1,0},{2,1},{3,2},{4,7},{5,4},{6,5},{7,6},{8,11},{9,8},{10,9... | collective-permute-start | bytes 294920 | tf_op jit(solution)/shard_map/ppermute | solution.py:269
  36.9 20.4 %copy-start.14 = (bf16[64,768]{1,0:T(8,128)(2,1)}, bf16[64,768]{1,0:T(8,128)(2,1)S(1)}, u32[]{:S(2)}) copy-start(bf16[64,768]{1,0:T(8,128)(2,1)S(1)} %collective-permute-done.1) | copy-start | bytes 294916
  38.9 15.6 %copy-start.15 = (bf16[64,768]{1,0:T(8,128)(2,1)}, bf16[64,768]{1,0:T(8,128)(2,1)S(1)}, u32[]{:S(2)}) copy-start(bf16[64,768]{1,0:T(8,128)(2,1)S(1)} %collective-permute-done.2) | copy-start | bytes 294916
  38.9 12.3 %collective-permute-start.3 = (bf16[256,1024]{1,0:T(8,128)(2,1)S(1)}, bf16[256,1024]{1,0:T(8,128)(2,1)S(1)}, u32[]{:S(2)}, u32[]{:S(2)}) collective-permute-start(bf16[256,1024]{1,0:T(8,128)(2,1)S(1)} %bitcast.41), channel_id=1, source_target_pairs={{0,448},{4,68},{64,0},{68,132},{128,64},{132,196},{192,128},{196,2... | collective-permute-start | bytes 1572872 | tf_op jit(solution)/shard_map/ppermute | solution.py:248
  45.0 12.3 %collective-permute-start.5 = (bf16[128,1024]{1,0:T(8,128)(2,1)}, bf16[128,1024]{1,0:T(8,128)(2,1)}, u32[]{:S(2)}, u32[]{:S(2)}) collective-permute-start(bf16[128,1024]{1,0:T(8,128)(2,1)} %constant_dynamic-slice_fusion.1), channel_id=1, source_target_pairs={{0,384},{4,132},{64,448},{68,196},{128,0},{132,260},{192,64},{196,... | collective-permute-start | bytes 786440 | tf_op jit(solution)/shard_map/ppermute | solution.py:249
  51.2 15.5 %collective-permute-start.4 = (bf16[256,1024]{1,0:T(8,128)(2,1)S(1)}, bf16[256,1024]{1,0:T(8,128)(2,1)S(1)}, u32[]{:S(2)}, u32[]{:S(2)}) collective-permute-start(bf16[256,1024]{1,0:T(8,128)(2,1)S(1)} %collective-permute-done.3.after_ref.near_ref), channel_id=1, source_target_pairs={{0,4},{4,0},{1,5},{5,1},{2,6},{6,2},{3,7},{7,3},{8,12},{12,8},{9,1... | collective-permute-start | bytes 1572872 | tf_op jit(solution)/shard_map/ppermute | solution.py:251
  57.3 9.3 %collective-permute-start.6 = (bf16[128,1024]{1,0:T(8,128)(2,1)}, bf16[128,1024]{1,0:T(8,128)(2,1)}, u32[]{:S(2)}, u32[]{:S(2)}) collective-permute-start(bf16[128,1024]{1,0:T(8,128)(2,1)} %collective-permute-done.5.far_ref), channel_id=1, source_target_pairs={{0,4},{4,0},{1,5},{5,1},{2,6},{6,2},{3,7},{7,3},{8,12},{12,8},{9,1... | collective-permute-start | bytes 786440 | tf_op jit(solution)/shard_map/ppermute | solution.py:252
  61.0 12.5 %all-to-all-start.2 = ((bf16[4,64,768]{2,1,0:T(8,128)(2,1)}), bf16[4,64,768]{2,1,0:T(8,128)(2,1)S(1)}, u32[]{:S(2)}, u32[]{:S(2)}) async-start(bf16[4,64,768]{2,1,0:T(8,128)(2,1)} %broadcast_in_dim.5), calls=%async_computation.2 | async-start | bytes 786432 | tf_op jit(solution)/shard_map/all_to_all | solution.py:229
  73.6 12.8 %all-to-all-start.1 = ((bf16[4,64,1024]{2,1,0:T(8,128)(2,1)}), bf16[4,64,1024]{2,1,0:T(8,128)(2,1)S(1)}, u32[]{:S(2)}, u32[]{:S(2)}) async-start(bf16[4,64,1024]{2,1,0:T(8,128)(2,1)} %bitcast.13), calls=%async_computation.1 | async-start | bytes 1048576 | tf_op jit(solution)/shard_map/all_to_all | solution.py:362
  78.5 1.4 copy-start.2
  80.0 6.4 %copy-start.3 = (bf16[3072,256]{1,0:T(8,128)(2,1)S(1)}, bf16[3072,256]{1,0:T(8,128)(2,1)}, u32[]{:S(2)}) copy-start(bf16[3072,256]{1,0:T(8,128)(2,1)} %all-gather.3.cloned.1.call-done) | copy-start | bytes 4718596
  86.3 12.5 %copy-start.8 = (bf16[2,512,768]{2,1,0:T(8,128)(2,1)S(1)}, bf16[2,512,768]{2,1,0:T(8,128)(2,1)}, u32[]{:S(2)}) copy-start(bf16[2,512,768]{2,1,0:T(8,128)(2,1)} %get-tuple-element.31.pick_ref) | copy-start | bytes 4718596
  86.3 12.5 %copy-start.9 = (bf16[2,3,512,256]{3,2,1,0:T(8,128)(2,1)S(1)}, bf16[2,3,512,256]{3,2,1,0:T(8,128)(2,1)}, u32[]{:S(2)}) copy-start(bf16[2,3,512,256]{3,2,1,0:T(8,128)(2,1)} %get-tuple-element.33.feat_ref) | copy-start | bytes 4718596
  86.3 12.5 %copy-start.10 = (f32[3,256,256]{2,1,0:T(8,128)S(1)}, f32[3,256,256]{2,1,0:T(8,128)}, u32[]{:S(2)}) copy-start(f32[3,256,256]{2,1,0:T(8,128)} %get-tuple-element.29.weights_ref) | copy-start | bytes 2359300
  86.3 12.5 %copy-start.11 = (bf16[2,512,256]{2,1,0:T(8,128)(2,1)S(1)}, bf16[2,512,256]{2,1,0:T(8,128)(2,1)}, u32[]{:S(2)}) copy-start(bf16[2,512,256]{2,1,0:T(8,128)(2,1)} %get-tuple-element.32.normed_ref) | copy-start | bytes 1572868
  86.4 12.5 %copy-start.12 = (bf16[256,576]{1,0:T(8,128)(2,1)S(1)}, bf16[256,576]{1,0:T(8,128)(2,1)}, u32[]{:S(2)}) copy-start(bf16[256,576]{1,0:T(8,128)(2,1)} %get-tuple-element.28.packed_ref) | copy-start | bytes 884740
  86.4 12.5 %copy-start.13 = (bf16[256,192]{1,0:T(8,128)(2,1)S(1)}, bf16[256,192]{1,0:T(8,128)(2,1)}, u32[]{:S(2)}) copy-start(bf16[256,192]{1,0:T(8,128)(2,1)} %get-tuple-element.30.mixed_ref) | copy-start | bytes 294916
  102.4 4.2 %collective-permute-start.7 = (bf16[512,768]{1,0:T(8,128)(2,1)S(1)}, bf16[512,768]{1,0:T(8,128)(2,1)S(1)}, u32[]{:S(2)}, u32[]{:S(2)}) collective-permute-start(bf16[512,768]{1,0:T(8,128)(2,1)S(1)} %get-tuple-element.36), channel_id=1, source_target_pairs={{0,4},{4,0},{1,5},{5,1},{2,6},{6,2},{3,7},{7,3},{8,12},{12,8},{9,1... | collective-permute-start | bytes 2359304 | tf_op jit(solution)/shard_map/ppermute | solution.py:399
  106.8 9.7 %collective-permute-start.8 = (bf16[256,768]{1,0:T(8,128)(2,1)S(1)}, bf16[256,768]{1,0:T(8,128)(2,1)S(1)}, u32[]{:S(2)}, u32[]{:S(2)}) collective-permute-start(bf16[256,768]{1,0:T(8,128)(2,1)S(1)} %fusion), channel_id=1, source_target_pairs={{0,64},{4,12},{8,72},{12,4},{64,0},{68,76},{72,8},{76,68},{1,65},{... | collective-permute-start | bytes 1179656 | tf_op jit(solution)/shard_map/ppermute | solution.py:411
  116.6 7.6 %collective-permute-start.9 = (bf16[128,768]{1,0:T(8,128)(2,1)S(1)}, bf16[128,768]{1,0:T(8,128)(2,1)S(1)}, u32[]{:S(2)}, u32[]{:S(2)}) collective-permute-start(bf16[128,768]{1,0:T(8,128)(2,1)S(1)} %fusion.2), channel_id=1, source_target_pairs={{0,8},{4,68},{8,0},{12,76},{64,72},{68,4},{72,64},{76,12},{1,9},{5... | collective-permute-start | bytes 589832 | tf_op jit(solution)/shard_map/ppermute | solution.py:411
Sparse Core Ops, SparseCore 0:
  22.3 32.2 all-gather.2

commit v4 on v2

--- a/solution.py
+++ b/solution.py
@@ -9,7 +9,8 @@
 BLOCK = 128
 F32 = jnp.float32
 BF16 = jnp.bfloat16
-CLIP = ("g", "yl", "z", "c")
+CLIP = ("g", "y", "z", "c")
+ANY = pl.BlockSpec(memory_space=pl.ANY)
 VMEM = pl.BlockSpec(memory_space=pltpu.VMEM)
 SMEM = pl.BlockSpec(memory_space=pltpu.SMEM)
 PARAMS = pltpu.CompilerParams(vmem_limit_bytes=20 * 1024 * 1024)
@@ -67,16 +68,21 @@
     return jnp.where(source == wanted, 1.0, 0.0).astype(BF16)
 
 
+def spread_kernel(qkv_ref, out_ref, spread_ref):
+    joined = jnp.concatenate([qkv_ref[...], out_ref[...]], 1)
+    spread_ref[...] = jnp.broadcast_to(joined[None], spread_ref.shape)
+
+
 def student_kernel(
-    shares, count_ref, core_ref, events_ref, qkv_ref, out_ref, clip_ref, gain_ref,
-    part_ref, normed_ref, packed_ref, mixed_ref, weights_ref, teacher_ref, pick_ref,
+    shares, columns, count_ref, core_ref, events_ref, qkv_ref, out_ref,
+    part_ref, normed_ref, packed_ref, mixed_ref, weights_ref, pick_ref,
 ):
     length, features = events_ref.shape
     heads = out_ref.shape[0] // HEAD
     normed = norm_rows(events_ref[...]).astype(BF16)
     for half in range(2):
         core = core_ref[0] if half == 0 else 1 - core_ref[0]
-        pick_ref[half] = pick_rows(features, shares, clip_ref.shape[1] // 4, core, None)
+        pick_ref[half] = pick_rows(features, shares, columns, core, None)
         normed_ref[half] = nt(pick_ref[half], normed).astype(BF16)
     packed = nt(normed, qkv_ref[...])
     packed_ref[...] = packed.astype(BF16)
@@ -91,18 +97,20 @@
     mixed = jnp.concatenate(mixed, axis=1).astype(BF16)
     mixed_ref[...] = mixed
     part_ref[...] = nn(mixed, out_ref[...]).astype(BF16)
-    teacher_ref[...] = (norm_rows(clip_ref[...]) * gain_ref[...]).astype(BF16)
+
+
+def teacher_norm_kernel(clip_ref, gain_ref, after_ref, normed_ref):
+    normed_ref[...] = (norm_rows(clip_ref[...]) * gain_ref[...]).astype(BF16)
 
 
 def teacher_kernel(
-    place_ref, align_ref, normed_ref, own_ref, near_ref, swap_ref, far_ref, fars_ref,
-    part_ref, full_ref, mixed_ref,
+    place_ref, align_ref, normed_ref, own_ref, other_ref, part_ref, parts_ref, mixed_ref
 ):
-    rows = own_ref.shape[0]
-    for i, piece in enumerate((own_ref, near_ref, swap_ref, far_ref, fars_ref)):
-        size = piece.shape[0]
-        full_ref[pl.ds(pl.multiple_of(place_ref[i], BLOCK), size), :] = piece[...]
-    width = full_ref.shape[1]
+    blocks, cores, rows, width = parts_ref.shape
+    for i, piece in enumerate((own_ref, other_ref)):
+        core = place_ref[0] if i == 0 else 1 - place_ref[0]
+        parts_ref[:, pl.ds(core, 1)] = piece[...].reshape(blocks, 1, rows, width)
+    full_ref = parts_ref[...].reshape(blocks * cores * rows, width)
     heads = width // (4 * HEAD)
     packed = nn(normed_ref[...], full_ref[:, : heads * 3 * HEAD])
     mixed = []
@@ -121,12 +129,20 @@
 
 def feature_kernel(shares, ways, place_ref, *refs):
     feat_refs = refs[:ways]
-    proj_ref, after_ref, extra_ref, pred_ref, feat_ref = refs[ways:]
-    features, columns = proj_ref.shape[1:]
+    own_ref, mine_ref, other_ref, after_ref, extra_ref, pred_ref, proj_ref, feat_ref = refs[ways:]
+    features, columns = own_ref.shape
     rows = feat_refs[0].shape[0]
+    half = features // 2
+    proj_ref[place_ref[1]] = own_ref[...]
     for k in range(ways):
         source = place_ref[1 + k]
         feat_ref[pl.ds(pl.multiple_of(source * rows, rows), rows), :] = feat_refs[k][...]
+        if k > 0:
+            first = pl.multiple_of(place_ref[0] * half, half)
+            second = pl.multiple_of((1 - place_ref[0]) * half, half)
+            proj_ref[source, pl.ds(first, half), :] = mine_ref[k - 1]
+            proj_ref[source, pl.ds(second, half), :] = other_ref[k - 1]
+    for k in range(ways):
         pred_ref[:, k * columns : (k + 1) * columns] = nn(feat_refs[0][...], proj_ref[k])
     feat = feat_ref[...]
     for half in range(2):
@@ -137,8 +153,10 @@
 
 
 def diff_kernel(
-    clips, count_ref, place_ref, parts_ref, tokens_ref, pred_ref, proj_ref, out_ref
+    clips, count_ref, place_ref, parts_ref, tokens_ref, pred_ref, source_ref, out_ref, proj_ref, sem
 ):
+    copy = pltpu.make_async_copy(source_ref, proj_ref, sem)
+    copy.start()
     rows, width = tokens_ref.shape
     ways, features, columns = proj_ref.shape
     branch = parts_ref[0].astype(F32)
@@ -152,6 +170,7 @@
     diff = jnp.where(live, pred_ref[...] - target, 0.0)
     squares = jnp.sum(diff * diff, -1, keepdims=True) / scale
     dpred = (diff * factor).astype(BF16)
+    copy.wait()
     dfeat = jnp.zeros((rows, features), F32)
     for k in range(ways):
         dfeat = dfeat + nt(dpred[:, k * columns : (k + 1) * columns], proj_ref[k])
@@ -211,38 +230,7 @@
             into[:, block] = total.astype(BF16)
 
 
-def gather_run(shard):
-    spread = lax.axis_size("z") * lax.axis_size("c")
-    return lax.all_to_all(
-        jnp.broadcast_to(shard[None], (spread, *shard.shape)), ("z", "c"), 0, 0
-    ).reshape(spread * shard.shape[0], shard.shape[1])
-
-
-def gather_runs(run, own_c, own_yl):
-    size = run.shape[0]
-    half = size // 2
-    ring = lax.axis_size("g") * lax.axis_size("yl")
-    near, far = [], []
-    for y in range(ring):
-        for c, sign in ((0, -1), (1, 1)):
-            near.append((y * 2 + c, (y + sign) % ring * 2 + c))
-            far.append((y * 2 + c, (y + 2 * sign) % ring * 2 + c))
-    first = lax.ppermute(run, ("g", "yl", "c"), near)
-    second = lax.ppermute(lax.dynamic_slice_in_dim(run, own_c * half, half, 0), ("g", "yl", "c"), far)
-    swap = [(0, 1), (1, 0)]
-    first_other = lax.ppermute(first, "c", swap)
-    second_other = lax.ppermute(second, "c", swap)
-    ways = lax.axis_size("yl")
-    step = 1 - 2 * own_c
-    opposite = (own_yl + 2) % ways * size
-    place = jnp.stack([
-        own_yl * size,
-        (own_yl + step + ways) % ways * size,
-        (own_yl - step + ways) % ways * size,
-        opposite + own_c * half,
-        opposite + (1 - own_c) * half,
-    ]).astype(jnp.int32)
-    return place, (run, first, first_other, second, second_other)
+SWAP = [(0, 1), (1, 0)]
 
 
 def from_peers(rows, axis):
@@ -251,6 +239,10 @@
         lax.ppermute(rows(k), axis, [(i, (i + k) % ways) for i in range(ways)])
         for k in range(1, ways)
     ]
+
+
+def add(a, b):
+    return a.astype(F32) + b.astype(F32)
 
 
 def result_kernel(parts_ref, q_ref, o_ref, p_ref):
@@ -275,81 +267,106 @@
     columns = projector.shape[1]
     ways = lax.axis_size("x")
     rows = length // ways
-    own_c, own_yl, own_x = lax.axis_index("c"), lax.axis_index("yl"), lax.axis_index("x")
+    own_c, own_x = lax.axis_index("c"), lax.axis_index("x")
     shares = 1
     for axis in CLIP:
         shares = shares * lax.axis_size(axis)
 
-    run = gather_run(jnp.concatenate([teacher_qkv, teacher_out_t], 1))
+    senders = lax.axis_size("y") * lax.axis_size("z")
+    shard = pl.pallas_call(
+        spread_kernel,
+        out_shape=shape(
+            (senders, teacher_qkv.shape[0], teacher_qkv.shape[1] + teacher_out_t.shape[1]), BF16
+        ),
+        compiler_params=PARAMS,
+        name="spread_rows",
+    )(teacher_qkv, teacher_out_t)
+    own_core = lax.all_to_all(shard, ("y", "z"), 0, 0)
+    half = features // 2
+    proj_half = lax.dynamic_slice_in_dim(projector, own_c * half, half, 0)
+    proj_halves = jnp.stack(from_peers(lambda k: proj_half, "x"))
 
     heads = student_out.shape[0] // HEAD
     each = features // shares
-    half = shares // 2 * (each + each * columns // features)
+    picked = shares // 2 * (each + each * columns // features)
     core = own_c.astype(jnp.int32).reshape(1)
-    part, normed_rows, packed, mixed, weights, teacher_normed, pick = pl.pallas_call(
-        lambda *refs: student_kernel(shares, *refs),
+    part, normed_rows, packed, mixed, weights, pick = pl.pallas_call(
+        lambda *refs: student_kernel(shares, columns, *refs),
         out_shape=(
             shape((length, features), BF16),
-            shape((2, half, length), BF16),
-            shape((length, 3 * HEAD * heads), BF16),
-            shape((length, HEAD * heads), BF16),
-            shape((heads, length, length), F32),
-            shape((length, width), BF16),
-            shape((2, half, features), BF16),
+            pltpu.HBM((2, picked, length), BF16),
+            pltpu.HBM((length, 3 * HEAD * heads), BF16),
+            pltpu.HBM((length, HEAD * heads), BF16),
+            pltpu.HBM((heads, length, length), F32),
+            pltpu.HBM((2, picked, features), BF16),
         ),
-        in_specs=[SMEM] * 2 + [VMEM] * 5,
-        out_specs=(VMEM,) * 7,
+        in_specs=[SMEM] * 2 + [VMEM] * 3,
+        out_specs=(VMEM,) + (pl.BlockSpec(),) * 5,
         compiler_params=PARAMS,
         cost_estimate=cost(4),
         name="student_forward",
-    )(valid_counts, core, events, student_qkv.T, student_out, clip, teacher_gain.reshape(1, width))
-
-    whole_proj = lax.all_gather(projector, "x", axis=0, tiled=False)
+    )(valid_counts, core, events, student_qkv.T, student_out)
+
     own_rows = lambda array, place: lax.dynamic_slice_in_dim(array, place * rows, rows, 0)
     branch = own_rows(part, own_x).astype(F32)
-    for received in from_peers(lambda k: own_rows(part, (own_x + k) % ways), "x"):
-        branch = branch + received.astype(F32)
+    received = from_peers(lambda k: own_rows(part, (own_x + k) % ways), "x")
+    for other in received:
+        branch = branch + other.astype(F32)
     feat_rows = (own_rows(events, own_x).astype(F32) + branch).astype(BF16)
-    run, feat_rows = lax.optimization_barrier((run, feat_rows))
-    place, pieces = gather_runs(run, own_c, own_yl)
     feats = [feat_rows] + from_peers(lambda k: feat_rows, "x")
+    own_core, feats, proj_halves = lax.optimization_barrier((own_core, feats, proj_halves))
+    other_core = lax.ppermute(own_core, "c", SWAP)
+    proj_others = lax.ppermute(proj_halves, "c", SWAP)
+    places = jnp.stack([own_c] + [(own_x - k + ways) % ways for k in range(ways)]).astype(jnp.int32)
+    teacher_normed = pl.pallas_call(
+        teacher_norm_kernel,
+        out_shape=shape((length, width), BF16),
+        in_specs=[VMEM] * 2 + [ANY],
+        out_specs=VMEM,
+        compiler_params=PARAMS,
+        cost_estimate=cost(1),
+        name="teacher_norm",
+    )(clip, teacher_gain.reshape(1, width), feat_rows)
 
     teacher_part = pl.pallas_call(
         teacher_kernel,
         out_shape=shape((length, width), BF16),
-        in_specs=[SMEM] * 2 + [VMEM] * 6,
+        in_specs=[SMEM] * 2 + [VMEM] * 3,
         out_specs=VMEM,
         scratch_shapes=[
-            pltpu.VMEM((width, teacher_qkv.shape[1] + teacher_out_t.shape[1]), BF16),
+            pltpu.VMEM((senders, 2, *shard.shape[1:]), BF16),
             pltpu.VMEM((length, teacher_out_t.shape[1]), F32),
         ],
         compiler_params=PARAMS,
         cost_estimate=cost(5),
         name="teacher",
-    )(place, align, teacher_normed, *pieces)
+    )(places, align, teacher_normed, own_core, other_core)
 
     teacher_parts = lax.all_to_all(teacher_part.reshape(ways, rows, width), "x", 0, 0)
     per_block = BLOCK // rows
     source = align[own_x // per_block] * BLOCK + own_x % per_block * rows
     own_tokens = lax.dynamic_slice_in_dim(clip, source, rows, 0)
-    places = jnp.stack([own_c] + [(own_x - k + ways) % ways for k in range(ways)]).astype(jnp.int32)
-    feat_extra, pred = pl.pallas_call(
+    feat_extra, pred, whole_proj = pl.pallas_call(
         lambda *refs: feature_kernel(shares, ways, *refs),
         out_shape=(
-            shape((2, features // columns, half, length), BF16), shape((rows, width), F32),
+            pltpu.HBM((2, features // columns, picked, length), BF16), shape((rows, width), F32),
+            pltpu.HBM((ways, features, columns), BF16),
         ),
-        in_specs=[SMEM] + [VMEM] * (ways + 1) + [pl.BlockSpec(memory_space=pl.ANY)],
-        out_specs=(VMEM,) * 2,
+        in_specs=[SMEM] + [pl.BlockSpec()] * (ways + 3) + [ANY],
+        out_specs=(pl.BlockSpec(), VMEM, pl.BlockSpec()),
         scratch_shapes=[pltpu.VMEM((length, features), BF16)],
         compiler_params=PARAMS,
         cost_estimate=cost(4),
         name="student_features",
-    )(places, *feats, whole_proj, teacher_part)
+    )(places, *feats, projector, proj_halves, proj_others, teacher_part)
     message = pl.pallas_call(
         lambda *refs: diff_kernel(shares, *refs),
         out_shape=shape((ways, rows, features + columns + BLOCK), BF16),
-        in_specs=[SMEM] * 2 + [VMEM] * 4,
+        in_specs=[SMEM] * 2 + [VMEM] * 3 + [ANY],
         out_specs=VMEM,
+        scratch_shapes=[
+            pltpu.VMEM((ways, features, columns), BF16), pltpu.SemaphoreType.DMA,
+        ],
         compiler_params=PARAMS,
         cost_estimate=cost(2),
         name="difference",
@@ -358,7 +375,7 @@
 
     keep, send, loss = pl.pallas_call(
         backward_kernel,
-        out_shape=(shape((half, features), BF16), shape((half, features), BF16), shape((1, 1), F32)),
+        out_shape=(shape((picked, features), BF16), shape((picked, features), BF16), shape((1, 1), F32)),
         in_specs=[VMEM] * 8,
         out_specs=(VMEM,) * 3,
         compiler_params=PARAMS,
@@ -366,9 +383,11 @@
         name="student_backward",
     )(back, packed, weights, mixed, student_out, pick, normed_rows, feat_extra)
 
+    total = add(keep, lax.ppermute(send, "c", SWAP)).astype(BF16)
     chips = shares // 2
-    both = (keep.astype(F32) + lax.ppermute(send, "c", [(0, 1), (1, 0)]).astype(F32)).astype(BF16)
-    spread = lax.all_to_all(both.reshape(chips, half // chips, features), ("g", "yl", "z"), 0, 0)
+    spread = lax.all_to_all(
+        total.reshape(chips, total.shape[0] // chips, features), CLIP[:3], 0, 0
+    )
     used = 3 * HEAD * heads
     grad_q, grad_o, grad_p = pl.pallas_call(
         result_kernel,
@@ -385,8 +404,8 @@
 
 
 def solution(mesh):
-    sizes = mesh.devices.shape
-    fine = Mesh(mesh.devices.reshape(sizes[0], 4, sizes[1] // 8, 2, sizes[2]), (*CLIP, "x"))
+    group, dp, tensor = mesh.devices.shape
+    fine = Mesh(mesh.devices.reshape(group, 4, dp // 8, 2, tensor), (*CLIP, "x"))
     dp = CLIP[1:]
     in_specs = (
         P(CLIP, None, None), P(), P(dp, "x"), P(dp, "x"), P(CLIP, None, None), P(CLIP), P(CLIP, None),

time: 161 us -> 144 us (0.89)
  waiting for transfers between devices: 22.3 us -> 5.69 us
  between operations: 15.8 us -> 2.4 us
  starting transfers between devices: 48.9 us -> 56.4 us
  Pallas kernels: 14.1 us -> 19.2 us
    ppermute x6 -> x9, starting transfers between devices: 21.6 us -> 31.6 us  [from_peers(): lax.ppermute(rows(k), axis, [(i, (i + k) % ways) for i in range(ways)])]
    ppermute x5 -> x3, waiting for transfers between devices: 11.5 us -> 2.26 us  [the longest x1 2.25 us: on_device(): total = add(keep, lax.ppermute(send, 'c', SWAP)).astype(BF16)]
    ppermute x5 -> x3, starting transfers between devices: 13.4 us -> 6.21 us  [the longest x1 2.4 us: on_device(): proj_others = lax.ppermute(proj_halves, 'c', SWAP)]
    ppermute x6 -> x9, waiting for transfers between devices: 5.2 us -> 0.02 us  [from_peers(): lax.ppermute(rows(k), axis, [(i, (i + k) % ways) for i in range(ways)])]
    all_to_all x1, starting transfers between devices: 10.4 us -> 13.8 us  [on_device(): own_core = lax.all_to_all(shard, ('y', 'z'), 0, 0)]
    pallas_call x2 -> x4, Pallas kernels: 6.19 us -> 9.01 us  [the longest x1 4.03 us: on_device(): pl.pallas_call(lambda *refs: student_kernel(shares, columns, *refs), out_...]
    unnamed x40 -> x44, local copies, waits for them, and re-layouts: 8.01 us -> 8.68 us
  transfers between devices with their start and end apart: 14 -> 14, of which waited for: 6 -> 2; matrix products, arithmetic and copies ran while one was open for 1% -> 2% of each run, Pallas kernels for 5% -> 9%
where the time goes in v4:
time: 144 us; the launch traced here: 143 us
  starting transfers between devices  56.4 us (39%)
  blocking collectives  47.3 us (33%)
  Pallas kernels  19.2 us (13%)
  local copies, waits for them, and re-layouts  9.5 us (7%)
  waiting for transfers between devices  5.69 us (4%)
  other arithmetic  2.82 us (2%)
  between operations  2.4 us (2%)
    all_to_all x1, blocking collectives, on_device(): lax.all_to_all(total.reshape(chips, total.shape[0] // chips, features), C...  35.5 us
    ppermute x9, starting transfers between devices, from_peers(): lax.ppermute(rows(k), axis, [(i, (i + k) % ways) for i in range(ways)])  31.6 us
    all_to_all x1, starting transfers between devices, on_device(): own_core = lax.all_to_all(shard, ('y', 'z'), 0, 0)  13.8 us
    all_to_all x1, blocking collectives, on_device(): lax.all_to_all(message, 'x', 0, 0)  11.8 us
    unnamed x44, local copies, waits for them, and re-layouts  8.68 us
    all_to_all x1, starting transfers between devices, on_device(): lax.all_to_all(teacher_part.reshape(ways, rows, width), 'x', 0, 0)  4.75 us
    pallas_call x1, Pallas kernels, on_device(): pl.pallas_call(teacher_kernel, out_shape=shape((length, width), BF16), in...  4.43 us
    pallas_call x1, Pallas kernels, on_device(): pl.pallas_call(lambda *refs: student_kernel(shares, columns, *refs), out_...  4.03 us
  transfers between devices with their start and end apart: 14, of which 2 were waited for; matrix products, arithmetic and copies ran while one was open for 2% of the time, Pallas kernels for 9%

profile of v4, /device:TPU:16, one launch (start us, length us, event | category | flops | bytes accessed | tf_op | source)
XLA Modules:
  0.0 143.4 jit_solution(3057378609594617683)
XLA Ops:
  0.7 0.8 copy-done.3
  2.1 1.1 spread_rows.1
  3.2 13.8 %all-to-all-start = ((bf16[32,16,1024]{2,1,0:T(8,128)(2,1)}), bf16[32,16,1024]{2,1,0:T(8,128)(2,1)S(1)}, u32[]{:S(2)}, u32[]{:S(2)}) async-start(bf16[32,16,1024]{2,1,0:T(8,128)(2,1)} %spread_rows.1), calls=%async_computation | async-start | bytes 2097152 | tf_op jit(solution)/shard_map/all_to_all | solution.py:284
  17.8 1.2 copy-done.5
  19.0 4.0 %student_forward.1 = (bf16[256,768]{1,0:T(8,128)(2,1)S(1)}, bf16[2,512,256]{2,1,0:T(8,128)(2,1)}, bf16[256,576]{1,0:T(8,128)(2,1)}, bf16[256,192]{1,0:T(8,128)(2...) custom-call(s32[1]{0:T(128)S(6)} %copy.14.refs_0_, s32[1]{0:T(128)} %bitcast.refs_1_, ...), custom_call_target="tpu_custom_call" | custom-call | flops 4000000000 | bytes 1000000 | tf_op jit(solution)/shard_map/student_forward/pallas_call | solution.py:293
  23.7 3.4 %collective-permute-start = (bf16[64,768]{1,0:T(8,128)(2,1)}, bf16[64,768]{1,0:T(8,128)(2,1)}, u32[]{:S(2)}, u32[]{:S(2)}) collective-permute-start(bf16[64,768]{1,0:T(8,128)(2,1)} %get-tuple-element.46), channel_id=1, source_target_pairs={{0,1},{1,2},{2,3},{3,0},{4,5},{5,6},{6,7},{7,4},{8,9},{9,10},{10,1... | collective-permute-start | bytes 294920 | tf_op jit(solution)/shard_map/ppermute | solution.py:239
  27.1 4.6 %collective-permute-start.1 = (bf16[64,768]{1,0:T(8,128)(2,1)}, bf16[64,768]{1,0:T(8,128)(2,1)}, u32[]{:S(2)}, u32[]{:S(2)}) collective-permute-start(bf16[64,768]{1,0:T(8,128)(2,1)} %get-tuple-element.48), channel_id=1, source_target_pairs={{0,2},{1,3},{2,0},{3,1},{4,6},{5,7},{6,4},{7,5},{8,10},{9,11},{10,... | collective-permute-start | bytes 294920 | tf_op jit(solution)/shard_map/ppermute | solution.py:239
  31.8 3.3 %collective-permute-start.2 = (bf16[64,768]{1,0:T(8,128)(2,1)S(1)}, bf16[64,768]{1,0:T(8,128)(2,1)}, u32[]{:S(2)}, u32[]{:S(2)}) collective-permute-start(bf16[64,768]{1,0:T(8,128)(2,1)S(1)} %get-tuple-element.47), channel_id=1, source_target_pairs={{0,3},{1,0},{2,1},{3,2},{4,7},{5,4},{6,5},{7,6},{8,11},{9,8},{10,9... | collective-permute-start | bytes 294920 | tf_op jit(solution)/shard_map/ppermute | solution.py:239
  35.2 2.5 %collective-permute-start.6 = (bf16[384,256]{1,0:T(8,128)(2,1)S(1)}, bf16[384,256]{1,0:T(8,128)(2,1)S(1)}, u32[]{:S(2)}, u32[]{:S(2)}) collective-permute-start(bf16[384,256]{1,0:T(8,128)(2,1)S(1)} %constant_dynamic-slice_fusion.1), channel_id=1, source_target_pairs={{0,1},{1,2},{2,3},{3,0},{4,5},{5,6},{6,7},{7,4},{8,9},{9,10},{10,1... | collective-permute-start | bytes 589832 | tf_op jit(solution)/shard_map/ppermute | solution.py:239
  37.7 2.8 %collective-permute-start.7 = (bf16[384,256]{1,0:T(8,128)(2,1)S(1)}, bf16[384,256]{1,0:T(8,128)(2,1)}, u32[]{:S(2)}, u32[]{:S(2)}) collective-permute-start(bf16[384,256]{1,0:T(8,128)(2,1)S(1)} %constant_dynamic-slice_fusion.1), channel_id=1, source_target_pairs={{0,2},{1,3},{2,0},{3,1},{4,6},{5,7},{6,4},{7,5},{8,10},{9,11},{10,... | collective-permute-start | bytes 589832 | tf_op jit(solution)/shard_map/ppermute | solution.py:239
  40.5 3.7 %collective-permute-start.8 = (bf16[384,256]{1,0:T(8,128)(2,1)S(1)}, bf16[384,256]{1,0:T(8,128)(2,1)S(1)}, u32[]{:S(2)}, u32[]{:S(2)}) collective-permute-start(bf16[384,256]{1,0:T(8,128)(2,1)S(1)} %constant_dynamic-slice_fusion.1), channel_id=1, source_target_pairs={{0,3},{1,0},{2,1},{3,2},{4,7},{5,4},{6,5},{7,6},{8,11},{9,8},{10,9... | collective-permute-start | bytes 589832 | tf_op jit(solution)/shard_map/ppermute | solution.py:239
  44.2 1.1 fusion.1.after_ref.refs_1_
  45.3 2.7 %collective-permute-start.3 = (bf16[64,768]{1,0:T(8,128)(2,1)S(1)}, bf16[64,768]{1,0:T(8,128)(2,1)S(1)}, u32[]{:S(2)}, u32[]{:S(2)}) collective-permute-start(bf16[64,768]{1,0:T(8,128)(2,1)S(1)} %fusion.1.after_ref.refs_1_), channel_id=1, source_target_pairs={{0,1},{1,2},{2,3},{3,0},{4,5},{5,6},{6,7},{7,4},{8,9},{9,10},{10,1... | collective-permute-start | bytes 294920 | tf_op jit(solution)/shard_map/ppermute | solution.py:239
  48.0 4.0 %collective-permute-start.4 = (bf16[64,768]{1,0:T(8,128)(2,1)S(1)}, bf16[64,768]{1,0:T(8,128)(2,1)S(1)}, u32[]{:S(2)}, u32[]{:S(2)}) collective-permute-start(bf16[64,768]{1,0:T(8,128)(2,1)S(1)} %fusion.1.after_ref.refs_1_), channel_id=1, source_target_pairs={{0,2},{1,3},{2,0},{3,1},{4,6},{5,7},{6,4},{7,5},{8,10},{9,11},{10,... | collective-permute-start | bytes 294920 | tf_op jit(solution)/shard_map/ppermute | solution.py:239
  52.0 4.5 %collective-permute-start.5 = (bf16[64,768]{1,0:T(8,128)(2,1)S(1)}, bf16[64,768]{1,0:T(8,128)(2,1)S(1)}, u32[]{:S(2)}, u32[]{:S(2)}) collective-permute-start(bf16[64,768]{1,0:T(8,128)(2,1)S(1)} %fusion.1.after_ref.refs_1_), channel_id=1, source_target_pairs={{0,3},{1,0},{2,1},{3,2},{4,7},{5,4},{6,5},{7,6},{8,11},{9,8},{10,9... | collective-permute-start | bytes 294920 | tf_op jit(solution)/shard_map/ppermute | solution.py:239
  56.6 1.0 pad_maximum_fusion.refs_6_
  59.5 1.9 %collective-permute-start.9 = (bf16[32,16,1024]{2,1,0:T(8,128)(2,1)S(1)}, bf16[32,16,1024]{2,1,0:T(8,128)(2,1)}, u32[]{:S(2)}, u32[]{:S(2)}) collective-permute-start(bf16[32,16,1024]{2,1,0:T(8,128)(2,1)S(1)} %all-to-all-done.own_ref), channel_id=1, source_target_pairs={{0,4},{4,0},{1,5},{5,1},{2,6},{6,2},{3,7},{7,3},{8,12},{12,8},{9,1... | collective-permute-start | bytes 3145736 | tf_op jit(solution)/shard_map/ppermute | solution.py:318
  62.8 2.4 %collective-permute-start.10 = (bf16[3,384,256]{2,1,0:T(8,128)(2,1)S(1)}, bf16[3,384,256]{2,1,0:T(8,128)(2,1)S(1)}, u32[]{:S(2)}, u32[]{:S(2)}) collective-permute-start(bf16[3,384,256]{2,1,0:T(8,128)(2,1)S(1)} %pad_maximum_fusion.refs_6_), channel_id=1, source_target_pairs={{0,4},{4,0},{1,5},{5,1},{2,6},{6,2},{3,7},{7,3},{8,12},{12,8},{9,1... | collective-permute-start | bytes 1769480 | tf_op jit(solution)/shard_map/ppermute | solution.py:319
  65.6 4.4 %teacher.1.refs_8_ = bf16[256,1024]{1,0:T(8,128)(2,1)} custom-call(s32[5]{0:T(128)S(1)} %stack.35.place_ref.refs_0_.refs_1_, s32[2]{0:T(128)S(1)} %bitcast.30, bf16[256,1024]{1,0:T(8,128)(2,1)S(1)} %teacher_norm.1.normed_ref, bf16[32,16,1024]{2,1,0:T(8,128)(2,1)S(1)} %all-to-all-done.own_ref, bf16[32,16,1024]{2,1,0:T(8,128)(2,1)} %collective-permute-done.9.other_ref), custom_call_target="tpu_custom_call" | custom-call | flops 5000000000 | bytes 1000000 | tf_op jit(solution)/shard_map/teacher/pallas_call | solution.py:331
  70.1 4.8 %all-to-all-start.1 = ((bf16[4,64,1024]{2,1,0:T(8,128)(2,1)}), bf16[4,64,1024]{2,1,0:T(8,128)(2,1)S(1)}, u32[]{:S(2)}, u32[]{:S(2)}) async-start(bf16[4,64,1024]{2,1,0:T(8,128)(2,1)} %bitcast.14), calls=%async_computation.1 | async-start | bytes 1048576 | tf_op jit(solution)/shard_map/all_to_all | solution.py:345
  74.8 0.9 copy-done.8
  75.7 0.9 copy-done.10
  76.6 0.9 copy-done.12
  77.5 3.5 %student_features.1 = (bf16[2,3,512,256]{3,2,1,0:T(8,128)(2,1)}, f32[64,1024]{1,0:T(8,128)S(1)}, bf16[4,768,256]{2,1,0:T(8,128)(2,1)}) custom-call(s32[5]{0:T(128)S(1)} %stack.35.place_ref.refs_0_.refs_1_, bf16[64,768]{1,0:T(8,128)(2,1)S(1)} %fusion.1.after_ref.refs_1_, bf16[64,768]{1,0:T(8,128)(2,1)S(1)} %copy-done.8, bf16[64,768]{1,0:T(8,128)(2,1)S(1)} %copy-done.10, ...), custom_call_target="tpu_custom_call" | custom-call | flops 4000000000 | bytes 1000000 | tf_op jit(solution)/shard_map/student_features/pallas_call | solution.py:349
  81.1 3.4 %all-to-all-done.1.refs_2_ = bf16[4,64,1024]{2,1,0:T(8,128)(2,1)S(1)} async-done(((bf16[4,64,1024]{2,1,0:T(8,128)(2,1)}), bf16[4,64,1024]{2,1,0:T(8,128)(2,1)S(1)}, u32[]{:S(2)}, u32[]{:S(2)}) %all-to-all-start.1) | async-done | bytes 524320 | tf_op jit(solution)/shard_map/all_to_all | solution.py:345
  84.5 1.4 copy-done.15
  85.9 1.5 %difference.1 = bf16[4,64,1152]{2,1,0:T(8,128)(2,1)S(1)} custom-call(s32[1]{0:T(128)S(6)} %copy.14.refs_0_, s32[5]{0:T(128)S(1)} %stack.35.place_ref.refs_0_.refs_1_, bf16[4,64,1024]{2,1,0:T(8,128)(2,1)S(1)} %all-to-all-done.1.refs_2_, bf16[64,1024]{1,0:T(8,128)(2,1)S(1)} %dynamic-slice_bitcast_fusion.refs_3_, f32[64,1024]{1,0:T(8,128)S(1)} %get-tuple-element.32.refs_4_, ...), custom_call_target="tpu_custom_call" | custom-call | flops 2000000000 | bytes 1000000 | tf_op jit(solution)/shard_map/difference/pallas_call | solution.py:362
  87.4 11.8 %all_to_all.20 = bf16[4,64,1152]{2,1,0:T(8,128)(2,1)S(1)} all-to-all(bf16[4,64,1152]{2,1,0:T(8,128)(2,1)S(1)} %difference.1), channel_id=1, replica_groups=mesh['g'=2,'y'=4,'z'=8,'c'=2,'x'=4] {'x'}, dimensions={0} | all-to-all | bytes 1179648 | tf_op jit(solution)/shard_map/all_to_all | solution.py:374
  99.3 3.5 %student_backward.1 = (bf16[512,768]{1,0:T(8,128)(2,1)S(1)}, bf16[512,768]{1,0:T(8,128)(2,1)S(1)}, f32[1,1]{1,0:T(1,128)}) custom-call(bf16[256,1152]{1,0:T(8,128)(2,1)S(1)} %bitcast.25, bf16[256,576]{1,0:T(8,128)(2,1)S(1)} %copy-done.20, f32[3,256,256]{2,1,0:T(8,128)S(1)} %copy-done.18, bf16[256,192]{1,0:T(8,128)(2,1)S(1)} %copy-done.21, ...), custom_call_target="tpu_custom_call" | custom-call | flops 4000000000 | bytes 1000000 | tf_op jit(solution)/shard_map/student_backward/pallas_call | solution.py:376
  102.8 1.9 %collective-permute-start.11 = (bf16[512,768]{1,0:T(8,128)(2,1)S(1)}, bf16[512,768]{1,0:T(8,128)(2,1)S(1)}, u32[]{:S(2)}, u32[]{:S(2)}) collective-permute-start(bf16[512,768]{1,0:T(8,128)(2,1)S(1)} %get-tuple-element.42), channel_id=1, source_target_pairs={{0,4},{4,0},{1,5},{5,1},{2,6},{6,2},{3,7},{7,3},{8,12},{12,8},{9,1... | collective-permute-start | bytes 2359304 | tf_op jit(solution)/shard_map/ppermute | solution.py:386
  104.7 2.3 %collective-permute-done.11 = bf16[512,768]{1,0:T(8,128)(2,1)S(1)} collective-permute-done((bf16[512,768]{1,0:T(8,128)(2,1)S(1)}, bf16[512,768]{1,0:T(8,128)(2,1)S(1)}, u32[]{:S(2)}, u32[]{:S(2)}) %collective-permute-start.11) | collective-permute-done | bytes 786464 | tf_op jit(solution)/shard_map/ppermute | solution.py:386
  107.1 35.5 %all_to_all.21.parts_ref = bf16[64,8,768]{2,1,0:T(8,128)(2,1)S(1)} all-to-all(bf16[64,8,768]{2,1,0:T(8,128)(2,1)S(1)} %fusion), channel_id=1, replica_groups=mesh['g'=2,'y'=4,'z'=8,'c'=2,'x'=4] {'g','y','z'}, dimensions={0} | all-to-all | bytes 1572864 | tf_op jit(solution)/shard_map/all_to_all | solution.py:388
  (58 shorter events, 5.4 us)
Async XLA Ops:
  0.6 17.2 %copy-start.2 = (bf16[1,256,768]{2,1,0:T(8,128)(2,1)S(1)}, bf16[1,256,768]{2,1,0:T(8,128)(2,1)}, u32[]{:S(2)}) copy-start(bf16[1,256,768]{2,1,0:T(8,128)(2,1)} %param.14) | copy-start | bytes 1179652
  0.6 0.8 copy-start.3
  2.1 15.7 %copy-start.6 = (bf16[192,768]{1,0:T(8,128)(2,1)S(1)}, bf16[192,768]{1,0:T(8,128)(2,1)}, u32[]{:S(2)}) copy-start(bf16[192,768]{1,0:T(8,128)(2,1)} %out_ref.3) | copy-start | bytes 884740
  3.2 56.3 %all-to-all-start = ((bf16[32,16,1024]{2,1,0:T(8,128)(2,1)}), bf16[32,16,1024]{2,1,0:T(8,128)(2,1)S(1)}, u32[]{:S(2)}, u32[]{:S(2)}) async-start(bf16[32,16,1024]{2,1,0:T(8,128)(2,1)} %spread_rows.1), calls=%async_computation | async-start | bytes 2097152 | tf_op jit(solution)/shard_map/all_to_all | solution.py:284
  17.8 1.2 copy-start.5
  19.0 16.1 %copy-start = (bf16[768,256]{1,0:T(8,128)(2,1)S(1)}, bf16[768,256]{1,0:T(8,128)(2,1)}, u32[]{:S(2)}) copy-start(bf16[768,256]{1,0:T(8,128)(2,1)} %refs_5_.1) | copy-start | bytes 1179652
  23.0 38.5 %copy-start.14 = (s32[1,2]{1,0:T(1,128)S(1)}, s32[1,2]{1,0:T(1,128)}, u32[]{:S(2)}) copy-start(s32[1,2]{1,0:T(1,128)} %param.16) | copy-start | bytes 28
  23.0 42.2 %copy-start.1 = (bf16[1,256,1024]{2,1,0:T(8,128)(2,1)S(1)}, bf16[1,256,1024]{2,1,0:T(8,128)(2,1)}, u32[]{:S(2)}) copy-start(bf16[1,256,1024]{2,1,0:T(8,128)(2,1)} %param.10) | copy-start | bytes 1572868
  23.0 42.2 %copy-start.13 = (f32[1024]{0:T(1024)S(1)}, f32[1024]{0:T(1024)}, u32[]{:S(2)}) copy-start(f32[1024]{0:T(1024)} %param.11) | copy-start | bytes 12292
  23.7 16.8 %collective-permute-start = (bf16[64,768]{1,0:T(8,128)(2,1)}, bf16[64,768]{1,0:T(8,128)(2,1)}, u32[]{:S(2)}, u32[]{:S(2)}) collective-permute-start(bf16[64,768]{1,0:T(8,128)(2,1)} %get-tuple-element.46), channel_id=1, source_target_pairs={{0,1},{1,2},{2,3},{3,0},{4,5},{5,6},{6,7},{7,4},{8,9},{9,10},{10,1... | collective-permute-start | bytes 294920 | tf_op jit(solution)/shard_map/ppermute | solution.py:239
  27.1 17.1 %collective-permute-start.1 = (bf16[64,768]{1,0:T(8,128)(2,1)}, bf16[64,768]{1,0:T(8,128)(2,1)}, u32[]{:S(2)}, u32[]{:S(2)}) collective-permute-start(bf16[64,768]{1,0:T(8,128)(2,1)} %get-tuple-element.48), channel_id=1, source_target_pairs={{0,2},{1,3},{2,0},{3,1},{4,6},{5,7},{6,4},{7,5},{8,10},{9,11},{10,... | collective-permute-start | bytes 294920 | tf_op jit(solution)/shard_map/ppermute | solution.py:239
  31.8 12.4 %collective-permute-start.2 = (bf16[64,768]{1,0:T(8,128)(2,1)S(1)}, bf16[64,768]{1,0:T(8,128)(2,1)}, u32[]{:S(2)}, u32[]{:S(2)}) collective-permute-start(bf16[64,768]{1,0:T(8,128)(2,1)S(1)} %get-tuple-element.47), channel_id=1, source_target_pairs={{0,3},{1,0},{2,1},{3,2},{4,7},{5,4},{6,5},{7,6},{8,11},{9,8},{10,9... | collective-permute-start | bytes 294920 | tf_op jit(solution)/shard_map/ppermute | solution.py:239
  35.2 16.9 %collective-permute-start.6 = (bf16[384,256]{1,0:T(8,128)(2,1)S(1)}, bf16[384,256]{1,0:T(8,128)(2,1)S(1)}, u32[]{:S(2)}, u32[]{:S(2)}) collective-permute-start(bf16[384,256]{1,0:T(8,128)(2,1)S(1)} %constant_dynamic-slice_fusion.1), channel_id=1, source_target_pairs={{0,1},{1,2},{2,3},{3,0},{4,5},{5,6},{6,7},{7,4},{8,9},{9,10},{10,1... | collective-permute-start | bytes 589832 | tf_op jit(solution)/shard_map/ppermute | solution.py:239
  37.7 18.9 %collective-permute-start.7 = (bf16[384,256]{1,0:T(8,128)(2,1)S(1)}, bf16[384,256]{1,0:T(8,128)(2,1)}, u32[]{:S(2)}, u32[]{:S(2)}) collective-permute-start(bf16[384,256]{1,0:T(8,128)(2,1)S(1)} %constant_dynamic-slice_fusion.1), channel_id=1, source_target_pairs={{0,2},{1,3},{2,0},{3,1},{4,6},{5,7},{6,4},{7,5},{8,10},{9,11},{10,... | collective-permute-start | bytes 589832 | tf_op jit(solution)/shard_map/ppermute | solution.py:239
  40.5 16.1 %collective-permute-start.8 = (bf16[384,256]{1,0:T(8,128)(2,1)S(1)}, bf16[384,256]{1,0:T(8,128)(2,1)S(1)}, u32[]{:S(2)}, u32[]{:S(2)}) collective-permute-start(bf16[384,256]{1,0:T(8,128)(2,1)S(1)} %constant_dynamic-slice_fusion.1), channel_id=1, source_target_pairs={{0,3},{1,0},{2,1},{3,2},{4,7},{5,4},{6,5},{7,6},{8,11},{9,8},{10,9... | collective-permute-start | bytes 589832 | tf_op jit(solution)/shard_map/ppermute | solution.py:239
  45.3 12.3 %collective-permute-start.3 = (bf16[64,768]{1,0:T(8,128)(2,1)S(1)}, bf16[64,768]{1,0:T(8,128)(2,1)S(1)}, u32[]{:S(2)}, u32[]{:S(2)}) collective-permute-start(bf16[64,768]{1,0:T(8,128)(2,1)S(1)} %fusion.1.after_ref.refs_1_), channel_id=1, source_target_pairs={{0,1},{1,2},{2,3},{3,0},{4,5},{5,6},{6,7},{7,4},{8,9},{9,10},{10,1... | collective-permute-start | bytes 294920 | tf_op jit(solution)/shard_map/ppermute | solution.py:239
  48.0 10.2 %collective-permute-start.4 = (bf16[64,768]{1,0:T(8,128)(2,1)S(1)}, bf16[64,768]{1,0:T(8,128)(2,1)S(1)}, u32[]{:S(2)}, u32[]{:S(2)}) collective-permute-start(bf16[64,768]{1,0:T(8,128)(2,1)S(1)} %fusion.1.after_ref.refs_1_), channel_id=1, source_target_pairs={{0,2},{1,3},{2,0},{3,1},{4,6},{5,7},{6,4},{7,5},{8,10},{9,11},{10,... | collective-permute-start | bytes 294920 | tf_op jit(solution)/shard_map/ppermute | solution.py:239
  52.0 6.9 %collective-permute-start.5 = (bf16[64,768]{1,0:T(8,128)(2,1)S(1)}, bf16[64,768]{1,0:T(8,128)(2,1)S(1)}, u32[]{:S(2)}, u32[]{:S(2)}) collective-permute-start(bf16[64,768]{1,0:T(8,128)(2,1)S(1)} %fusion.1.after_ref.refs_1_), channel_id=1, source_target_pairs={{0,3},{1,0},{2,1},{3,2},{4,7},{5,4},{6,5},{7,6},{8,11},{9,8},{10,9... | collective-permute-start | bytes 294920 | tf_op jit(solution)/shard_map/ppermute | solution.py:239
  59.5 6.1 %collective-permute-start.9 = (bf16[32,16,1024]{2,1,0:T(8,128)(2,1)S(1)}, bf16[32,16,1024]{2,1,0:T(8,128)(2,1)}, u32[]{:S(2)}, u32[]{:S(2)}) collective-permute-start(bf16[32,16,1024]{2,1,0:T(8,128)(2,1)S(1)} %all-to-all-done.own_ref), channel_id=1, source_target_pairs={{0,4},{4,0},{1,5},{5,1},{2,6},{6,2},{3,7},{7,3},{8,12},{12,8},{9,1... | collective-permute-start | bytes 3145736 | tf_op jit(solution)/shard_map/ppermute | solution.py:318
  62.8 12.0 %collective-permute-start.10 = (bf16[3,384,256]{2,1,0:T(8,128)(2,1)S(1)}, bf16[3,384,256]{2,1,0:T(8,128)(2,1)S(1)}, u32[]{:S(2)}, u32[]{:S(2)}) collective-permute-start(bf16[3,384,256]{2,1,0:T(8,128)(2,1)S(1)} %pad_maximum_fusion.refs_6_), channel_id=1, source_target_pairs={{0,4},{4,0},{1,5},{5,1},{2,6},{6,2},{3,7},{7,3},{8,12},{12,8},{9,1... | collective-permute-start | bytes 1769480 | tf_op jit(solution)/shard_map/ppermute | solution.py:319
  70.1 14.4 %all-to-all-start.1 = ((bf16[4,64,1024]{2,1,0:T(8,128)(2,1)}), bf16[4,64,1024]{2,1,0:T(8,128)(2,1)S(1)}, u32[]{:S(2)}, u32[]{:S(2)}) async-start(bf16[4,64,1024]{2,1,0:T(8,128)(2,1)} %bitcast.14), calls=%async_computation.1 | async-start | bytes 1048576 | tf_op jit(solution)/shard_map/all_to_all | solution.py:345
  74.8 0.9 copy-start.8
  75.7 0.9 copy-start.10
  76.6 0.9 copy-start.12
  84.5 1.4 copy-start.15
  85.9 13.4 %copy-start.16 = (bf16[2,512,768]{2,1,0:T(8,128)(2,1)S(1)}, bf16[2,512,768]{2,1,0:T(8,128)(2,1)}, u32[]{:S(2)}) copy-start(bf16[2,512,768]{2,1,0:T(8,128)(2,1)} %get-tuple-element.37.pick_ref) | copy-start | bytes 4718596
  85.9 13.4 %copy-start.17 = (bf16[2,3,512,256]{3,2,1,0:T(8,128)(2,1)S(1)}, bf16[2,3,512,256]{3,2,1,0:T(8,128)(2,1)}, u32[]{:S(2)}) copy-start(bf16[2,3,512,256]{3,2,1,0:T(8,128)(2,1)} %get-tuple-element.39.feat_ref) | copy-start | bytes 4718596
  85.9 13.4 %copy-start.18 = (f32[3,256,256]{2,1,0:T(8,128)S(1)}, f32[3,256,256]{2,1,0:T(8,128)}, u32[]{:S(2)}) copy-start(f32[3,256,256]{2,1,0:T(8,128)} %get-tuple-element.35.weights_ref) | copy-start | bytes 2359300
  85.9 13.4 %copy-start.19 = (bf16[2,512,256]{2,1,0:T(8,128)(2,1)S(1)}, bf16[2,512,256]{2,1,0:T(8,128)(2,1)}, u32[]{:S(2)}) copy-start(bf16[2,512,256]{2,1,0:T(8,128)(2,1)} %get-tuple-element.38.normed_ref) | copy-start | bytes 1572868
  85.9 13.4 %copy-start.20 = (bf16[256,576]{1,0:T(8,128)(2,1)S(1)}, bf16[256,576]{1,0:T(8,128)(2,1)}, u32[]{:S(2)}) copy-start(bf16[256,576]{1,0:T(8,128)(2,1)} %get-tuple-element.34.packed_ref) | copy-start | bytes 884740
  85.9 13.4 %copy-start.21 = (bf16[256,192]{1,0:T(8,128)(2,1)S(1)}, bf16[256,192]{1,0:T(8,128)(2,1)}, u32[]{:S(2)}) copy-start(bf16[256,192]{1,0:T(8,128)(2,1)} %get-tuple-element.36.mixed_ref) | copy-start | bytes 294916
  102.8 4.2 %collective-permute-start.11 = (bf16[512,768]{1,0:T(8,128)(2,1)S(1)}, bf16[512,768]{1,0:T(8,128)(2,1)S(1)}, u32[]{:S(2)}, u32[]{:S(2)}) collective-permute-start(bf16[512,768]{1,0:T(8,128)(2,1)S(1)} %get-tuple-element.42), channel_id=1, source_target_pairs={{0,4},{4,0},{1,5},{5,1},{2,6},{6,2},{3,7},{7,3},{8,12},{12,8},{9,1... | collective-permute-start | bytes 2359304 | tf_op jit(solution)/shard_map/ppermute | solution.py:386
  (4 other events, 2.6 us)

commit v5 on v4

--- a/solution.py
+++ b/solution.py
@@ -11,9 +11,11 @@
 BF16 = jnp.bfloat16
 CLIP = ("g", "y", "z", "c")
 ANY = pl.BlockSpec(memory_space=pl.ANY)
+HBM = pl.BlockSpec(memory_space=pltpu.HBM)
 VMEM = pl.BlockSpec(memory_space=pltpu.VMEM)
 SMEM = pl.BlockSpec(memory_space=pltpu.SMEM)
 PARAMS = pltpu.CompilerParams(vmem_limit_bytes=20 * 1024 * 1024)
+FETCHING = pltpu.CompilerParams(vmem_limit_bytes=52 * 1024 * 1024)
 
 
 def cost(microseconds):
@@ -74,14 +76,17 @@
 
 
 def student_kernel(
-    shares, columns, count_ref, core_ref, events_ref, qkv_ref, out_ref,
-    part_ref, normed_ref, packed_ref, mixed_ref, weights_ref, pick_ref,
+    shares, count_ref, place_ref, events_ref, qkv_ref, out_ref, proj_ref, *refs
 ):
+    ways = len(refs) - 6
+    own_ref, peer_refs = refs[0], refs[1:ways]
+    normed_ref, packed_ref, mixed_ref, weights_ref, pick_ref, part_ref = refs[ways:]
+    columns = proj_ref.shape[1]
     length, features = events_ref.shape
     heads = out_ref.shape[0] // HEAD
     normed = norm_rows(events_ref[...]).astype(BF16)
     for half in range(2):
-        core = core_ref[0] if half == 0 else 1 - core_ref[0]
+        core = place_ref[0] if half == 0 else 1 - place_ref[0]
         pick_ref[half] = pick_rows(features, shares, columns, core, None)
         normed_ref[half] = nt(pick_ref[half], normed).astype(BF16)
     packed = nt(normed, qkv_ref[...])
@@ -96,7 +101,34 @@
         mixed.append(nn(weights.astype(BF16), values))
     mixed = jnp.concatenate(mixed, axis=1).astype(BF16)
     mixed_ref[...] = mixed
-    part_ref[...] = nn(mixed, out_ref[...]).astype(BF16)
+    part_ref[...] = nn(mixed, out_ref[...])
+    rows = own_ref.shape[0]
+    half = features // 2
+    blocks = features // columns
+    proj_half = proj_ref[pl.ds(pl.multiple_of(place_ref[0] * half, half), half), :]
+    for k in range(ways):
+        first = pl.multiple_of(place_ref[1 + k] * rows, rows)
+        chosen = part_ref[pl.ds(first, rows), :].astype(BF16)
+        if k == 0:
+            own_ref[...] = chosen
+            continue
+        for b in range(blocks):
+            peer_refs[k - 1][b * rows : (b + 1) * rows] = chosen[:, b * columns : (b + 1) * columns]
+        peer_refs[k - 1][blocks * rows :] = proj_half
+
+
+def rows_kernel(ways, events_ref, own_ref, *refs):
+    peer_refs, (feat_ref, proj_ref) = refs[: ways - 1], refs[ways - 1 :]
+    rows, features = own_ref.shape
+    columns = proj_ref.shape[2]
+    for b in range(features // columns):
+        block = slice(b * columns, (b + 1) * columns)
+        branch = own_ref[:, block].astype(F32)
+        for peer in peer_refs:
+            branch = branch + peer[b * rows : (b + 1) * rows].astype(F32)
+        feat_ref[:, block] = (events_ref[:, block].astype(F32) + branch).astype(BF16)
+    for k, peer in enumerate(peer_refs):
+        proj_ref[k] = peer[features // columns * rows :]
 
 
 def teacher_norm_kernel(clip_ref, gain_ref, after_ref, normed_ref):
@@ -104,7 +136,7 @@
 
 
 def teacher_kernel(
-    place_ref, align_ref, normed_ref, own_ref, other_ref, part_ref, parts_ref, mixed_ref
+    place_ref, align_ref, normed_ref, own_ref, other_ref, feat_ref, part_ref, parts_ref, mixed_ref
 ):
     blocks, cores, rows, width = parts_ref.shape
     for i, piece in enumerate((own_ref, other_ref)):
@@ -119,32 +151,39 @@
         weights = softmax(nt(query, keys) * HEAD ** (-0.5))
         mixed.append(nn(weights.astype(BF16), values))
     mixed_ref[...] = jnp.concatenate(mixed, axis=1)
+    ways, shared = part_ref.shape[:2]
+    per_block = BLOCK // shared
+    outputs = blocks * cores * rows
     for i in range(align_ref.shape[0]):
         first = pl.multiple_of(align_ref[i] * BLOCK, BLOCK)
         chosen = mixed_ref[pl.ds(first, BLOCK), :].astype(BF16)
-        part_ref[i * BLOCK : (i + 1) * BLOCK, :] = nt(
-            chosen, full_ref[:, heads * 3 * HEAD :]
-        ).astype(BF16)
-
-
-def feature_kernel(shares, ways, place_ref, *refs):
-    feat_refs = refs[:ways]
-    own_ref, mine_ref, other_ref, after_ref, extra_ref, pred_ref, proj_ref, feat_ref = refs[ways:]
+        part = nt(chosen, full_ref[:, heads * 3 * HEAD :]).astype(BF16)
+        for k in range(per_block):
+            part_ref[i * per_block + k, :, :outputs] = part[k * shared : (k + 1) * shared]
+    for i in range(ways):
+        part_ref[i, :, outputs:] = feat_ref[...]
+
+
+def predict_kernel(
+    ways, place_ref, feat_ref, own_ref, mine_ref, other_ref, after_ref, pred_ref, proj_ref
+):
     features, columns = own_ref.shape
-    rows = feat_refs[0].shape[0]
     half = features // 2
+    first = pl.multiple_of(place_ref[0] * half, half)
+    second = pl.multiple_of((1 - place_ref[0]) * half, half)
     proj_ref[place_ref[1]] = own_ref[...]
+    for k in range(1, ways):
+        source = place_ref[1 + k]
+        proj_ref[source, pl.ds(first, half), :] = mine_ref[k - 1]
+        proj_ref[source, pl.ds(second, half), :] = other_ref[k - 1]
     for k in range(ways):
-        source = place_ref[1 + k]
-        feat_ref[pl.ds(pl.multiple_of(source * rows, rows), rows), :] = feat_refs[k][...]
-        if k > 0:
-            first = pl.multiple_of(place_ref[0] * half, half)
-            second = pl.multiple_of((1 - place_ref[0]) * half, half)
-            proj_ref[source, pl.ds(first, half), :] = mine_ref[k - 1]
-            proj_ref[source, pl.ds(second, half), :] = other_ref[k - 1]
-    for k in range(ways):
-        pred_ref[:, k * columns : (k + 1) * columns] = nn(feat_refs[0][...], proj_ref[k])
-    feat = feat_ref[...]
+        pred_ref[:, k * columns : (k + 1) * columns] = nn(feat_ref[...], proj_ref[k])
+
+
+def extra_kernel(shares, columns, place_ref, parts_ref, after_ref, extra_ref):
+    features = extra_ref.shape[1] * columns
+    rows = parts_ref.shape[0] * parts_ref.shape[1]
+    feat = parts_ref[...].reshape(rows, parts_ref.shape[2])[:, -features:]
     for half in range(2):
         core = place_ref[0] if half == 0 else 1 - place_ref[0]
         for b in range(features // columns):
@@ -159,9 +198,9 @@
     copy.start()
     rows, width = tokens_ref.shape
     ways, features, columns = proj_ref.shape
-    branch = parts_ref[0].astype(F32)
+    branch = parts_ref[0, :, :width].astype(F32)
     for i in range(1, ways):
-        branch = branch + parts_ref[i].astype(F32)
+        branch = branch + parts_ref[i, :, :width].astype(F32)
     target = (tokens_ref[...].astype(F32) + branch).astype(BF16).astype(F32)
     count = count_ref[0]
     live = lax.broadcasted_iota(jnp.int32, (rows, 1), 0) + place_ref[1] * rows < count
@@ -188,10 +227,19 @@
         out_ref[i, :, features + columns :] = tail
 
 
-def backward_kernel(
-    back_ref, packed_ref, weights_ref, mixed_ref, out_ref, pick_ref, normed_ref, feat_ref,
-    keep_ref, send_ref, loss_ref,
-):
+def backward_kernel(back_ref, *refs):
+    held = (len(refs) - 4) // 2
+    sources, (keep_ref, send_ref, loss_ref) = refs[:held], refs[held : held + 3]
+    buffers, sems = refs[held + 3 : -1], refs[-1]
+    copies = [
+        pltpu.make_async_copy(source, buffer, sems.at[i])
+        for i, (source, buffer) in enumerate(zip(sources, buffers))
+    ]
+    for copy in copies:
+        copy.start()
+    out_ref, packed_ref, weights_ref, mixed_ref, pick_ref, normed_ref, feat_ref = buffers
+    for copy in copies[:4]:
+        copy.wait()
     features = out_ref.shape[1]
     heads = out_ref.shape[0] // HEAD
     dfeat = back_ref[:, :features]
@@ -219,6 +267,8 @@
     mixed = jnp.concatenate(
         [jnp.zeros((length, used - tailed), F32), mixed_ref[...].astype(F32)], 1
     ).astype(BF16)
+    for copy in copies[4:]:
+        copy.wait()
     for half, into in enumerate((keep_ref, send_ref)):
         dfeat_rows = nt(pick_ref[half], dfeat).astype(BF16)
         normed_rows = normed_ref[half]
@@ -282,42 +332,48 @@
         name="spread_rows",
     )(teacher_qkv, teacher_out_t)
     own_core = lax.all_to_all(shard, ("y", "z"), 0, 0)
-    half = features // 2
-    proj_half = lax.dynamic_slice_in_dim(projector, own_c * half, half, 0)
-    proj_halves = jnp.stack(from_peers(lambda k: proj_half, "x"))
-
     heads = student_out.shape[0] // HEAD
     each = features // shares
     picked = shares // 2 * (each + each * columns // features)
-    core = own_c.astype(jnp.int32).reshape(1)
-    part, normed_rows, packed, mixed, weights, pick = pl.pallas_call(
-        lambda *refs: student_kernel(shares, columns, *refs),
+    places = jnp.stack([own_c] + [(own_x + k) % ways for k in range(ways)]).astype(jnp.int32)
+    message_rows = rows * features // columns + features // 2
+    outs = pl.pallas_call(
+        lambda *refs: student_kernel(shares, *refs),
         out_shape=(
-            shape((length, features), BF16),
+            shape((rows, features), BF16),
+            *[shape((message_rows, columns), BF16)] * (ways - 1),
             pltpu.HBM((2, picked, length), BF16),
             pltpu.HBM((length, 3 * HEAD * heads), BF16),
             pltpu.HBM((length, HEAD * heads), BF16),
             pltpu.HBM((heads, length, length), F32),
             pltpu.HBM((2, picked, features), BF16),
         ),
-        in_specs=[SMEM] * 2 + [VMEM] * 3,
-        out_specs=(VMEM,) + (pl.BlockSpec(),) * 5,
+        in_specs=[SMEM] * 2 + [VMEM] * 4,
+        out_specs=(VMEM,) * ways + (pl.BlockSpec(),) * 5,
+        scratch_shapes=[pltpu.VMEM((length, features), F32)],
         compiler_params=PARAMS,
         cost_estimate=cost(4),
         name="student_forward",
-    )(valid_counts, core, events, student_qkv.T, student_out)
-
-    own_rows = lambda array, place: lax.dynamic_slice_in_dim(array, place * rows, rows, 0)
-    branch = own_rows(part, own_x).astype(F32)
-    received = from_peers(lambda k: own_rows(part, (own_x + k) % ways), "x")
-    for other in received:
-        branch = branch + other.astype(F32)
-    feat_rows = (own_rows(events, own_x).astype(F32) + branch).astype(BF16)
-    feats = [feat_rows] + from_peers(lambda k: feat_rows, "x")
-    own_core, feats, proj_halves = lax.optimization_barrier((own_core, feats, proj_halves))
+    )(valid_counts, places, events, student_qkv.T, student_out, projector)
+    own_part, peer_parts = outs[0], outs[1:ways]
+    normed_rows, packed, mixed, weights, pick = outs[ways:]
+
+    received = from_peers(lambda k: peer_parts[k - 1], "x")
+    own_events = lax.dynamic_slice_in_dim(events, own_x * rows, rows, 0)
+    feat_rows, proj_halves = pl.pallas_call(
+        lambda *refs: rows_kernel(ways, *refs),
+        out_shape=(
+            shape((rows, features), BF16), shape((ways - 1, features // 2, columns), BF16),
+        ),
+        in_specs=[VMEM] * (ways + 1),
+        out_specs=(VMEM,) * 2,
+        compiler_params=PARAMS,
+        cost_estimate=cost(1),
+        name="student_rows",
+    )(own_events, own_part, *received)
+    own_core, feat_rows, proj_halves = lax.optimization_barrier((own_core, feat_rows, proj_halves))
     other_core = lax.ppermute(own_core, "c", SWAP)
     proj_others = lax.ppermute(proj_halves, "c", SWAP)
-    places = jnp.stack([own_c] + [(own_x - k + ways) % ways for k in range(ways)]).astype(jnp.int32)
     teacher_normed = pl.pallas_call(
         teacher_norm_kernel,
         out_shape=shape((length, width), BF16),
@@ -330,8 +386,8 @@
 
     teacher_part = pl.pallas_call(
         teacher_kernel,
-        out_shape=shape((length, width), BF16),
-        in_specs=[SMEM] * 2 + [VMEM] * 3,
+        out_shape=shape((ways, rows, width + features), BF16),
+        in_specs=[SMEM] * 2 + [VMEM] * 4,
         out_specs=VMEM,
         scratch_shapes=[
             pltpu.VMEM((senders, 2, *shard.shape[1:]), BF16),
@@ -340,48 +396,59 @@
         compiler_params=PARAMS,
         cost_estimate=cost(5),
         name="teacher",
-    )(places, align, teacher_normed, own_core, other_core)
-
-    teacher_parts = lax.all_to_all(teacher_part.reshape(ways, rows, width), "x", 0, 0)
+    )(places, align, teacher_normed, own_core, other_core, feat_rows)
+
+    teacher_parts = lax.all_to_all(teacher_part, "x", 0, 0)
     per_block = BLOCK // rows
     source = align[own_x // per_block] * BLOCK + own_x % per_block * rows
     own_tokens = lax.dynamic_slice_in_dim(clip, source, rows, 0)
-    feat_extra, pred, whole_proj = pl.pallas_call(
-        lambda *refs: feature_kernel(shares, ways, *refs),
-        out_shape=(
-            pltpu.HBM((2, features // columns, picked, length), BF16), shape((rows, width), F32),
-            pltpu.HBM((ways, features, columns), BF16),
-        ),
-        in_specs=[SMEM] + [pl.BlockSpec()] * (ways + 3) + [ANY],
-        out_specs=(pl.BlockSpec(), VMEM, pl.BlockSpec()),
-        scratch_shapes=[pltpu.VMEM((length, features), BF16)],
-        compiler_params=PARAMS,
-        cost_estimate=cost(4),
-        name="student_features",
-    )(places, *feats, projector, proj_halves, proj_others, teacher_part)
+    sources = jnp.stack([own_c] + [(own_x - k + ways) % ways for k in range(ways)]).astype(jnp.int32)
+    pred, whole_proj = pl.pallas_call(
+        lambda *refs: predict_kernel(ways, *refs),
+        out_shape=(shape((rows, width), F32), pltpu.HBM((ways, features, columns), BF16)),
+        in_specs=[SMEM] + [VMEM] * 4 + [ANY],
+        out_specs=(VMEM, pl.BlockSpec()),
+        compiler_params=PARAMS,
+        cost_estimate=cost(2),
+        name="student_predict",
+    )(sources, feat_rows, projector, proj_halves, proj_others, teacher_part)
     message = pl.pallas_call(
         lambda *refs: diff_kernel(shares, *refs),
         out_shape=shape((ways, rows, features + columns + BLOCK), BF16),
-        in_specs=[SMEM] * 2 + [VMEM] * 3 + [ANY],
+        in_specs=[SMEM] * 2 + [VMEM] * 3 + [HBM],
         out_specs=VMEM,
         scratch_shapes=[
             pltpu.VMEM((ways, features, columns), BF16), pltpu.SemaphoreType.DMA,
         ],
-        compiler_params=PARAMS,
+        compiler_params=FETCHING,
         cost_estimate=cost(2),
         name="difference",
     )(valid_counts, places, teacher_parts, own_tokens, pred, whole_proj)
+    feat_extra = pl.pallas_call(
+        lambda *refs: extra_kernel(shares, columns, *refs),
+        out_shape=pltpu.HBM((2, features // columns, picked, length), BF16),
+        in_specs=[SMEM, VMEM, ANY],
+        out_specs=pl.BlockSpec(),
+        compiler_params=PARAMS,
+        cost_estimate=cost(3),
+        name="student_extra",
+    )(sources, teacher_parts, message)
     back = lax.all_to_all(message, "x", 0, 0).reshape(length, features + columns + BLOCK)
 
+    held = (student_out, packed, weights, mixed, pick, normed_rows, feat_extra)
     keep, send, loss = pl.pallas_call(
         backward_kernel,
-        out_shape=(shape((picked, features), BF16), shape((picked, features), BF16), shape((1, 1), F32)),
-        in_specs=[VMEM] * 8,
+        out_shape=(
+            shape((picked, features), BF16), shape((picked, features), BF16), shape((1, 1), F32),
+        ),
+        in_specs=[VMEM] + [HBM] * len(held),
         out_specs=(VMEM,) * 3,
-        compiler_params=PARAMS,
+        scratch_shapes=[pltpu.VMEM(array.shape, array.dtype) for array in held]
+        + [pltpu.SemaphoreType.DMA((len(held),))],
+        compiler_params=FETCHING,
         cost_estimate=cost(4),
         name="student_backward",
-    )(back, packed, weights, mixed, student_out, pick, normed_rows, feat_extra)
+    )(back, *held)
 
     total = add(keep, lax.ppermute(send, "c", SWAP)).astype(BF16)
     chips = shares // 2

time: 144 us -> 140 us (0.972)
  waiting for transfers between devices: 5.69 us -> 26.9 us
  starting transfers between devices: 56.4 us -> 39.4 us
  blocking collectives: 47.3 us -> 35.5 us
  Pallas kernels: 19.2 us -> 25 us
  local copies, waits for them, and re-layouts: 9.5 us -> 7.93 us
    ppermute x9 -> x3, starting transfers between devices: 31.6 us -> 11.4 us  [from_peers(): lax.ppermute(rows(k), axis, [(i, (i + k) % ways) for i in range(ways)])]
    all_to_all x1 -> x2, waiting for transfers between devices: 3.41 us -> 17 us  [the longest x1 10.7 us: on_device(): teacher_parts = lax.all_to_all(teacher_part, 'x', 0, 0)]
    all_to_all x1 -> x0, blocking collectives: 11.8 us -> none  [on_device(): lax.all_to_all(message, 'x', 0, 0)]
    ppermute x9 -> x3, waiting for transfers between devices: 0.02 us -> 7.45 us  [from_peers(): lax.ppermute(rows(k), axis, [(i, (i + k) % ways) for i in range(ways)])]
    all_to_all x1 -> x2, starting transfers between devices: 4.75 us -> 7.82 us  [the longest x1 4.33 us: on_device(): teacher_parts = lax.all_to_all(teacher_part, 'x', 0, 0)]
    pallas_call x1, Pallas kernels: 3.51 us -> 5.66 us  [on_device(): pl.pallas_call(backward_kernel, out_shape=(shape((picked, features), BF16...]
    pallas_call x1, Pallas kernels: 1.47 us -> 3.53 us  [on_device(): pl.pallas_call(lambda *refs: diff_kernel(shares, *refs), out_shape=shape(...]
    pallas_call x3 -> x5, Pallas kernels: 12 us -> 13.6 us  [the longest x1 4.71 us: on_device(): pl.pallas_call(lambda *refs: student_kernel(shares, *refs), out_shape=(sh...]
  transfers between devices with their start and end apart: 14 -> 9, of which waited for: 2 -> 6; matrix products, arithmetic and copies ran while one was open for 2% -> 1% of each run, Pallas kernels for 9% -> 10%
where the time goes in v5:
time: 140 us; the launch traced here: 139 us
  starting transfers between devices  39.4 us (28%)
  blocking collectives  35.5 us (25%)
  waiting for transfers between devices  26.9 us (19%)
  Pallas kernels  25 us (18%)
  local copies, waits for them, and re-layouts  7.93 us (6%)
  between operations  2.21 us (2%)
  other arithmetic  1.9 us (1%)
    all_to_all x1, blocking collectives, on_device(): lax.all_to_all(total.reshape(chips, total.shape[0] // chips, features), C...  35.5 us
    all_to_all x1, starting transfers between devices, on_device(): own_core = lax.all_to_all(shard, ('y', 'z'), 0, 0)  13.9 us
    ppermute x3, starting transfers between devices, from_peers(): lax.ppermute(rows(k), axis, [(i, (i + k) % ways) for i in range(ways)])  11.4 us
    all_to_all x1, waiting for transfers between devices, on_device(): teacher_parts = lax.all_to_all(teacher_part, 'x', 0, 0)  10.7 us
    unnamed x40, local copies, waits for them, and re-layouts  7.74 us
    ppermute x3, waiting for transfers between devices, from_peers(): lax.ppermute(rows(k), axis, [(i, (i + k) % ways) for i in range(ways)])  7.45 us
    all_to_all x1, waiting for transfers between devices, on_device(): lax.all_to_all(message, 'x', 0, 0)  6.26 us
    pallas_call x1, Pallas kernels, on_device(): pl.pallas_call(backward_kernel, out_shape=(shape((picked, features), BF16...  5.66 us
  transfers between devices with their start and end apart: 9, of which 6 were waited for; matrix products, arithmetic and copies ran while one was open for 1% of the time, Pallas kernels for 10%

profile of v5, /device:TPU:16, one launch (start us, length us, event | category | flops | bytes accessed | tf_op | source)
XLA Modules:
  0.0 138.8 jit_solution(3222870303799425824)
XLA Ops:
  0.7 0.8 copy-done.2
  2.1 1.1 spread_rows.1
  3.2 13.9 %all-to-all-start = ((bf16[32,16,1024]{2,1,0:T(8,128)(2,1)}), bf16[32,16,1024]{2,1,0:T(8,128)(2,1)S(1)}, u32[]{:S(2)}, u32[]{:S(2)}) async-start(bf16[32,16,1024]{2,1,0:T(8,128)(2,1)} %spread_rows.1), calls=%async_computation | async-start | bytes 2097152 | tf_op jit(solution)/shard_map/all_to_all | solution.py:334
  17.9 4.7 %student_forward.1 = (bf16[64,768]{1,0:T(8,128)(2,1)S(1)}, bf16[576,256]{1,0:T(8,128)(2,1)}, bf16[576,256]{1,0:T(8,128)(2,1)}, bf16[576,256]{1,0:T(8,128)(2,1)S(...) custom-call(s32[1]{0:T(128)S(6)} %copy.14.refs_0_, ...), custom_call_target="tpu_custom_call" | custom-call | flops 4000000000 | bytes 1000000 | tf_op jit(solution)/shard_map/student_forward/pallas_call | solution.py:340
  22.6 3.4 %collective-permute-start = (bf16[576,256]{1,0:T(8,128)(2,1)}, bf16[576,256]{1,0:T(8,128)(2,1)S(1)}, u32[]{:S(2)}, u32[]{:S(2)}) collective-permute-start(bf16[576,256]{1,0:T(8,128)(2,1)} %get-tuple-element.27), channel_id=1, source_target_pairs={{0,1},{1,2},{2,3},{3,0},{4,5},{5,6},{6,7},{7,4},{8,9},{9,10},{10,1... | collective-permute-start | bytes 884744 | tf_op jit(solution)/shard_map/ppermute | solution.py:289
  26.0 4.6 %collective-permute-start.1 = (bf16[576,256]{1,0:T(8,128)(2,1)}, bf16[576,256]{1,0:T(8,128)(2,1)S(1)}, u32[]{:S(2)}, u32[]{:S(2)}) collective-permute-start(bf16[576,256]{1,0:T(8,128)(2,1)} %get-tuple-element.28), channel_id=1, source_target_pairs={{0,2},{1,3},{2,0},{3,1},{4,6},{5,7},{6,4},{7,5},{8,10},{9,11},{10,... | collective-permute-start | bytes 884744 | tf_op jit(solution)/shard_map/ppermute | solution.py:289
  30.6 3.3 %collective-permute-start.2 = (bf16[576,256]{1,0:T(8,128)(2,1)S(1)}, bf16[576,256]{1,0:T(8,128)(2,1)S(1)}, u32[]{:S(2)}, u32[]{:S(2)}) collective-permute-start(bf16[576,256]{1,0:T(8,128)(2,1)S(1)} %get-tuple-element.29), channel_id=1, source_target_pairs={{0,3},{1,0},{2,1},{3,2},{4,7},{5,4},{6,5},{7,6},{8,11},{9,8},{10,9... | collective-permute-start | bytes 884744 | tf_op jit(solution)/shard_map/ppermute | solution.py:289
  34.0 0.9 collective-permute-done.refs_2_
  34.9 0.7 copy-done.7
  35.6 5.8 %collective-permute-done.1.refs_3_ = bf16[576,256]{1,0:T(8,128)(2,1)S(1)} collective-permute-done((bf16[576,256]{1,0:T(8,128)(2,1)}, bf16[576,256]{1,0:T(8,128)(2,1)S(1)}, u32[]{:S(2)}, u32[]{:S(2)}) %collective-permute-start.1) | collective-permute-done | bytes 294944 | tf_op jit(solution)/shard_map/ppermute | solution.py:289
  42.1 0.8 collective-permute-done.2.refs_4_
  42.9 0.7 copy-done.11
  43.6 1.0 copy-done.8
  44.6 1.0 copy-done.10
  45.6 1.0 copy-done.12
  46.5 0.9 copy-done.16
  47.5 2.1 %collective-permute-start.3 = (bf16[32,16,1024]{2,1,0:T(8,128)(2,1)S(1)}, bf16[32,16,1024]{2,1,0:T(8,128)(2,1)S(1)}, u32[]{:S(2)}, u32[]{:S(2)}) collective-permute-start(bf16[32,16,1024]{2,1,0:T(8,128)(2,1)S(1)} %all-to-all-done.own_ref), channel_id=1, source_target_pairs={{0,4},{4,0},{1,5},{5,1},{2,6},{6,2},{3,7},{7,3},{8,12},{12,8},{9,1... | collective-permute-start | bytes 3145736 | tf_op jit(solution)/shard_map/ppermute | solution.py:375
  49.6 2.4 %collective-permute-start.4 = (bf16[3,384,256]{2,1,0:T(8,128)(2,1)S(1)}, bf16[3,384,256]{2,1,0:T(8,128)(2,1)S(1)}, u32[]{:S(2)}, u32[]{:S(2)}) collective-permute-start(bf16[3,384,256]{2,1,0:T(8,128)(2,1)S(1)} %get-tuple-element.34.refs_3_), channel_id=1, source_target_pairs={{0,4},{4,0},{1,5},{5,1},{2,6},{6,2},{3,7},{7,3},{8,12},{12,8},{9,1... | collective-permute-start | bytes 1769480 | tf_op jit(solution)/shard_map/ppermute | solution.py:376
  52.7 3.9 %teacher.1.refs_5_ = bf16[4,64,1792]{2,1,0:T(8,128)(2,1)} custom-call(s32[5]{0:T(128)S(1)} %stack.33.refs_1_.place_ref, s32[2]{0:T(128)S(1)} %bitcast.26, bf16[256,1024]{1,0:T(8,128)(2,1)S(1)} %teacher_norm.1.normed_ref, bf16[32,16,1024]{2,1,0:T(8,128)(2,1)S(1)} %all-to-all-done.own_ref, bf16[32,16,1024]{2,1,0:T(8,128)(2,1)S(1)} %collective-permute-done.3.other_ref, ...), custom_call_target="tpu_custom_call" | custom-call | flops 5000000000 | bytes 1000000 | tf_op jit(solution)/shard_map/teacher/pallas_call | solution.py:387
  56.5 4.3 %all-to-all-start.1 = ((bf16[4,64,1792]{2,1,0:T(8,128)(2,1)}), bf16[4,64,1792]{2,1,0:T(8,128)(2,1)S(1)}, u32[]{:S(2)}, u32[]{:S(2)}) async-start(bf16[4,64,1792]{2,1,0:T(8,128)(2,1)} %teacher.1.refs_5_), calls=%async_computation.1 | async-start | bytes 1835008 | tf_op jit(solution)/shard_map/all_to_all | solution.py:401
  62.2 1.8 %student_predict.1 = (f32[64,1024]{1,0:T(8,128)S(1)}, bf16[4,768,256]{2,1,0:T(8,128)(2,1)}) custom-call(s32[5]{0:T(128)S(1)} %stack.35.refs_0_, bf16[64,768]{1,0:T(8,128)(2,1)S(1)} %get-tuple-element.32.after_ref.feat_ref.refs_1_, bf16[768,256]{1,0:T(8,128)(2,1)S(1)} %copy-done.5, bf16[3,384,256]{2,1,0:T(8,128)(2,1)S(1)} %get-tuple-element.34.refs_3_, ...), custom_call_target="tpu_custom_call" | custom-call | flops 2000000000 | bytes 1000000 | tf_op jit(solution)/shard_map/student_predict/pallas_call | solution.py:406
  64.0 10.7 %all-to-all-done.1.refs_2_.refs_1_ = bf16[4,64,1792]{2,1,0:T(8,128)(2,1)S(1)} async-done(((bf16[4,64,1792]{2,1,0:T(8,128)(2,1)}), bf16[4,64,1792]{2,1,0:T(8,128)(2,1)S(1)}, u32[]{:S(2)}, u32[]{:S(2)}) %all-to-all-start.1) | async-done | bytes 917536 | tf_op jit(solution)/shard_map/all_to_all | solution.py:401
  74.7 3.5 %difference.1.refs_2_ = bf16[4,64,1152]{2,1,0:T(8,128)(2,1)} custom-call(s32[1]{0:T(128)S(6)} %copy.14.refs_0_, s32[5]{0:T(128)S(1)} %stack.33.refs_1_.place_ref, bf16[4,64,1792]{2,1,0:T(8,128)(2,1)S(1)} %all-to-all-done.1.refs_2_.refs_1_, bf16[64,1024]{1,0:T(8,128)(2,1)S(1)} %dynamic-slice_bitcast_fusion.refs_3_, f32[64,1024]{1,0:T(8,128)S(1)} %get-tuple-element.35.refs_4_, ...), custom_call_target="tpu_custom_call" | custom-call | flops 2000000000 | bytes 1000000 | tf_op jit(solution)/shard_map/difference/pallas_call | solution.py:415
  78.3 3.5 %all-to-all-start.2 = ((bf16[4,64,1152]{2,1,0:T(8,128)(2,1)}), bf16[4,64,1152]{2,1,0:T(8,128)(2,1)S(1)}, u32[]{:S(2)}, u32[]{:S(2)}) async-start(bf16[4,64,1152]{2,1,0:T(8,128)(2,1)} %difference.1.refs_2_), calls=%async_computation.2 | async-start | bytes 1179648 | tf_op jit(solution)/shard_map/all_to_all | solution.py:436
  81.8 3.1 %student_extra.1.refs_6_ = bf16[2,3,512,256]{3,2,1,0:T(8,128)(2,1)} custom-call(s32[5]{0:T(128)S(1)} %stack.35.refs_0_, bf16[4,64,1792]{2,1,0:T(8,128)(2,1)S(1)} %all-to-all-done.1.refs_2_.refs_1_, bf16[4,64,1152]{2,1,0:T(8,128)(2,1)} %difference.1.refs_2_), custom_call_target="tpu_custom_call" | custom-call | flops 3000000000 | bytes 1000000 | tf_op jit(solution)/shard_map/student_extra/pallas_call | solution.py:427
  84.9 6.3 %all-to-all-done.2 = bf16[4,64,1152]{2,1,0:T(8,128)(2,1)S(1)} async-done(((bf16[4,64,1152]{2,1,0:T(8,128)(2,1)}), bf16[4,64,1152]{2,1,0:T(8,128)(2,1)S(1)}, u32[]{:S(2)}, u32[]{:S(2)}) %all-to-all-start.2) | async-done | bytes 589856 | tf_op jit(solution)/shard_map/all_to_all | solution.py:436
  91.2 5.7 %student_backward.1 = (bf16[512,768]{1,0:T(8,128)(2,1)}, bf16[512,768]{1,0:T(8,128)(2,1)}, f32[1,1]{1,0:T(1,128)}) custom-call(bf16[256,1152]{1,0:T(8,128)(2,1)S(1)} %bitcast.21, bf16[192,768]{1,0:T(8,128)(2,1)S(1)} %copy-done.6, bf16[256,576]{1,0:T(8,128)(2,1)S(1)} %copy-done.18, f32[3,256,256]{2,1,0:T(8,128)} %get-tuple-element.38.refs_2_, ...), custom_call_target="tpu_custom_call" | custom-call | flops 4000000000 | bytes 1000000 | tf_op jit(solution)/shard_map/student_backward/pallas_call | solution.py:439
  96.9 1.9 %collective-permute-start.5 = (bf16[512,768]{1,0:T(8,128)(2,1)}, bf16[512,768]{1,0:T(8,128)(2,1)S(1)}, u32[]{:S(2)}, u32[]{:S(2)}) collective-permute-start(bf16[512,768]{1,0:T(8,128)(2,1)} %get-tuple-element.44), channel_id=1, source_target_pairs={{0,4},{4,0},{1,5},{5,1},{2,6},{6,2},{3,7},{7,3},{8,12},{12,8},{9,1... | collective-permute-start | bytes 2359304 | tf_op jit(solution)/shard_map/ppermute | solution.py:453
  98.8 2.5 %collective-permute-done.5 = bf16[512,768]{1,0:T(8,128)(2,1)S(1)} collective-permute-done((bf16[512,768]{1,0:T(8,128)(2,1)}, bf16[512,768]{1,0:T(8,128)(2,1)S(1)}, u32[]{:S(2)}, u32[]{:S(2)}) %collective-permute-start.5) | collective-permute-done | bytes 786464 | tf_op jit(solution)/shard_map/ppermute | solution.py:453
  101.3 1.3 fusion
  102.6 35.5 %all_to_all.20.parts_ref = bf16[64,8,768]{2,1,0:T(8,128)(2,1)S(1)} all-to-all(bf16[64,8,768]{2,1,0:T(8,128)(2,1)S(1)} %fusion), channel_id=1, replica_groups=mesh['g'=2,'y'=4,'z'=8,'c'=2,'x'=4] {'g','y','z'}, dimensions={0} | all-to-all | bytes 1572864 | tf_op jit(solution)/shard_map/all_to_all | solution.py:455
  138.1 0.8 gradient_rows.1
  (43 shorter events, 3.0 us)
Async XLA Ops:
  0.6 17.2 %copy-start.1 = (bf16[1,256,768]{2,1,0:T(8,128)(2,1)S(1)}, bf16[1,256,768]{2,1,0:T(8,128)(2,1)}, u32[]{:S(2)}) copy-start(bf16[1,256,768]{2,1,0:T(8,128)(2,1)} %param.14) | copy-start | bytes 1179652
  0.6 0.8 copy-start.2
  1.4 0.7 copy-start.3
  2.1 15.7 %copy-start.4 = (bf16[768,576]{0,1:T(8,128)(2,1)S(1)}, bf16[768,576]{0,1:T(8,128)(2,1)}, u32[]{:S(2)}) copy-start(bf16[768,576]{0,1:T(8,128)(2,1)} %param.17) | copy-start | bytes 2654212
  2.1 15.7 %copy-start.5 = (bf16[768,256]{1,0:T(8,128)(2,1)S(1)}, bf16[768,256]{1,0:T(8,128)(2,1)}, u32[]{:S(2)}) copy-start(bf16[768,256]{1,0:T(8,128)(2,1)} %refs_2_.1) | copy-start | bytes 1179652
  2.1 15.7 %copy-start.6 = (bf16[192,768]{1,0:T(8,128)(2,1)S(1)}, bf16[192,768]{1,0:T(8,128)(2,1)}, u32[]{:S(2)}) copy-start(bf16[192,768]{1,0:T(8,128)(2,1)} %refs_0_.3) | copy-start | bytes 884740
  3.2 44.3 %all-to-all-start = ((bf16[32,16,1024]{2,1,0:T(8,128)(2,1)}), bf16[32,16,1024]{2,1,0:T(8,128)(2,1)S(1)}, u32[]{:S(2)}, u32[]{:S(2)}) async-start(bf16[32,16,1024]{2,1,0:T(8,128)(2,1)} %spread_rows.1), calls=%async_computation | async-start | bytes 2097152 | tf_op jit(solution)/shard_map/all_to_all | solution.py:334
  22.6 20.3 %copy-start.15 = (bf16[64,768]{1,0:T(8,128)(2,1)}, bf16[64,768]{1,0:T(8,128)(2,1)S(1)}, u32[]{:S(2)}) copy-start(bf16[64,768]{1,0:T(8,128)(2,1)S(1)} %get-tuple-element.26.refs_1_) | copy-start | bytes 294916
  22.6 12.3 %collective-permute-start = (bf16[576,256]{1,0:T(8,128)(2,1)}, bf16[576,256]{1,0:T(8,128)(2,1)S(1)}, u32[]{:S(2)}, u32[]{:S(2)}) collective-permute-start(bf16[576,256]{1,0:T(8,128)(2,1)} %get-tuple-element.27), channel_id=1, source_target_pairs={{0,1},{1,2},{2,3},{3,0},{4,5},{5,6},{6,7},{7,4},{8,9},{9,10},{10,1... | collective-permute-start | bytes 884744 | tf_op jit(solution)/shard_map/ppermute | solution.py:289
  26.0 15.4 %collective-permute-start.1 = (bf16[576,256]{1,0:T(8,128)(2,1)}, bf16[576,256]{1,0:T(8,128)(2,1)S(1)}, u32[]{:S(2)}, u32[]{:S(2)}) collective-permute-start(bf16[576,256]{1,0:T(8,128)(2,1)} %get-tuple-element.28), channel_id=1, source_target_pairs={{0,2},{1,3},{2,0},{3,1},{4,6},{5,7},{6,4},{7,5},{8,10},{9,11},{10,... | collective-permute-start | bytes 884744 | tf_op jit(solution)/shard_map/ppermute | solution.py:289
  30.6 12.3 %collective-permute-start.2 = (bf16[576,256]{1,0:T(8,128)(2,1)S(1)}, bf16[576,256]{1,0:T(8,128)(2,1)S(1)}, u32[]{:S(2)}, u32[]{:S(2)}) collective-permute-start(bf16[576,256]{1,0:T(8,128)(2,1)S(1)} %get-tuple-element.29), channel_id=1, source_target_pairs={{0,3},{1,0},{2,1},{3,2},{4,7},{5,4},{6,5},{7,6},{8,11},{9,8},{10,9... | collective-permute-start | bytes 884744 | tf_op jit(solution)/shard_map/ppermute | solution.py:289
  34.9 0.7 copy-start.7
  41.4 0.7 copy-start.9
  42.9 0.7 copy-start.11
  43.6 1.0 copy-start.8
  44.6 1.0 copy-start.10
  45.6 1.0 copy-start.12
  46.5 0.9 copy-start.16
  47.4 4.6 %copy-start = (bf16[1,256,1024]{2,1,0:T(8,128)(2,1)S(1)}, bf16[1,256,1024]{2,1,0:T(8,128)(2,1)}, u32[]{:S(2)}) copy-start(bf16[1,256,1024]{2,1,0:T(8,128)(2,1)} %param.10) | copy-start | bytes 1572868
  47.4 4.6 %copy-start.13 = (f32[1024]{0:T(1024)S(1)}, f32[1024]{0:T(1024)}, u32[]{:S(2)}) copy-start(f32[1024]{0:T(1024)} %param.11) | copy-start | bytes 12292
  47.5 4.9 %collective-permute-start.3 = (bf16[32,16,1024]{2,1,0:T(8,128)(2,1)S(1)}, bf16[32,16,1024]{2,1,0:T(8,128)(2,1)S(1)}, u32[]{:S(2)}, u32[]{:S(2)}) collective-permute-start(bf16[32,16,1024]{2,1,0:T(8,128)(2,1)S(1)} %all-to-all-done.own_ref), channel_id=1, source_target_pairs={{0,4},{4,0},{1,5},{5,1},{2,6},{6,2},{3,7},{7,3},{8,12},{12,8},{9,1... | collective-permute-start | bytes 3145736 | tf_op jit(solution)/shard_map/ppermute | solution.py:375
  49.6 12.7 %collective-permute-start.4 = (bf16[3,384,256]{2,1,0:T(8,128)(2,1)S(1)}, bf16[3,384,256]{2,1,0:T(8,128)(2,1)S(1)}, u32[]{:S(2)}, u32[]{:S(2)}) collective-permute-start(bf16[3,384,256]{2,1,0:T(8,128)(2,1)S(1)} %get-tuple-element.34.refs_3_), channel_id=1, source_target_pairs={{0,4},{4,0},{1,5},{5,1},{2,6},{6,2},{3,7},{7,3},{8,12},{12,8},{9,1... | collective-permute-start | bytes 1769480 | tf_op jit(solution)/shard_map/ppermute | solution.py:376
  52.0 0.7 copy-start.14
  56.5 18.2 %all-to-all-start.1 = ((bf16[4,64,1792]{2,1,0:T(8,128)(2,1)}), bf16[4,64,1792]{2,1,0:T(8,128)(2,1)S(1)}, u32[]{:S(2)}, u32[]{:S(2)}) async-start(bf16[4,64,1792]{2,1,0:T(8,128)(2,1)} %teacher.1.refs_5_), calls=%async_computation.1 | async-start | bytes 1835008 | tf_op jit(solution)/shard_map/all_to_all | solution.py:401
  78.3 12.9 %all-to-all-start.2 = ((bf16[4,64,1152]{2,1,0:T(8,128)(2,1)}), bf16[4,64,1152]{2,1,0:T(8,128)(2,1)S(1)}, u32[]{:S(2)}, u32[]{:S(2)}) async-start(bf16[4,64,1152]{2,1,0:T(8,128)(2,1)} %difference.1.refs_2_), calls=%async_computation.2 | async-start | bytes 1179648 | tf_op jit(solution)/shard_map/all_to_all | solution.py:436
  81.8 9.4 %copy-start.17 = (bf16[2,512,256]{2,1,0:T(8,128)(2,1)S(1)}, bf16[2,512,256]{2,1,0:T(8,128)(2,1)}, u32[]{:S(2)}) copy-start(bf16[2,512,256]{2,1,0:T(8,128)(2,1)} %get-tuple-element.41.refs_5_) | copy-start | bytes 1572868
  81.8 9.4 %copy-start.18 = (bf16[256,576]{1,0:T(8,128)(2,1)S(1)}, bf16[256,576]{1,0:T(8,128)(2,1)}, u32[]{:S(2)}) copy-start(bf16[256,576]{1,0:T(8,128)(2,1)} %get-tuple-element.37.refs_1_) | copy-start | bytes 884740
  81.8 9.4 %copy-start.19 = (bf16[256,192]{1,0:T(8,128)(2,1)S(1)}, bf16[256,192]{1,0:T(8,128)(2,1)}, u32[]{:S(2)}) copy-start(bf16[256,192]{1,0:T(8,128)(2,1)} %get-tuple-element.39.refs_3_) | copy-start | bytes 294916
  96.9 4.4 %collective-permute-start.5 = (bf16[512,768]{1,0:T(8,128)(2,1)}, bf16[512,768]{1,0:T(8,128)(2,1)S(1)}, u32[]{:S(2)}, u32[]{:S(2)}) collective-permute-start(bf16[512,768]{1,0:T(8,128)(2,1)} %get-tuple-element.44), channel_id=1, source_target_pairs={{0,4},{4,0},{1,5},{5,1},{2,6},{6,2},{3,7},{7,3},{8,12},{12,8},{9,1... | collective-permute-start | bytes 2359304 | tf_op jit(solution)/shard_map/ppermute | solution.py:453

commit v6 on v5

--- a/solution.py
+++ b/solution.py
@@ -15,11 +15,30 @@
 VMEM = pl.BlockSpec(memory_space=pltpu.VMEM)
 SMEM = pl.BlockSpec(memory_space=pltpu.SMEM)
 PARAMS = pltpu.CompilerParams(vmem_limit_bytes=20 * 1024 * 1024)
-FETCHING = pltpu.CompilerParams(vmem_limit_bytes=52 * 1024 * 1024)
 
 
 def cost(microseconds):
     return pl.CostEstimate(flops=microseconds * 10**9, bytes_accessed=10**6, transcendentals=0)
+
+
+def fetch(sources, buffers, sems):
+    copies = [
+        pltpu.make_async_copy(source, buffer, sems.at[i])
+        for i, (source, buffer) in enumerate(zip(sources, buffers))
+    ]
+    for copy in copies:
+        copy.start()
+    return copies
+
+
+def buffers(arrays):
+    return [pltpu.VMEM(array.shape, array.dtype) for array in arrays] + [
+        pltpu.SemaphoreType.DMA((len(arrays),))
+    ]
+
+
+def in_place(arrays):
+    return [pltpu.HBM(array.shape, array.dtype) for array in arrays]
 
 
 def shape(dims, dtype):
@@ -62,32 +81,28 @@
     place = lax.broadcasted_iota(jnp.int32, (shares // 2 * block, 1), 0)
     chip, row = place // block, place % block
     base = (chip * 2 + core) * each
-    if extra is None:
+    if extra:
+        wanted = jnp.where(row >= each, base + (row - each) * (rows // columns), -1)
+    else:
         wanted = jnp.where(row < each, base + row, -1)
-    else:
-        wanted = jnp.where(row >= each, base + (row - each) * (rows // columns) + extra, -1)
     source = lax.broadcasted_iota(jnp.int32, (shares // 2 * block, rows), 1)
     return jnp.where(source == wanted, 1.0, 0.0).astype(BF16)
-
-
-def spread_kernel(qkv_ref, out_ref, spread_ref):
-    joined = jnp.concatenate([qkv_ref[...], out_ref[...]], 1)
-    spread_ref[...] = jnp.broadcast_to(joined[None], spread_ref.shape)
 
 
 def student_kernel(
     shares, count_ref, place_ref, events_ref, qkv_ref, out_ref, proj_ref, *refs
 ):
-    ways = len(refs) - 6
+    ways = len(refs) - 7
     own_ref, peer_refs = refs[0], refs[1:ways]
-    normed_ref, packed_ref, mixed_ref, weights_ref, pick_ref, part_ref = refs[ways:]
+    normed_ref, packed_ref, mixed_ref, weights_ref, pick_ref, kept_ref, part_ref = refs[ways:]
+    kept_ref[...] = out_ref[...]
     columns = proj_ref.shape[1]
     length, features = events_ref.shape
     heads = out_ref.shape[0] // HEAD
     normed = norm_rows(events_ref[...]).astype(BF16)
     for half in range(2):
         core = place_ref[0] if half == 0 else 1 - place_ref[0]
-        pick_ref[half] = pick_rows(features, shares, columns, core, None)
+        pick_ref[half] = pick_rows(features, shares, columns, core, False)
         normed_ref[half] = nt(pick_ref[half], normed).astype(BF16)
     packed = nt(normed, qkv_ref[...])
     packed_ref[...] = packed.astype(BF16)
@@ -117,8 +132,11 @@
         peer_refs[k - 1][blocks * rows :] = proj_half
 
 
-def rows_kernel(ways, events_ref, own_ref, *refs):
-    peer_refs, (feat_ref, proj_ref) = refs[: ways - 1], refs[ways - 1 :]
+def rows_kernel(ways, *refs):
+    sources, (feat_ref, proj_ref), held = refs[: ways + 1], refs[ways + 1 : ways + 3], refs[-ways - 2 : -1]
+    for copy in fetch(sources, held, refs[-1]):
+        copy.wait()
+    events_ref, own_ref, *peer_refs = held
     rows, features = own_ref.shape
     columns = proj_ref.shape[2]
     for b in range(features // columns):
@@ -136,7 +154,7 @@
 
 
 def teacher_kernel(
-    place_ref, align_ref, normed_ref, own_ref, other_ref, feat_ref, part_ref, parts_ref, mixed_ref
+    place_ref, align_ref, normed_ref, own_ref, other_ref, part_ref, parts_ref, mixed_ref
 ):
     blocks, cores, rows, width = parts_ref.shape
     for i, piece in enumerate((own_ref, other_ref)):
@@ -151,17 +169,14 @@
         weights = softmax(nt(query, keys) * HEAD ** (-0.5))
         mixed.append(nn(weights.astype(BF16), values))
     mixed_ref[...] = jnp.concatenate(mixed, axis=1)
-    ways, shared = part_ref.shape[:2]
+    shared = part_ref.shape[1]
     per_block = BLOCK // shared
-    outputs = blocks * cores * rows
     for i in range(align_ref.shape[0]):
         first = pl.multiple_of(align_ref[i] * BLOCK, BLOCK)
         chosen = mixed_ref[pl.ds(first, BLOCK), :].astype(BF16)
         part = nt(chosen, full_ref[:, heads * 3 * HEAD :]).astype(BF16)
         for k in range(per_block):
-            part_ref[i * per_block + k, :, :outputs] = part[k * shared : (k + 1) * shared]
-    for i in range(ways):
-        part_ref[i, :, outputs:] = feat_ref[...]
+            part_ref[i * per_block + k] = part[k * shared : (k + 1) * shared]
 
 
 def predict_kernel(
@@ -180,27 +195,36 @@
         pred_ref[:, k * columns : (k + 1) * columns] = nn(feat_ref[...], proj_ref[k])
 
 
-def extra_kernel(shares, columns, place_ref, parts_ref, after_ref, extra_ref):
-    features = extra_ref.shape[1] * columns
-    rows = parts_ref.shape[0] * parts_ref.shape[1]
-    feat = parts_ref[...].reshape(rows, parts_ref.shape[2])[:, -features:]
+def extra_kernel(shares, columns, ways, place_ref, *refs):
+    sources, (after_ref, extra_ref) = refs[:ways], refs[ways : ways + 2]
+    pieces, feat_ref, sems = refs[ways + 2 : -2], refs[-2], refs[-1]
+    copies = fetch(sources, pieces, sems)
+    rows, features = pieces[0].shape
+    for k in range(ways):
+        copies[k].wait()
+        first = pl.multiple_of(place_ref[1 + k] * rows, rows)
+        feat_ref[pl.ds(first, rows), :] = pieces[k][...]
+    feat = feat_ref[...]
+    shifted = [feat]
+    for b in range(1, features // columns):
+        shifted.append(jnp.concatenate([feat[:, b:], feat[:, :b]], 1))
     for half in range(2):
         core = place_ref[0] if half == 0 else 1 - place_ref[0]
+        pick = pick_rows(features, shares, columns, core, True)
         for b in range(features // columns):
-            pick = pick_rows(features, shares, columns, core, b)
-            extra_ref[half, b] = nt(pick, feat).astype(BF16)
+            extra_ref[half, b] = nt(pick, shifted[b]).astype(BF16)
 
 
 def diff_kernel(
-    clips, count_ref, place_ref, parts_ref, tokens_ref, pred_ref, source_ref, out_ref, proj_ref, sem
+    clips, count_ref, place_ref, parts_ref, tokens_ref, pred_ref, source_ref,
+    out_ref, kept_ref, proj_ref, sems,
 ):
-    copy = pltpu.make_async_copy(source_ref, proj_ref, sem)
-    copy.start()
+    (copy,) = fetch([source_ref], [proj_ref], sems)
     rows, width = tokens_ref.shape
     ways, features, columns = proj_ref.shape
-    branch = parts_ref[0, :, :width].astype(F32)
+    branch = parts_ref[0].astype(F32)
     for i in range(1, ways):
-        branch = branch + parts_ref[i, :, :width].astype(F32)
+        branch = branch + parts_ref[i].astype(F32)
     target = (tokens_ref[...].astype(F32) + branch).astype(BF16).astype(F32)
     count = count_ref[0]
     live = lax.broadcasted_iota(jnp.int32, (rows, 1), 0) + place_ref[1] * rows < count
@@ -227,19 +251,11 @@
         out_ref[i, :, features + columns :] = tail
 
 
-def backward_kernel(back_ref, *refs):
-    held = (len(refs) - 4) // 2
+def backward_kernel(held, back_ref, *refs):
     sources, (keep_ref, send_ref, loss_ref) = refs[:held], refs[held : held + 3]
-    buffers, sems = refs[held + 3 : -1], refs[-1]
-    copies = [
-        pltpu.make_async_copy(source, buffer, sems.at[i])
-        for i, (source, buffer) in enumerate(zip(sources, buffers))
-    ]
-    for copy in copies:
-        copy.start()
-    out_ref, packed_ref, weights_ref, mixed_ref, pick_ref, normed_ref, feat_ref = buffers
-    for copy in copies[:4]:
-        copy.wait()
+    copies = fetch(sources, refs[2 * held + 3 : -1], refs[-1])
+    out_ref, packed_ref, weights_ref, mixed_ref, normed_ref, pick_ref, feat_ref = refs[2 * held + 3 : -1]
+    copies[0].wait()
     features = out_ref.shape[1]
     heads = out_ref.shape[0] // HEAD
     dfeat = back_ref[:, :features]
@@ -248,6 +264,8 @@
     tail = back_ref[:, features + columns :].astype(F32)
     loss_ref[...] = jnp.sum(jnp.sum(tail, 0, keepdims=True), 1, keepdims=True)
     dmixed = nt(dfeat, out_ref[...])
+    for copy in copies[1:3]:
+        copy.wait()
     packed = packed_ref[...].astype(F32)
     pieces = []
     for head in range(heads):
@@ -263,12 +281,12 @@
     used = dpacked.shape[1]
     length = dpacked.shape[0]
     right = jnp.concatenate([dpacked, jnp.zeros((length, features - used), F32)], 1).astype(BF16)
+    for copy in copies[3:]:
+        copy.wait()
     tailed = features - columns
     mixed = jnp.concatenate(
         [jnp.zeros((length, used - tailed), F32), mixed_ref[...].astype(F32)], 1
     ).astype(BF16)
-    for copy in copies[4:]:
-        copy.wait()
     for half, into in enumerate((keep_ref, send_ref)):
         dfeat_rows = nt(pick_ref[half], dfeat).astype(BF16)
         normed_rows = normed_ref[half]
@@ -323,14 +341,8 @@
         shares = shares * lax.axis_size(axis)
 
     senders = lax.axis_size("y") * lax.axis_size("z")
-    shard = pl.pallas_call(
-        spread_kernel,
-        out_shape=shape(
-            (senders, teacher_qkv.shape[0], teacher_qkv.shape[1] + teacher_out_t.shape[1]), BF16
-        ),
-        compiler_params=PARAMS,
-        name="spread_rows",
-    )(teacher_qkv, teacher_out_t)
+    shard = jnp.concatenate([teacher_qkv, teacher_out_t], 1)
+    shard = jnp.broadcast_to(shard[None], (senders, *shard.shape))
     own_core = lax.all_to_all(shard, ("y", "z"), 0, 0)
     heads = student_out.shape[0] // HEAD
     each = features // shares
@@ -340,23 +352,24 @@
     outs = pl.pallas_call(
         lambda *refs: student_kernel(shares, *refs),
         out_shape=(
-            shape((rows, features), BF16),
+            pltpu.HBM((rows, features), BF16),
             *[shape((message_rows, columns), BF16)] * (ways - 1),
             pltpu.HBM((2, picked, length), BF16),
             pltpu.HBM((length, 3 * HEAD * heads), BF16),
             pltpu.HBM((length, HEAD * heads), BF16),
             pltpu.HBM((heads, length, length), F32),
             pltpu.HBM((2, picked, features), BF16),
+            *in_place([student_out]),
         ),
         in_specs=[SMEM] * 2 + [VMEM] * 4,
-        out_specs=(VMEM,) * ways + (pl.BlockSpec(),) * 5,
+        out_specs=(pl.BlockSpec(),) + (VMEM,) * (ways - 1) + (pl.BlockSpec(),) * 6,
         scratch_shapes=[pltpu.VMEM((length, features), F32)],
         compiler_params=PARAMS,
         cost_estimate=cost(4),
         name="student_forward",
     )(valid_counts, places, events, student_qkv.T, student_out, projector)
     own_part, peer_parts = outs[0], outs[1:ways]
-    normed_rows, packed, mixed, weights, pick = outs[ways:]
+    normed_rows, packed, mixed, weights, pick, kept_out = outs[ways:]
 
     received = from_peers(lambda k: peer_parts[k - 1], "x")
     own_events = lax.dynamic_slice_in_dim(events, own_x * rows, rows, 0)
@@ -364,13 +377,16 @@
         lambda *refs: rows_kernel(ways, *refs),
         out_shape=(
             shape((rows, features), BF16), shape((ways - 1, features // 2, columns), BF16),
+            *in_place(received),
         ),
-        in_specs=[VMEM] * (ways + 1),
-        out_specs=(VMEM,) * 2,
+        in_specs=[ANY] * 2 + [HBM] * (ways - 1),
+        out_specs=(VMEM,) * 2 + (HBM,) * (ways - 1),
+        input_output_aliases={2 + k: 2 + k for k in range(ways - 1)},
+        scratch_shapes=buffers((own_events, own_part, *received)),
         compiler_params=PARAMS,
         cost_estimate=cost(1),
         name="student_rows",
-    )(own_events, own_part, *received)
+    )(own_events, own_part, *received)[:2]
     own_core, feat_rows, proj_halves = lax.optimization_barrier((own_core, feat_rows, proj_halves))
     other_core = lax.ppermute(own_core, "c", SWAP)
     proj_others = lax.ppermute(proj_halves, "c", SWAP)
@@ -386,8 +402,8 @@
 
     teacher_part = pl.pallas_call(
         teacher_kernel,
-        out_shape=shape((ways, rows, width + features), BF16),
-        in_specs=[SMEM] * 2 + [VMEM] * 4,
+        out_shape=shape((ways, rows, width), BF16),
+        in_specs=[SMEM] * 2 + [VMEM] * 3,
         out_specs=VMEM,
         scratch_shapes=[
             pltpu.VMEM((senders, 2, *shard.shape[1:]), BF16),
@@ -396,9 +412,11 @@
         compiler_params=PARAMS,
         cost_estimate=cost(5),
         name="teacher",
-    )(places, align, teacher_normed, own_core, other_core, feat_rows)
+    )(places, align, teacher_normed, own_core, other_core)
 
     teacher_parts = lax.all_to_all(teacher_part, "x", 0, 0)
+    after_teacher, _ = lax.optimization_barrier((feat_rows, teacher_part))
+    feats = [feat_rows] + from_peers(lambda k: after_teacher, "x")
     per_block = BLOCK // rows
     source = align[own_x // per_block] * BLOCK + own_x % per_block * rows
     own_tokens = lax.dynamic_slice_in_dim(clip, source, rows, 0)
@@ -412,43 +430,48 @@
         cost_estimate=cost(2),
         name="student_predict",
     )(sources, feat_rows, projector, proj_halves, proj_others, teacher_part)
-    message = pl.pallas_call(
+    pred, feats[1], feats[-1] = lax.optimization_barrier((pred, feats[1], feats[-1]))
+    message, _ = pl.pallas_call(
         lambda *refs: diff_kernel(shares, *refs),
-        out_shape=shape((ways, rows, features + columns + BLOCK), BF16),
+        out_shape=(
+            shape((ways, rows, features + columns + BLOCK), BF16), *in_place([whole_proj]),
+        ),
         in_specs=[SMEM] * 2 + [VMEM] * 3 + [HBM],
-        out_specs=VMEM,
-        scratch_shapes=[
-            pltpu.VMEM((ways, features, columns), BF16), pltpu.SemaphoreType.DMA,
-        ],
-        compiler_params=FETCHING,
+        out_specs=(VMEM, HBM),
+        scratch_shapes=buffers([whole_proj]),
+        input_output_aliases={5: 1},
+        compiler_params=PARAMS,
         cost_estimate=cost(2),
         name="difference",
-    )(valid_counts, places, teacher_parts, own_tokens, pred, whole_proj)
+    )(valid_counts, sources, teacher_parts, own_tokens, pred, whole_proj)
     feat_extra = pl.pallas_call(
-        lambda *refs: extra_kernel(shares, columns, *refs),
+        lambda *refs: extra_kernel(shares, columns, ways, *refs),
         out_shape=pltpu.HBM((2, features // columns, picked, length), BF16),
-        in_specs=[SMEM, VMEM, ANY],
+        in_specs=[SMEM] + [ANY] * (ways + 1),
         out_specs=pl.BlockSpec(),
+        scratch_shapes=buffers(feats)[:-1]
+        + [pltpu.VMEM((length, features), BF16), buffers(feats)[-1]],
         compiler_params=PARAMS,
         cost_estimate=cost(3),
         name="student_extra",
-    )(sources, teacher_parts, message)
+    )(sources, *feats, message)
     back = lax.all_to_all(message, "x", 0, 0).reshape(length, features + columns + BLOCK)
 
-    held = (student_out, packed, weights, mixed, pick, normed_rows, feat_extra)
+    held = (kept_out, packed, weights, mixed, normed_rows, pick, feat_extra)
     keep, send, loss = pl.pallas_call(
-        backward_kernel,
+        lambda *refs: backward_kernel(len(held), *refs),
         out_shape=(
             shape((picked, features), BF16), shape((picked, features), BF16), shape((1, 1), F32),
+            *in_place(held),
         ),
         in_specs=[VMEM] + [HBM] * len(held),
-        out_specs=(VMEM,) * 3,
-        scratch_shapes=[pltpu.VMEM(array.shape, array.dtype) for array in held]
-        + [pltpu.SemaphoreType.DMA((len(held),))],
-        compiler_params=FETCHING,
+        out_specs=(VMEM,) * 3 + (HBM,) * len(held),
+        scratch_shapes=buffers(held),
+        input_output_aliases={1 + i: 3 + i for i in range(len(held))},
+        compiler_params=PARAMS,
         cost_estimate=cost(4),
         name="student_backward",
-    )(back, *held)
+    )(back, *held)[:3]
 
     total = add(keep, lax.ppermute(send, "c", SWAP)).astype(BF16)
     chips = shares // 2

time: 140 us -> 140 us (level)
  starting transfers between devices: 39.4 us -> 51.8 us
  waiting for transfers between devices: 26.9 us -> 20.4 us
  local copies, waits for them, and re-layouts: 7.93 us -> 3.23 us
    ppermute x3 -> x6, starting transfers between devices: 11.4 us -> 23.8 us  [from_peers(): lax.ppermute(rows(k), axis, [(i, (i + k) % ways) for i in range(ways)])]
    ppermute x3 -> x6, waiting for transfers between devices: 7.45 us -> 18.2 us  [from_peers(): lax.ppermute(rows(k), axis, [(i, (i + k) % ways) for i in range(ways)])]
    all_to_all x1, waiting for transfers between devices: 10.7 us -> 0.01 us  [on_device(): teacher_parts = lax.all_to_all(teacher_part, 'x', 0, 0)]
    all_to_all x1, waiting for transfers between devices: 6.26 us -> 0.01 us  [on_device(): lax.all_to_all(message, 'x', 0, 0)]
    unnamed x40 -> x22, local copies, waits for them, and re-layouts: 7.74 us -> 1.92 us
    pallas_call x6 -> x5, Pallas kernels: 22 us -> 19.8 us  [the longest x1 4.45 us: on_device(): pl.pallas_call(lambda *refs: backward_kernel(len(held), *refs), out_shape...]
    pallas_call x1, Pallas kernels: 0.08 us -> 1.49 us  [on_device(): pl.pallas_call(lambda *refs: rows_kernel(ways, *refs), out_shape=(shape((...]
  transfers between devices with their start and end apart: 9 -> 12, of which waited for: 6 -> 7; matrix products, arithmetic and copies ran while one was open for 1% -> 1% of each run, Pallas kernels for 10% -> 11%
where the time goes in v6:
time: 140 us; the launch traced here: 139 us
  starting transfers between devices  51.8 us (37%)
  blocking collectives  35.5 us (25%)
  Pallas kernels  24.2 us (17%)
  waiting for transfers between devices  20.4 us (15%)
  local copies, waits for them, and re-layouts  3.23 us (2%)
  between operations  2.22 us (2%)
  other arithmetic  1.52 us (1%)
    all_to_all x1, blocking collectives, on_device(): lax.all_to_all(total.reshape(chips, total.shape[0] // chips, features), C...  35.5 us
    ppermute x6, starting transfers between devices, from_peers(): lax.ppermute(rows(k), axis, [(i, (i + k) % ways) for i in range(ways)])  23.8 us
    ppermute x6, waiting for transfers between devices, from_peers(): lax.ppermute(rows(k), axis, [(i, (i + k) % ways) for i in range(ways)])  18.2 us
    all_to_all x1, starting transfers between devices, on_device(): own_core = lax.all_to_all(shard, ('y', 'z'), 0, 0)  13.9 us
    pallas_call x1, Pallas kernels, on_device(): pl.pallas_call(lambda *refs: backward_kernel(len(held), *refs), out_shape...  4.45 us
    pallas_call x1, Pallas kernels, on_device(): pl.pallas_call(lambda *refs: student_kernel(shares, *refs), out_shape=(pl...  4.37 us
    all_to_all x1, starting transfers between devices, on_device(): teacher_parts = lax.all_to_all(teacher_part, 'x', 0, 0)  4.35 us
    pallas_call x1, Pallas kernels, on_device(): pl.pallas_call(lambda *refs: extra_kernel(shares, columns, ways, *refs),...  3.77 us
  transfers between devices with their start and end apart: 12, of which 7 were waited for; matrix products, arithmetic and copies ran while one was open for 1% of the time, Pallas kernels for 11%

profile of v6, /device:TPU:16, one launch (start us, length us, event | category | flops | bytes accessed | tf_op | source)
XLA Modules:
  0.0 138.9 jit_solution(7294049666253083732)
XLA Ops:
  0.6 0.8 pad_maximum_fusion
  1.4 1.1 broadcast_in_dim.2
  2.5 13.9 %all-to-all-start = ((bf16[32,16,1024]{2,1,0:T(8,128)(2,1)}), bf16[32,16,1024]{2,1,0:T(8,128)(2,1)S(1)}, u32[]{:S(2)}, u32[]{:S(2)}) async-start(bf16[32,16,1024]{2,1,0:T(8,128)(2,1)} %broadcast_in_dim.2), calls=%async_computation | async-start | bytes 2097152 | tf_op jit(solution)/shard_map/all_to_all | solution.py:346
  17.2 4.4 %student_forward.1 = (bf16[64,768]{1,0:T(8,128)(2,1)}, bf16[576,256]{1,0:T(8,128)(2,1)}, bf16[576,256]{1,0:T(8,128)(2,1)}, bf16[576,256]{1,0:T(8,128)(2,1)S(1)},...) custom-call(s32[1]{0:T(128)S(6)} %copy.36.refs_0_, ...), custom_call_target="tpu_custom_call" | custom-call | flops 4000000000 | bytes 1000000 | tf_op jit(solution)/shard_map/student_forward/pallas_call | solution.py:352
  21.5 3.4 %collective-permute-start = (bf16[576,256]{1,0:T(8,128)(2,1)}, bf16[576,256]{1,0:T(8,128)(2,1)S(1)}, u32[]{:S(2)}, u32[]{:S(2)}) collective-permute-start(bf16[576,256]{1,0:T(8,128)(2,1)} %get-tuple-element.33), channel_id=1, source_target_pairs={{0,1},{1,2},{2,3},{3,0},{4,5},{5,6},{6,7},{7,4},{8,9},{9,10},{10,1... | collective-permute-start | bytes 884744 | tf_op jit(solution)/shard_map/ppermute | solution.py:307
  24.9 4.6 %collective-permute-start.1 = (bf16[576,256]{1,0:T(8,128)(2,1)}, bf16[576,256]{1,0:T(8,128)(2,1)S(1)}, u32[]{:S(2)}, u32[]{:S(2)}) collective-permute-start(bf16[576,256]{1,0:T(8,128)(2,1)} %get-tuple-element.34), channel_id=1, source_target_pairs={{0,2},{1,3},{2,0},{3,1},{4,6},{5,7},{6,4},{7,5},{8,10},{9,11},{10,... | collective-permute-start | bytes 884744 | tf_op jit(solution)/shard_map/ppermute | solution.py:307
  29.6 3.3 %collective-permute-start.2 = (bf16[576,256]{1,0:T(8,128)(2,1)S(1)}, bf16[576,256]{1,0:T(8,128)(2,1)S(1)}, u32[]{:S(2)}, u32[]{:S(2)}) collective-permute-start(bf16[576,256]{1,0:T(8,128)(2,1)S(1)} %get-tuple-element.35), channel_id=1, source_target_pairs={{0,3},{1,0},{2,1},{3,2},{4,7},{5,4},{6,5},{7,6},{8,11},{9,8},{10,9... | collective-permute-start | bytes 884744 | tf_op jit(solution)/shard_map/ppermute | solution.py:307
  33.0 0.8 collective-permute-done.refs_2_
  33.8 6.5 %collective-permute-done.1.refs_3_ = bf16[576,256]{1,0:T(8,128)(2,1)S(1)} collective-permute-done((bf16[576,256]{1,0:T(8,128)(2,1)}, bf16[576,256]{1,0:T(8,128)(2,1)S(1)}, u32[]{:S(2)}, u32[]{:S(2)}) %collective-permute-start.1) | collective-permute-done | bytes 294944 | tf_op jit(solution)/shard_map/ppermute | solution.py:307
  40.3 1.5 %collective-permute-done.2.refs_4_ = bf16[576,256]{1,0:T(8,128)(2,1)S(1)} collective-permute-done((bf16[576,256]{1,0:T(8,128)(2,1)S(1)}, bf16[576,256]{1,0:T(8,128)(2,1)S(1)}, u32[]{:S(2)}, u32[]{:S(2)}) %collective-permute-start.2) | collective-permute-done | bytes 294944 | tf_op jit(solution)/shard_map/ppermute | solution.py:307
  41.9 0.7 copy-done.10
  42.6 0.9 copy-done.7
  43.5 1.5 %student_rows.1 = (bf16[64,768]{1,0:T(8,128)(2,1)S(1)}, bf16[3,384,256]{2,1,0:T(8,128)(2,1)S(1)}, bf16[576,256]{1,0:T(8,128)(2,1)}, bf16[576,256]{1,0:T(8,128)(2,1)}, bf16[576,256]{1,0:T(8,128)(2,1)}) custom-call(bf16[64,768]{1,0:T(8,128)(2,1)S(1)} %dynamic-slice_bitcast_fusion.1.refs_0_, ...), custom_call_target="tpu_custom_call", output_to_operand_aliasing={{2}: (2, {}), {3}: (3, {}), {4}: (4, {})} | custom-call | flops 1000000000 | bytes 1000000 | tf_op jit(solution)/shard_map/student_rows/pallas_call | solution.py:376
  45.0 1.9 %collective-permute-start.3 = (bf16[32,16,1024]{2,1,0:T(8,128)(2,1)S(1)}, bf16[32,16,1024]{2,1,0:T(8,128)(2,1)S(1)}, u32[]{:S(2)}, u32[]{:S(2)}) collective-permute-start(bf16[32,16,1024]{2,1,0:T(8,128)(2,1)S(1)} %all-to-all-done.own_ref), channel_id=1, source_target_pairs={{0,4},{4,0},{1,5},{5,1},{2,6},{6,2},{3,7},{7,3},{8,12},{12,8},{9,1... | collective-permute-start | bytes 3145736 | tf_op jit(solution)/shard_map/ppermute | solution.py:391
  46.9 2.4 %collective-permute-start.4 = (bf16[3,384,256]{2,1,0:T(8,128)(2,1)S(1)}, bf16[3,384,256]{2,1,0:T(8,128)(2,1)S(1)}, u32[]{:S(2)}, u32[]{:S(2)}) collective-permute-start(bf16[3,384,256]{2,1,0:T(8,128)(2,1)S(1)} %get-tuple-element.40.refs_3_), channel_id=1, source_target_pairs={{0,4},{4,0},{1,5},{5,1},{2,6},{6,2},{3,7},{7,3},{8,12},{12,8},{9,1... | collective-permute-start | bytes 1769480 | tf_op jit(solution)/shard_map/ppermute | solution.py:392
  50.0 3.7 %teacher.1.refs_5_ = bf16[4,64,1024]{2,1,0:T(8,128)(2,1)} custom-call(s32[5]{0:T(128)S(1)} %stack.35.refs_1_.place_ref, s32[2]{0:T(128)S(1)} %bitcast.26, bf16[256,1024]{1,0:T(8,128)(2,1)S(1)} %teacher_norm.1.normed_ref, bf16[32,16,1024]{2,1,0:T(8,128)(2,1)S(1)} %all-to-all-done.own_ref, bf16[32,16,1024]{2,1,0:T(8,128)(2,1)S(1)} %collective-permute-done.3.other_ref), custom_call_target="tpu_custom_call" | custom-call | flops 5000000000 | bytes 1000000 | tf_op jit(solution)/shard_map/teacher/pallas_call | solution.py:403
  53.7 4.3 %all-to-all-start.1 = ((bf16[4,64,1024]{2,1,0:T(8,128)(2,1)}), bf16[4,64,1024]{2,1,0:T(8,128)(2,1)S(1)}, u32[]{:S(2)}, u32[]{:S(2)}) async-start(bf16[4,64,1024]{2,1,0:T(8,128)(2,1)} %teacher.1.refs_5_), calls=%async_computation.1 | async-start | bytes 1048576 | tf_op jit(solution)/shard_map/all_to_all | solution.py:417
  58.1 0.6 fusion.1
  59.4 5.1 %collective-permute-start.6 = (bf16[64,768]{1,0:T(8,128)(2,1)S(1)}, bf16[64,768]{1,0:T(8,128)(2,1)S(1)}, u32[]{:S(2)}, u32[]{:S(2)}) collective-permute-start(bf16[64,768]{1,0:T(8,128)(2,1)S(1)} %get-tuple-element.42.after_ref.refs_1_), channel_id=1, source_target_pairs={{0,3},{1,0},{2,1},{3,2},{4,7},{5,4},{6,5},{7,6},{8,11},{9,8},{10,9... | collective-permute-start | bytes 294920 | tf_op jit(solution)/shard_map/ppermute | solution.py:307
  64.6 1.9 %collective-permute-start.5 = (bf16[64,768]{1,0:T(8,128)(2,1)S(1)}, bf16[64,768]{1,0:T(8,128)(2,1)S(1)}, u32[]{:S(2)}, u32[]{:S(2)}) collective-permute-start(bf16[64,768]{1,0:T(8,128)(2,1)S(1)} %get-tuple-element.42.after_ref.refs_1_), channel_id=1, source_target_pairs={{0,1},{1,2},{2,3},{3,0},{4,5},{5,6},{6,7},{7,4},{8,9},{9,10},{10,1... | collective-permute-start | bytes 294920 | tf_op jit(solution)/shard_map/ppermute | solution.py:307
  66.5 1.8 %student_predict.1 = (f32[64,1024]{1,0:T(8,128)S(1)}, bf16[4,768,256]{2,1,0:T(8,128)(2,1)}) custom-call(s32[5]{0:T(128)S(1)} %stack.33.refs_0_.refs_1_, bf16[64,768]{1,0:T(8,128)(2,1)S(1)} %get-tuple-element.42.after_ref.refs_1_, bf16[768,256]{1,0:T(8,128)(2,1)S(1)} %copy-done.3, bf16[3,384,256]{2,1,0:T(8,128)(2,1)S(1)} %get-tuple-element.40.refs_3_, ...), custom_call_target="tpu_custom_call" | custom-call | flops 2000000000 | bytes 1000000 | tf_op jit(solution)/shard_map/student_predict/pallas_call | solution.py:424
  68.4 3.9 %collective-permute-done.5.refs_2_ = bf16[64,768]{1,0:T(8,128)(2,1)S(1)} collective-permute-done((bf16[64,768]{1,0:T(8,128)(2,1)S(1)}, bf16[64,768]{1,0:T(8,128)(2,1)S(1)}, u32[]{:S(2)}, u32[]{:S(2)}) %collective-permute-start.5) | collective-permute-done | bytes 98336 | tf_op jit(solution)/shard_map/ppermute | solution.py:307
  72.3 3.5 %difference.1 = (bf16[4,64,1152]{2,1,0:T(8,128)(2,1)}, bf16[4,768,256]{2,1,0:T(8,128)(2,1)}) custom-call(s32[1]{0:T(128)S(6)} %copy.36.refs_0_, s32[5]{0:T(128)S(1)} %stack.33.refs_0_.refs_1_, bf16[4,64,1024]{2,1,0:T(8,128)(2,1)S(1)} %all-to-all-done.1.refs_2_, ...), custom_call_target="tpu_custom_call", output_to_operand_aliasing={{1}: (5, {})} | custom-call | flops 2000000000 | bytes 1000000 | tf_op jit(solution)/shard_map/difference/pallas_call | solution.py:434
  75.8 3.5 %all-to-all-start.2 = ((bf16[4,64,1152]{2,1,0:T(8,128)(2,1)}), bf16[4,64,1152]{2,1,0:T(8,128)(2,1)S(1)}, u32[]{:S(2)}, u32[]{:S(2)}) async-start(bf16[4,64,1152]{2,1,0:T(8,128)(2,1)} %get-tuple-element.45.refs_5_), calls=%async_computation.2 | async-start | bytes 1179648 | tf_op jit(solution)/shard_map/all_to_all | solution.py:458
  79.3 5.4 %collective-permute-start.7 = (bf16[64,768]{1,0:T(8,128)(2,1)S(1)}, bf16[64,768]{1,0:T(8,128)(2,1)S(1)}, u32[]{:S(2)}, u32[]{:S(2)}) collective-permute-start(bf16[64,768]{1,0:T(8,128)(2,1)S(1)} %get-tuple-element.42.after_ref.refs_1_), channel_id=1, source_target_pairs={{0,2},{1,3},{2,0},{3,1},{4,6},{5,7},{6,4},{7,5},{8,10},{9,11},{10,... | collective-permute-start | bytes 294920 | tf_op jit(solution)/shard_map/ppermute | solution.py:307
  84.7 5.3 %collective-permute-done.7.refs_3_ = bf16[64,768]{1,0:T(8,128)(2,1)S(1)} collective-permute-done((bf16[64,768]{1,0:T(8,128)(2,1)S(1)}, bf16[64,768]{1,0:T(8,128)(2,1)S(1)}, u32[]{:S(2)}, u32[]{:S(2)}) %collective-permute-start.7) | collective-permute-done | bytes 98336 | tf_op jit(solution)/shard_map/ppermute | solution.py:307
  90.0 3.8 %student_extra.1.refs_7_ = bf16[2,3,512,256]{3,2,1,0:T(8,128)(2,1)} custom-call(s32[5]{0:T(128)S(1)} %stack.33.refs_0_.refs_1_, bf16[64,768]{1,0:T(8,128)(2,1)S(1)} %get-tuple-element.42.after_ref.refs_1_, bf16[64,768]{1,0:T(8,128)(2,1)S(1)} %collective-permute-done.5.refs_2_, bf16[64,768]{1,0:T(8,128)(2,1)S(1)} %collective-permute-done.7.refs_3_, ...), custom_call_target="tpu_custom_call" | custom-call | flops 3000000000 | bytes 1000000 | tf_op jit(solution)/shard_map/student_extra/pallas_call | solution.py:447
  93.8 4.4 %student_backward.1 = (bf16[512,768]{1,0:T(8,128)(2,1)S(1)}, bf16[512,768]{1,0:T(8,128)(2,1)S(1)}, f32[1,1]{1,0:T(1,128)}, bf16[192,768]{1,0:T(8,128)(2,1)}, bf1...) custom-call(bf16[256,1152]{1,0:T(8,128)(2,1)S(1)} %bitcast.21, ...), custom_call_target="tpu_custom_call", output_to_operand_aliasing={{3}: (1, {}), {4}: (2, {}), {5}: (3, {}), {6}: (4, {}), {7}... | custom-call | flops 4000000000 | bytes 1000000 | tf_op jit(solution)/shard_map/student_backward/pallas_call | solution.py:461
  98.3 1.9 %collective-permute-start.8 = (bf16[512,768]{1,0:T(8,128)(2,1)S(1)}, bf16[512,768]{1,0:T(8,128)(2,1)S(1)}, u32[]{:S(2)}, u32[]{:S(2)}) collective-permute-start(bf16[512,768]{1,0:T(8,128)(2,1)S(1)} %get-tuple-element.56), channel_id=1, source_target_pairs={{0,4},{4,0},{1,5},{5,1},{2,6},{6,2},{3,7},{7,3},{8,12},{12,8},{9,1... | collective-permute-start | bytes 2359304 | tf_op jit(solution)/shard_map/ppermute | solution.py:476
  100.2 2.3 %collective-permute-done.8 = bf16[512,768]{1,0:T(8,128)(2,1)S(1)} collective-permute-done((bf16[512,768]{1,0:T(8,128)(2,1)S(1)}, bf16[512,768]{1,0:T(8,128)(2,1)S(1)}, u32[]{:S(2)}, u32[]{:S(2)}) %collective-permute-start.8) | collective-permute-done | bytes 786464 | tf_op jit(solution)/shard_map/ppermute | solution.py:476
  102.6 35.5 %all_to_all.20.parts_ref = bf16[64,8,768]{2,1,0:T(8,128)(2,1)S(1)} all-to-all(bf16[64,8,768]{2,1,0:T(8,128)(2,1)S(1)} %fusion), channel_id=1, replica_groups=mesh['g'=2,'y'=4,'z'=8,'c'=2,'x'=4] {'g','y','z'}, dimensions={0} | all-to-all | bytes 1572864 | tf_op jit(solution)/shard_map/all_to_all | solution.py:478
  138.1 0.8 gradient_rows.1
  (32 shorter events, 1.2 us)
Async XLA Ops:
  1.4 15.8 %copy-start.1 = (bf16[1,256,768]{2,1,0:T(8,128)(2,1)S(1)}, bf16[1,256,768]{2,1,0:T(8,128)(2,1)}, u32[]{:S(2)}) copy-start(bf16[1,256,768]{2,1,0:T(8,128)(2,1)} %param.14) | copy-start | bytes 1179652
  1.4 15.8 %copy-start.2 = (bf16[768,576]{0,1:T(8,128)(2,1)S(1)}, bf16[768,576]{0,1:T(8,128)(2,1)}, u32[]{:S(2)}) copy-start(bf16[768,576]{0,1:T(8,128)(2,1)} %param.17) | copy-start | bytes 2654212
  1.4 15.8 %copy-start.3 = (bf16[768,256]{1,0:T(8,128)(2,1)S(1)}, bf16[768,256]{1,0:T(8,128)(2,1)}, u32[]{:S(2)}) copy-start(bf16[768,256]{1,0:T(8,128)(2,1)} %refs_2_.1) | copy-start | bytes 1179652
  1.4 15.8 %copy-start.4 = (bf16[192,768]{1,0:T(8,128)(2,1)S(1)}, bf16[192,768]{1,0:T(8,128)(2,1)}, u32[]{:S(2)}) copy-start(bf16[192,768]{1,0:T(8,128)(2,1)} %refs_4_.1) | copy-start | bytes 884740
  2.5 42.5 %all-to-all-start = ((bf16[32,16,1024]{2,1,0:T(8,128)(2,1)}), bf16[32,16,1024]{2,1,0:T(8,128)(2,1)S(1)}, u32[]{:S(2)}, u32[]{:S(2)}) async-start(bf16[32,16,1024]{2,1,0:T(8,128)(2,1)} %broadcast_in_dim.2), calls=%async_computation | async-start | bytes 2097152 | tf_op jit(solution)/shard_map/all_to_all | solution.py:346
  21.5 12.3 %collective-permute-start = (bf16[576,256]{1,0:T(8,128)(2,1)}, bf16[576,256]{1,0:T(8,128)(2,1)S(1)}, u32[]{:S(2)}, u32[]{:S(2)}) collective-permute-start(bf16[576,256]{1,0:T(8,128)(2,1)} %get-tuple-element.33), channel_id=1, source_target_pairs={{0,1},{1,2},{2,3},{3,0},{4,5},{5,6},{6,7},{7,4},{8,9},{9,10},{10,1... | collective-permute-start | bytes 884744 | tf_op jit(solution)/shard_map/ppermute | solution.py:307
  24.9 15.4 %collective-permute-start.1 = (bf16[576,256]{1,0:T(8,128)(2,1)}, bf16[576,256]{1,0:T(8,128)(2,1)S(1)}, u32[]{:S(2)}, u32[]{:S(2)}) collective-permute-start(bf16[576,256]{1,0:T(8,128)(2,1)} %get-tuple-element.34), channel_id=1, source_target_pairs={{0,2},{1,3},{2,0},{3,1},{4,6},{5,7},{6,4},{7,5},{8,10},{9,11},{10,... | collective-permute-start | bytes 884744 | tf_op jit(solution)/shard_map/ppermute | solution.py:307
  29.6 12.3 %collective-permute-start.2 = (bf16[576,256]{1,0:T(8,128)(2,1)S(1)}, bf16[576,256]{1,0:T(8,128)(2,1)S(1)}, u32[]{:S(2)}, u32[]{:S(2)}) collective-permute-start(bf16[576,256]{1,0:T(8,128)(2,1)S(1)} %get-tuple-element.35), channel_id=1, source_target_pairs={{0,3},{1,0},{2,1},{3,2},{4,7},{5,4},{6,5},{7,6},{8,11},{9,8},{10,9... | collective-permute-start | bytes 884744 | tf_op jit(solution)/shard_map/ppermute | solution.py:307
  33.8 8.8 %copy-start.8 = (bf16[576,256]{1,0:T(8,128)(2,1)}, bf16[576,256]{1,0:T(8,128)(2,1)S(1)}, u32[]{:S(2)}) copy-start(bf16[576,256]{1,0:T(8,128)(2,1)S(1)} %collective-permute-done.refs_2_) | copy-start | bytes 884740
  40.3 1.5 %copy-start.9 = (bf16[576,256]{1,0:T(8,128)(2,1)}, bf16[576,256]{1,0:T(8,128)(2,1)S(1)}, u32[]{:S(2)}) copy-start(bf16[576,256]{1,0:T(8,128)(2,1)S(1)} %collective-permute-done.1.refs_3_) | copy-start | bytes 884740
  41.9 0.7 copy-start.10
  42.6 0.9 copy-start.7
  43.5 5.9 %copy-start = (bf16[1,256,1024]{2,1,0:T(8,128)(2,1)S(1)}, bf16[1,256,1024]{2,1,0:T(8,128)(2,1)}, u32[]{:S(2)}) copy-start(bf16[1,256,1024]{2,1,0:T(8,128)(2,1)} %param.10) | copy-start | bytes 1572868
  43.5 5.9 %copy-start.5 = (f32[1024]{0:T(1024)S(1)}, f32[1024]{0:T(1024)}, u32[]{:S(2)}) copy-start(f32[1024]{0:T(1024)} %param.11) | copy-start | bytes 12292
  45.0 4.7 %collective-permute-start.3 = (bf16[32,16,1024]{2,1,0:T(8,128)(2,1)S(1)}, bf16[32,16,1024]{2,1,0:T(8,128)(2,1)S(1)}, u32[]{:S(2)}, u32[]{:S(2)}) collective-permute-start(bf16[32,16,1024]{2,1,0:T(8,128)(2,1)S(1)} %all-to-all-done.own_ref), channel_id=1, source_target_pairs={{0,4},{4,0},{1,5},{5,1},{2,6},{6,2},{3,7},{7,3},{8,12},{12,8},{9,1... | collective-permute-start | bytes 3145736 | tf_op jit(solution)/shard_map/ppermute | solution.py:391
  46.9 19.6 %collective-permute-start.4 = (bf16[3,384,256]{2,1,0:T(8,128)(2,1)S(1)}, bf16[3,384,256]{2,1,0:T(8,128)(2,1)S(1)}, u32[]{:S(2)}, u32[]{:S(2)}) collective-permute-start(bf16[3,384,256]{2,1,0:T(8,128)(2,1)S(1)} %get-tuple-element.40.refs_3_), channel_id=1, source_target_pairs={{0,4},{4,0},{1,5},{5,1},{2,6},{6,2},{3,7},{7,3},{8,12},{12,8},{9,1... | collective-permute-start | bytes 1769480 | tf_op jit(solution)/shard_map/ppermute | solution.py:392
  49.3 0.7 copy-start.6
  53.7 18.6 %all-to-all-start.1 = ((bf16[4,64,1024]{2,1,0:T(8,128)(2,1)}), bf16[4,64,1024]{2,1,0:T(8,128)(2,1)S(1)}, u32[]{:S(2)}, u32[]{:S(2)}) async-start(bf16[4,64,1024]{2,1,0:T(8,128)(2,1)} %teacher.1.refs_5_), calls=%async_computation.1 | async-start | bytes 1048576 | tf_op jit(solution)/shard_map/all_to_all | solution.py:417
  59.4 9.0 %collective-permute-start.6 = (bf16[64,768]{1,0:T(8,128)(2,1)S(1)}, bf16[64,768]{1,0:T(8,128)(2,1)S(1)}, u32[]{:S(2)}, u32[]{:S(2)}) collective-permute-start(bf16[64,768]{1,0:T(8,128)(2,1)S(1)} %get-tuple-element.42.after_ref.refs_1_), channel_id=1, source_target_pairs={{0,3},{1,0},{2,1},{3,2},{4,7},{5,4},{6,5},{7,6},{8,11},{9,8},{10,9... | collective-permute-start | bytes 294920 | tf_op jit(solution)/shard_map/ppermute | solution.py:307
  64.6 7.7 %collective-permute-start.5 = (bf16[64,768]{1,0:T(8,128)(2,1)S(1)}, bf16[64,768]{1,0:T(8,128)(2,1)S(1)}, u32[]{:S(2)}, u32[]{:S(2)}) collective-permute-start(bf16[64,768]{1,0:T(8,128)(2,1)S(1)} %get-tuple-element.42.after_ref.refs_1_), channel_id=1, source_target_pairs={{0,1},{1,2},{2,3},{3,0},{4,5},{5,6},{6,7},{7,4},{8,9},{9,10},{10,1... | collective-permute-start | bytes 294920 | tf_op jit(solution)/shard_map/ppermute | solution.py:307
  75.8 18.0 %all-to-all-start.2 = ((bf16[4,64,1152]{2,1,0:T(8,128)(2,1)}), bf16[4,64,1152]{2,1,0:T(8,128)(2,1)S(1)}, u32[]{:S(2)}, u32[]{:S(2)}) async-start(bf16[4,64,1152]{2,1,0:T(8,128)(2,1)} %get-tuple-element.45.refs_5_), calls=%async_computation.2 | async-start | bytes 1179648 | tf_op jit(solution)/shard_map/all_to_all | solution.py:458
  79.3 10.7 %collective-permute-start.7 = (bf16[64,768]{1,0:T(8,128)(2,1)S(1)}, bf16[64,768]{1,0:T(8,128)(2,1)S(1)}, u32[]{:S(2)}, u32[]{:S(2)}) collective-permute-start(bf16[64,768]{1,0:T(8,128)(2,1)S(1)} %get-tuple-element.42.after_ref.refs_1_), channel_id=1, source_target_pairs={{0,2},{1,3},{2,0},{3,1},{4,6},{5,7},{6,4},{7,5},{8,10},{9,11},{10,... | collective-permute-start | bytes 294920 | tf_op jit(solution)/shard_map/ppermute | solution.py:307
  98.3 4.2 %collective-permute-start.8 = (bf16[512,768]{1,0:T(8,128)(2,1)S(1)}, bf16[512,768]{1,0:T(8,128)(2,1)S(1)}, u32[]{:S(2)}, u32[]{:S(2)}) collective-permute-start(bf16[512,768]{1,0:T(8,128)(2,1)S(1)} %get-tuple-element.56), channel_id=1, source_target_pairs={{0,4},{4,0},{1,5},{5,1},{2,6},{6,2},{3,7},{7,3},{8,12},{12,8},{9,1... | collective-permute-start | bytes 2359304 | tf_op jit(solution)/shard_map/ppermute | solution.py:476

commit v7 on v6

--- a/solution.py
+++ b/solution.py
@@ -75,35 +75,50 @@
     return weights / jnp.sum(weights, -1, keepdims=True)
 
 
-def pick_rows(rows, shares, columns, core, extra):
+def pick_matrix(wanted, width):
+    source = lax.broadcasted_iota(jnp.int32, (wanted.shape[0], width), 1)
+    return jnp.where(source == wanted, 1.0, 0.0).astype(BF16)
+
+
+def pick_rows(rows, shares, block, core):
     each = rows // shares
-    block = each + each * columns // rows
     place = lax.broadcasted_iota(jnp.int32, (shares // 2 * block, 1), 0)
     chip, row = place // block, place % block
-    base = (chip * 2 + core) * each
-    if extra:
-        wanted = jnp.where(row >= each, base + (row - each) * (rows // columns), -1)
-    else:
-        wanted = jnp.where(row < each, base + row, -1)
-    source = lax.broadcasted_iota(jnp.int32, (shares // 2 * block, rows), 1)
-    return jnp.where(source == wanted, 1.0, 0.0).astype(BF16)
-
-
-def student_kernel(
-    shares, count_ref, place_ref, events_ref, qkv_ref, out_ref, proj_ref, *refs
-):
-    ways = len(refs) - 7
-    own_ref, peer_refs = refs[0], refs[1:ways]
-    normed_ref, packed_ref, mixed_ref, weights_ref, pick_ref, kept_ref, part_ref = refs[ways:]
-    kept_ref[...] = out_ref[...]
-    columns = proj_ref.shape[1]
+    return pick_matrix(jnp.where(row < each, (chip * 2 + core) * each + row, -1), rows)
+
+
+def pick_extra(rows, shares, extra, core):
+    each = rows // shares
+    place = lax.broadcasted_iota(jnp.int32, (shares // 2 * extra, 1), 0)
+    chip, row = place // extra, place % extra
+    return pick_matrix((chip * 2 + core) * each + row * (each // extra), rows)
+
+
+def spread_extra(shares, block, extra):
+    place = lax.broadcasted_iota(jnp.int32, (shares // 2 * block, 1), 0)
+    chip, row = place // block, place % block
+    kept = block - extra
+    return pick_matrix(jnp.where(row >= kept, chip * extra + row - kept, -1), shares // 2 * extra)
+
+
+def picks_kernel(shares, place_ref, normed_ref, after_ref, rows_ref, pick_ref):
+    features = pick_ref.shape[2]
+    block = pick_ref.shape[1] // (shares // 2)
+    for half in range(2):
+        core = place_ref[0] if half == 0 else 1 - place_ref[0]
+        pick_ref[half] = pick_rows(features, shares, block, core)
+        rows_ref[half] = nt(pick_ref[half], normed_ref[...]).astype(BF16)
+
+
+def student_kernel(count_ref, place_ref, events_ref, qkv_ref, out_ref, *refs):
+    ways = len(refs) - 6
+    part_refs = refs[:ways]
+    normed_ref, packed_ref, mixed_ref, weights_ref, kept_ref, part_ref = refs[ways:]
     length, features = events_ref.shape
     heads = out_ref.shape[0] // HEAD
+    kept_ref[...] = out_ref[...]
     normed = norm_rows(events_ref[...]).astype(BF16)
-    for half in range(2):
-        core = place_ref[0] if half == 0 else 1 - place_ref[0]
-        pick_ref[half] = pick_rows(features, shares, columns, core, False)
-        normed_ref[half] = nt(pick_ref[half], normed).astype(BF16)
+    normed_ref[...] = normed
     packed = nt(normed, qkv_ref[...])
     packed_ref[...] = packed.astype(BF16)
     usable = lax.broadcasted_iota(jnp.int32, (length, length), 1) < count_ref[0]
@@ -111,42 +126,16 @@
     for head in range(heads):
         query, keys, values = split_head(packed, head)
         scores = jnp.where(usable, nt(query, keys) * HEAD ** (-0.5), -1e30)
-        weights = softmax(scores)
+        weights = softmax(scores).astype(BF16)
         weights_ref[head] = weights
-        mixed.append(nn(weights.astype(BF16), values))
+        mixed.append(nn(weights, values))
     mixed = jnp.concatenate(mixed, axis=1).astype(BF16)
     mixed_ref[...] = mixed
     part_ref[...] = nn(mixed, out_ref[...])
-    rows = own_ref.shape[0]
-    half = features // 2
-    blocks = features // columns
-    proj_half = proj_ref[pl.ds(pl.multiple_of(place_ref[0] * half, half), half), :]
+    rows = part_refs[0].shape[0]
     for k in range(ways):
         first = pl.multiple_of(place_ref[1 + k] * rows, rows)
-        chosen = part_ref[pl.ds(first, rows), :].astype(BF16)
-        if k == 0:
-            own_ref[...] = chosen
-            continue
-        for b in range(blocks):
-            peer_refs[k - 1][b * rows : (b + 1) * rows] = chosen[:, b * columns : (b + 1) * columns]
-        peer_refs[k - 1][blocks * rows :] = proj_half
-
-
-def rows_kernel(ways, *refs):
-    sources, (feat_ref, proj_ref), held = refs[: ways + 1], refs[ways + 1 : ways + 3], refs[-ways - 2 : -1]
-    for copy in fetch(sources, held, refs[-1]):
-        copy.wait()
-    events_ref, own_ref, *peer_refs = held
-    rows, features = own_ref.shape
-    columns = proj_ref.shape[2]
-    for b in range(features // columns):
-        block = slice(b * columns, (b + 1) * columns)
-        branch = own_ref[:, block].astype(F32)
-        for peer in peer_refs:
-            branch = branch + peer[b * rows : (b + 1) * rows].astype(F32)
-        feat_ref[:, block] = (events_ref[:, block].astype(F32) + branch).astype(BF16)
-    for k, peer in enumerate(peer_refs):
-        proj_ref[k] = peer[features // columns * rows :]
+        part_refs[k][...] = part_ref[pl.ds(first, rows), :].astype(BF16)
 
 
 def teacher_norm_kernel(clip_ref, gain_ref, after_ref, normed_ref):
@@ -180,22 +169,25 @@
 
 
 def predict_kernel(
-    ways, place_ref, feat_ref, own_ref, mine_ref, other_ref, after_ref, pred_ref, proj_ref
+    ways, place_ref, feat_ref, own_ref, near_ref, near_other_ref, far_ref, far_other_ref, after_ref,
+    pred_ref, proj_ref,
 ):
-    features, columns = own_ref.shape
-    half = features // 2
-    first = pl.multiple_of(place_ref[0] * half, half)
-    second = pl.multiple_of((1 - place_ref[0]) * half, half)
+    columns = own_ref.shape[1]
+    half = far_ref.shape[0]
+    core = place_ref[0]
+    first = pl.multiple_of(core * half, half)
+    second = pl.multiple_of((1 - core) * half, half)
     proj_ref[place_ref[1]] = own_ref[...]
-    for k in range(1, ways):
-        source = place_ref[1 + k]
-        proj_ref[source, pl.ds(first, half), :] = mine_ref[k - 1]
-        proj_ref[source, pl.ds(second, half), :] = other_ref[k - 1]
+    before, opposite, behind = place_ref[2], place_ref[3], place_ref[4]
+    proj_ref[jnp.where(core == 0, behind, before)] = near_ref[...]
+    proj_ref[jnp.where(core == 0, before, behind)] = near_other_ref[...]
+    proj_ref[opposite, pl.ds(first, half), :] = far_ref[...]
+    proj_ref[opposite, pl.ds(second, half), :] = far_other_ref[...]
     for k in range(ways):
         pred_ref[:, k * columns : (k + 1) * columns] = nn(feat_ref[...], proj_ref[k])
 
 
-def extra_kernel(shares, columns, ways, place_ref, *refs):
+def extra_kernel(shares, ways, place_ref, *refs):
     sources, (after_ref, extra_ref) = refs[:ways], refs[ways : ways + 2]
     pieces, feat_ref, sems = refs[ways + 2 : -2], refs[-2], refs[-1]
     copies = fetch(sources, pieces, sems)
@@ -205,21 +197,21 @@
         first = pl.multiple_of(place_ref[1 + k] * rows, rows)
         feat_ref[pl.ds(first, rows), :] = pieces[k][...]
     feat = feat_ref[...]
-    shifted = [feat]
-    for b in range(1, features // columns):
-        shifted.append(jnp.concatenate([feat[:, b:], feat[:, :b]], 1))
-    for half in range(2):
-        core = place_ref[0] if half == 0 else 1 - place_ref[0]
-        pick = pick_rows(features, shares, columns, core, True)
-        for b in range(features // columns):
-            extra_ref[half, b] = nt(pick, shifted[b]).astype(BF16)
+    blocks, runs = extra_ref.shape[1:3]
+    for b in range(blocks):
+        shifted = feat if b == 0 else jnp.concatenate([feat[:, b:], feat[:, :b]], 1)
+        for half in range(2):
+            core = place_ref[0] if half == 0 else 1 - place_ref[0]
+            pick = pick_extra(features, shares, 2 * runs // shares, core)
+            extra_ref[half, b] = nt(pick, shifted).astype(BF16)
 
 
 def diff_kernel(
     clips, count_ref, place_ref, parts_ref, tokens_ref, pred_ref, source_ref,
     out_ref, kept_ref, proj_ref, sems,
 ):
-    (copy,) = fetch([source_ref], [proj_ref], sems)
+    blocks = range(proj_ref.shape[0])
+    copies = fetch([source_ref.at[k] for k in blocks], [proj_ref.at[k] for k in blocks], sems)
     rows, width = tokens_ref.shape
     ways, features, columns = proj_ref.shape
     branch = parts_ref[0].astype(F32)
@@ -233,9 +225,9 @@
     diff = jnp.where(live, pred_ref[...] - target, 0.0)
     squares = jnp.sum(diff * diff, -1, keepdims=True) / scale
     dpred = (diff * factor).astype(BF16)
-    copy.wait()
     dfeat = jnp.zeros((rows, features), F32)
     for k in range(ways):
+        copies[k].wait()
         dfeat = dfeat + nt(dpred[:, k * columns : (k + 1) * columns], proj_ref[k])
     dfeat = dfeat.astype(BF16)
     high = squares.astype(BF16)
@@ -251,10 +243,10 @@
         out_ref[i, :, features + columns :] = tail
 
 
-def backward_kernel(held, back_ref, *refs):
+def backward_kernel(shares, held, back_ref, *refs):
     sources, (keep_ref, send_ref, loss_ref) = refs[:held], refs[held : held + 3]
     copies = fetch(sources, refs[2 * held + 3 : -1], refs[-1])
-    out_ref, packed_ref, weights_ref, mixed_ref, normed_ref, pick_ref, feat_ref = refs[2 * held + 3 : -1]
+    out_ref, packed_ref, weights_ref, pick_ref, mixed_ref, normed_ref, feat_ref = refs[2 * held + 3 : -1]
     copies[0].wait()
     features = out_ref.shape[1]
     heads = out_ref.shape[0] // HEAD
@@ -270,9 +262,10 @@
     pieces = []
     for head in range(heads):
         query, keys, values = split_head(packed, head)
-        weights = weights_ref[head]
+        rounded = weights_ref[head]
+        weights = rounded.astype(F32)
         cot = dmixed[:, head * HEAD : (head + 1) * HEAD].astype(BF16)
-        dvalues = tn(weights.astype(BF16), cot)
+        dvalues = tn(rounded, cot)
         dweights = nt(cot, values)
         inner = jnp.sum(dweights * weights, -1, keepdims=True)
         dscores = (weights * (dweights - inner) * HEAD ** (-0.5)).astype(BF16)
@@ -287,25 +280,28 @@
     mixed = jnp.concatenate(
         [jnp.zeros((length, used - tailed), F32), mixed_ref[...].astype(F32)], 1
     ).astype(BF16)
+    block, extra = pick_ref.shape[1] * 2 // shares, feat_ref.shape[2] * 2 // shares
+    placed = spread_extra(shares, block, extra)
     for half, into in enumerate((keep_ref, send_ref)):
         dfeat_rows = nt(pick_ref[half], dfeat).astype(BF16)
         normed_rows = normed_ref[half]
         for b in range(features // columns):
-            block = slice(b * columns, (b + 1) * columns)
-            total = nn(normed_rows, right[:, block]) + nn(feat_ref[half, b], dpred)
+            lanes = slice(b * columns, (b + 1) * columns)
+            runs = nn(feat_ref[half, b], dpred).astype(BF16)
+            total = nn(normed_rows, right[:, lanes]) + nn(placed, runs)
             if b == features // columns - 1:
                 total = total + nn(dfeat_rows, mixed)
-            into[:, block] = total.astype(BF16)
+            into[:, lanes] = total.astype(BF16)
 
 
 SWAP = [(0, 1), (1, 0)]
 
 
-def from_peers(rows, axis):
+def from_peers(rows, axis, places=None):
     ways = lax.axis_size(axis)
     return [
         lax.ppermute(rows(k), axis, [(i, (i + k) % ways) for i in range(ways)])
-        for k in range(1, ways)
+        for k in (range(1, ways) if places is None else places)
     ]
 
 
@@ -348,48 +344,56 @@
     each = features // shares
     picked = shares // 2 * (each + each * columns // features)
     places = jnp.stack([own_c] + [(own_x + k) % ways for k in range(ways)]).astype(jnp.int32)
-    message_rows = rows * features // columns + features // 2
     outs = pl.pallas_call(
-        lambda *refs: student_kernel(shares, *refs),
+        student_kernel,
         out_shape=(
             pltpu.HBM((rows, features), BF16),
-            *[shape((message_rows, columns), BF16)] * (ways - 1),
-            pltpu.HBM((2, picked, length), BF16),
+            *[shape((rows, features), BF16)] * (ways - 1),
+            shape((length, features), BF16),
             pltpu.HBM((length, 3 * HEAD * heads), BF16),
             pltpu.HBM((length, HEAD * heads), BF16),
-            pltpu.HBM((heads, length, length), F32),
-            pltpu.HBM((2, picked, features), BF16),
+            pltpu.HBM((heads, length, length), BF16),
             *in_place([student_out]),
         ),
-        in_specs=[SMEM] * 2 + [VMEM] * 4,
-        out_specs=(pl.BlockSpec(),) + (VMEM,) * (ways - 1) + (pl.BlockSpec(),) * 6,
+        in_specs=[SMEM] * 2 + [VMEM] * 3,
+        out_specs=(pl.BlockSpec(),) + (VMEM,) * ways + (pl.BlockSpec(),) * 4,
         scratch_shapes=[pltpu.VMEM((length, features), F32)],
         compiler_params=PARAMS,
         cost_estimate=cost(4),
         name="student_forward",
-    )(valid_counts, places, events, student_qkv.T, student_out, projector)
+    )(valid_counts, places, events, student_qkv.T, student_out)
     own_part, peer_parts = outs[0], outs[1:ways]
-    normed_rows, packed, mixed, weights, pick, kept_out = outs[ways:]
+    normed, packed, mixed, weights, kept_out = outs[ways:]
 
     received = from_peers(lambda k: peer_parts[k - 1], "x")
     own_events = lax.dynamic_slice_in_dim(events, own_x * rows, rows, 0)
-    feat_rows, proj_halves = pl.pallas_call(
-        lambda *refs: rows_kernel(ways, *refs),
+    feat_rows = own_events.astype(F32) + own_part.astype(F32)
+    for other in received:
+        feat_rows = feat_rows + other.astype(F32)
+    feat_rows = feat_rows.astype(BF16)
+    one_on = [
+        (c * ways + x, c * ways + (x + (1 if c else -1)) % ways) for x in range(ways) for c in range(2)
+    ]
+    near = lax.ppermute(projector, ("c", "x"), one_on)
+    picked_rows, pick = pl.pallas_call(
+        lambda *refs: picks_kernel(shares, *refs),
         out_shape=(
-            shape((rows, features), BF16), shape((ways - 1, features // 2, columns), BF16),
-            *in_place(received),
+            pltpu.HBM((2, picked, length), BF16), pltpu.HBM((2, picked, features), BF16),
         ),
-        in_specs=[ANY] * 2 + [HBM] * (ways - 1),
-        out_specs=(VMEM,) * 2 + (HBM,) * (ways - 1),
-        input_output_aliases={2 + k: 2 + k for k in range(ways - 1)},
-        scratch_shapes=buffers((own_events, own_part, *received)),
-        compiler_params=PARAMS,
-        cost_estimate=cost(1),
-        name="student_rows",
-    )(own_events, own_part, *received)[:2]
-    own_core, feat_rows, proj_halves = lax.optimization_barrier((own_core, feat_rows, proj_halves))
+        in_specs=[SMEM, VMEM, ANY],
+        out_specs=(pl.BlockSpec(),) * 2,
+        compiler_params=PARAMS,
+        cost_estimate=cost(2),
+        name="student_picks",
+    )(places, normed, near)
+    feats = [feat_rows] + from_peers(lambda k: feat_rows, "x", (1, ways - 1))
+    own_core, feat_rows, near, feats, picked_rows = lax.optimization_barrier(
+        (own_core, feat_rows, near, feats, picked_rows)
+    )
     other_core = lax.ppermute(own_core, "c", SWAP)
-    proj_others = lax.ppermute(proj_halves, "c", SWAP)
+    half = features // 2
+    far = lax.ppermute(lax.dynamic_slice_in_dim(near, own_c * half, half, 0), ("c", "x"), one_on)
+    near_other, far_other = (lax.ppermute(array, "c", SWAP) for array in (near, far))
     teacher_normed = pl.pallas_call(
         teacher_norm_kernel,
         out_shape=shape((length, width), BF16),
@@ -416,7 +420,7 @@
 
     teacher_parts = lax.all_to_all(teacher_part, "x", 0, 0)
     after_teacher, _ = lax.optimization_barrier((feat_rows, teacher_part))
-    feats = [feat_rows] + from_peers(lambda k: after_teacher, "x")
+    feats[2:-1] = from_peers(lambda k: after_teacher, "x", range(2, ways - 1))
     per_block = BLOCK // rows
     source = align[own_x // per_block] * BLOCK + own_x % per_block * rows
     own_tokens = lax.dynamic_slice_in_dim(clip, source, rows, 0)
@@ -424,13 +428,13 @@
     pred, whole_proj = pl.pallas_call(
         lambda *refs: predict_kernel(ways, *refs),
         out_shape=(shape((rows, width), F32), pltpu.HBM((ways, features, columns), BF16)),
-        in_specs=[SMEM] + [VMEM] * 4 + [ANY],
+        in_specs=[SMEM] + [VMEM] * 6 + [ANY],
         out_specs=(VMEM, pl.BlockSpec()),
         compiler_params=PARAMS,
         cost_estimate=cost(2),
         name="student_predict",
-    )(sources, feat_rows, projector, proj_halves, proj_others, teacher_part)
-    pred, feats[1], feats[-1] = lax.optimization_barrier((pred, feats[1], feats[-1]))
+    )(sources, feat_rows, projector, near, near_other, far, far_other, teacher_part)
+    pred, feats = lax.optimization_barrier((pred, feats))
     message, _ = pl.pallas_call(
         lambda *refs: diff_kernel(shares, *refs),
         out_shape=(
@@ -438,15 +442,17 @@
         ),
         in_specs=[SMEM] * 2 + [VMEM] * 3 + [HBM],
         out_specs=(VMEM, HBM),
-        scratch_shapes=buffers([whole_proj]),
+        scratch_shapes=[
+            pltpu.VMEM(whole_proj.shape, BF16), pltpu.SemaphoreType.DMA((ways,)),
+        ],
         input_output_aliases={5: 1},
         compiler_params=PARAMS,
         cost_estimate=cost(2),
         name="difference",
     )(valid_counts, sources, teacher_parts, own_tokens, pred, whole_proj)
     feat_extra = pl.pallas_call(
-        lambda *refs: extra_kernel(shares, columns, ways, *refs),
-        out_shape=pltpu.HBM((2, features // columns, picked, length), BF16),
+        lambda *refs: extra_kernel(shares, ways, *refs),
+        out_shape=pltpu.HBM((2, features // columns, picked - shares // 2 * each, length), BF16),
         in_specs=[SMEM] + [ANY] * (ways + 1),
         out_specs=pl.BlockSpec(),
         scratch_shapes=buffers(feats)[:-1]
@@ -457,9 +463,9 @@
     )(sources, *feats, message)
     back = lax.all_to_all(message, "x", 0, 0).reshape(length, features + columns + BLOCK)
 
-    held = (kept_out, packed, weights, mixed, normed_rows, pick, feat_extra)
+    held = (kept_out, packed, weights, pick, mixed, picked_rows, feat_extra)
     keep, send, loss = pl.pallas_call(
-        lambda *refs: backward_kernel(len(held), *refs),
+        lambda *refs: backward_kernel(shares, len(held), *refs),
         out_shape=(
             shape((picked, features), BF16), shape((picked, features), BF16), shape((1, 1), F32),
             *in_place(held),

time: 140 us -> 146 us (1.043)
  starting transfers between devices: 51.8 us -> 59.1 us
  waiting for transfers between devices: 20.4 us -> 15.7 us
  local copies, waits for them, and re-layouts: 3.23 us -> 6.26 us
    ppermute x6, waiting for transfers between devices: 18.2 us -> 6.19 us  [from_peers(): lax.ppermute(rows(k), axis, [(i, (i + k) % ways) for i in range(ways)])]
    ppermute x1 -> x4, starting transfers between devices: 2.41 us -> 12.5 us  [the longest x1 4.67 us: on_device(): near = lax.ppermute(projector, ('c', 'x'), one_on)]
    all_to_all x1, waiting for transfers between devices: 0.01 us -> 7.25 us  [on_device(): lax.all_to_all(message, 'x', 0, 0)]
    ppermute x6, starting transfers between devices: 23.8 us -> 20.9 us  [from_peers(): lax.ppermute(rows(k), axis, [(i, (i + k) % ways) for i in range(ways)])]
    unnamed x22 -> x26, local copies, waits for them, and re-layouts: 1.92 us -> 4.28 us
  transfers between devices with their start and end apart: 12 -> 15, of which waited for: 7 -> 6; matrix products, arithmetic and copies ran while one was open for 1% -> 2% of each run, Pallas kernels for 11% -> 10%
where the time goes in v7:
time: 146 us; the launch traced here: 145 us
  starting transfers between devices  59.1 us (40%)
  blocking collectives  35.5 us (24%)
  Pallas kernels  23.8 us (16%)
  waiting for transfers between devices  15.7 us (11%)
  local copies, waits for them, and re-layouts  6.26 us (4%)
  other arithmetic  2.49 us (2%)
  between operations  2.28 us (2%)
    all_to_all x1, blocking collectives, on_device(): lax.all_to_all(total.reshape(chips, total.shape[0] // chips, features), C...  35.5 us
    ppermute x6, starting transfers between devices, from_peers(): lax.ppermute(rows(k), axis, [(i, (i + k) % ways) for i in range(ways)])  20.9 us
    all_to_all x1, starting transfers between devices, on_device(): own_core = lax.all_to_all(shard, ('y', 'z'), 0, 0)  13.9 us
    all_to_all x1, waiting for transfers between devices, on_device(): lax.all_to_all(message, 'x', 0, 0)  7.25 us
    ppermute x6, waiting for transfers between devices, from_peers(): lax.ppermute(rows(k), axis, [(i, (i + k) % ways) for i in range(ways)])  6.19 us
    pallas_call x1, Pallas kernels, on_device(): pl.pallas_call(lambda *refs: backward_kernel(shares, len(held), *refs), o...  4.9 us
    ppermute x1, starting transfers between devices, on_device(): near = lax.ppermute(projector, ('c', 'x'), one_on)  4.67 us
    all_to_all x1, starting transfers between devices, on_device(): lax.all_to_all(message, 'x', 0, 0)  4.52 us
  transfers between devices with their start and end apart: 15, of which 6 were waited for; matrix products, arithmetic and copies ran while one was open for 2% of the time, Pallas kernels for 10%

profile of v7, /device:TPU:16, one launch (start us, length us, event | category | flops | bytes accessed | tf_op | source)
XLA Modules:
  0.0 145.1 jit_solution(1382254246484316834)
XLA Ops:
  1.4 1.1 broadcast_in_dim.2
  2.5 13.9 %all-to-all-start = ((bf16[32,16,1024]{2,1,0:T(8,128)(2,1)}), bf16[32,16,1024]{2,1,0:T(8,128)(2,1)S(1)}, u32[]{:S(2)}, u32[]{:S(2)}) async-start(bf16[32,16,1024]{2,1,0:T(8,128)(2,1)} %broadcast_in_dim.2), calls=%async_computation | async-start | bytes 2097152 | tf_op jit(solution)/shard_map/all_to_all | solution.py:342
  16.4 4.7 %collective-permute-start.3 = (bf16[768,256]{1,0:T(8,128)(2,1)S(1)}, bf16[768,256]{1,0:T(8,128)(2,1)S(1)}, u32[]{:S(2)}, u32[]{:S(2)}) collective-permute-start(bf16[768,256]{1,0:T(8,128)(2,1)S(1)} %copy-done.3), channel_id=1, source_target_pairs={{0,3},{4,5},{1,0},{5,6},{2,1},{6,7},{3,2},{7,4},{8,11},{12,13},{9,... | collective-permute-start | bytes 1179656 | tf_op jit(solution)/shard_map/ppermute | solution.py:377
  21.8 1.0 copy-done.4
  22.8 3.2 %student_forward.1 = (bf16[64,768]{1,0:T(8,128)(2,1)}, bf16[64,768]{1,0:T(8,128)(2,1)S(1)}, bf16[64,768]{1,0:T(8,128)(2,1)S(1)}, bf16[64,768]{1,0:T(8,128)(2,1)S...) custom-call(s32[1]{0:T(128)S(6)} %copy.30.count_ref.refs_0_, ...), custom_call_target="tpu_custom_call" | custom-call | flops 4000000000 | bytes 1000000 | tf_op jit(solution)/shard_map/student_forward/pallas_call | solution.py:347
  26.7 1.9 %collective-permute-start = (bf16[64,768]{1,0:T(8,128)(2,1)S(1)}, bf16[64,768]{1,0:T(8,128)(2,1)S(1)}, u32[]{:S(2)}, u32[]{:S(2)}) collective-permute-start(bf16[64,768]{1,0:T(8,128)(2,1)S(1)} %get-tuple-element.38), channel_id=1, source_target_pairs={{0,1},{1,2},{2,3},{3,0},{4,5},{5,6},{6,7},{7,4},{8,9},{9,10},{10,1... | collective-permute-start | bytes 294920 | tf_op jit(solution)/shard_map/ppermute | solution.py:303
  28.7 4.2 %collective-permute-start.1 = (bf16[64,768]{1,0:T(8,128)(2,1)S(1)}, bf16[64,768]{1,0:T(8,128)(2,1)S(1)}, u32[]{:S(2)}, u32[]{:S(2)}) collective-permute-start(bf16[64,768]{1,0:T(8,128)(2,1)S(1)} %get-tuple-element.39), channel_id=1, source_target_pairs={{0,2},{1,3},{2,0},{3,1},{4,6},{5,7},{6,4},{7,5},{8,10},{9,11},{10,... | collective-permute-start | bytes 294920 | tf_op jit(solution)/shard_map/ppermute | solution.py:303
  32.9 3.1 %collective-permute-start.2 = (bf16[64,768]{1,0:T(8,128)(2,1)S(1)}, bf16[64,768]{1,0:T(8,128)(2,1)S(1)}, u32[]{:S(2)}, u32[]{:S(2)}) collective-permute-start(bf16[64,768]{1,0:T(8,128)(2,1)S(1)} %get-tuple-element.40), channel_id=1, source_target_pairs={{0,3},{1,0},{2,1},{3,2},{4,7},{5,4},{6,5},{7,6},{8,11},{9,8},{10,9... | collective-permute-start | bytes 294920 | tf_op jit(solution)/shard_map/ppermute | solution.py:303
  36.7 2.7 %collective-permute-done.2 = bf16[64,768]{1,0:T(8,128)(2,1)S(1)} collective-permute-done((bf16[64,768]{1,0:T(8,128)(2,1)S(1)}, bf16[64,768]{1,0:T(8,128)(2,1)S(1)}, u32[]{:S(2)}, u32[]{:S(2)}) %collective-permute-start.2) | collective-permute-done | bytes 98336 | tf_op jit(solution)/shard_map/ppermute | solution.py:303
  39.4 1.0 fusion.4.after_ref.refs_1_
  40.3 4.5 %collective-permute-start.5 = (bf16[64,768]{1,0:T(8,128)(2,1)S(1)}, bf16[64,768]{1,0:T(8,128)(2,1)S(1)}, u32[]{:S(2)}, u32[]{:S(2)}) collective-permute-start(bf16[64,768]{1,0:T(8,128)(2,1)S(1)} %fusion.4.after_ref.refs_1_), channel_id=1, source_target_pairs={{0,3},{1,0},{2,1},{3,2},{4,7},{5,4},{6,5},{7,6},{8,11},{9,8},{10,9... | collective-permute-start | bytes 294920 | tf_op jit(solution)/shard_map/ppermute | solution.py:303
  44.8 1.9 %collective-permute-start.4 = (bf16[64,768]{1,0:T(8,128)(2,1)S(1)}, bf16[64,768]{1,0:T(8,128)(2,1)S(1)}, u32[]{:S(2)}, u32[]{:S(2)}) collective-permute-start(bf16[64,768]{1,0:T(8,128)(2,1)S(1)} %fusion.4.after_ref.refs_1_), channel_id=1, source_target_pairs={{0,1},{1,2},{2,3},{3,0},{4,5},{5,6},{6,7},{7,4},{8,9},{9,10},{10,1... | collective-permute-start | bytes 294920 | tf_op jit(solution)/shard_map/ppermute | solution.py:303
  46.8 1.0 copy-done.12
  47.8 2.5 %student_picks.1 = (bf16[2,512,256]{2,1,0:T(8,128)(2,1)}, bf16[2,512,768]{2,1,0:T(8,128)(2,1)}) custom-call(s32[5]{0:T(128)S(1)} %stack.35.place_ref.refs_0_, bf16[256,768]{1,0:T(8,128)(2,1)S(1)} %copy-done.12, bf16[768,256]{1,0:T(8,128)(2,1)S(1)} %collective-permute-done.3.refs_2_.refs_3_), custom_call_target="tpu_custom_call" | custom-call | flops 2000000000 | bytes 1000000 | tf_op jit(solution)/shard_map/student_picks/pallas_call | solution.py:378
  50.9 1.6 %collective-permute-done.4.refs_2_ = bf16[64,768]{1,0:T(8,128)(2,1)S(1)} collective-permute-done((bf16[64,768]{1,0:T(8,128)(2,1)S(1)}, bf16[64,768]{1,0:T(8,128)(2,1)S(1)}, u32[]{:S(2)}, u32[]{:S(2)}) %collective-permute-start.4) | collective-permute-done | bytes 98336 | tf_op jit(solution)/shard_map/ppermute | solution.py:303
  53.2 1.9 %collective-permute-start.6 = (bf16[32,16,1024]{2,1,0:T(8,128)(2,1)S(1)}, bf16[32,16,1024]{2,1,0:T(8,128)(2,1)S(1)}, u32[]{:S(2)}, u32[]{:S(2)}) collective-permute-start(bf16[32,16,1024]{2,1,0:T(8,128)(2,1)S(1)} %all-to-all-done.own_ref), channel_id=1, source_target_pairs={{0,4},{4,0},{1,5},{5,1},{2,6},{6,2},{3,7},{7,3},{8,12},{12,8},{9,1... | collective-permute-start | bytes 3145736 | tf_op jit(solution)/shard_map/ppermute | solution.py:393
  55.1 2.4 %collective-permute-start.7 = (bf16[768,256]{1,0:T(8,128)(2,1)S(1)}, bf16[768,256]{1,0:T(8,128)(2,1)}, u32[]{:S(2)}, u32[]{:S(2)}) collective-permute-start(bf16[768,256]{1,0:T(8,128)(2,1)S(1)} %collective-permute-done.3.refs_2_.refs_3_), channel_id=1, source_target_pairs={{0,4},{4,0},{1,5},{5,1},{2,6},{6,2},{3,7},{7,3},{8,12},{12,8},{9,1... | collective-permute-start | bytes 1179656 | tf_op jit(solution)/shard_map/ppermute | solution.py:396
  58.2 3.5 %collective-permute-start.8 = (bf16[384,256]{1,0:T(8,128)(2,1)}, bf16[384,256]{1,0:T(8,128)(2,1)}, u32[]{:S(2)}, u32[]{:S(2)}) collective-permute-start(bf16[384,256]{1,0:T(8,128)(2,1)} %constant_dynamic-slice_fusion), channel_id=1, source_target_pairs={{0,3},{4,5},{1,0},{5,6},{2,1},{6,7},{3,2},{7,4},{8,11},{12,13},{9,... | collective-permute-start | bytes 589832 | tf_op jit(solution)/shard_map/ppermute | solution.py:395
  62.4 3.7 %teacher.1.refs_7_ = bf16[4,64,1024]{2,1,0:T(8,128)(2,1)} custom-call(s32[5]{0:T(128)S(1)} %stack.35.place_ref.refs_0_, s32[2]{0:T(128)S(1)} %bitcast.27, bf16[256,1024]{1,0:T(8,128)(2,1)S(1)} %teacher_norm.1.normed_ref, bf16[32,16,1024]{2,1,0:T(8,128)(2,1)S(1)} %all-to-all-done.own_ref, bf16[32,16,1024]{2,1,0:T(8,128)(2,1)S(1)} %collective-permute-done.6.other_ref), custom_call_target="tpu_custom_call" | custom-call | flops 5000000000 | bytes 1000000 | tf_op jit(solution)/shard_map/teacher/pallas_call | solution.py:407
  66.1 3.5 %all-to-all-start.1 = ((bf16[4,64,1024]{2,1,0:T(8,128)(2,1)}), bf16[4,64,1024]{2,1,0:T(8,128)(2,1)S(1)}, u32[]{:S(2)}, u32[]{:S(2)}) async-start(bf16[4,64,1024]{2,1,0:T(8,128)(2,1)} %teacher.1.refs_7_), calls=%async_computation.1 | async-start | bytes 1048576 | tf_op jit(solution)/shard_map/all_to_all | solution.py:421
  69.6 1.9 %collective-permute-start.9 = (bf16[384,256]{1,0:T(8,128)(2,1)}, bf16[384,256]{1,0:T(8,128)(2,1)S(1)}, u32[]{:S(2)}, u32[]{:S(2)}) collective-permute-start(bf16[384,256]{1,0:T(8,128)(2,1)} %collective-permute-done.8.refs_5_), channel_id=1, source_target_pairs={{0,4},{4,0},{1,5},{5,1},{2,6},{6,2},{3,7},{7,3},{8,12},{12,8},{9,1... | collective-permute-start | bytes 589832 | tf_op jit(solution)/shard_map/ppermute | solution.py:396
  72.9 5.4 %collective-permute-start.10 = (bf16[64,768]{1,0:T(8,128)(2,1)S(1)}, bf16[64,768]{1,0:T(8,128)(2,1)S(1)}, u32[]{:S(2)}, u32[]{:S(2)}) collective-permute-start(bf16[64,768]{1,0:T(8,128)(2,1)S(1)} %fusion.4.after_ref.refs_1_), channel_id=1, source_target_pairs={{0,2},{1,3},{2,0},{3,1},{4,6},{5,7},{6,4},{7,5},{8,10},{9,11},{10,... | collective-permute-start | bytes 294920 | tf_op jit(solution)/shard_map/ppermute | solution.py:303
  78.3 2.3 %student_predict.1 = (f32[64,1024]{1,0:T(8,128)S(1)}, bf16[4,768,256]{2,1,0:T(8,128)(2,1)}) custom-call(s32[5]{0:T(128)S(1)} %stack.33.refs_0_.refs_1_, bf16[64,768]{1,0:T(8,128)(2,1)S(1)} %fusion.4.after_ref.refs_1_, bf16[768,256]{1,0:T(8,128)(2,1)S(1)} %copy-done.3, bf16[768,256]{1,0:T(8,128)(2,1)S(1)} %collective-permute-done.3.refs_2_.refs_3_, ...), custom_call_target="tpu_custom_call" | custom-call | flops 2000000000 | bytes 1000000 | tf_op jit(solution)/shard_map/student_predict/pallas_call | solution.py:428
  80.7 1.1 collective-permute-done.10.refs_3_
  81.8 3.3 %difference.1 = (bf16[4,64,1152]{2,1,0:T(8,128)(2,1)}, bf16[4,768,256]{2,1,0:T(8,128)(2,1)}) custom-call(s32[1]{0:T(128)S(6)} %copy.30.count_ref.refs_0_, s32[5]{0:T(128)S(1)} %stack.33.refs_0_.refs_1_, bf16[4,64,1024]{2,1,0:T(8,128)(2,1)S(1)} %all-to-all-done.1.refs_2_, ...), custom_call_target="tpu_custom_call", output_to_operand_aliasing={{1}: (5, {})} | custom-call | flops 2000000000 | bytes 1000000 | tf_op jit(solution)/shard_map/difference/pallas_call | solution.py:438
  85.1 4.5 %all-to-all-start.2 = ((bf16[4,64,1152]{2,1,0:T(8,128)(2,1)}), bf16[4,64,1152]{2,1,0:T(8,128)(2,1)S(1)}, u32[]{:S(2)}, u32[]{:S(2)}) async-start(bf16[4,64,1152]{2,1,0:T(8,128)(2,1)} %get-tuple-element.53.refs_5_), calls=%async_computation.2 | async-start | bytes 1179648 | tf_op jit(solution)/shard_map/all_to_all | solution.py:464
  89.6 2.8 %student_extra.1.refs_7_ = bf16[2,3,128,256]{3,2,1,0:T(8,128)(2,1)} custom-call(s32[5]{0:T(128)S(1)} %stack.33.refs_0_.refs_1_, bf16[64,768]{1,0:T(8,128)(2,1)S(1)} %fusion.4.after_ref.refs_1_, bf16[64,768]{1,0:T(8,128)(2,1)S(1)} %copy-done.8, bf16[64,768]{1,0:T(8,128)(2,1)S(1)} %collective-permute-done.10.refs_3_, bf16[64,768]{1,0:T(8,128)(2,1)S(1)} %copy-done.6, ...), custom_call_target="tpu_custom_call" | custom-call | flops 3000000000 | bytes 1000000 | tf_op jit(solution)/shard_map/student_extra/pallas_call | solution.py:453
  92.4 7.2 %all-to-all-done.2 = bf16[4,64,1152]{2,1,0:T(8,128)(2,1)S(1)} async-done(((bf16[4,64,1152]{2,1,0:T(8,128)(2,1)}), bf16[4,64,1152]{2,1,0:T(8,128)(2,1)S(1)}, u32[]{:S(2)}, u32[]{:S(2)}) %all-to-all-start.2) | async-done | bytes 589856 | tf_op jit(solution)/shard_map/all_to_all | solution.py:464
  99.6 4.9 %student_backward.1 = (bf16[512,768]{1,0:T(8,128)(2,1)S(1)}, bf16[512,768]{1,0:T(8,128)(2,1)S(1)}, f32[1,1]{1,0:T(1,128)}, bf16[192,768]{1,0:T(8,128)(2,1)}, bf1...) custom-call(bf16[256,1152]{1,0:T(8,128)(2,1)S(1)} %bitcast.22, ...), custom_call_target="tpu_custom_call", output_to_operand_aliasing={{3}: (1, {}), {4}: (2, {}), {5}: (3, {}), {6}: (4, {}), {7}... | custom-call | flops 4000000000 | bytes 1000000 | tf_op jit(solution)/shard_map/student_backward/pallas_call | solution.py:467
  104.5 1.9 %collective-permute-start.11 = (bf16[512,768]{1,0:T(8,128)(2,1)S(1)}, bf16[512,768]{1,0:T(8,128)(2,1)S(1)}, u32[]{:S(2)}, u32[]{:S(2)}) collective-permute-start(bf16[512,768]{1,0:T(8,128)(2,1)S(1)} %get-tuple-element.66), channel_id=1, source_target_pairs={{0,4},{4,0},{1,5},{5,1},{2,6},{6,2},{3,7},{7,3},{8,12},{12,8},{9,1... | collective-permute-start | bytes 2359304 | tf_op jit(solution)/shard_map/ppermute | solution.py:482
  106.5 2.3 %collective-permute-done.11 = bf16[512,768]{1,0:T(8,128)(2,1)S(1)} collective-permute-done((bf16[512,768]{1,0:T(8,128)(2,1)S(1)}, bf16[512,768]{1,0:T(8,128)(2,1)S(1)}, u32[]{:S(2)}, u32[]{:S(2)}) %collective-permute-start.11) | collective-permute-done | bytes 786464 | tf_op jit(solution)/shard_map/ppermute | solution.py:482
  108.9 35.5 %all_to_all.20.parts_ref = bf16[64,8,768]{2,1,0:T(8,128)(2,1)S(1)} all-to-all(bf16[64,8,768]{2,1,0:T(8,128)(2,1)S(1)} %fusion), channel_id=1, replica_groups=mesh['g'=2,'y'=4,'z'=8,'c'=2,'x'=4] {'g','y','z'}, dimensions={0} | all-to-all | bytes 1572864 | tf_op jit(solution)/shard_map/all_to_all | solution.py:484
  (43 shorter events, 6.6 us)
Async XLA Ops:
  1.4 15.0 %copy-start.3 = (bf16[768,256]{1,0:T(8,128)(2,1)S(1)}, bf16[768,256]{1,0:T(8,128)(2,1)}, u32[]{:S(2)}) copy-start(bf16[768,256]{1,0:T(8,128)(2,1)} %refs_2_.1) | copy-start | bytes 1179652
  1.4 20.4 %copy-start.1 = (bf16[1,256,768]{2,1,0:T(8,128)(2,1)S(1)}, bf16[1,256,768]{2,1,0:T(8,128)(2,1)}, u32[]{:S(2)}) copy-start(bf16[1,256,768]{2,1,0:T(8,128)(2,1)} %param.14) | copy-start | bytes 1179652
  1.4 20.4 %copy-start.2 = (bf16[768,576]{0,1:T(8,128)(2,1)S(1)}, bf16[768,576]{0,1:T(8,128)(2,1)}, u32[]{:S(2)}) copy-start(bf16[768,576]{0,1:T(8,128)(2,1)} %param.17) | copy-start | bytes 2654212
  2.5 50.7 %all-to-all-start = ((bf16[32,16,1024]{2,1,0:T(8,128)(2,1)}), bf16[32,16,1024]{2,1,0:T(8,128)(2,1)S(1)}, u32[]{:S(2)}, u32[]{:S(2)}) async-start(bf16[32,16,1024]{2,1,0:T(8,128)(2,1)} %broadcast_in_dim.2), calls=%async_computation | async-start | bytes 2097152 | tf_op jit(solution)/shard_map/all_to_all | solution.py:342
  16.4 30.4 %collective-permute-start.3 = (bf16[768,256]{1,0:T(8,128)(2,1)S(1)}, bf16[768,256]{1,0:T(8,128)(2,1)S(1)}, u32[]{:S(2)}, u32[]{:S(2)}) collective-permute-start(bf16[768,256]{1,0:T(8,128)(2,1)S(1)} %copy-done.3), channel_id=1, source_target_pairs={{0,3},{4,5},{1,0},{5,6},{2,1},{6,7},{3,2},{7,4},{8,11},{12,13},{9,... | collective-permute-start | bytes 1179656 | tf_op jit(solution)/shard_map/ppermute | solution.py:377
  21.8 1.0 copy-start.4
  26.0 0.8 copy-start.11
  26.7 9.2 %collective-permute-start = (bf16[64,768]{1,0:T(8,128)(2,1)S(1)}, bf16[64,768]{1,0:T(8,128)(2,1)S(1)}, u32[]{:S(2)}, u32[]{:S(2)}) collective-permute-start(bf16[64,768]{1,0:T(8,128)(2,1)S(1)} %get-tuple-element.38), channel_id=1, source_target_pairs={{0,1},{1,2},{2,3},{3,0},{4,5},{5,6},{6,7},{7,4},{8,9},{9,10},{10,1... | collective-permute-start | bytes 294920 | tf_op jit(solution)/shard_map/ppermute | solution.py:303
  28.7 8.0 %collective-permute-start.1 = (bf16[64,768]{1,0:T(8,128)(2,1)S(1)}, bf16[64,768]{1,0:T(8,128)(2,1)S(1)}, u32[]{:S(2)}, u32[]{:S(2)}) collective-permute-start(bf16[64,768]{1,0:T(8,128)(2,1)S(1)} %get-tuple-element.39), channel_id=1, source_target_pairs={{0,2},{1,3},{2,0},{3,1},{4,6},{5,7},{6,4},{7,5},{8,10},{9,11},{10,... | collective-permute-start | bytes 294920 | tf_op jit(solution)/shard_map/ppermute | solution.py:303
  32.9 6.5 %collective-permute-start.2 = (bf16[64,768]{1,0:T(8,128)(2,1)S(1)}, bf16[64,768]{1,0:T(8,128)(2,1)S(1)}, u32[]{:S(2)}, u32[]{:S(2)}) collective-permute-start(bf16[64,768]{1,0:T(8,128)(2,1)S(1)} %get-tuple-element.40), channel_id=1, source_target_pairs={{0,3},{1,0},{2,1},{3,2},{4,7},{5,4},{6,5},{7,6},{8,11},{9,8},{10,9... | collective-permute-start | bytes 294920 | tf_op jit(solution)/shard_map/ppermute | solution.py:303
  40.3 10.0 %collective-permute-start.5 = (bf16[64,768]{1,0:T(8,128)(2,1)S(1)}, bf16[64,768]{1,0:T(8,128)(2,1)S(1)}, u32[]{:S(2)}, u32[]{:S(2)}) collective-permute-start(bf16[64,768]{1,0:T(8,128)(2,1)S(1)} %fusion.4.after_ref.refs_1_), channel_id=1, source_target_pairs={{0,3},{1,0},{2,1},{3,2},{4,7},{5,4},{6,5},{7,6},{8,11},{9,8},{10,9... | collective-permute-start | bytes 294920 | tf_op jit(solution)/shard_map/ppermute | solution.py:303
  44.8 7.7 %collective-permute-start.4 = (bf16[64,768]{1,0:T(8,128)(2,1)S(1)}, bf16[64,768]{1,0:T(8,128)(2,1)S(1)}, u32[]{:S(2)}, u32[]{:S(2)}) collective-permute-start(bf16[64,768]{1,0:T(8,128)(2,1)S(1)} %fusion.4.after_ref.refs_1_), channel_id=1, source_target_pairs={{0,1},{1,2},{2,3},{3,0},{4,5},{5,6},{6,7},{7,4},{8,9},{9,10},{10,1... | collective-permute-start | bytes 294920 | tf_op jit(solution)/shard_map/ppermute | solution.py:303
  46.8 1.0 copy-start.12
  47.8 13.9 %copy-start = (bf16[1,256,1024]{2,1,0:T(8,128)(2,1)S(1)}, bf16[1,256,1024]{2,1,0:T(8,128)(2,1)}, u32[]{:S(2)}) copy-start(bf16[1,256,1024]{2,1,0:T(8,128)(2,1)} %param.10) | copy-start | bytes 1572868
  47.8 14.0 %copy-start.9 = (f32[1024]{0:T(1024)S(1)}, f32[1024]{0:T(1024)}, u32[]{:S(2)}) copy-start(f32[1024]{0:T(1024)} %param.11) | copy-start | bytes 12292
  50.3 0.6 copy-start.5
  52.5 0.6 copy-start.7
  53.2 8.9 %collective-permute-start.6 = (bf16[32,16,1024]{2,1,0:T(8,128)(2,1)S(1)}, bf16[32,16,1024]{2,1,0:T(8,128)(2,1)S(1)}, u32[]{:S(2)}, u32[]{:S(2)}) collective-permute-start(bf16[32,16,1024]{2,1,0:T(8,128)(2,1)S(1)} %all-to-all-done.own_ref), channel_id=1, source_target_pairs={{0,4},{4,0},{1,5},{5,1},{2,6},{6,2},{3,7},{7,3},{8,12},{12,8},{9,1... | collective-permute-start | bytes 3145736 | tf_op jit(solution)/shard_map/ppermute | solution.py:393
  55.1 23.2 %collective-permute-start.7 = (bf16[768,256]{1,0:T(8,128)(2,1)S(1)}, bf16[768,256]{1,0:T(8,128)(2,1)}, u32[]{:S(2)}, u32[]{:S(2)}) collective-permute-start(bf16[768,256]{1,0:T(8,128)(2,1)S(1)} %collective-permute-done.3.refs_2_.refs_3_), channel_id=1, source_target_pairs={{0,4},{4,0},{1,5},{5,1},{2,6},{6,2},{3,7},{7,3},{8,12},{12,8},{9,1... | collective-permute-start | bytes 1179656 | tf_op jit(solution)/shard_map/ppermute | solution.py:396
  58.2 11.4 %collective-permute-start.8 = (bf16[384,256]{1,0:T(8,128)(2,1)}, bf16[384,256]{1,0:T(8,128)(2,1)}, u32[]{:S(2)}, u32[]{:S(2)}) collective-permute-start(bf16[384,256]{1,0:T(8,128)(2,1)} %constant_dynamic-slice_fusion), channel_id=1, source_target_pairs={{0,3},{4,5},{1,0},{5,6},{2,1},{6,7},{3,2},{7,4},{8,11},{12,13},{9,... | collective-permute-start | bytes 589832 | tf_op jit(solution)/shard_map/ppermute | solution.py:395
  61.7 0.7 copy-start.10
  66.1 15.6 %all-to-all-start.1 = ((bf16[4,64,1024]{2,1,0:T(8,128)(2,1)}), bf16[4,64,1024]{2,1,0:T(8,128)(2,1)S(1)}, u32[]{:S(2)}, u32[]{:S(2)}) async-start(bf16[4,64,1024]{2,1,0:T(8,128)(2,1)} %teacher.1.refs_7_), calls=%async_computation.1 | async-start | bytes 1048576 | tf_op jit(solution)/shard_map/all_to_all | solution.py:421
  69.6 8.7 %collective-permute-start.9 = (bf16[384,256]{1,0:T(8,128)(2,1)}, bf16[384,256]{1,0:T(8,128)(2,1)S(1)}, u32[]{:S(2)}, u32[]{:S(2)}) collective-permute-start(bf16[384,256]{1,0:T(8,128)(2,1)} %collective-permute-done.8.refs_5_), channel_id=1, source_target_pairs={{0,4},{4,0},{1,5},{5,1},{2,6},{6,2},{3,7},{7,3},{8,12},{12,8},{9,1... | collective-permute-start | bytes 589832 | tf_op jit(solution)/shard_map/ppermute | solution.py:396
  72.9 8.8 %collective-permute-start.10 = (bf16[64,768]{1,0:T(8,128)(2,1)S(1)}, bf16[64,768]{1,0:T(8,128)(2,1)S(1)}, u32[]{:S(2)}, u32[]{:S(2)}) collective-permute-start(bf16[64,768]{1,0:T(8,128)(2,1)S(1)} %fusion.4.after_ref.refs_1_), channel_id=1, source_target_pairs={{0,2},{1,3},{2,0},{3,1},{4,6},{5,7},{6,4},{7,5},{8,10},{9,11},{10,... | collective-permute-start | bytes 294920 | tf_op jit(solution)/shard_map/ppermute | solution.py:303
  81.8 7.8 %copy-start.6 = (bf16[64,768]{1,0:T(8,128)(2,1)S(1)}, bf16[64,768]{1,0:T(8,128)(2,1)}, u32[]{:S(2)}) copy-start(bf16[64,768]{1,0:T(8,128)(2,1)} %copy-done.5) | copy-start | bytes 294916
  81.8 7.8 %copy-start.8 = (bf16[64,768]{1,0:T(8,128)(2,1)S(1)}, bf16[64,768]{1,0:T(8,128)(2,1)}, u32[]{:S(2)}) copy-start(bf16[64,768]{1,0:T(8,128)(2,1)} %copy-done.7) | copy-start | bytes 294916
  85.1 14.6 %all-to-all-start.2 = ((bf16[4,64,1152]{2,1,0:T(8,128)(2,1)}), bf16[4,64,1152]{2,1,0:T(8,128)(2,1)S(1)}, u32[]{:S(2)}, u32[]{:S(2)}) async-start(bf16[4,64,1152]{2,1,0:T(8,128)(2,1)} %get-tuple-element.53.refs_5_), calls=%async_computation.2 | async-start | bytes 1179648 | tf_op jit(solution)/shard_map/all_to_all | solution.py:464
  104.5 4.2 %collective-permute-start.11 = (bf16[512,768]{1,0:T(8,128)(2,1)S(1)}, bf16[512,768]{1,0:T(8,128)(2,1)S(1)}, u32[]{:S(2)}, u32[]{:S(2)}) collective-permute-start(bf16[512,768]{1,0:T(8,128)(2,1)S(1)} %get-tuple-element.66), channel_id=1, source_target_pairs={{0,4},{4,0},{1,5},{5,1},{2,6},{6,2},{3,7},{7,3},{8,12},{12,8},{9,1... | collective-permute-start | bytes 2359304 | tf_op jit(solution)/shard_map/ppermute | solution.py:482

commit v8 on v6

--- a/solution.py
+++ b/solution.py
@@ -154,7 +154,7 @@
 
 
 def teacher_kernel(
-    place_ref, align_ref, normed_ref, own_ref, other_ref, part_ref, parts_ref, mixed_ref
+    place_ref, align_ref, normed_ref, own_ref, other_ref, feat_ref, part_ref, parts_ref, mixed_ref
 ):
     blocks, cores, rows, width = parts_ref.shape
     for i, piece in enumerate((own_ref, other_ref)):
@@ -169,19 +169,20 @@
         weights = softmax(nt(query, keys) * HEAD ** (-0.5))
         mixed.append(nn(weights.astype(BF16), values))
     mixed_ref[...] = jnp.concatenate(mixed, axis=1)
-    shared = part_ref.shape[1]
+    ways, shared = part_ref.shape[:2]
+    outputs = blocks * cores * rows
     per_block = BLOCK // shared
     for i in range(align_ref.shape[0]):
         first = pl.multiple_of(align_ref[i] * BLOCK, BLOCK)
         chosen = mixed_ref[pl.ds(first, BLOCK), :].astype(BF16)
         part = nt(chosen, full_ref[:, heads * 3 * HEAD :]).astype(BF16)
         for k in range(per_block):
-            part_ref[i * per_block + k] = part[k * shared : (k + 1) * shared]
-
-
-def predict_kernel(
-    ways, place_ref, feat_ref, own_ref, mine_ref, other_ref, after_ref, pred_ref, proj_ref
-):
+            part_ref[i * per_block + k, :, :outputs] = part[k * shared : (k + 1) * shared]
+    for i in range(ways):
+        part_ref[i, :, outputs:] = feat_ref[...]
+
+
+def assemble_kernel(ways, place_ref, own_ref, mine_ref, other_ref, proj_ref):
     features, columns = own_ref.shape
     half = features // 2
     first = pl.multiple_of(place_ref[0] * half, half)
@@ -191,20 +192,18 @@
         source = place_ref[1 + k]
         proj_ref[source, pl.ds(first, half), :] = mine_ref[k - 1]
         proj_ref[source, pl.ds(second, half), :] = other_ref[k - 1]
+
+
+def predict_kernel(feat_ref, proj_ref, pred_ref):
+    ways, features, columns = proj_ref.shape
     for k in range(ways):
         pred_ref[:, k * columns : (k + 1) * columns] = nn(feat_ref[...], proj_ref[k])
 
 
-def extra_kernel(shares, columns, ways, place_ref, *refs):
-    sources, (after_ref, extra_ref) = refs[:ways], refs[ways : ways + 2]
-    pieces, feat_ref, sems = refs[ways + 2 : -2], refs[-2], refs[-1]
-    copies = fetch(sources, pieces, sems)
-    rows, features = pieces[0].shape
-    for k in range(ways):
-        copies[k].wait()
-        first = pl.multiple_of(place_ref[1 + k] * rows, rows)
-        feat_ref[pl.ds(first, rows), :] = pieces[k][...]
-    feat = feat_ref[...]
+def extra_kernel(shares, columns, place_ref, parts_ref, after_ref, extra_ref):
+    features = extra_ref.shape[1] * columns
+    rows = parts_ref.shape[0] * parts_ref.shape[1]
+    feat = parts_ref[...].reshape(rows, parts_ref.shape[2])[:, -features:]
     shifted = [feat]
     for b in range(1, features // columns):
         shifted.append(jnp.concatenate([feat[:, b:], feat[:, :b]], 1))
@@ -216,15 +215,13 @@
 
 
 def diff_kernel(
-    clips, count_ref, place_ref, parts_ref, tokens_ref, pred_ref, source_ref,
-    out_ref, kept_ref, proj_ref, sems,
+    clips, count_ref, place_ref, parts_ref, tokens_ref, pred_ref, proj_ref, out_ref
 ):
-    (copy,) = fetch([source_ref], [proj_ref], sems)
     rows, width = tokens_ref.shape
     ways, features, columns = proj_ref.shape
-    branch = parts_ref[0].astype(F32)
+    branch = parts_ref[0, :, :width].astype(F32)
     for i in range(1, ways):
-        branch = branch + parts_ref[i].astype(F32)
+        branch = branch + parts_ref[i, :, :width].astype(F32)
     target = (tokens_ref[...].astype(F32) + branch).astype(BF16).astype(F32)
     count = count_ref[0]
     live = lax.broadcasted_iota(jnp.int32, (rows, 1), 0) + place_ref[1] * rows < count
@@ -233,7 +230,6 @@
     diff = jnp.where(live, pred_ref[...] - target, 0.0)
     squares = jnp.sum(diff * diff, -1, keepdims=True) / scale
     dpred = (diff * factor).astype(BF16)
-    copy.wait()
     dfeat = jnp.zeros((rows, features), F32)
     for k in range(ways):
         dfeat = dfeat + nt(dpred[:, k * columns : (k + 1) * columns], proj_ref[k])
@@ -301,11 +297,11 @@
 SWAP = [(0, 1), (1, 0)]
 
 
-def from_peers(rows, axis):
+def from_peers(rows, axis, places=None):
     ways = lax.axis_size(axis)
     return [
         lax.ppermute(rows(k), axis, [(i, (i + k) % ways) for i in range(ways)])
-        for k in range(1, ways)
+        for k in (range(1, ways) if places is None else places)
     ]
 
 
@@ -402,8 +398,8 @@
 
     teacher_part = pl.pallas_call(
         teacher_kernel,
-        out_shape=shape((ways, rows, width), BF16),
-        in_specs=[SMEM] * 2 + [VMEM] * 3,
+        out_shape=shape((ways, rows, width + features), BF16),
+        in_specs=[SMEM] * 2 + [VMEM] * 4,
         out_specs=VMEM,
         scratch_shapes=[
             pltpu.VMEM((senders, 2, *shard.shape[1:]), BF16),
@@ -412,49 +408,49 @@
         compiler_params=PARAMS,
         cost_estimate=cost(5),
         name="teacher",
-    )(places, align, teacher_normed, own_core, other_core)
+    )(places, align, teacher_normed, own_core, other_core, feat_rows)
 
     teacher_parts = lax.all_to_all(teacher_part, "x", 0, 0)
-    after_teacher, _ = lax.optimization_barrier((feat_rows, teacher_part))
-    feats = [feat_rows] + from_peers(lambda k: after_teacher, "x")
     per_block = BLOCK // rows
     source = align[own_x // per_block] * BLOCK + own_x % per_block * rows
     own_tokens = lax.dynamic_slice_in_dim(clip, source, rows, 0)
     sources = jnp.stack([own_c] + [(own_x - k + ways) % ways for k in range(ways)]).astype(jnp.int32)
-    pred, whole_proj = pl.pallas_call(
-        lambda *refs: predict_kernel(ways, *refs),
-        out_shape=(shape((rows, width), F32), pltpu.HBM((ways, features, columns), BF16)),
-        in_specs=[SMEM] + [VMEM] * 4 + [ANY],
-        out_specs=(VMEM, pl.BlockSpec()),
+    whole_proj = pl.pallas_call(
+        lambda *refs: assemble_kernel(ways, *refs),
+        out_shape=pltpu.HBM((ways, features, columns), BF16),
+        in_specs=[SMEM] + [VMEM] * 3,
+        out_specs=pl.BlockSpec(),
+        compiler_params=PARAMS,
+        cost_estimate=cost(1),
+        name="projector",
+    )(sources, projector, proj_halves, proj_others)
+    pred = pl.pallas_call(
+        predict_kernel,
+        out_shape=shape((rows, width), F32),
+        in_specs=[VMEM] * 2,
+        out_specs=VMEM,
         compiler_params=PARAMS,
         cost_estimate=cost(2),
         name="student_predict",
-    )(sources, feat_rows, projector, proj_halves, proj_others, teacher_part)
-    pred, feats[1], feats[-1] = lax.optimization_barrier((pred, feats[1], feats[-1]))
-    message, _ = pl.pallas_call(
+    )(feat_rows, whole_proj)
+    message = pl.pallas_call(
         lambda *refs: diff_kernel(shares, *refs),
-        out_shape=(
-            shape((ways, rows, features + columns + BLOCK), BF16), *in_place([whole_proj]),
-        ),
-        in_specs=[SMEM] * 2 + [VMEM] * 3 + [HBM],
-        out_specs=(VMEM, HBM),
-        scratch_shapes=buffers([whole_proj]),
-        input_output_aliases={5: 1},
+        out_shape=shape((ways, rows, features + columns + BLOCK), BF16),
+        in_specs=[SMEM] * 2 + [VMEM] * 4,
+        out_specs=VMEM,
         compiler_params=PARAMS,
         cost_estimate=cost(2),
         name="difference",
     )(valid_counts, sources, teacher_parts, own_tokens, pred, whole_proj)
     feat_extra = pl.pallas_call(
-        lambda *refs: extra_kernel(shares, columns, ways, *refs),
+        lambda *refs: extra_kernel(shares, columns, *refs),
         out_shape=pltpu.HBM((2, features // columns, picked, length), BF16),
-        in_specs=[SMEM] + [ANY] * (ways + 1),
+        in_specs=[SMEM, VMEM, ANY],
         out_specs=pl.BlockSpec(),
-        scratch_shapes=buffers(feats)[:-1]
-        + [pltpu.VMEM((length, features), BF16), buffers(feats)[-1]],
         compiler_params=PARAMS,
         cost_estimate=cost(3),
         name="student_extra",
-    )(sources, *feats, message)
+    )(sources, teacher_parts, message)
     back = lax.all_to_all(message, "x", 0, 0).reshape(length, features + columns + BLOCK)
 
     held = (kept_out, packed, weights, mixed, normed_rows, pick, feat_extra)

time: 140 us -> 133 us (0.950)
  starting transfers between devices: 51.8 us -> 39.3 us
  waiting for transfers between devices: 20.4 us -> 26.3 us
  Pallas kernels: 24.2 us -> 22.7 us
    ppermute x6 -> x3, starting transfers between devices: 23.8 us -> 11.4 us  [from_peers(): lax.ppermute(rows(k), axis, [(i, (i + k) % ways) for i in range(ways)])]
    ppermute x6 -> x3, waiting for transfers between devices: 18.2 us -> 8.88 us  [from_peers(): lax.ppermute(rows(k), axis, [(i, (i + k) % ways) for i in range(ways)])]
    all_to_all x1, waiting for transfers between devices: 0.01 us -> 8.91 us  [on_device(): teacher_parts = lax.all_to_all(teacher_part, 'x', 0, 0)]
    all_to_all x1, waiting for transfers between devices: 0.01 us -> 6.25 us  [on_device(): lax.all_to_all(message, 'x', 0, 0)]
    pallas_call x4 -> x5, Pallas kernels: 12.8 us -> 11.2 us  [the longest x1 3.86 us: on_device(): pl.pallas_call(teacher_kernel, out_shape=shape((ways, rows, width + featu...]
    unnamed x22 -> x26, local copies, waits for them, and re-layouts: 1.92 us -> 3.32 us
  transfers between devices with their start and end apart: 12 -> 9, of which waited for: 7 -> 6; matrix products, arithmetic and copies ran while one was open for 1% -> 1% of each run, Pallas kernels for 11% -> 12%
where the time goes in v8:
time: 133 us; the launch traced here: 132 us
  starting transfers between devices  39.3 us (30%)
  blocking collectives  35.5 us (27%)
  waiting for transfers between devices  26.3 us (20%)
  Pallas kernels  22.7 us (17%)
  local copies, waits for them, and re-layouts  4.63 us (3%)
  between operations  2.18 us (2%)
  other arithmetic  1.52 us (1%)
    all_to_all x1, blocking collectives, on_device(): lax.all_to_all(total.reshape(chips, total.shape[0] // chips, features), C...  35.5 us
    all_to_all x1, starting transfers between devices, on_device(): own_core = lax.all_to_all(shard, ('y', 'z'), 0, 0)  13.9 us
    ppermute x3, starting transfers between devices, from_peers(): lax.ppermute(rows(k), axis, [(i, (i + k) % ways) for i in range(ways)])  11.4 us
    all_to_all x1, waiting for transfers between devices, on_device(): teacher_parts = lax.all_to_all(teacher_part, 'x', 0, 0)  8.91 us
    ppermute x3, waiting for transfers between devices, from_peers(): lax.ppermute(rows(k), axis, [(i, (i + k) % ways) for i in range(ways)])  8.88 us
    all_to_all x1, waiting for transfers between devices, on_device(): lax.all_to_all(message, 'x', 0, 0)  6.25 us
    pallas_call x1, Pallas kernels, on_device(): pl.pallas_call(lambda *refs: backward_kernel(len(held), *refs), out_shape...  4.44 us
    pallas_call x1, Pallas kernels, on_device(): pl.pallas_call(lambda *refs: student_kernel(shares, *refs), out_shape=(pl...  4.43 us
  transfers between devices with their start and end apart: 9, of which 6 were waited for; matrix products, arithmetic and copies ran while one was open for 1% of the time, Pallas kernels for 12%

profile of v8, /device:TPU:16, one launch (start us, length us, event | category | flops | bytes accessed | tf_op | source)
XLA Modules:
  0.0 132.1 jit_solution(9281192557667260529)
XLA Ops:
  0.6 0.8 pad_maximum_fusion
  1.4 1.1 broadcast_in_dim.2
  2.5 13.9 %all-to-all-start = ((bf16[32,16,1024]{2,1,0:T(8,128)(2,1)}), bf16[32,16,1024]{2,1,0:T(8,128)(2,1)S(1)}, u32[]{:S(2)}, u32[]{:S(2)}) async-start(bf16[32,16,1024]{2,1,0:T(8,128)(2,1)} %broadcast_in_dim.2), calls=%async_computation | async-start | bytes 2097152 | tf_op jit(solution)/shard_map/all_to_all | solution.py:342
  17.2 4.4 %student_forward.1 = (bf16[64,768]{1,0:T(8,128)(2,1)}, bf16[576,256]{1,0:T(8,128)(2,1)}, bf16[576,256]{1,0:T(8,128)(2,1)}, bf16[576,256]{1,0:T(8,128)(2,1)S(1)},...) custom-call(s32[1]{0:T(128)S(6)} %copy.34.refs_0_, ...), custom_call_target="tpu_custom_call" | custom-call | flops 4000000000 | bytes 1000000 | tf_op jit(solution)/shard_map/student_forward/pallas_call | solution.py:348
  21.6 3.4 %collective-permute-start = (bf16[576,256]{1,0:T(8,128)(2,1)}, bf16[576,256]{1,0:T(8,128)(2,1)S(1)}, u32[]{:S(2)}, u32[]{:S(2)}) collective-permute-start(bf16[576,256]{1,0:T(8,128)(2,1)} %get-tuple-element.26), channel_id=1, source_target_pairs={{0,1},{1,2},{2,3},{3,0},{4,5},{5,6},{6,7},{7,4},{8,9},{9,10},{10,1... | collective-permute-start | bytes 884744 | tf_op jit(solution)/shard_map/ppermute | solution.py:303
  25.0 4.6 %collective-permute-start.1 = (bf16[576,256]{1,0:T(8,128)(2,1)}, bf16[576,256]{1,0:T(8,128)(2,1)S(1)}, u32[]{:S(2)}, u32[]{:S(2)}) collective-permute-start(bf16[576,256]{1,0:T(8,128)(2,1)} %get-tuple-element.27), channel_id=1, source_target_pairs={{0,2},{1,3},{2,0},{3,1},{4,6},{5,7},{6,4},{7,5},{8,10},{9,11},{10,... | collective-permute-start | bytes 884744 | tf_op jit(solution)/shard_map/ppermute | solution.py:303
  29.6 3.3 %collective-permute-start.2 = (bf16[576,256]{1,0:T(8,128)(2,1)S(1)}, bf16[576,256]{1,0:T(8,128)(2,1)S(1)}, u32[]{:S(2)}, u32[]{:S(2)}) collective-permute-start(bf16[576,256]{1,0:T(8,128)(2,1)S(1)} %get-tuple-element.28), channel_id=1, source_target_pairs={{0,3},{1,0},{2,1},{3,2},{4,7},{5,4},{6,5},{7,6},{8,11},{9,8},{10,9... | collective-permute-start | bytes 884744 | tf_op jit(solution)/shard_map/ppermute | solution.py:303
  33.0 0.8 collective-permute-done.refs_2_
  33.9 6.5 %collective-permute-done.1.refs_3_ = bf16[576,256]{1,0:T(8,128)(2,1)S(1)} collective-permute-done((bf16[576,256]{1,0:T(8,128)(2,1)}, bf16[576,256]{1,0:T(8,128)(2,1)S(1)}, u32[]{:S(2)}, u32[]{:S(2)}) %collective-permute-start.1) | collective-permute-done | bytes 294944 | tf_op jit(solution)/shard_map/ppermute | solution.py:303
  40.4 1.5 %collective-permute-done.2.refs_4_ = bf16[576,256]{1,0:T(8,128)(2,1)S(1)} collective-permute-done((bf16[576,256]{1,0:T(8,128)(2,1)S(1)}, bf16[576,256]{1,0:T(8,128)(2,1)S(1)}, u32[]{:S(2)}, u32[]{:S(2)}) %collective-permute-start.2) | collective-permute-done | bytes 294944 | tf_op jit(solution)/shard_map/ppermute | solution.py:303
  41.9 0.7 copy-done.12
  42.6 0.9 copy-done.9
  43.5 1.5 %student_rows.1 = (bf16[64,768]{1,0:T(8,128)(2,1)S(1)}, bf16[3,384,256]{2,1,0:T(8,128)(2,1)S(1)}, bf16[576,256]{1,0:T(8,128)(2,1)}, bf16[576,256]{1,0:T(8,128)(2,1)}, bf16[576,256]{1,0:T(8,128)(2,1)}) custom-call(bf16[64,768]{1,0:T(8,128)(2,1)S(1)} %dynamic-slice_bitcast_fusion.1.refs_0_, ...), custom_call_target="tpu_custom_call", output_to_operand_aliasing={{2}: (2, {}), {3}: (3, {}), {4}: (4, {})} | custom-call | flops 1000000000 | bytes 1000000 | tf_op jit(solution)/shard_map/student_rows/pallas_call | solution.py:372
  45.0 1.9 %collective-permute-start.3 = (bf16[32,16,1024]{2,1,0:T(8,128)(2,1)S(1)}, bf16[32,16,1024]{2,1,0:T(8,128)(2,1)S(1)}, u32[]{:S(2)}, u32[]{:S(2)}) collective-permute-start(bf16[32,16,1024]{2,1,0:T(8,128)(2,1)S(1)} %all-to-all-done.own_ref), channel_id=1, source_target_pairs={{0,4},{4,0},{1,5},{5,1},{2,6},{6,2},{3,7},{7,3},{8,12},{12,8},{9,1... | collective-permute-start | bytes 3145736 | tf_op jit(solution)/shard_map/ppermute | solution.py:387
  47.0 2.4 %collective-permute-start.4 = (bf16[3,384,256]{2,1,0:T(8,128)(2,1)S(1)}, bf16[3,384,256]{2,1,0:T(8,128)(2,1)S(1)}, u32[]{:S(2)}, u32[]{:S(2)}) collective-permute-start(bf16[3,384,256]{2,1,0:T(8,128)(2,1)S(1)} %get-tuple-element.33.refs_2_), channel_id=1, source_target_pairs={{0,4},{4,0},{1,5},{5,1},{2,6},{6,2},{3,7},{7,3},{8,12},{12,8},{9,1... | collective-permute-start | bytes 1769480 | tf_op jit(solution)/shard_map/ppermute | solution.py:388
  49.4 0.4 teacher_norm.1.normed_ref
  50.1 3.9 %teacher.1 = bf16[4,64,1792]{2,1,0:T(8,128)(2,1)} custom-call(s32[5]{0:T(128)S(1)} %stack.35.refs_1_.place_ref, s32[2]{0:T(128)S(1)} %bitcast.26, bf16[256,1024]{1,0:T(8,128)(2,1)S(1)} %teacher_norm.1.normed_ref, bf16[32,16,1024]{2,1,0:T(8,128)(2,1)S(1)} %all-to-all-done.own_ref, bf16[32,16,1024]{2,1,0:T(8,128)(2,1)S(1)} %collective-permute-done.3.other_ref, ...), custom_call_target="tpu_custom_call" | custom-call | flops 5000000000 | bytes 1000000 | tf_op jit(solution)/shard_map/teacher/pallas_call | solution.py:399
  53.9 4.3 %all-to-all-start.1 = ((bf16[4,64,1792]{2,1,0:T(8,128)(2,1)}), bf16[4,64,1792]{2,1,0:T(8,128)(2,1)S(1)}, u32[]{:S(2)}, u32[]{:S(2)}) async-start(bf16[4,64,1792]{2,1,0:T(8,128)(2,1)} %teacher.1), calls=%async_computation.1 | async-start | bytes 1835008 | tf_op jit(solution)/shard_map/all_to_all | solution.py:413
  58.3 0.6 fusion.1
  59.6 1.8 %projector.1.proj_ref.refs_5_ = bf16[4,768,256]{2,1,0:T(8,128)(2,1)} custom-call(s32[5]{0:T(128)S(1)} %stack.33.refs_0_.refs_1_, bf16[768,256]{1,0:T(8,128)(2,1)S(1)} %copy-done.3, bf16[3,384,256]{2,1,0:T(8,128)(2,1)S(1)} %get-tuple-element.33.refs_2_, bf16[3,384,256]{2,1,0:T(8,128)(2,1)S(1)} %collective-permute-done.4.refs_3_), custom_call_target="tpu_custom_call" | custom-call | flops 1000000000 | bytes 1000000 | tf_op jit(solution)/shard_map/projector/pallas_call | solution.py:418
  61.4 1.4 %copy-done.7 = bf16[4,768,256]{2,1,0:T(8,128)(2,1)S(1)} copy-done((bf16[4,768,256]{2,1,0:T(8,128)(2,1)S(1)}, bf16[4,768,256]{2,1,0:T(8,128)(2,1)}, u32[]{:S(2)}) %copy-start.7) | copy-done | bytes 1572888
  62.8 0.4 student_predict.1.refs_4_
  63.2 8.9 %all-to-all-done.1.refs_2_.refs_1_ = bf16[4,64,1792]{2,1,0:T(8,128)(2,1)S(1)} async-done(((bf16[4,64,1792]{2,1,0:T(8,128)(2,1)}), bf16[4,64,1792]{2,1,0:T(8,128)(2,1)S(1)}, u32[]{:S(2)}, u32[]{:S(2)}) %all-to-all-start.1) | async-done | bytes 917536 | tf_op jit(solution)/shard_map/all_to_all | solution.py:413
  72.1 2.0 %difference.1.refs_2_ = bf16[4,64,1152]{2,1,0:T(8,128)(2,1)} custom-call(s32[1]{0:T(128)S(6)} %copy.34.refs_0_, s32[5]{0:T(128)S(1)} %stack.33.refs_0_.refs_1_, bf16[4,64,1792]{2,1,0:T(8,128)(2,1)S(1)} %all-to-all-done.1.refs_2_.refs_1_, bf16[64,1024]{1,0:T(8,128)(2,1)S(1)} %dynamic-slice_bitcast_fusion.refs_3_, f32[64,1024]{1,0:T(8,128)S(1)} %student_predict.1.refs_4_, ...), custom_call_target="tpu_custom_call" | custom-call | flops 2000000000 | bytes 1000000 | tf_op jit(solution)/shard_map/difference/pallas_call | solution.py:436
  74.1 3.5 %all-to-all-start.2 = ((bf16[4,64,1152]{2,1,0:T(8,128)(2,1)}), bf16[4,64,1152]{2,1,0:T(8,128)(2,1)S(1)}, u32[]{:S(2)}, u32[]{:S(2)}) async-start(bf16[4,64,1152]{2,1,0:T(8,128)(2,1)} %difference.1.refs_2_), calls=%async_computation.2 | async-start | bytes 1179648 | tf_op jit(solution)/shard_map/all_to_all | solution.py:454
  77.6 3.2 %student_extra.1.refs_7_ = bf16[2,3,512,256]{3,2,1,0:T(8,128)(2,1)} custom-call(s32[5]{0:T(128)S(1)} %stack.33.refs_0_.refs_1_, bf16[4,64,1792]{2,1,0:T(8,128)(2,1)S(1)} %all-to-all-done.1.refs_2_.refs_1_, bf16[4,64,1152]{2,1,0:T(8,128)(2,1)} %difference.1.refs_2_), custom_call_target="tpu_custom_call" | custom-call | flops 3000000000 | bytes 1000000 | tf_op jit(solution)/shard_map/student_extra/pallas_call | solution.py:445
  80.8 6.2 %all-to-all-done.2 = bf16[4,64,1152]{2,1,0:T(8,128)(2,1)S(1)} async-done(((bf16[4,64,1152]{2,1,0:T(8,128)(2,1)}), bf16[4,64,1152]{2,1,0:T(8,128)(2,1)S(1)}, u32[]{:S(2)}, u32[]{:S(2)}) %all-to-all-start.2) | async-done | bytes 589856 | tf_op jit(solution)/shard_map/all_to_all | solution.py:454
  87.0 4.4 %student_backward.1 = (bf16[512,768]{1,0:T(8,128)(2,1)S(1)}, bf16[512,768]{1,0:T(8,128)(2,1)S(1)}, f32[1,1]{1,0:T(1,128)}, bf16[192,768]{1,0:T(8,128)(2,1)}, bf1...) custom-call(bf16[256,1152]{1,0:T(8,128)(2,1)S(1)} %bitcast.21, ...), custom_call_target="tpu_custom_call", output_to_operand_aliasing={{3}: (1, {}), {4}: (2, {}), {5}: (3, {}), {6}: (4, {}), {7}... | custom-call | flops 4000000000 | bytes 1000000 | tf_op jit(solution)/shard_map/student_backward/pallas_call | solution.py:457
  91.5 1.9 %collective-permute-start.5 = (bf16[512,768]{1,0:T(8,128)(2,1)S(1)}, bf16[512,768]{1,0:T(8,128)(2,1)S(1)}, u32[]{:S(2)}, u32[]{:S(2)}) collective-permute-start(bf16[512,768]{1,0:T(8,128)(2,1)S(1)} %get-tuple-element.42), channel_id=1, source_target_pairs={{0,4},{4,0},{1,5},{5,1},{2,6},{6,2},{3,7},{7,3},{8,12},{12,8},{9,1... | collective-permute-start | bytes 2359304 | tf_op jit(solution)/shard_map/ppermute | solution.py:472
  93.4 2.3 %collective-permute-done.5 = bf16[512,768]{1,0:T(8,128)(2,1)S(1)} collective-permute-done((bf16[512,768]{1,0:T(8,128)(2,1)S(1)}, bf16[512,768]{1,0:T(8,128)(2,1)S(1)}, u32[]{:S(2)}, u32[]{:S(2)}) %collective-permute-start.5) | collective-permute-done | bytes 786464 | tf_op jit(solution)/shard_map/ppermute | solution.py:472
  95.8 35.5 %all_to_all.20.parts_ref = bf16[64,8,768]{2,1,0:T(8,128)(2,1)S(1)} all-to-all(bf16[64,8,768]{2,1,0:T(8,128)(2,1)S(1)} %fusion), channel_id=1, replica_groups=mesh['g'=2,'y'=4,'z'=8,'c'=2,'x'=4] {'g','y','z'}, dimensions={0} | all-to-all | bytes 1572864 | tf_op jit(solution)/shard_map/all_to_all | solution.py:474
  131.3 0.8 gradient_rows.1
  (31 shorter events, 0.7 us)
Async XLA Ops:
  1.4 15.8 %copy-start.1 = (bf16[1,256,768]{2,1,0:T(8,128)(2,1)S(1)}, bf16[1,256,768]{2,1,0:T(8,128)(2,1)}, u32[]{:S(2)}) copy-start(bf16[1,256,768]{2,1,0:T(8,128)(2,1)} %param.14) | copy-start | bytes 1179652
  1.4 15.8 %copy-start.2 = (bf16[768,576]{0,1:T(8,128)(2,1)S(1)}, bf16[768,576]{0,1:T(8,128)(2,1)}, u32[]{:S(2)}) copy-start(bf16[768,576]{0,1:T(8,128)(2,1)} %param.17) | copy-start | bytes 2654212
  1.4 15.8 %copy-start.3 = (bf16[768,256]{1,0:T(8,128)(2,1)S(1)}, bf16[768,256]{1,0:T(8,128)(2,1)}, u32[]{:S(2)}) copy-start(bf16[768,256]{1,0:T(8,128)(2,1)} %refs_1_.1) | copy-start | bytes 1179652
  1.4 15.8 %copy-start.4 = (bf16[192,768]{1,0:T(8,128)(2,1)S(1)}, bf16[192,768]{1,0:T(8,128)(2,1)}, u32[]{:S(2)}) copy-start(bf16[192,768]{1,0:T(8,128)(2,1)} %refs_4_.1) | copy-start | bytes 884740
  2.5 42.5 %all-to-all-start = ((bf16[32,16,1024]{2,1,0:T(8,128)(2,1)}), bf16[32,16,1024]{2,1,0:T(8,128)(2,1)S(1)}, u32[]{:S(2)}, u32[]{:S(2)}) async-start(bf16[32,16,1024]{2,1,0:T(8,128)(2,1)} %broadcast_in_dim.2), calls=%async_computation | async-start | bytes 2097152 | tf_op jit(solution)/shard_map/all_to_all | solution.py:342
  21.6 12.3 %collective-permute-start = (bf16[576,256]{1,0:T(8,128)(2,1)}, bf16[576,256]{1,0:T(8,128)(2,1)S(1)}, u32[]{:S(2)}, u32[]{:S(2)}) collective-permute-start(bf16[576,256]{1,0:T(8,128)(2,1)} %get-tuple-element.26), channel_id=1, source_target_pairs={{0,1},{1,2},{2,3},{3,0},{4,5},{5,6},{6,7},{7,4},{8,9},{9,10},{10,1... | collective-permute-start | bytes 884744 | tf_op jit(solution)/shard_map/ppermute | solution.py:303
  25.0 15.4 %collective-permute-start.1 = (bf16[576,256]{1,0:T(8,128)(2,1)}, bf16[576,256]{1,0:T(8,128)(2,1)S(1)}, u32[]{:S(2)}, u32[]{:S(2)}) collective-permute-start(bf16[576,256]{1,0:T(8,128)(2,1)} %get-tuple-element.27), channel_id=1, source_target_pairs={{0,2},{1,3},{2,0},{3,1},{4,6},{5,7},{6,4},{7,5},{8,10},{9,11},{10,... | collective-permute-start | bytes 884744 | tf_op jit(solution)/shard_map/ppermute | solution.py:303
  29.6 12.3 %collective-permute-start.2 = (bf16[576,256]{1,0:T(8,128)(2,1)S(1)}, bf16[576,256]{1,0:T(8,128)(2,1)S(1)}, u32[]{:S(2)}, u32[]{:S(2)}) collective-permute-start(bf16[576,256]{1,0:T(8,128)(2,1)S(1)} %get-tuple-element.28), channel_id=1, source_target_pairs={{0,3},{1,0},{2,1},{3,2},{4,7},{5,4},{6,5},{7,6},{8,11},{9,8},{10,9... | collective-permute-start | bytes 884744 | tf_op jit(solution)/shard_map/ppermute | solution.py:303
  33.9 8.8 %copy-start.10 = (bf16[576,256]{1,0:T(8,128)(2,1)}, bf16[576,256]{1,0:T(8,128)(2,1)S(1)}, u32[]{:S(2)}) copy-start(bf16[576,256]{1,0:T(8,128)(2,1)S(1)} %collective-permute-done.refs_2_) | copy-start | bytes 884740
  40.4 1.5 %copy-start.11 = (bf16[576,256]{1,0:T(8,128)(2,1)}, bf16[576,256]{1,0:T(8,128)(2,1)S(1)}, u32[]{:S(2)}) copy-start(bf16[576,256]{1,0:T(8,128)(2,1)S(1)} %collective-permute-done.1.refs_3_) | copy-start | bytes 884740
  41.9 0.7 copy-start.12
  42.6 0.9 copy-start.9
  43.5 5.9 %copy-start = (bf16[1,256,1024]{2,1,0:T(8,128)(2,1)S(1)}, bf16[1,256,1024]{2,1,0:T(8,128)(2,1)}, u32[]{:S(2)}) copy-start(bf16[1,256,1024]{2,1,0:T(8,128)(2,1)} %param.10) | copy-start | bytes 1572868
  43.5 5.9 %copy-start.5 = (f32[1024]{0:T(1024)S(1)}, f32[1024]{0:T(1024)}, u32[]{:S(2)}) copy-start(f32[1024]{0:T(1024)} %param.11) | copy-start | bytes 12292
  45.0 4.7 %collective-permute-start.3 = (bf16[32,16,1024]{2,1,0:T(8,128)(2,1)S(1)}, bf16[32,16,1024]{2,1,0:T(8,128)(2,1)S(1)}, u32[]{:S(2)}, u32[]{:S(2)}) collective-permute-start(bf16[32,16,1024]{2,1,0:T(8,128)(2,1)S(1)} %all-to-all-done.own_ref), channel_id=1, source_target_pairs={{0,4},{4,0},{1,5},{5,1},{2,6},{6,2},{3,7},{7,3},{8,12},{12,8},{9,1... | collective-permute-start | bytes 3145736 | tf_op jit(solution)/shard_map/ppermute | solution.py:387
  47.0 12.6 %collective-permute-start.4 = (bf16[3,384,256]{2,1,0:T(8,128)(2,1)S(1)}, bf16[3,384,256]{2,1,0:T(8,128)(2,1)S(1)}, u32[]{:S(2)}, u32[]{:S(2)}) collective-permute-start(bf16[3,384,256]{2,1,0:T(8,128)(2,1)S(1)} %get-tuple-element.33.refs_2_), channel_id=1, source_target_pairs={{0,4},{4,0},{1,5},{5,1},{2,6},{6,2},{3,7},{7,3},{8,12},{12,8},{9,1... | collective-permute-start | bytes 1769480 | tf_op jit(solution)/shard_map/ppermute | solution.py:388
  49.4 0.7 copy-start.6
  53.9 18.2 %all-to-all-start.1 = ((bf16[4,64,1792]{2,1,0:T(8,128)(2,1)}), bf16[4,64,1792]{2,1,0:T(8,128)(2,1)S(1)}, u32[]{:S(2)}, u32[]{:S(2)}) async-start(bf16[4,64,1792]{2,1,0:T(8,128)(2,1)} %teacher.1), calls=%async_computation.1 | async-start | bytes 1835008 | tf_op jit(solution)/shard_map/all_to_all | solution.py:413
  61.4 1.4 %copy-start.7 = (bf16[4,768,256]{2,1,0:T(8,128)(2,1)S(1)}, bf16[4,768,256]{2,1,0:T(8,128)(2,1)}, u32[]{:S(2)}) copy-start(bf16[4,768,256]{2,1,0:T(8,128)(2,1)} %projector.1.proj_ref.refs_5_) | copy-start | bytes 4718596
  62.8 9.3 %copy-start.8 = (bf16[4,768,256]{2,1,0:T(8,128)(2,1)S(1)}, bf16[4,768,256]{2,1,0:T(8,128)(2,1)}, u32[]{:S(2)}) copy-start(bf16[4,768,256]{2,1,0:T(8,128)(2,1)} %projector.1.proj_ref.refs_5_) | copy-start | bytes 4718596
  74.1 12.9 %all-to-all-start.2 = ((bf16[4,64,1152]{2,1,0:T(8,128)(2,1)}), bf16[4,64,1152]{2,1,0:T(8,128)(2,1)S(1)}, u32[]{:S(2)}, u32[]{:S(2)}) async-start(bf16[4,64,1152]{2,1,0:T(8,128)(2,1)} %difference.1.refs_2_), calls=%async_computation.2 | async-start | bytes 1179648 | tf_op jit(solution)/shard_map/all_to_all | solution.py:454
  91.5 4.2 %collective-permute-start.5 = (bf16[512,768]{1,0:T(8,128)(2,1)S(1)}, bf16[512,768]{1,0:T(8,128)(2,1)S(1)}, u32[]{:S(2)}, u32[]{:S(2)}) collective-permute-start(bf16[512,768]{1,0:T(8,128)(2,1)S(1)} %get-tuple-element.42), channel_id=1, source_target_pairs={{0,4},{4,0},{1,5},{5,1},{2,6},{6,2},{3,7},{7,3},{8,12},{12,8},{9,1... | collective-permute-start | bytes 2359304 | tf_op jit(solution)/shard_map/ppermute | solution.py:472

commit v9 on v8

--- a/solution.py
+++ b/solution.py
@@ -89,21 +89,24 @@
     return jnp.where(source == wanted, 1.0, 0.0).astype(BF16)
 
 
-def student_kernel(
-    shares, count_ref, place_ref, events_ref, qkv_ref, out_ref, proj_ref, *refs
-):
-    ways = len(refs) - 7
+def picks_kernel(shares, columns, place_ref, normed_ref, after_ref, rows_ref, pick_ref):
+    features = pick_ref.shape[2]
+    for half in range(2):
+        core = place_ref[0] if half == 0 else 1 - place_ref[0]
+        pick_ref[half] = pick_rows(features, shares, columns, core, False)
+        rows_ref[half] = nt(pick_ref[half], normed_ref[...]).astype(BF16)
+
+
+def student_kernel(count_ref, place_ref, events_ref, qkv_ref, out_ref, proj_ref, *refs):
+    ways = len(refs) - 6
     own_ref, peer_refs = refs[0], refs[1:ways]
-    normed_ref, packed_ref, mixed_ref, weights_ref, pick_ref, kept_ref, part_ref = refs[ways:]
+    normed_ref, packed_ref, mixed_ref, weights_ref, kept_ref, part_ref = refs[ways:]
     kept_ref[...] = out_ref[...]
     columns = proj_ref.shape[1]
     length, features = events_ref.shape
     heads = out_ref.shape[0] // HEAD
     normed = norm_rows(events_ref[...]).astype(BF16)
-    for half in range(2):
-        core = place_ref[0] if half == 0 else 1 - place_ref[0]
-        pick_ref[half] = pick_rows(features, shares, columns, core, False)
-        normed_ref[half] = nt(pick_ref[half], normed).astype(BF16)
+    normed_ref[...] = normed
     packed = nt(normed, qkv_ref[...])
     packed_ref[...] = packed.astype(BF16)
     usable = lax.broadcasted_iota(jnp.int32, (length, length), 1) < count_ref[0]
@@ -111,9 +114,9 @@
     for head in range(heads):
         query, keys, values = split_head(packed, head)
         scores = jnp.where(usable, nt(query, keys) * HEAD ** (-0.5), -1e30)
-        weights = softmax(scores)
+        weights = softmax(scores).astype(BF16)
         weights_ref[head] = weights
-        mixed.append(nn(weights.astype(BF16), values))
+        mixed.append(nn(weights, values))
     mixed = jnp.concatenate(mixed, axis=1).astype(BF16)
     mixed_ref[...] = mixed
     part_ref[...] = nn(mixed, out_ref[...])
@@ -124,8 +127,8 @@
     for k in range(ways):
         first = pl.multiple_of(place_ref[1 + k] * rows, rows)
         chosen = part_ref[pl.ds(first, rows), :].astype(BF16)
-        if k == 0:
-            own_ref[...] = chosen
+        if k not in (1, ways - 1):
+            (own_ref if k == 0 else peer_refs[k - 1])[...] = chosen
             continue
         for b in range(blocks):
             peer_refs[k - 1][b * rows : (b + 1) * rows] = chosen[:, b * columns : (b + 1) * columns]
@@ -133,20 +136,22 @@
 
 
 def rows_kernel(ways, *refs):
-    sources, (feat_ref, proj_ref), held = refs[: ways + 1], refs[ways + 1 : ways + 3], refs[-ways - 2 : -1]
+    sources, (feat_ref, proj_ref), held = refs[: ways + 2], refs[ways + 2 : ways + 4], refs[-ways - 3 : -1]
     for copy in fetch(sources, held, refs[-1]):
         copy.wait()
-    events_ref, own_ref, *peer_refs = held
+    events_ref, own_ref, before_ref, opposite_ref, behind_ref, far_ref = held
     rows, features = own_ref.shape
     columns = proj_ref.shape[2]
-    for b in range(features // columns):
-        block = slice(b * columns, (b + 1) * columns)
-        branch = own_ref[:, block].astype(F32)
-        for peer in peer_refs:
+    blocks = features // columns
+    for b in range(blocks):
+        lanes = slice(b * columns, (b + 1) * columns)
+        branch = own_ref[:, lanes].astype(F32) + opposite_ref[:, lanes].astype(F32)
+        for peer in (before_ref, behind_ref):
             branch = branch + peer[b * rows : (b + 1) * rows].astype(F32)
-        feat_ref[:, block] = (events_ref[:, block].astype(F32) + branch).astype(BF16)
-    for k, peer in enumerate(peer_refs):
-        proj_ref[k] = peer[features // columns * rows :]
+        feat_ref[:, lanes] = (events_ref[:, lanes].astype(F32) + branch).astype(BF16)
+    proj_ref[0] = before_ref[blocks * rows :]
+    proj_ref[1] = far_ref[...]
+    proj_ref[2] = behind_ref[blocks * rows :]
 
 
 def teacher_norm_kernel(clip_ref, gain_ref, after_ref, normed_ref):
@@ -266,9 +271,10 @@
     pieces = []
     for head in range(heads):
         query, keys, values = split_head(packed, head)
-        weights = weights_ref[head]
+        rounded = weights_ref[head]
+        weights = rounded.astype(F32)
         cot = dmixed[:, head * HEAD : (head + 1) * HEAD].astype(BF16)
-        dvalues = tn(weights.astype(BF16), cot)
+        dvalues = tn(rounded, cot)
         dweights = nt(cot, values)
         inner = jnp.sum(dweights * weights, -1, keepdims=True)
         dscores = (weights * (dweights - inner) * HEAD ** (-0.5)).astype(BF16)
@@ -345,29 +351,45 @@
     picked = shares // 2 * (each + each * columns // features)
     places = jnp.stack([own_c] + [(own_x + k) % ways for k in range(ways)]).astype(jnp.int32)
     message_rows = rows * features // columns + features // 2
+    half = features // 2
+    proj_half = lax.dynamic_slice_in_dim(projector, own_c * half, half, 0)
+    far = from_peers(lambda k: proj_half, "x", range(2, ways - 1))
     outs = pl.pallas_call(
-        lambda *refs: student_kernel(shares, *refs),
+        student_kernel,
         out_shape=(
             pltpu.HBM((rows, features), BF16),
-            *[shape((message_rows, columns), BF16)] * (ways - 1),
-            pltpu.HBM((2, picked, length), BF16),
+            *[
+                shape((message_rows, columns) if k in (1, ways - 1) else (rows, features), BF16)
+                for k in range(1, ways)
+            ],
+            pltpu.HBM((length, features), BF16),
             pltpu.HBM((length, 3 * HEAD * heads), BF16),
             pltpu.HBM((length, HEAD * heads), BF16),
-            pltpu.HBM((heads, length, length), F32),
-            pltpu.HBM((2, picked, features), BF16),
+            pltpu.HBM((heads, length, length), BF16),
             *in_place([student_out]),
         ),
         in_specs=[SMEM] * 2 + [VMEM] * 4,
-        out_specs=(pl.BlockSpec(),) + (VMEM,) * (ways - 1) + (pl.BlockSpec(),) * 6,
+        out_specs=(pl.BlockSpec(),) + (VMEM,) * (ways - 1) + (pl.BlockSpec(),) * 5,
         scratch_shapes=[pltpu.VMEM((length, features), F32)],
         compiler_params=PARAMS,
         cost_estimate=cost(4),
         name="student_forward",
     )(valid_counts, places, events, student_qkv.T, student_out, projector)
     own_part, peer_parts = outs[0], outs[1:ways]
-    normed_rows, packed, mixed, weights, pick, kept_out = outs[ways:]
-
-    received = from_peers(lambda k: peer_parts[k - 1], "x")
+    normed, packed, mixed, weights, kept_out = outs[ways:]
+    normed_rows, pick = pl.pallas_call(
+        lambda *refs: picks_kernel(shares, columns, *refs),
+        out_shape=(
+            pltpu.HBM((2, picked, length), BF16), pltpu.HBM((2, picked, features), BF16),
+        ),
+        in_specs=[SMEM, VMEM, ANY],
+        out_specs=(pl.BlockSpec(),) * 2,
+        compiler_params=PARAMS,
+        cost_estimate=cost(2),
+        name="student_picks",
+    )(places, normed, far[0])
+
+    received = from_peers(lambda k: peer_parts[k - 1], "x") + far
     own_events = lax.dynamic_slice_in_dim(events, own_x * rows, rows, 0)
     feat_rows, proj_halves = pl.pallas_call(
         lambda *refs: rows_kernel(ways, *refs),
@@ -375,15 +397,17 @@
             shape((rows, features), BF16), shape((ways - 1, features // 2, columns), BF16),
             *in_place(received),
         ),
-        in_specs=[ANY] * 2 + [HBM] * (ways - 1),
-        out_specs=(VMEM,) * 2 + (HBM,) * (ways - 1),
-        input_output_aliases={2 + k: 2 + k for k in range(ways - 1)},
+        in_specs=[ANY] * 2 + [HBM] * ways,
+        out_specs=(VMEM,) * 2 + (HBM,) * ways,
+        input_output_aliases={2 + k: 2 + k for k in range(ways)},
         scratch_shapes=buffers((own_events, own_part, *received)),
         compiler_params=PARAMS,
         cost_estimate=cost(1),
         name="student_rows",
     )(own_events, own_part, *received)[:2]
-    own_core, feat_rows, proj_halves = lax.optimization_barrier((own_core, feat_rows, proj_halves))
+    own_core, feat_rows, proj_halves, normed_rows = lax.optimization_barrier(
+        (own_core, feat_rows, proj_halves, normed_rows)
+    )
     other_core = lax.ppermute(own_core, "c", SWAP)
     proj_others = lax.ppermute(proj_halves, "c", SWAP)
     teacher_normed = pl.pallas_call(

time: 133 us -> 131 us (0.985)
  waiting for transfers between devices: 26.3 us -> 19.7 us
  starting transfers between devices: 39.3 us -> 42.4 us
  Pallas kernels: 22.7 us -> 24.2 us
    ppermute x3 -> x4, waiting for transfers between devices: 8.88 us -> 1.95 us  [from_peers(): lax.ppermute(rows(k), axis, [(i, (i + k) % ways) for i in range(ways)])]
    ppermute x3 -> x4, starting transfers between devices: 11.4 us -> 14.4 us  [from_peers(): lax.ppermute(rows(k), axis, [(i, (i + k) % ways) for i in range(ways)])]
    pallas_call x1 -> x2, Pallas kernels: 4.43 us -> 5.98 us  [the longest x1 3.39 us: on_device(): pl.pallas_call(student_kernel, out_shape=(pltpu.HBM((rows, features), BF1...]
    unnamed x26 -> x32, local copies, waits for them, and re-layouts: 3.32 us -> 3.41 us
  transfers between devices with their start and end apart: 9 -> 10, of which waited for: 6 -> 6; matrix products, arithmetic and copies ran while one was open for 1% -> 1% of each run, Pallas kernels for 12% -> 13%
where the time goes in v9:
time: 131 us
  starting transfers between devices  42.4 us (32%)
  blocking collectives  35.1 us (27%)
  Pallas kernels  24.2 us (18%)
  waiting for transfers between devices  19.7 us (15%)
  local copies, waits for them, and re-layouts  5.42 us (4%)
  between operations  2.22 us (2%)
  other arithmetic  1.52 us (1%)
    all_to_all x1, blocking collectives, on_device(): lax.all_to_all(total.reshape(chips, total.shape[0] // chips, features), C...  35.1 us
    ppermute x4, starting transfers between devices, from_peers(): lax.ppermute(rows(k), axis, [(i, (i + k) % ways) for i in range(ways)])  14.4 us
    all_to_all x1, starting transfers between devices, on_device(): own_core = lax.all_to_all(shard, ('y', 'z'), 0, 0)  14 us
    all_to_all x1, waiting for transfers between devices, on_device(): teacher_parts = lax.all_to_all(teacher_part, 'x', 0, 0)  8.91 us
    all_to_all x1, waiting for transfers between devices, on_device(): lax.all_to_all(message, 'x', 0, 0)  6.25 us
    pallas_call x1, Pallas kernels, on_device(): pl.pallas_call(lambda *refs: backward_kernel(len(held), *refs), out_shape...  4.44 us
    all_to_all x1, starting transfers between devices, on_device(): teacher_parts = lax.all_to_all(teacher_part, 'x', 0, 0)  4.3 us
    pallas_call x1, Pallas kernels, on_device(): pl.pallas_call(teacher_kernel, out_shape=shape((ways, rows, width + featu...  3.85 us
  transfers between devices with their start and end apart: 10, of which 6 were waited for; matrix products, arithmetic and copies ran while one was open for 1% of the time, Pallas kernels for 13%

profile of v9, /device:TPU:16, one launch (start us, length us, event | category | flops | bytes accessed | tf_op | source)
XLA Modules:
  0.0 130.6 jit_solution(18172123967809291456)
XLA Ops:
  0.6 0.8 pad_maximum_fusion
  1.4 1.1 broadcast_in_dim.2
  2.5 14.0 %all-to-all-start = ((bf16[32,16,1024]{2,1,0:T(8,128)(2,1)}), bf16[32,16,1024]{2,1,0:T(8,128)(2,1)S(1)}, u32[]{:S(2)}, u32[]{:S(2)}) async-start(bf16[32,16,1024]{2,1,0:T(8,128)(2,1)} %broadcast_in_dim.2), calls=%async_computation | async-start | bytes 2097152 | tf_op jit(solution)/shard_map/all_to_all | solution.py:348
  16.5 0.7 constant_dynamic-slice_fusion.1
  17.2 4.9 %collective-permute-start.3 = (bf16[384,256]{1,0:T(8,128)(2,1)}, bf16[384,256]{1,0:T(8,128)(2,1)}, u32[]{:S(2)}, u32[]{:S(2)}) collective-permute-start(bf16[384,256]{1,0:T(8,128)(2,1)} %constant_dynamic-slice_fusion.1), channel_id=1, source_target_pairs={{0,2},{1,3},{2,0},{3,1},{4,6},{5,7},{6,4},{7,5},{8,10},{9,11},{10,... | collective-permute-start | bytes 589832 | tf_op jit(solution)/shard_map/ppermute | solution.py:309
  22.9 3.4 %student_forward.1 = (bf16[64,768]{1,0:T(8,128)(2,1)}, bf16[576,256]{1,0:T(8,128)(2,1)}, bf16[64,768]{1,0:T(8,128)(2,1)S(1)}, bf16[576,256]{1,0:T(8,128)(2,1)S(1...) custom-call(s32[1]{0:T(128)S(6)} %copy.36.count_ref.refs_0_, ...), custom_call_target="tpu_custom_call" | custom-call | flops 4000000000 | bytes 1000000 | tf_op jit(solution)/shard_map/student_forward/pallas_call | solution.py:357
  26.3 2.4 %collective-permute-start.1 = (bf16[64,768]{1,0:T(8,128)(2,1)S(1)}, bf16[64,768]{1,0:T(8,128)(2,1)S(1)}, u32[]{:S(2)}, u32[]{:S(2)}) collective-permute-start(bf16[64,768]{1,0:T(8,128)(2,1)S(1)} %get-tuple-element.29), channel_id=1, source_target_pairs={{0,2},{1,3},{2,0},{3,1},{4,6},{5,7},{6,4},{7,5},{8,10},{9,11},{10,... | collective-permute-start | bytes 294920 | tf_op jit(solution)/shard_map/ppermute | solution.py:309
  28.7 3.4 %collective-permute-start = (bf16[576,256]{1,0:T(8,128)(2,1)}, bf16[576,256]{1,0:T(8,128)(2,1)S(1)}, u32[]{:S(2)}, u32[]{:S(2)}) collective-permute-start(bf16[576,256]{1,0:T(8,128)(2,1)} %get-tuple-element.28), channel_id=1, source_target_pairs={{0,1},{1,2},{2,3},{3,0},{4,5},{5,6},{6,7},{7,4},{8,9},{9,10},{10,1... | collective-permute-start | bytes 884744 | tf_op jit(solution)/shard_map/ppermute | solution.py:309
  32.1 3.7 %collective-permute-start.2 = (bf16[576,256]{1,0:T(8,128)(2,1)S(1)}, bf16[576,256]{1,0:T(8,128)(2,1)S(1)}, u32[]{:S(2)}, u32[]{:S(2)}) collective-permute-start(bf16[576,256]{1,0:T(8,128)(2,1)S(1)} %get-tuple-element.30), channel_id=1, source_target_pairs={{0,3},{1,0},{2,1},{3,2},{4,7},{5,4},{6,5},{7,6},{8,11},{9,8},{10,9... | collective-permute-start | bytes 884744 | tf_op jit(solution)/shard_map/ppermute | solution.py:309
  35.8 1.0 copy-done.12
  36.8 2.6 %student_picks.1 = (bf16[2,512,256]{2,1,0:T(8,128)(2,1)}, bf16[2,512,768]{2,1,0:T(8,128)(2,1)}) custom-call(s32[5]{0:T(128)S(1)} %stack.35.place_ref.refs_0_, bf16[256,768]{1,0:T(8,128)(2,1)S(1)} %copy-done.12, bf16[384,256]{1,0:T(8,128)(2,1)} %collective-permute-done.3.refs_5_.refs_2_), custom_call_target="tpu_custom_call" | custom-call | flops 2000000000 | bytes 1000000 | tf_op jit(solution)/shard_map/student_picks/pallas_call | solution.py:380
  39.4 1.2 collective-permute-done.refs_2_
  40.6 0.7 collective-permute-done.2.refs_4_
  41.4 0.7 copy-done.14
  42.1 1.5 %student_rows.1 = (bf16[64,768]{1,0:T(8,128)(2,1)S(1)}, bf16[3,384,256]{2,1,0:T(8,128)(2,1)S(1)}, bf16[576,256]{1,0:T(8,128)(2,1)}, bf16[64,768]{1,0:T(8,128)(2,...) custom-call(bf16[64,768]{1,0:T(8,128)(2,1)S(1)} %dynamic-slice_bitca, ...), custom_call_target="tpu_custom_call", output_to_operand_aliasing={{2}: (2, {}), {3}: (3, {}), {4}: (4, {}), {5}: (5, {})} | custom-call | flops 1000000000 | bytes 1000000 | tf_op jit(solution)/shard_map/student_rows/pallas_call | solution.py:394
  43.9 1.9 %collective-permute-start.4 = (bf16[32,16,1024]{2,1,0:T(8,128)(2,1)S(1)}, bf16[32,16,1024]{2,1,0:T(8,128)(2,1)S(1)}, u32[]{:S(2)}, u32[]{:S(2)}) collective-permute-start(bf16[32,16,1024]{2,1,0:T(8,128)(2,1)S(1)} %all-to-all-done.own_ref), channel_id=1, source_target_pairs={{0,4},{4,0},{1,5},{5,1},{2,6},{6,2},{3,7},{7,3},{8,12},{12,8},{9,1... | collective-permute-start | bytes 3145736 | tf_op jit(solution)/shard_map/ppermute | solution.py:411
  45.9 2.4 %collective-permute-start.5 = (bf16[3,384,256]{2,1,0:T(8,128)(2,1)S(1)}, bf16[3,384,256]{2,1,0:T(8,128)(2,1)S(1)}, u32[]{:S(2)}, u32[]{:S(2)}) collective-permute-start(bf16[3,384,256]{2,1,0:T(8,128)(2,1)S(1)} %get-tuple-element.37.refs_2_), channel_id=1, source_target_pairs={{0,4},{4,0},{1,5},{5,1},{2,6},{6,2},{3,7},{7,3},{8,12},{12,8},{9,1... | collective-permute-start | bytes 1769480 | tf_op jit(solution)/shard_map/ppermute | solution.py:412
  48.9 3.8 %teacher.1 = bf16[4,64,1792]{2,1,0:T(8,128)(2,1)} custom-call(s32[5]{0:T(128)S(1)} %stack.35.place_ref.refs_0_, s32[2]{0:T(128)S(1)} %bitcast.26, bf16[256,1024]{1,0:T(8,128)(2,1)S(1)} %teacher_norm.1.normed_ref, bf16[32,16,1024]{2,1,0:T(8,128)(2,1)S(1)} %all-to-all-done.own_ref, bf16[32,16,1024]{2,1,0:T(8,128)(2,1)S(1)} %collective-permute-done.4.other_ref, ...), custom_call_target="tpu_custom_call" | custom-call | flops 5000000000 | bytes 1000000 | tf_op jit(solution)/shard_map/teacher/pallas_call | solution.py:423
  52.8 4.3 %all-to-all-start.1 = ((bf16[4,64,1792]{2,1,0:T(8,128)(2,1)}), bf16[4,64,1792]{2,1,0:T(8,128)(2,1)S(1)}, u32[]{:S(2)}, u32[]{:S(2)}) async-start(bf16[4,64,1792]{2,1,0:T(8,128)(2,1)} %teacher.1), calls=%async_computation.1 | async-start | bytes 1835008 | tf_op jit(solution)/shard_map/all_to_all | solution.py:437
  57.1 0.6 fusion.1
  58.5 1.8 %projector.1.proj_ref.refs_5_ = bf16[4,768,256]{2,1,0:T(8,128)(2,1)} custom-call(s32[5]{0:T(128)S(1)} %stack.33.refs_0_.refs_1_, bf16[768,256]{1,0:T(8,128)(2,1)S(1)} %copy-done, bf16[3,384,256]{2,1,0:T(8,128)(2,1)S(1)} %get-tuple-element.37.refs_2_, bf16[3,384,256]{2,1,0:T(8,128)(2,1)S(1)} %collective-permute-done.5.refs_3_), custom_call_target="tpu_custom_call" | custom-call | flops 1000000000 | bytes 1000000 | tf_op jit(solution)/shard_map/projector/pallas_call | solution.py:442
  60.2 1.4 %copy-done.7 = bf16[4,768,256]{2,1,0:T(8,128)(2,1)S(1)} copy-done((bf16[4,768,256]{2,1,0:T(8,128)(2,1)S(1)}, bf16[4,768,256]{2,1,0:T(8,128)(2,1)}, u32[]{:S(2)}) %copy-start.7) | copy-done | bytes 1572888
  62.0 8.9 %all-to-all-done.1.refs_2_.refs_1_ = bf16[4,64,1792]{2,1,0:T(8,128)(2,1)S(1)} async-done(((bf16[4,64,1792]{2,1,0:T(8,128)(2,1)}), bf16[4,64,1792]{2,1,0:T(8,128)(2,1)S(1)}, u32[]{:S(2)}, u32[]{:S(2)}) %all-to-all-start.1) | async-done | bytes 917536 | tf_op jit(solution)/shard_map/all_to_all | solution.py:437
  71.0 2.0 %difference.1.refs_2_ = bf16[4,64,1152]{2,1,0:T(8,128)(2,1)} custom-call(s32[1]{0:T(128)S(6)} %copy.36.count_ref.refs_0_, s32[5]{0:T(128)S(1)} %stack.33.refs_0_.refs_1_, bf16[4,64,1792]{2,1,0:T(8,128)(2,1)S(1)} %all-to-all-done.1.refs_2_.refs_1_, bf16[64,1024]{1,0:T(8,128)(2,1)S(1)} %dynamic-slice_bitcast_fusion.refs_3_, ...), custom_call_target="tpu_custom_call" | custom-call | flops 2000000000 | bytes 1000000 | tf_op jit(solution)/shard_map/difference/pallas_call | solution.py:460
  72.9 3.5 %all-to-all-start.2 = ((bf16[4,64,1152]{2,1,0:T(8,128)(2,1)}), bf16[4,64,1152]{2,1,0:T(8,128)(2,1)S(1)}, u32[]{:S(2)}, u32[]{:S(2)}) async-start(bf16[4,64,1152]{2,1,0:T(8,128)(2,1)} %difference.1.refs_2_), calls=%async_computation.2 | async-start | bytes 1179648 | tf_op jit(solution)/shard_map/all_to_all | solution.py:478
  76.4 3.2 %student_extra.1.refs_7_ = bf16[2,3,512,256]{3,2,1,0:T(8,128)(2,1)} custom-call(s32[5]{0:T(128)S(1)} %stack.33.refs_0_.refs_1_, bf16[4,64,1792]{2,1,0:T(8,128)(2,1)S(1)} %all-to-all-done.1.refs_2_.refs_1_, bf16[4,64,1152]{2,1,0:T(8,128)(2,1)} %difference.1.refs_2_), custom_call_target="tpu_custom_call" | custom-call | flops 3000000000 | bytes 1000000 | tf_op jit(solution)/shard_map/student_extra/pallas_call | solution.py:469
  79.6 6.3 %all-to-all-done.2 = bf16[4,64,1152]{2,1,0:T(8,128)(2,1)S(1)} async-done(((bf16[4,64,1152]{2,1,0:T(8,128)(2,1)}), bf16[4,64,1152]{2,1,0:T(8,128)(2,1)S(1)}, u32[]{:S(2)}, u32[]{:S(2)}) %all-to-all-start.2) | async-done | bytes 589856 | tf_op jit(solution)/shard_map/all_to_all | solution.py:478
  85.8 4.4 %student_backward.1 = (bf16[512,768]{1,0:T(8,128)(2,1)S(1)}, bf16[512,768]{1,0:T(8,128)(2,1)S(1)}, f32[1,1]{1,0:T(1,128)}, bf16[192,768]{1,0:T(8,128)(2,1)}, bf1...) custom-call(bf16[256,1152]{1,0:T(8,128)(2,1)S(1)} %bitcast.21, ...), custom_call_target="tpu_custom_call", output_to_operand_aliasing={{3}: (1, {}), {4}: (2, {}), {5}: (3, {}), {6}: (4, {}), {7}... | custom-call | flops 4000000000 | bytes 1000000 | tf_op jit(solution)/shard_map/student_backward/pallas_call | solution.py:481
  90.3 1.9 %collective-permute-start.6 = (bf16[512,768]{1,0:T(8,128)(2,1)S(1)}, bf16[512,768]{1,0:T(8,128)(2,1)S(1)}, u32[]{:S(2)}, u32[]{:S(2)}) collective-permute-start(bf16[512,768]{1,0:T(8,128)(2,1)S(1)} %get-tuple-element.46), channel_id=1, source_target_pairs={{0,4},{4,0},{1,5},{5,1},{2,6},{6,2},{3,7},{7,3},{8,12},{12,8},{9,1... | collective-permute-start | bytes 2359304 | tf_op jit(solution)/shard_map/ppermute | solution.py:496
  92.2 2.3 %collective-permute-done.6 = bf16[512,768]{1,0:T(8,128)(2,1)S(1)} collective-permute-done((bf16[512,768]{1,0:T(8,128)(2,1)S(1)}, bf16[512,768]{1,0:T(8,128)(2,1)S(1)}, u32[]{:S(2)}, u32[]{:S(2)}) %collective-permute-start.6) | collective-permute-done | bytes 786464 | tf_op jit(solution)/shard_map/ppermute | solution.py:496
  94.7 35.1 %all_to_all.20.parts_ref = bf16[64,8,768]{2,1,0:T(8,128)(2,1)S(1)} all-to-all(bf16[64,8,768]{2,1,0:T(8,128)(2,1)S(1)} %fusion), channel_id=1, replica_groups=mesh['g'=2,'y'=4,'z'=8,'c'=2,'x'=4] {'g','y','z'}, dimensions={0} | all-to-all | bytes 1572864 | tf_op jit(solution)/shard_map/all_to_all | solution.py:498
  129.8 0.8 gradient_rows.1
  (41 shorter events, 1.7 us)
Async XLA Ops:
  1.4 15.1 %copy-start = (bf16[768,256]{1,0:T(8,128)(2,1)S(1)}, bf16[768,256]{1,0:T(8,128)(2,1)}, u32[]{:S(2)}) copy-start(bf16[768,256]{1,0:T(8,128)(2,1)} %refs_1_.1) | copy-start | bytes 1179652
  2.5 20.4 %copy-start.2 = (bf16[1,256,768]{2,1,0:T(8,128)(2,1)S(1)}, bf16[1,256,768]{2,1,0:T(8,128)(2,1)}, u32[]{:S(2)}) copy-start(bf16[1,256,768]{2,1,0:T(8,128)(2,1)} %param.14) | copy-start | bytes 1179652
  2.5 20.4 %copy-start.3 = (bf16[768,576]{0,1:T(8,128)(2,1)S(1)}, bf16[768,576]{0,1:T(8,128)(2,1)}, u32[]{:S(2)}) copy-start(bf16[768,576]{0,1:T(8,128)(2,1)} %param.17) | copy-start | bytes 2654212
  2.5 20.4 %copy-start.4 = (bf16[192,768]{1,0:T(8,128)(2,1)S(1)}, bf16[192,768]{1,0:T(8,128)(2,1)}, u32[]{:S(2)}) copy-start(bf16[192,768]{1,0:T(8,128)(2,1)} %out_ref.1) | copy-start | bytes 884740
  2.5 41.4 %all-to-all-start = ((bf16[32,16,1024]{2,1,0:T(8,128)(2,1)}), bf16[32,16,1024]{2,1,0:T(8,128)(2,1)S(1)}, u32[]{:S(2)}, u32[]{:S(2)}) async-start(bf16[32,16,1024]{2,1,0:T(8,128)(2,1)} %broadcast_in_dim.2), calls=%async_computation | async-start | bytes 2097152 | tf_op jit(solution)/shard_map/all_to_all | solution.py:348
  17.2 18.6 %collective-permute-start.3 = (bf16[384,256]{1,0:T(8,128)(2,1)}, bf16[384,256]{1,0:T(8,128)(2,1)}, u32[]{:S(2)}, u32[]{:S(2)}) collective-permute-start(bf16[384,256]{1,0:T(8,128)(2,1)} %constant_dynamic-slice_fusion.1), channel_id=1, source_target_pairs={{0,2},{1,3},{2,0},{3,1},{4,6},{5,7},{6,4},{7,5},{8,10},{9,11},{10,... | collective-permute-start | bytes 589832 | tf_op jit(solution)/shard_map/ppermute | solution.py:309
  26.3 13.1 %collective-permute-start.1 = (bf16[64,768]{1,0:T(8,128)(2,1)S(1)}, bf16[64,768]{1,0:T(8,128)(2,1)S(1)}, u32[]{:S(2)}, u32[]{:S(2)}) collective-permute-start(bf16[64,768]{1,0:T(8,128)(2,1)S(1)} %get-tuple-element.29), channel_id=1, source_target_pairs={{0,2},{1,3},{2,0},{3,1},{4,6},{5,7},{6,4},{7,5},{8,10},{9,11},{10,... | collective-permute-start | bytes 294920 | tf_op jit(solution)/shard_map/ppermute | solution.py:309
  28.7 11.9 %collective-permute-start = (bf16[576,256]{1,0:T(8,128)(2,1)}, bf16[576,256]{1,0:T(8,128)(2,1)S(1)}, u32[]{:S(2)}, u32[]{:S(2)}) collective-permute-start(bf16[576,256]{1,0:T(8,128)(2,1)} %get-tuple-element.28), channel_id=1, source_target_pairs={{0,1},{1,2},{2,3},{3,0},{4,5},{5,6},{6,7},{7,4},{8,9},{9,10},{10,1... | collective-permute-start | bytes 884744 | tf_op jit(solution)/shard_map/ppermute | solution.py:309
  32.1 9.2 %collective-permute-start.2 = (bf16[576,256]{1,0:T(8,128)(2,1)S(1)}, bf16[576,256]{1,0:T(8,128)(2,1)S(1)}, u32[]{:S(2)}, u32[]{:S(2)}) collective-permute-start(bf16[576,256]{1,0:T(8,128)(2,1)S(1)} %get-tuple-element.30), channel_id=1, source_target_pairs={{0,3},{1,0},{2,1},{3,2},{4,7},{5,4},{6,5},{7,6},{8,11},{9,8},{10,9... | collective-permute-start | bytes 884744 | tf_op jit(solution)/shard_map/ppermute | solution.py:309
  35.8 1.0 copy-start.12
  36.8 5.3 %copy-start.11 = (bf16[64,768]{1,0:T(8,128)(2,1)S(1)}, bf16[64,768]{1,0:T(8,128)(2,1)}, u32[]{:S(2)}) copy-start(bf16[64,768]{1,0:T(8,128)(2,1)} %get-tuple-element.27.refs_1_) | copy-start | bytes 294916
  39.4 2.7 %copy-start.15 = (bf16[64,768]{1,0:T(8,128)(2,1)}, bf16[64,768]{1,0:T(8,128)(2,1)S(1)}, u32[]{:S(2)}) copy-start(bf16[64,768]{1,0:T(8,128)(2,1)S(1)} %collective-permute-done.1.refs_3_) | copy-start | bytes 294916
  40.6 0.7 copy-start.13
  41.4 0.7 copy-start.14
  42.1 6.2 %copy-start.1 = (bf16[1,256,1024]{2,1,0:T(8,128)(2,1)S(1)}, bf16[1,256,1024]{2,1,0:T(8,128)(2,1)}, u32[]{:S(2)}) copy-start(bf16[1,256,1024]{2,1,0:T(8,128)(2,1)} %param.10) | copy-start | bytes 1572868
  42.1 6.2 %copy-start.5 = (f32[1024]{0:T(1024)S(1)}, f32[1024]{0:T(1024)}, u32[]{:S(2)}) copy-start(f32[1024]{0:T(1024)} %param.11) | copy-start | bytes 12292
  43.6 5.0 %copy-start.9 = (bf16[64,768]{1,0:T(8,128)(2,1)}, bf16[64,768]{1,0:T(8,128)(2,1)S(1)}, u32[]{:S(2)}) copy-start(bf16[64,768]{1,0:T(8,128)(2,1)S(1)} %get-tuple-element.35.after_ref.feat_ref) | copy-start | bytes 294916
  43.9 4.7 %collective-permute-start.4 = (bf16[32,16,1024]{2,1,0:T(8,128)(2,1)S(1)}, bf16[32,16,1024]{2,1,0:T(8,128)(2,1)S(1)}, u32[]{:S(2)}, u32[]{:S(2)}) collective-permute-start(bf16[32,16,1024]{2,1,0:T(8,128)(2,1)S(1)} %all-to-all-done.own_ref), channel_id=1, source_target_pairs={{0,4},{4,0},{1,5},{5,1},{2,6},{6,2},{3,7},{7,3},{8,12},{12,8},{9,1... | collective-permute-start | bytes 3145736 | tf_op jit(solution)/shard_map/ppermute | solution.py:411
  45.9 12.6 %collective-permute-start.5 = (bf16[3,384,256]{2,1,0:T(8,128)(2,1)S(1)}, bf16[3,384,256]{2,1,0:T(8,128)(2,1)S(1)}, u32[]{:S(2)}, u32[]{:S(2)}) collective-permute-start(bf16[3,384,256]{2,1,0:T(8,128)(2,1)S(1)} %get-tuple-element.37.refs_2_), channel_id=1, source_target_pairs={{0,4},{4,0},{1,5},{5,1},{2,6},{6,2},{3,7},{7,3},{8,12},{12,8},{9,1... | collective-permute-start | bytes 1769480 | tf_op jit(solution)/shard_map/ppermute | solution.py:412
  48.3 0.7 copy-start.6
  52.8 18.2 %all-to-all-start.1 = ((bf16[4,64,1792]{2,1,0:T(8,128)(2,1)}), bf16[4,64,1792]{2,1,0:T(8,128)(2,1)S(1)}, u32[]{:S(2)}, u32[]{:S(2)}) async-start(bf16[4,64,1792]{2,1,0:T(8,128)(2,1)} %teacher.1), calls=%async_computation.1 | async-start | bytes 1835008 | tf_op jit(solution)/shard_map/all_to_all | solution.py:437
  58.4 1.8 %copy-start.10 = (bf16[64,768]{1,0:T(8,128)(2,1)S(1)}, bf16[64,768]{1,0:T(8,128)(2,1)}, u32[]{:S(2)}) copy-start(bf16[64,768]{1,0:T(8,128)(2,1)} %copy-done.9) | copy-start | bytes 294916
  60.2 1.4 %copy-start.7 = (bf16[4,768,256]{2,1,0:T(8,128)(2,1)S(1)}, bf16[4,768,256]{2,1,0:T(8,128)(2,1)}, u32[]{:S(2)}) copy-start(bf16[4,768,256]{2,1,0:T(8,128)(2,1)} %projector.1.proj_ref.refs_5_) | copy-start | bytes 4718596
  61.7 9.3 %copy-start.8 = (bf16[4,768,256]{2,1,0:T(8,128)(2,1)S(1)}, bf16[4,768,256]{2,1,0:T(8,128)(2,1)}, u32[]{:S(2)}) copy-start(bf16[4,768,256]{2,1,0:T(8,128)(2,1)} %projector.1.proj_ref.refs_5_) | copy-start | bytes 4718596
  72.9 12.9 %all-to-all-start.2 = ((bf16[4,64,1152]{2,1,0:T(8,128)(2,1)}), bf16[4,64,1152]{2,1,0:T(8,128)(2,1)S(1)}, u32[]{:S(2)}, u32[]{:S(2)}) async-start(bf16[4,64,1152]{2,1,0:T(8,128)(2,1)} %difference.1.refs_2_), calls=%async_computation.2 | async-start | bytes 1179648 | tf_op jit(solution)/shard_map/all_to_all | solution.py:478
  90.3 4.2 %collective-permute-start.6 = (bf16[512,768]{1,0:T(8,128)(2,1)S(1)}, bf16[512,768]{1,0:T(8,128)(2,1)S(1)}, u32[]{:S(2)}, u32[]{:S(2)}) collective-permute-start(bf16[512,768]{1,0:T(8,128)(2,1)S(1)} %get-tuple-element.46), channel_id=1, source_target_pairs={{0,4},{4,0},{1,5},{5,1},{2,6},{6,2},{3,7},{7,3},{8,12},{12,8},{9,1... | collective-permute-start | bytes 2359304 | tf_op jit(solution)/shard_map/ppermute | solution.py:496

commit v10 on v9

--- a/solution.py
+++ b/solution.py
@@ -159,13 +159,13 @@
 
 
 def teacher_kernel(
-    place_ref, align_ref, normed_ref, own_ref, other_ref, feat_ref, part_ref, parts_ref, mixed_ref
+    place_ref, align_ref, normed_ref, own_ref, other_ref, feat_ref, part_ref, full_ref, mixed_ref
 ):
-    blocks, cores, rows, width = parts_ref.shape
+    blocks, rows, width = own_ref.shape
     for i, piece in enumerate((own_ref, other_ref)):
         core = place_ref[0] if i == 0 else 1 - place_ref[0]
-        parts_ref[:, pl.ds(core, 1)] = piece[...].reshape(blocks, 1, rows, width)
-    full_ref = parts_ref[...].reshape(blocks * cores * rows, width)
+        for b in range(blocks):
+            full_ref[pl.ds(pl.multiple_of((2 * b + core) * rows, rows), rows), :] = piece[b]
     heads = width // (4 * HEAD)
     packed = nn(normed_ref[...], full_ref[:, : heads * 3 * HEAD])
     mixed = []
@@ -175,7 +175,7 @@
         mixed.append(nn(weights.astype(BF16), values))
     mixed_ref[...] = jnp.concatenate(mixed, axis=1)
     ways, shared = part_ref.shape[:2]
-    outputs = blocks * cores * rows
+    outputs = full_ref.shape[0]
     per_block = BLOCK // shared
     for i in range(align_ref.shape[0]):
         first = pl.multiple_of(align_ref[i] * BLOCK, BLOCK)
@@ -187,22 +187,22 @@
         part_ref[i, :, outputs:] = feat_ref[...]
 
 
-def assemble_kernel(ways, place_ref, own_ref, mine_ref, other_ref, proj_ref):
+def assemble_kernel(ways, place_ref, own_ref, mine_ref, other_ref, proj_ref, whole_ref):
     features, columns = own_ref.shape
     half = features // 2
     first = pl.multiple_of(place_ref[0] * half, half)
     second = pl.multiple_of((1 - place_ref[0]) * half, half)
-    proj_ref[place_ref[1]] = own_ref[...]
+    proj_ref[place_ref[1]] = own_ref[...].T
     for k in range(1, ways):
-        source = place_ref[1 + k]
-        proj_ref[source, pl.ds(first, half), :] = mine_ref[k - 1]
-        proj_ref[source, pl.ds(second, half), :] = other_ref[k - 1]
+        whole_ref[pl.ds(first, half), :] = mine_ref[k - 1]
+        whole_ref[pl.ds(second, half), :] = other_ref[k - 1]
+        proj_ref[place_ref[1 + k]] = whole_ref[...].T
 
 
 def predict_kernel(feat_ref, proj_ref, pred_ref):
-    ways, features, columns = proj_ref.shape
+    ways, columns, features = proj_ref.shape
     for k in range(ways):
-        pred_ref[:, k * columns : (k + 1) * columns] = nn(feat_ref[...], proj_ref[k])
+        pred_ref[:, k * columns : (k + 1) * columns] = nt(feat_ref[...], proj_ref[k])
 
 
 def extra_kernel(shares, columns, place_ref, parts_ref, after_ref, extra_ref):
@@ -223,7 +223,7 @@
     clips, count_ref, place_ref, parts_ref, tokens_ref, pred_ref, proj_ref, out_ref
 ):
     rows, width = tokens_ref.shape
-    ways, features, columns = proj_ref.shape
+    ways, columns, features = proj_ref.shape
     branch = parts_ref[0, :, :width].astype(F32)
     for i in range(1, ways):
         branch = branch + parts_ref[i, :, :width].astype(F32)
@@ -237,7 +237,7 @@
     dpred = (diff * factor).astype(BF16)
     dfeat = jnp.zeros((rows, features), F32)
     for k in range(ways):
-        dfeat = dfeat + nt(dpred[:, k * columns : (k + 1) * columns], proj_ref[k])
+        dfeat = dfeat + nn(dpred[:, k * columns : (k + 1) * columns], proj_ref[k])
     dfeat = dfeat.astype(BF16)
     high = squares.astype(BF16)
     rest = squares - high.astype(F32)
@@ -252,10 +252,10 @@
         out_ref[i, :, features + columns :] = tail
 
 
-def backward_kernel(held, back_ref, *refs):
+def backward_kernel(held, back_ref, feat_ref, *refs):
     sources, (keep_ref, send_ref, loss_ref) = refs[:held], refs[held : held + 3]
     copies = fetch(sources, refs[2 * held + 3 : -1], refs[-1])
-    out_ref, packed_ref, weights_ref, mixed_ref, normed_ref, pick_ref, feat_ref = refs[2 * held + 3 : -1]
+    out_ref, packed_ref, weights_ref, mixed_ref, normed_ref, pick_ref = refs[2 * held + 3 : -1]
     copies[0].wait()
     features = out_ref.shape[1]
     heads = out_ref.shape[0] // HEAD
@@ -426,7 +426,7 @@
         in_specs=[SMEM] * 2 + [VMEM] * 4,
         out_specs=VMEM,
         scratch_shapes=[
-            pltpu.VMEM((senders, 2, *shard.shape[1:]), BF16),
+            pltpu.VMEM((senders * 2 * shard.shape[1], shard.shape[2]), BF16),
             pltpu.VMEM((length, teacher_out_t.shape[1]), F32),
         ],
         compiler_params=PARAMS,
@@ -441,9 +441,10 @@
     sources = jnp.stack([own_c] + [(own_x - k + ways) % ways for k in range(ways)]).astype(jnp.int32)
     whole_proj = pl.pallas_call(
         lambda *refs: assemble_kernel(ways, *refs),
-        out_shape=pltpu.HBM((ways, features, columns), BF16),
+        out_shape=pltpu.HBM((ways, columns, features), BF16),
         in_specs=[SMEM] + [VMEM] * 3,
         out_specs=pl.BlockSpec(),
+        scratch_shapes=[pltpu.VMEM((features, columns), BF16)],
         compiler_params=PARAMS,
         cost_estimate=cost(1),
         name="projector",
@@ -468,30 +469,30 @@
     )(valid_counts, sources, teacher_parts, own_tokens, pred, whole_proj)
     feat_extra = pl.pallas_call(
         lambda *refs: extra_kernel(shares, columns, *refs),
-        out_shape=pltpu.HBM((2, features // columns, picked, length), BF16),
+        out_shape=shape((2, features // columns, picked, length), BF16),
         in_specs=[SMEM, VMEM, ANY],
-        out_specs=pl.BlockSpec(),
+        out_specs=VMEM,
         compiler_params=PARAMS,
         cost_estimate=cost(3),
         name="student_extra",
     )(sources, teacher_parts, message)
     back = lax.all_to_all(message, "x", 0, 0).reshape(length, features + columns + BLOCK)
 
-    held = (kept_out, packed, weights, mixed, normed_rows, pick, feat_extra)
+    held = (kept_out, packed, weights, mixed, normed_rows, pick)
     keep, send, loss = pl.pallas_call(
         lambda *refs: backward_kernel(len(held), *refs),
         out_shape=(
             shape((picked, features), BF16), shape((picked, features), BF16), shape((1, 1), F32),
             *in_place(held),
         ),
-        in_specs=[VMEM] + [HBM] * len(held),
+        in_specs=[VMEM] * 2 + [HBM] * len(held),
         out_specs=(VMEM,) * 3 + (HBM,) * len(held),
         scratch_shapes=buffers(held),
-        input_output_aliases={1 + i: 3 + i for i in range(len(held))},
+        input_output_aliases={2 + i: 3 + i for i in range(len(held))},
         compiler_params=PARAMS,
         cost_estimate=cost(4),
         name="student_backward",
-    )(back, *held)[:3]
+    )(back, feat_extra, *held)[:3]
 
     total = add(keep, lax.ppermute(send, "c", SWAP)).astype(BF16)
     chips = shares // 2

time: 131 us -> 131 us (level)
  no operation moved by 1% of the time
where the time goes in v10:
time: 131 us; the launch traced here: 130 us
  starting transfers between devices  42.4 us (32%)
  blocking collectives  35.1 us (27%)
  Pallas kernels  23.5 us (18%)
  waiting for transfers between devices  20.2 us (15%)
  local copies, waits for them, and re-layouts  5.42 us (4%)
  between operations  2.22 us (2%)
  other arithmetic  1.52 us (1%)
    all_to_all x1, blocking collectives, on_device(): lax.all_to_all(total.reshape(chips, total.shape[0] // chips, features), C...  35.1 us
    ppermute x4, starting transfers between devices, from_peers(): lax.ppermute(rows(k), axis, [(i, (i + k) % ways) for i in range(ways)])  14.4 us
    all_to_all x1, starting transfers between devices, on_device(): own_core = lax.all_to_all(shard, ('y', 'z'), 0, 0)  14 us
    all_to_all x1, waiting for transfers between devices, on_device(): teacher_parts = lax.all_to_all(teacher_part, 'x', 0, 0)  8.35 us
    all_to_all x1, waiting for transfers between devices, on_device(): lax.all_to_all(message, 'x', 0, 0)  7.4 us
    pallas_call x1, Pallas kernels, on_device(): pl.pallas_call(lambda *refs: backward_kernel(len(held), *refs), out_shape...  4.44 us
    all_to_all x1, starting transfers between devices, on_device(): teacher_parts = lax.all_to_all(teacher_part, 'x', 0, 0)  4.3 us
    pallas_call x1, Pallas kernels, on_device(): pl.pallas_call(teacher_kernel, out_shape=shape((ways, rows, width + featu...  3.84 us
  transfers between devices with their start and end apart: 10, of which 6 were waited for; matrix products, arithmetic and copies ran while one was open for 1% of the time, Pallas kernels for 13%

profile of v10, /device:TPU:16, one launch (start us, length us, event | category | flops | bytes accessed | tf_op | source)
XLA Modules:
  0.0 130.4 jit_solution(4822653956254160693)
XLA Ops:
  0.6 0.8 pad_maximum_fusion
  1.4 1.1 broadcast_in_dim.2
  2.5 14.0 %all-to-all-start = ((bf16[32,16,1024]{2,1,0:T(8,128)(2,1)}), bf16[32,16,1024]{2,1,0:T(8,128)(2,1)S(1)}, u32[]{:S(2)}, u32[]{:S(2)}) async-start(bf16[32,16,1024]{2,1,0:T(8,128)(2,1)} %broadcast_in_dim.2), calls=%async_computation | async-start | bytes 2097152 | tf_op jit(solution)/shard_map/all_to_all | solution.py:348
  16.5 0.7 constant_dynamic-slice_fusion.1
  17.2 4.9 %collective-permute-start.3 = (bf16[384,256]{1,0:T(8,128)(2,1)}, bf16[384,256]{1,0:T(8,128)(2,1)}, u32[]{:S(2)}, u32[]{:S(2)}) collective-permute-start(bf16[384,256]{1,0:T(8,128)(2,1)} %constant_dynamic-slice_fusion.1), channel_id=1, source_target_pairs={{0,2},{1,3},{2,0},{3,1},{4,6},{5,7},{6,4},{7,5},{8,10},{9,11},{10,... | collective-permute-start | bytes 589832 | tf_op jit(solution)/shard_map/ppermute | solution.py:309
  22.9 3.4 %student_forward.1 = (bf16[64,768]{1,0:T(8,128)(2,1)}, bf16[576,256]{1,0:T(8,128)(2,1)}, bf16[64,768]{1,0:T(8,128)(2,1)S(1)}, bf16[576,256]{1,0:T(8,128)(2,1)S(1...) custom-call(s32[1]{0:T(128)S(6)} %copy.34.count_ref.refs_0_, ...), custom_call_target="tpu_custom_call" | custom-call | flops 4000000000 | bytes 1000000 | tf_op jit(solution)/shard_map/student_forward/pallas_call | solution.py:357
  26.3 2.4 %collective-permute-start.1 = (bf16[64,768]{1,0:T(8,128)(2,1)S(1)}, bf16[64,768]{1,0:T(8,128)(2,1)S(1)}, u32[]{:S(2)}, u32[]{:S(2)}) collective-permute-start(bf16[64,768]{1,0:T(8,128)(2,1)S(1)} %get-tuple-element.29), channel_id=1, source_target_pairs={{0,2},{1,3},{2,0},{3,1},{4,6},{5,7},{6,4},{7,5},{8,10},{9,11},{10,... | collective-permute-start | bytes 294920 | tf_op jit(solution)/shard_map/ppermute | solution.py:309
  28.7 3.4 %collective-permute-start = (bf16[576,256]{1,0:T(8,128)(2,1)}, bf16[576,256]{1,0:T(8,128)(2,1)S(1)}, u32[]{:S(2)}, u32[]{:S(2)}) collective-permute-start(bf16[576,256]{1,0:T(8,128)(2,1)} %get-tuple-element.28), channel_id=1, source_target_pairs={{0,1},{1,2},{2,3},{3,0},{4,5},{5,6},{6,7},{7,4},{8,9},{9,10},{10,1... | collective-permute-start | bytes 884744 | tf_op jit(solution)/shard_map/ppermute | solution.py:309
  32.1 3.7 %collective-permute-start.2 = (bf16[576,256]{1,0:T(8,128)(2,1)S(1)}, bf16[576,256]{1,0:T(8,128)(2,1)S(1)}, u32[]{:S(2)}, u32[]{:S(2)}) collective-permute-start(bf16[576,256]{1,0:T(8,128)(2,1)S(1)} %get-tuple-element.30), channel_id=1, source_target_pairs={{0,3},{1,0},{2,1},{3,2},{4,7},{5,4},{6,5},{7,6},{8,11},{9,8},{10,9... | collective-permute-start | bytes 884744 | tf_op jit(solution)/shard_map/ppermute | solution.py:309
  35.8 1.0 copy-done.12
  36.8 2.6 %student_picks.1 = (bf16[2,512,256]{2,1,0:T(8,128)(2,1)}, bf16[2,512,768]{2,1,0:T(8,128)(2,1)}) custom-call(s32[5]{0:T(128)S(1)} %stack.35.place_ref.refs_0_, bf16[256,768]{1,0:T(8,128)(2,1)S(1)} %copy-done.12, bf16[384,256]{1,0:T(8,128)(2,1)} %collective-permute-done.3.refs_5_.refs_2_), custom_call_target="tpu_custom_call" | custom-call | flops 2000000000 | bytes 1000000 | tf_op jit(solution)/shard_map/student_picks/pallas_call | solution.py:380
  39.4 1.2 collective-permute-done.refs_2_
  40.6 0.7 collective-permute-done.2.refs_4_
  41.4 0.7 copy-done.14
  42.1 1.5 %student_rows.1 = (bf16[64,768]{1,0:T(8,128)(2,1)S(1)}, bf16[3,384,256]{2,1,0:T(8,128)(2,1)S(1)}, bf16[576,256]{1,0:T(8,128)(2,1)}, bf16[64,768]{1,0:T(8,128)(2,...) custom-call(bf16[64,768]{1,0:T(8,128)(2,1)S(1)} %dynamic-slice_bitca, ...), custom_call_target="tpu_custom_call", output_to_operand_aliasing={{2}: (2, {}), {3}: (3, {}), {4}: (4, {}), {5}: (5, {})} | custom-call | flops 1000000000 | bytes 1000000 | tf_op jit(solution)/shard_map/student_rows/pallas_call | solution.py:394
  43.9 1.9 %collective-permute-start.4 = (bf16[32,16,1024]{2,1,0:T(8,128)(2,1)S(1)}, bf16[32,16,1024]{2,1,0:T(8,128)(2,1)S(1)}, u32[]{:S(2)}, u32[]{:S(2)}) collective-permute-start(bf16[32,16,1024]{2,1,0:T(8,128)(2,1)S(1)} %all-to-all-done.own_ref), channel_id=1, source_target_pairs={{0,4},{4,0},{1,5},{5,1},{2,6},{6,2},{3,7},{7,3},{8,12},{12,8},{9,1... | collective-permute-start | bytes 3145736 | tf_op jit(solution)/shard_map/ppermute | solution.py:411
  45.9 2.4 %collective-permute-start.5 = (bf16[3,384,256]{2,1,0:T(8,128)(2,1)S(1)}, bf16[3,384,256]{2,1,0:T(8,128)(2,1)S(1)}, u32[]{:S(2)}, u32[]{:S(2)}) collective-permute-start(bf16[3,384,256]{2,1,0:T(8,128)(2,1)S(1)} %get-tuple-element.37.refs_2_), channel_id=1, source_target_pairs={{0,4},{4,0},{1,5},{5,1},{2,6},{6,2},{3,7},{7,3},{8,12},{12,8},{9,1... | collective-permute-start | bytes 1769480 | tf_op jit(solution)/shard_map/ppermute | solution.py:412
  48.9 3.8 %teacher.1 = bf16[4,64,1792]{2,1,0:T(8,128)(2,1)} custom-call(s32[5]{0:T(128)S(1)} %stack.35.place_ref.refs_0_, s32[2]{0:T(128)S(1)} %bitcast.26, bf16[256,1024]{1,0:T(8,128)(2,1)S(1)} %teacher_norm.1.normed_ref, bf16[32,16,1024]{2,1,0:T(8,128)(2,1)S(1)} %all-to-all-done.own_ref, bf16[32,16,1024]{2,1,0:T(8,128)(2,1)S(1)} %collective-permute-done.4.other_ref, ...), custom_call_target="tpu_custom_call" | custom-call | flops 5000000000 | bytes 1000000 | tf_op jit(solution)/shard_map/teacher/pallas_call | solution.py:423
  52.8 4.3 %all-to-all-start.1 = ((bf16[4,64,1792]{2,1,0:T(8,128)(2,1)}), bf16[4,64,1792]{2,1,0:T(8,128)(2,1)S(1)}, u32[]{:S(2)}, u32[]{:S(2)}) async-start(bf16[4,64,1792]{2,1,0:T(8,128)(2,1)} %teacher.1), calls=%async_computation.1 | async-start | bytes 1835008 | tf_op jit(solution)/shard_map/all_to_all | solution.py:437
  58.5 2.1 %projector.1.proj_ref.refs_5_ = bf16[4,256,768]{2,1,0:T(8,128)(2,1)} custom-call(s32[5]{0:T(128)S(1)} %stack.33.refs_0_.refs_1_, bf16[768,256]{1,0:T(8,128)(2,1)S(1)} %copy-done, bf16[3,384,256]{2,1,0:T(8,128)(2,1)S(1)} %get-tuple-element.37.refs_2_, bf16[3,384,256]{2,1,0:T(8,128)(2,1)S(1)} %collective-permute-done.5.refs_3_), custom_call_target="tpu_custom_call" | custom-call | flops 1000000000 | bytes 1000000 | tf_op jit(solution)/shard_map/projector/pallas_call | solution.py:442
  60.6 1.4 %copy-done.7 = bf16[4,256,768]{2,1,0:T(8,128)(2,1)S(1)} copy-done((bf16[4,256,768]{2,1,0:T(8,128)(2,1)S(1)}, bf16[4,256,768]{2,1,0:T(8,128)(2,1)}, u32[]{:S(2)}) %copy-start.7) | copy-done | bytes 1572888
  62.0 0.6 student_predict.1.refs_4_
  62.6 8.3 %all-to-all-done.1.refs_2_.refs_1_ = bf16[4,64,1792]{2,1,0:T(8,128)(2,1)S(1)} async-done(((bf16[4,64,1792]{2,1,0:T(8,128)(2,1)}), bf16[4,64,1792]{2,1,0:T(8,128)(2,1)S(1)}, u32[]{:S(2)}, u32[]{:S(2)}) %all-to-all-start.1) | async-done | bytes 917536 | tf_op jit(solution)/shard_map/all_to_all | solution.py:437
  71.0 1.8 %difference.1.refs_2_ = bf16[4,64,1152]{2,1,0:T(8,128)(2,1)} custom-call(s32[1]{0:T(128)S(6)} %copy.34.count_ref.refs_0_, s32[5]{0:T(128)S(1)} %stack.33.refs_0_.refs_1_, bf16[4,64,1792]{2,1,0:T(8,128)(2,1)S(1)} %all-to-all-done.1.refs_2_.refs_1_, bf16[64,1024]{1,0:T(8,128)(2,1)S(1)} %dynamic-slice_bitcast_fusion.refs_3_, ...), custom_call_target="tpu_custom_call" | custom-call | flops 2000000000 | bytes 1000000 | tf_op jit(solution)/shard_map/difference/pallas_call | solution.py:461
  72.7 3.5 %all-to-all-start.2 = ((bf16[4,64,1152]{2,1,0:T(8,128)(2,1)}), bf16[4,64,1152]{2,1,0:T(8,128)(2,1)S(1)}, u32[]{:S(2)}, u32[]{:S(2)}) async-start(bf16[4,64,1152]{2,1,0:T(8,128)(2,1)} %difference.1.refs_2_), calls=%async_computation.2 | async-start | bytes 1179648 | tf_op jit(solution)/shard_map/all_to_all | solution.py:479
  76.2 2.0 %student_extra.1.refs_1_ = bf16[2,3,512,256]{3,2,1,0:T(8,128)(2,1)S(1)} custom-call(s32[5]{0:T(128)S(1)} %stack.33.refs_0_.refs_1_, bf16[4,64,1792]{2,1,0:T(8,128)(2,1)S(1)} %all-to-all-done.1.refs_2_.refs_1_, bf16[4,64,1152]{2,1,0:T(8,128)(2,1)} %difference.1.refs_2_), custom_call_target="tpu_custom_call" | custom-call | flops 3000000000 | bytes 1000000 | tf_op jit(solution)/shard_map/student_extra/pallas_call | solution.py:470
  78.3 7.4 %all-to-all-done.2 = bf16[4,64,1152]{2,1,0:T(8,128)(2,1)S(1)} async-done(((bf16[4,64,1152]{2,1,0:T(8,128)(2,1)}), bf16[4,64,1152]{2,1,0:T(8,128)(2,1)S(1)}, u32[]{:S(2)}, u32[]{:S(2)}) %all-to-all-start.2) | async-done | bytes 589856 | tf_op jit(solution)/shard_map/all_to_all | solution.py:479
  85.7 4.4 %student_backward.1 = (bf16[512,768]{1,0:T(8,128)(2,1)S(1)}, bf16[512,768]{1,0:T(8,128)(2,1)S(1)}, f32[1,1]{1,0:T(1,128)}, bf16[192,768]{1,0:T(8,128)(2,1)}, bf1...) custom-call(bf16[256,1152]{1,0:T(8,128)(2,1)S(1)} %bitcast.21, ...), custom_call_target="tpu_custom_call", output_to_operand_aliasing={{3}: (2, {}), {4}: (3, {}), {5}: (4, {}), {6}: (5, {}), {7}... | custom-call | flops 4000000000 | bytes 1000000 | tf_op jit(solution)/shard_map/student_backward/pallas_call | solution.py:482
  90.1 1.9 %collective-permute-start.6 = (bf16[512,768]{1,0:T(8,128)(2,1)S(1)}, bf16[512,768]{1,0:T(8,128)(2,1)S(1)}, u32[]{:S(2)}, u32[]{:S(2)}) collective-permute-start(bf16[512,768]{1,0:T(8,128)(2,1)S(1)} %get-tuple-element.46), channel_id=1, source_target_pairs={{0,4},{4,0},{1,5},{5,1},{2,6},{6,2},{3,7},{7,3},{8,12},{12,8},{9,1... | collective-permute-start | bytes 2359304 | tf_op jit(solution)/shard_map/ppermute | solution.py:497
  92.0 2.3 %collective-permute-done.6 = bf16[512,768]{1,0:T(8,128)(2,1)S(1)} collective-permute-done((bf16[512,768]{1,0:T(8,128)(2,1)S(1)}, bf16[512,768]{1,0:T(8,128)(2,1)S(1)}, u32[]{:S(2)}, u32[]{:S(2)}) %collective-permute-start.6) | collective-permute-done | bytes 786464 | tf_op jit(solution)/shard_map/ppermute | solution.py:497
  94.5 35.1 %all_to_all.20.parts_ref = bf16[64,8,768]{2,1,0:T(8,128)(2,1)S(1)} all-to-all(bf16[64,8,768]{2,1,0:T(8,128)(2,1)S(1)} %fusion), channel_id=1, replica_groups=mesh['g'=2,'y'=4,'z'=8,'c'=2,'x'=4] {'g','y','z'}, dimensions={0} | all-to-all | bytes 1572864 | tf_op jit(solution)/shard_map/all_to_all | solution.py:499
  129.6 0.8 gradient_rows.1
  (41 shorter events, 1.9 us)
Async XLA Ops:
  1.4 15.1 %copy-start = (bf16[768,256]{1,0:T(8,128)(2,1)S(1)}, bf16[768,256]{1,0:T(8,128)(2,1)}, u32[]{:S(2)}) copy-start(bf16[768,256]{1,0:T(8,128)(2,1)} %refs_1_.1) | copy-start | bytes 1179652
  2.5 20.4 %copy-start.2 = (bf16[1,256,768]{2,1,0:T(8,128)(2,1)S(1)}, bf16[1,256,768]{2,1,0:T(8,128)(2,1)}, u32[]{:S(2)}) copy-start(bf16[1,256,768]{2,1,0:T(8,128)(2,1)} %param.14) | copy-start | bytes 1179652
  2.5 20.4 %copy-start.3 = (bf16[768,576]{0,1:T(8,128)(2,1)S(1)}, bf16[768,576]{0,1:T(8,128)(2,1)}, u32[]{:S(2)}) copy-start(bf16[768,576]{0,1:T(8,128)(2,1)} %param.17) | copy-start | bytes 2654212
  2.5 20.4 %copy-start.4 = (bf16[192,768]{1,0:T(8,128)(2,1)S(1)}, bf16[192,768]{1,0:T(8,128)(2,1)}, u32[]{:S(2)}) copy-start(bf16[192,768]{1,0:T(8,128)(2,1)} %out_ref.1) | copy-start | bytes 884740
  2.5 41.4 %all-to-all-start = ((bf16[32,16,1024]{2,1,0:T(8,128)(2,1)}), bf16[32,16,1024]{2,1,0:T(8,128)(2,1)S(1)}, u32[]{:S(2)}, u32[]{:S(2)}) async-start(bf16[32,16,1024]{2,1,0:T(8,128)(2,1)} %broadcast_in_dim.2), calls=%async_computation | async-start | bytes 2097152 | tf_op jit(solution)/shard_map/all_to_all | solution.py:348
  17.2 18.6 %collective-permute-start.3 = (bf16[384,256]{1,0:T(8,128)(2,1)}, bf16[384,256]{1,0:T(8,128)(2,1)}, u32[]{:S(2)}, u32[]{:S(2)}) collective-permute-start(bf16[384,256]{1,0:T(8,128)(2,1)} %constant_dynamic-slice_fusion.1), channel_id=1, source_target_pairs={{0,2},{1,3},{2,0},{3,1},{4,6},{5,7},{6,4},{7,5},{8,10},{9,11},{10,... | collective-permute-start | bytes 589832 | tf_op jit(solution)/shard_map/ppermute | solution.py:309
  26.3 13.1 %collective-permute-start.1 = (bf16[64,768]{1,0:T(8,128)(2,1)S(1)}, bf16[64,768]{1,0:T(8,128)(2,1)S(1)}, u32[]{:S(2)}, u32[]{:S(2)}) collective-permute-start(bf16[64,768]{1,0:T(8,128)(2,1)S(1)} %get-tuple-element.29), channel_id=1, source_target_pairs={{0,2},{1,3},{2,0},{3,1},{4,6},{5,7},{6,4},{7,5},{8,10},{9,11},{10,... | collective-permute-start | bytes 294920 | tf_op jit(solution)/shard_map/ppermute | solution.py:309
  28.7 11.9 %collective-permute-start = (bf16[576,256]{1,0:T(8,128)(2,1)}, bf16[576,256]{1,0:T(8,128)(2,1)S(1)}, u32[]{:S(2)}, u32[]{:S(2)}) collective-permute-start(bf16[576,256]{1,0:T(8,128)(2,1)} %get-tuple-element.28), channel_id=1, source_target_pairs={{0,1},{1,2},{2,3},{3,0},{4,5},{5,6},{6,7},{7,4},{8,9},{9,10},{10,1... | collective-permute-start | bytes 884744 | tf_op jit(solution)/shard_map/ppermute | solution.py:309
  32.1 9.2 %collective-permute-start.2 = (bf16[576,256]{1,0:T(8,128)(2,1)S(1)}, bf16[576,256]{1,0:T(8,128)(2,1)S(1)}, u32[]{:S(2)}, u32[]{:S(2)}) collective-permute-start(bf16[576,256]{1,0:T(8,128)(2,1)S(1)} %get-tuple-element.30), channel_id=1, source_target_pairs={{0,3},{1,0},{2,1},{3,2},{4,7},{5,4},{6,5},{7,6},{8,11},{9,8},{10,9... | collective-permute-start | bytes 884744 | tf_op jit(solution)/shard_map/ppermute | solution.py:309
  35.8 1.0 copy-start.12
  36.8 5.3 %copy-start.11 = (bf16[64,768]{1,0:T(8,128)(2,1)S(1)}, bf16[64,768]{1,0:T(8,128)(2,1)}, u32[]{:S(2)}) copy-start(bf16[64,768]{1,0:T(8,128)(2,1)} %get-tuple-element.27.refs_1_) | copy-start | bytes 294916
  39.4 2.7 %copy-start.15 = (bf16[64,768]{1,0:T(8,128)(2,1)}, bf16[64,768]{1,0:T(8,128)(2,1)S(1)}, u32[]{:S(2)}) copy-start(bf16[64,768]{1,0:T(8,128)(2,1)S(1)} %collective-permute-done.1.refs_3_) | copy-start | bytes 294916
  40.6 0.7 copy-start.13
  41.4 0.7 copy-start.14
  42.1 6.2 %copy-start.1 = (bf16[1,256,1024]{2,1,0:T(8,128)(2,1)S(1)}, bf16[1,256,1024]{2,1,0:T(8,128)(2,1)}, u32[]{:S(2)}) copy-start(bf16[1,256,1024]{2,1,0:T(8,128)(2,1)} %param.10) | copy-start | bytes 1572868
  42.1 6.2 %copy-start.5 = (f32[1024]{0:T(1024)S(1)}, f32[1024]{0:T(1024)}, u32[]{:S(2)}) copy-start(f32[1024]{0:T(1024)} %param.11) | copy-start | bytes 12292
  43.6 5.0 %copy-start.9 = (bf16[64,768]{1,0:T(8,128)(2,1)}, bf16[64,768]{1,0:T(8,128)(2,1)S(1)}, u32[]{:S(2)}) copy-start(bf16[64,768]{1,0:T(8,128)(2,1)S(1)} %get-tuple-element.35.after_ref.feat_ref) | copy-start | bytes 294916
  43.9 4.7 %collective-permute-start.4 = (bf16[32,16,1024]{2,1,0:T(8,128)(2,1)S(1)}, bf16[32,16,1024]{2,1,0:T(8,128)(2,1)S(1)}, u32[]{:S(2)}, u32[]{:S(2)}) collective-permute-start(bf16[32,16,1024]{2,1,0:T(8,128)(2,1)S(1)} %all-to-all-done.own_ref), channel_id=1, source_target_pairs={{0,4},{4,0},{1,5},{5,1},{2,6},{6,2},{3,7},{7,3},{8,12},{12,8},{9,1... | collective-permute-start | bytes 3145736 | tf_op jit(solution)/shard_map/ppermute | solution.py:411
  45.9 12.6 %collective-permute-start.5 = (bf16[3,384,256]{2,1,0:T(8,128)(2,1)S(1)}, bf16[3,384,256]{2,1,0:T(8,128)(2,1)S(1)}, u32[]{:S(2)}, u32[]{:S(2)}) collective-permute-start(bf16[3,384,256]{2,1,0:T(8,128)(2,1)S(1)} %get-tuple-element.37.refs_2_), channel_id=1, source_target_pairs={{0,4},{4,0},{1,5},{5,1},{2,6},{6,2},{3,7},{7,3},{8,12},{12,8},{9,1... | collective-permute-start | bytes 1769480 | tf_op jit(solution)/shard_map/ppermute | solution.py:412
  48.3 0.7 copy-start.6
  52.8 18.2 %all-to-all-start.1 = ((bf16[4,64,1792]{2,1,0:T(8,128)(2,1)}), bf16[4,64,1792]{2,1,0:T(8,128)(2,1)S(1)}, u32[]{:S(2)}, u32[]{:S(2)}) async-start(bf16[4,64,1792]{2,1,0:T(8,128)(2,1)} %teacher.1), calls=%async_computation.1 | async-start | bytes 1835008 | tf_op jit(solution)/shard_map/all_to_all | solution.py:437
  58.4 2.2 %copy-start.10 = (bf16[64,768]{1,0:T(8,128)(2,1)S(1)}, bf16[64,768]{1,0:T(8,128)(2,1)}, u32[]{:S(2)}) copy-start(bf16[64,768]{1,0:T(8,128)(2,1)} %copy-done.9) | copy-start | bytes 294916
  60.6 1.4 %copy-start.7 = (bf16[4,256,768]{2,1,0:T(8,128)(2,1)S(1)}, bf16[4,256,768]{2,1,0:T(8,128)(2,1)}, u32[]{:S(2)}) copy-start(bf16[4,256,768]{2,1,0:T(8,128)(2,1)} %projector.1.proj_ref.refs_5_) | copy-start | bytes 4718596
  62.0 8.9 %copy-start.8 = (bf16[4,256,768]{2,1,0:T(8,128)(2,1)S(1)}, bf16[4,256,768]{2,1,0:T(8,128)(2,1)}, u32[]{:S(2)}) copy-start(bf16[4,256,768]{2,1,0:T(8,128)(2,1)} %projector.1.proj_ref.refs_5_) | copy-start | bytes 4718596
  72.7 12.9 %all-to-all-start.2 = ((bf16[4,64,1152]{2,1,0:T(8,128)(2,1)}), bf16[4,64,1152]{2,1,0:T(8,128)(2,1)S(1)}, u32[]{:S(2)}, u32[]{:S(2)}) async-start(bf16[4,64,1152]{2,1,0:T(8,128)(2,1)} %difference.1.refs_2_), calls=%async_computation.2 | async-start | bytes 1179648 | tf_op jit(solution)/shard_map/all_to_all | solution.py:479
  90.1 4.2 %collective-permute-start.6 = (bf16[512,768]{1,0:T(8,128)(2,1)S(1)}, bf16[512,768]{1,0:T(8,128)(2,1)S(1)}, u32[]{:S(2)}, u32[]{:S(2)}) collective-permute-start(bf16[512,768]{1,0:T(8,128)(2,1)S(1)} %get-tuple-element.46), channel_id=1, source_target_pairs={{0,4},{4,0},{1,5},{5,1},{2,6},{6,2},{3,7},{7,3},{8,12},{12,8},{9,1... | collective-permute-start | bytes 2359304 | tf_op jit(solution)/shard_map/ppermute | solution.py:497

commit v11 on v10

--- a/solution.py
+++ b/solution.py
@@ -66,13 +66,12 @@
 
 def split_head(packed, head):
     first = head * 3 * HEAD
-    return [packed[:, first + i * HEAD : first + (i + 1) * HEAD].astype(BF16) for i in range(3)]
-
-
-def softmax(scores):
-    top = jnp.max(scores, -1, keepdims=True)
-    weights = jnp.exp(scores - top)
-    return weights / jnp.sum(weights, -1, keepdims=True)
+    return [packed[:, first + i * HEAD : first + (i + 1) * HEAD] for i in range(3)]
+
+
+def exponentials(scores):
+    weights = jnp.exp(scores - jnp.max(scores, -1, keepdims=True))
+    return weights, 1.0 / jnp.sum(weights, -1, keepdims=True)
 
 
 def pick_rows(rows, shares, columns, core, extra):
@@ -107,14 +106,15 @@
     heads = out_ref.shape[0] // HEAD
     normed = norm_rows(events_ref[...]).astype(BF16)
     normed_ref[...] = normed
-    packed = nt(normed, qkv_ref[...])
-    packed_ref[...] = packed.astype(BF16)
+    packed = nt(normed, qkv_ref[...]).astype(BF16)
+    packed_ref[...] = packed
     usable = lax.broadcasted_iota(jnp.int32, (length, length), 1) < count_ref[0]
     mixed = []
     for head in range(heads):
         query, keys, values = split_head(packed, head)
         scores = jnp.where(usable, nt(query, keys) * HEAD ** (-0.5), -1e30)
-        weights = softmax(scores).astype(BF16)
+        weights, share = exponentials(scores)
+        weights = (weights * share).astype(BF16)
         weights_ref[head] = weights
         mixed.append(nn(weights, values))
     mixed = jnp.concatenate(mixed, axis=1).astype(BF16)
@@ -167,12 +167,12 @@
         for b in range(blocks):
             full_ref[pl.ds(pl.multiple_of((2 * b + core) * rows, rows), rows), :] = piece[b]
     heads = width // (4 * HEAD)
-    packed = nn(normed_ref[...], full_ref[:, : heads * 3 * HEAD])
+    packed = nn(normed_ref[...], full_ref[:, : heads * 3 * HEAD]).astype(BF16)
     mixed = []
     for head in range(heads):
         query, keys, values = split_head(packed, head)
-        weights = softmax(nt(query, keys) * HEAD ** (-0.5))
-        mixed.append(nn(weights.astype(BF16), values))
+        weights, share = exponentials(nt(query, keys) * HEAD ** (-0.5))
+        mixed.append(nn(weights.astype(BF16), values) * share)
     mixed_ref[...] = jnp.concatenate(mixed, axis=1)
     ways, shared = part_ref.shape[:2]
     outputs = full_ref.shape[0]
@@ -256,7 +256,6 @@
     sources, (keep_ref, send_ref, loss_ref) = refs[:held], refs[held : held + 3]
     copies = fetch(sources, refs[2 * held + 3 : -1], refs[-1])
     out_ref, packed_ref, weights_ref, mixed_ref, normed_ref, pick_ref = refs[2 * held + 3 : -1]
-    copies[0].wait()
     features = out_ref.shape[1]
     heads = out_ref.shape[0] // HEAD
     dfeat = back_ref[:, :features]
@@ -264,31 +263,30 @@
     dpred = back_ref[:, features : features + columns]
     tail = back_ref[:, features + columns :].astype(F32)
     loss_ref[...] = jnp.sum(jnp.sum(tail, 0, keepdims=True), 1, keepdims=True)
-    dmixed = nt(dfeat, out_ref[...])
+    copies[0].wait()
+    dmixed = nt(dfeat, out_ref[...]).astype(BF16)
     for copy in copies[1:3]:
         copy.wait()
-    packed = packed_ref[...].astype(F32)
+    packed = packed_ref[...]
     pieces = []
     for head in range(heads):
         query, keys, values = split_head(packed, head)
         rounded = weights_ref[head]
         weights = rounded.astype(F32)
-        cot = dmixed[:, head * HEAD : (head + 1) * HEAD].astype(BF16)
+        cot = dmixed[:, head * HEAD : (head + 1) * HEAD]
         dvalues = tn(rounded, cot)
         dweights = nt(cot, values)
         inner = jnp.sum(dweights * weights, -1, keepdims=True)
         dscores = (weights * (dweights - inner) * HEAD ** (-0.5)).astype(BF16)
-        pieces += [nn(dscores, keys), tn(dscores, query), dvalues]
+        pieces += [piece.astype(BF16) for piece in (nn(dscores, keys), tn(dscores, query), dvalues)]
     dpacked = jnp.concatenate(pieces, axis=1)
     used = dpacked.shape[1]
     length = dpacked.shape[0]
-    right = jnp.concatenate([dpacked, jnp.zeros((length, features - used), F32)], 1).astype(BF16)
+    right = jnp.concatenate([dpacked, jnp.zeros((length, features - used), BF16)], 1)
     for copy in copies[3:]:
         copy.wait()
     tailed = features - columns
-    mixed = jnp.concatenate(
-        [jnp.zeros((length, used - tailed), F32), mixed_ref[...].astype(F32)], 1
-    ).astype(BF16)
+    mixed = jnp.concatenate([jnp.zeros((length, used - tailed), BF16), mixed_ref[...]], 1)
     for half, into in enumerate((keep_ref, send_ref)):
         dfeat_rows = nt(pick_ref[half], dfeat).astype(BF16)
         normed_rows = normed_ref[half]

time: 131 us -> 131 us (level)
  transfers between devices with their start and end apart: 10 -> 10, of which waited for: 6 -> 6; matrix products, arithmetic and copies ran while one was open for 1% -> 1% of each run, Pallas kernels for 13% -> 12%
where the time goes in v11:
time: 131 us; the launch traced here: 130 us
  starting transfers between devices  42.4 us (32%)
  blocking collectives  35.2 us (27%)
  Pallas kernels  23.2 us (18%)
  waiting for transfers between devices  20.2 us (15%)
  local copies, waits for them, and re-layouts  5.42 us (4%)
  between operations  2.22 us (2%)
  other arithmetic  1.52 us (1%)
    all_to_all x1, blocking collectives, on_device(): lax.all_to_all(total.reshape(chips, total.shape[0] // chips, features), C...  35.2 us
    ppermute x4, starting transfers between devices, from_peers(): lax.ppermute(rows(k), axis, [(i, (i + k) % ways) for i in range(ways)])  14.4 us
    all_to_all x1, starting transfers between devices, on_device(): own_core = lax.all_to_all(shard, ('y', 'z'), 0, 0)  14 us
    all_to_all x1, waiting for transfers between devices, on_device(): teacher_parts = lax.all_to_all(teacher_part, 'x', 0, 0)  8.35 us
    all_to_all x1, waiting for transfers between devices, on_device(): lax.all_to_all(message, 'x', 0, 0)  7.4 us
    pallas_call x1, Pallas kernels, on_device(): pl.pallas_call(lambda *refs: backward_kernel(len(held), *refs), out_shape...  4.43 us
    all_to_all x1, starting transfers between devices, on_device(): teacher_parts = lax.all_to_all(teacher_part, 'x', 0, 0)  4.29 us
    pallas_call x1, Pallas kernels, on_device(): pl.pallas_call(teacher_kernel, out_shape=shape((ways, rows, width + featu...  3.56 us
  transfers between devices with their start and end apart: 10, of which 6 were waited for; matrix products, arithmetic and copies ran while one was open for 1% of the time, Pallas kernels for 12%

profile of v11, /device:TPU:16, one launch (start us, length us, event | category | flops | bytes accessed | tf_op | source)
XLA Modules:
  0.0 130.1 jit_solution(9822928011052643580)
XLA Ops:
  0.6 0.8 pad_maximum_fusion
  1.4 1.1 broadcast_in_dim.2
  2.5 14.0 %all-to-all-start = ((bf16[32,16,1024]{2,1,0:T(8,128)(2,1)}), bf16[32,16,1024]{2,1,0:T(8,128)(2,1)S(1)}, u32[]{:S(2)}, u32[]{:S(2)}) async-start(bf16[32,16,1024]{2,1,0:T(8,128)(2,1)} %broadcast_in_dim.2), calls=%async_computation | async-start | bytes 2097152 | tf_op jit(solution)/shard_map/all_to_all | solution.py:346
  16.5 0.7 constant_dynamic-slice_fusion.1
  17.2 4.9 %collective-permute-start.3 = (bf16[384,256]{1,0:T(8,128)(2,1)}, bf16[384,256]{1,0:T(8,128)(2,1)}, u32[]{:S(2)}, u32[]{:S(2)}) collective-permute-start(bf16[384,256]{1,0:T(8,128)(2,1)} %constant_dynamic-slice_fusion.1), channel_id=1, source_target_pairs={{0,2},{1,3},{2,0},{3,1},{4,6},{5,7},{6,4},{7,5},{8,10},{9,11},{10,... | collective-permute-start | bytes 589832 | tf_op jit(solution)/shard_map/ppermute | solution.py:307
  22.9 3.4 %student_forward.1 = (bf16[64,768]{1,0:T(8,128)(2,1)}, bf16[576,256]{1,0:T(8,128)(2,1)}, bf16[64,768]{1,0:T(8,128)(2,1)S(1)}, bf16[576,256]{1,0:T(8,128)(2,1)S(1...) custom-call(s32[1]{0:T(128)S(6)} %copy.34.count_ref.refs_0_, ...), custom_call_target="tpu_custom_call" | custom-call | flops 4000000000 | bytes 1000000 | tf_op jit(solution)/shard_map/student_forward/pallas_call | solution.py:355
  26.3 2.4 %collective-permute-start.1 = (bf16[64,768]{1,0:T(8,128)(2,1)S(1)}, bf16[64,768]{1,0:T(8,128)(2,1)S(1)}, u32[]{:S(2)}, u32[]{:S(2)}) collective-permute-start(bf16[64,768]{1,0:T(8,128)(2,1)S(1)} %get-tuple-element.29), channel_id=1, source_target_pairs={{0,2},{1,3},{2,0},{3,1},{4,6},{5,7},{6,4},{7,5},{8,10},{9,11},{10,... | collective-permute-start | bytes 294920 | tf_op jit(solution)/shard_map/ppermute | solution.py:307
  28.7 3.4 %collective-permute-start = (bf16[576,256]{1,0:T(8,128)(2,1)}, bf16[576,256]{1,0:T(8,128)(2,1)S(1)}, u32[]{:S(2)}, u32[]{:S(2)}) collective-permute-start(bf16[576,256]{1,0:T(8,128)(2,1)} %get-tuple-element.28), channel_id=1, source_target_pairs={{0,1},{1,2},{2,3},{3,0},{4,5},{5,6},{6,7},{7,4},{8,9},{9,10},{10,1... | collective-permute-start | bytes 884744 | tf_op jit(solution)/shard_map/ppermute | solution.py:307
  32.1 3.7 %collective-permute-start.2 = (bf16[576,256]{1,0:T(8,128)(2,1)S(1)}, bf16[576,256]{1,0:T(8,128)(2,1)S(1)}, u32[]{:S(2)}, u32[]{:S(2)}) collective-permute-start(bf16[576,256]{1,0:T(8,128)(2,1)S(1)} %get-tuple-element.30), channel_id=1, source_target_pairs={{0,3},{1,0},{2,1},{3,2},{4,7},{5,4},{6,5},{7,6},{8,11},{9,8},{10,9... | collective-permute-start | bytes 884744 | tf_op jit(solution)/shard_map/ppermute | solution.py:307
  35.8 1.0 copy-done.12
  36.8 2.6 %student_picks.1 = (bf16[2,512,256]{2,1,0:T(8,128)(2,1)}, bf16[2,512,768]{2,1,0:T(8,128)(2,1)}) custom-call(s32[5]{0:T(128)S(1)} %stack.35.place_ref.refs_0_, bf16[256,768]{1,0:T(8,128)(2,1)S(1)} %copy-done.12, bf16[384,256]{1,0:T(8,128)(2,1)} %collective-permute-done.3.refs_5_.refs_2_), custom_call_target="tpu_custom_call" | custom-call | flops 2000000000 | bytes 1000000 | tf_op jit(solution)/shard_map/student_picks/pallas_call | solution.py:378
  39.4 1.2 collective-permute-done.refs_2_
  40.6 0.7 collective-permute-done.2.refs_4_
  41.4 0.7 copy-done.14
  42.1 1.5 %student_rows.1 = (bf16[64,768]{1,0:T(8,128)(2,1)S(1)}, bf16[3,384,256]{2,1,0:T(8,128)(2,1)S(1)}, bf16[576,256]{1,0:T(8,128)(2,1)}, bf16[64,768]{1,0:T(8,128)(2,...) custom-call(bf16[64,768]{1,0:T(8,128)(2,1)S(1)} %dynamic-slice_bitca, ...), custom_call_target="tpu_custom_call", output_to_operand_aliasing={{2}: (2, {}), {3}: (3, {}), {4}: (4, {}), {5}: (5, {})} | custom-call | flops 1000000000 | bytes 1000000 | tf_op jit(solution)/shard_map/student_rows/pallas_call | solution.py:392
  43.9 1.9 %collective-permute-start.4 = (bf16[32,16,1024]{2,1,0:T(8,128)(2,1)S(1)}, bf16[32,16,1024]{2,1,0:T(8,128)(2,1)S(1)}, u32[]{:S(2)}, u32[]{:S(2)}) collective-permute-start(bf16[32,16,1024]{2,1,0:T(8,128)(2,1)S(1)} %all-to-all-done.own_ref), channel_id=1, source_target_pairs={{0,4},{4,0},{1,5},{5,1},{2,6},{6,2},{3,7},{7,3},{8,12},{12,8},{9,1... | collective-permute-start | bytes 3145736 | tf_op jit(solution)/shard_map/ppermute | solution.py:409
  45.9 2.4 %collective-permute-start.5 = (bf16[3,384,256]{2,1,0:T(8,128)(2,1)S(1)}, bf16[3,384,256]{2,1,0:T(8,128)(2,1)S(1)}, u32[]{:S(2)}, u32[]{:S(2)}) collective-permute-start(bf16[3,384,256]{2,1,0:T(8,128)(2,1)S(1)} %get-tuple-element.37.refs_2_), channel_id=1, source_target_pairs={{0,4},{4,0},{1,5},{5,1},{2,6},{6,2},{3,7},{7,3},{8,12},{12,8},{9,1... | collective-permute-start | bytes 1769480 | tf_op jit(solution)/shard_map/ppermute | solution.py:410
  48.9 3.6 %teacher.1 = bf16[4,64,1792]{2,1,0:T(8,128)(2,1)} custom-call(s32[5]{0:T(128)S(1)} %stack.35.place_ref.refs_0_, s32[2]{0:T(128)S(1)} %bitcast.26, bf16[256,1024]{1,0:T(8,128)(2,1)S(1)} %teacher_norm.1.normed_ref, bf16[32,16,1024]{2,1,0:T(8,128)(2,1)S(1)} %all-to-all-done.own_ref, bf16[32,16,1024]{2,1,0:T(8,128)(2,1)S(1)} %collective-permute-done.4.other_ref, ...), custom_call_target="tpu_custom_call" | custom-call | flops 5000000000 | bytes 1000000 | tf_op jit(solution)/shard_map/teacher/pallas_call | solution.py:421
  52.5 4.3 %all-to-all-start.1 = ((bf16[4,64,1792]{2,1,0:T(8,128)(2,1)}), bf16[4,64,1792]{2,1,0:T(8,128)(2,1)S(1)}, u32[]{:S(2)}, u32[]{:S(2)}) async-start(bf16[4,64,1792]{2,1,0:T(8,128)(2,1)} %teacher.1), calls=%async_computation.1 | async-start | bytes 1835008 | tf_op jit(solution)/shard_map/all_to_all | solution.py:435
  58.2 2.1 %projector.1.proj_ref.refs_5_ = bf16[4,256,768]{2,1,0:T(8,128)(2,1)} custom-call(s32[5]{0:T(128)S(1)} %stack.33.refs_0_.refs_1_, bf16[768,256]{1,0:T(8,128)(2,1)S(1)} %copy-done, bf16[3,384,256]{2,1,0:T(8,128)(2,1)S(1)} %get-tuple-element.37.refs_2_, bf16[3,384,256]{2,1,0:T(8,128)(2,1)S(1)} %collective-permute-done.5.refs_3_), custom_call_target="tpu_custom_call" | custom-call | flops 1000000000 | bytes 1000000 | tf_op jit(solution)/shard_map/projector/pallas_call | solution.py:440
  60.3 1.4 %copy-done.7 = bf16[4,256,768]{2,1,0:T(8,128)(2,1)S(1)} copy-done((bf16[4,256,768]{2,1,0:T(8,128)(2,1)S(1)}, bf16[4,256,768]{2,1,0:T(8,128)(2,1)}, u32[]{:S(2)}) %copy-start.7) | copy-done | bytes 1572888
  61.7 0.6 student_predict.1.refs_4_
  62.3 8.3 %all-to-all-done.1.refs_2_.refs_1_ = bf16[4,64,1792]{2,1,0:T(8,128)(2,1)S(1)} async-done(((bf16[4,64,1792]{2,1,0:T(8,128)(2,1)}), bf16[4,64,1792]{2,1,0:T(8,128)(2,1)S(1)}, u32[]{:S(2)}, u32[]{:S(2)}) %all-to-all-start.1) | async-done | bytes 917536 | tf_op jit(solution)/shard_map/all_to_all | solution.py:435
  70.7 1.8 %difference.1.refs_2_ = bf16[4,64,1152]{2,1,0:T(8,128)(2,1)} custom-call(s32[1]{0:T(128)S(6)} %copy.34.count_ref.refs_0_, s32[5]{0:T(128)S(1)} %stack.33.refs_0_.refs_1_, bf16[4,64,1792]{2,1,0:T(8,128)(2,1)S(1)} %all-to-all-done.1.refs_2_.refs_1_, bf16[64,1024]{1,0:T(8,128)(2,1)S(1)} %dynamic-slice_bitcast_fusion.refs_3_, ...), custom_call_target="tpu_custom_call" | custom-call | flops 2000000000 | bytes 1000000 | tf_op jit(solution)/shard_map/difference/pallas_call | solution.py:459
  72.4 3.5 %all-to-all-start.2 = ((bf16[4,64,1152]{2,1,0:T(8,128)(2,1)}), bf16[4,64,1152]{2,1,0:T(8,128)(2,1)S(1)}, u32[]{:S(2)}, u32[]{:S(2)}) async-start(bf16[4,64,1152]{2,1,0:T(8,128)(2,1)} %difference.1.refs_2_), calls=%async_computation.2 | async-start | bytes 1179648 | tf_op jit(solution)/shard_map/all_to_all | solution.py:477
  75.9 2.0 %student_extra.1.refs_1_ = bf16[2,3,512,256]{3,2,1,0:T(8,128)(2,1)S(1)} custom-call(s32[5]{0:T(128)S(1)} %stack.33.refs_0_.refs_1_, bf16[4,64,1792]{2,1,0:T(8,128)(2,1)S(1)} %all-to-all-done.1.refs_2_.refs_1_, bf16[4,64,1152]{2,1,0:T(8,128)(2,1)} %difference.1.refs_2_), custom_call_target="tpu_custom_call" | custom-call | flops 3000000000 | bytes 1000000 | tf_op jit(solution)/shard_map/student_extra/pallas_call | solution.py:468
  78.0 7.4 %all-to-all-done.2 = bf16[4,64,1152]{2,1,0:T(8,128)(2,1)S(1)} async-done(((bf16[4,64,1152]{2,1,0:T(8,128)(2,1)}), bf16[4,64,1152]{2,1,0:T(8,128)(2,1)S(1)}, u32[]{:S(2)}, u32[]{:S(2)}) %all-to-all-start.2) | async-done | bytes 589856 | tf_op jit(solution)/shard_map/all_to_all | solution.py:477
  85.4 4.4 %student_backward.1 = (bf16[512,768]{1,0:T(8,128)(2,1)S(1)}, bf16[512,768]{1,0:T(8,128)(2,1)S(1)}, f32[1,1]{1,0:T(1,128)}, bf16[192,768]{1,0:T(8,128)(2,1)}, bf1...) custom-call(bf16[256,1152]{1,0:T(8,128)(2,1)S(1)} %bitcast.21, ...), custom_call_target="tpu_custom_call", output_to_operand_aliasing={{3}: (2, {}), {4}: (3, {}), {5}: (4, {}), {6}: (5, {}), {7}... | custom-call | flops 4000000000 | bytes 1000000 | tf_op jit(solution)/shard_map/student_backward/pallas_call | solution.py:480
  89.8 1.9 %collective-permute-start.6 = (bf16[512,768]{1,0:T(8,128)(2,1)S(1)}, bf16[512,768]{1,0:T(8,128)(2,1)S(1)}, u32[]{:S(2)}, u32[]{:S(2)}) collective-permute-start(bf16[512,768]{1,0:T(8,128)(2,1)S(1)} %get-tuple-element.46), channel_id=1, source_target_pairs={{0,4},{4,0},{1,5},{5,1},{2,6},{6,2},{3,7},{7,3},{8,12},{12,8},{9,1... | collective-permute-start | bytes 2359304 | tf_op jit(solution)/shard_map/ppermute | solution.py:495
  91.7 2.3 %collective-permute-done.6 = bf16[512,768]{1,0:T(8,128)(2,1)S(1)} collective-permute-done((bf16[512,768]{1,0:T(8,128)(2,1)S(1)}, bf16[512,768]{1,0:T(8,128)(2,1)S(1)}, u32[]{:S(2)}, u32[]{:S(2)}) %collective-permute-start.6) | collective-permute-done | bytes 786464 | tf_op jit(solution)/shard_map/ppermute | solution.py:495
  94.2 35.2 %all_to_all.20.parts_ref = bf16[64,8,768]{2,1,0:T(8,128)(2,1)S(1)} all-to-all(bf16[64,8,768]{2,1,0:T(8,128)(2,1)S(1)} %fusion), channel_id=1, replica_groups=mesh['g'=2,'y'=4,'z'=8,'c'=2,'x'=4] {'g','y','z'}, dimensions={0} | all-to-all | bytes 1572864 | tf_op jit(solution)/shard_map/all_to_all | solution.py:497
  129.3 0.8 gradient_rows.1
  (41 shorter events, 1.9 us)
Async XLA Ops:
  1.4 15.1 %copy-start = (bf16[768,256]{1,0:T(8,128)(2,1)S(1)}, bf16[768,256]{1,0:T(8,128)(2,1)}, u32[]{:S(2)}) copy-start(bf16[768,256]{1,0:T(8,128)(2,1)} %refs_1_.1) | copy-start | bytes 1179652
  2.5 20.4 %copy-start.2 = (bf16[1,256,768]{2,1,0:T(8,128)(2,1)S(1)}, bf16[1,256,768]{2,1,0:T(8,128)(2,1)}, u32[]{:S(2)}) copy-start(bf16[1,256,768]{2,1,0:T(8,128)(2,1)} %param.14) | copy-start | bytes 1179652
  2.5 20.4 %copy-start.3 = (bf16[768,576]{0,1:T(8,128)(2,1)S(1)}, bf16[768,576]{0,1:T(8,128)(2,1)}, u32[]{:S(2)}) copy-start(bf16[768,576]{0,1:T(8,128)(2,1)} %param.17) | copy-start | bytes 2654212
  2.5 20.4 %copy-start.4 = (bf16[192,768]{1,0:T(8,128)(2,1)S(1)}, bf16[192,768]{1,0:T(8,128)(2,1)}, u32[]{:S(2)}) copy-start(bf16[192,768]{1,0:T(8,128)(2,1)} %out_ref.1) | copy-start | bytes 884740
  2.5 41.4 %all-to-all-start = ((bf16[32,16,1024]{2,1,0:T(8,128)(2,1)}), bf16[32,16,1024]{2,1,0:T(8,128)(2,1)S(1)}, u32[]{:S(2)}, u32[]{:S(2)}) async-start(bf16[32,16,1024]{2,1,0:T(8,128)(2,1)} %broadcast_in_dim.2), calls=%async_computation | async-start | bytes 2097152 | tf_op jit(solution)/shard_map/all_to_all | solution.py:346
  17.2 18.6 %collective-permute-start.3 = (bf16[384,256]{1,0:T(8,128)(2,1)}, bf16[384,256]{1,0:T(8,128)(2,1)}, u32[]{:S(2)}, u32[]{:S(2)}) collective-permute-start(bf16[384,256]{1,0:T(8,128)(2,1)} %constant_dynamic-slice_fusion.1), channel_id=1, source_target_pairs={{0,2},{1,3},{2,0},{3,1},{4,6},{5,7},{6,4},{7,5},{8,10},{9,11},{10,... | collective-permute-start | bytes 589832 | tf_op jit(solution)/shard_map/ppermute | solution.py:307
  26.3 13.1 %collective-permute-start.1 = (bf16[64,768]{1,0:T(8,128)(2,1)S(1)}, bf16[64,768]{1,0:T(8,128)(2,1)S(1)}, u32[]{:S(2)}, u32[]{:S(2)}) collective-permute-start(bf16[64,768]{1,0:T(8,128)(2,1)S(1)} %get-tuple-element.29), channel_id=1, source_target_pairs={{0,2},{1,3},{2,0},{3,1},{4,6},{5,7},{6,4},{7,5},{8,10},{9,11},{10,... | collective-permute-start | bytes 294920 | tf_op jit(solution)/shard_map/ppermute | solution.py:307
  28.7 11.9 %collective-permute-start = (bf16[576,256]{1,0:T(8,128)(2,1)}, bf16[576,256]{1,0:T(8,128)(2,1)S(1)}, u32[]{:S(2)}, u32[]{:S(2)}) collective-permute-start(bf16[576,256]{1,0:T(8,128)(2,1)} %get-tuple-element.28), channel_id=1, source_target_pairs={{0,1},{1,2},{2,3},{3,0},{4,5},{5,6},{6,7},{7,4},{8,9},{9,10},{10,1... | collective-permute-start | bytes 884744 | tf_op jit(solution)/shard_map/ppermute | solution.py:307
  32.1 9.2 %collective-permute-start.2 = (bf16[576,256]{1,0:T(8,128)(2,1)S(1)}, bf16[576,256]{1,0:T(8,128)(2,1)S(1)}, u32[]{:S(2)}, u32[]{:S(2)}) collective-permute-start(bf16[576,256]{1,0:T(8,128)(2,1)S(1)} %get-tuple-element.30), channel_id=1, source_target_pairs={{0,3},{1,0},{2,1},{3,2},{4,7},{5,4},{6,5},{7,6},{8,11},{9,8},{10,9... | collective-permute-start | bytes 884744 | tf_op jit(solution)/shard_map/ppermute | solution.py:307
  35.8 1.0 copy-start.12
  36.8 5.3 %copy-start.11 = (bf16[64,768]{1,0:T(8,128)(2,1)S(1)}, bf16[64,768]{1,0:T(8,128)(2,1)}, u32[]{:S(2)}) copy-start(bf16[64,768]{1,0:T(8,128)(2,1)} %get-tuple-element.27.refs_1_) | copy-start | bytes 294916
  39.4 2.7 %copy-start.15 = (bf16[64,768]{1,0:T(8,128)(2,1)}, bf16[64,768]{1,0:T(8,128)(2,1)S(1)}, u32[]{:S(2)}) copy-start(bf16[64,768]{1,0:T(8,128)(2,1)S(1)} %collective-permute-done.1.refs_3_) | copy-start | bytes 294916
  40.6 0.7 copy-start.13
  41.4 0.7 copy-start.14
  42.1 6.2 %copy-start.1 = (bf16[1,256,1024]{2,1,0:T(8,128)(2,1)S(1)}, bf16[1,256,1024]{2,1,0:T(8,128)(2,1)}, u32[]{:S(2)}) copy-start(bf16[1,256,1024]{2,1,0:T(8,128)(2,1)} %param.10) | copy-start | bytes 1572868
  42.1 6.2 %copy-start.5 = (f32[1024]{0:T(1024)S(1)}, f32[1024]{0:T(1024)}, u32[]{:S(2)}) copy-start(f32[1024]{0:T(1024)} %param.11) | copy-start | bytes 12292
  43.6 5.0 %copy-start.9 = (bf16[64,768]{1,0:T(8,128)(2,1)}, bf16[64,768]{1,0:T(8,128)(2,1)S(1)}, u32[]{:S(2)}) copy-start(bf16[64,768]{1,0:T(8,128)(2,1)S(1)} %get-tuple-element.35.after_ref.feat_ref) | copy-start | bytes 294916
  43.9 4.7 %collective-permute-start.4 = (bf16[32,16,1024]{2,1,0:T(8,128)(2,1)S(1)}, bf16[32,16,1024]{2,1,0:T(8,128)(2,1)S(1)}, u32[]{:S(2)}, u32[]{:S(2)}) collective-permute-start(bf16[32,16,1024]{2,1,0:T(8,128)(2,1)S(1)} %all-to-all-done.own_ref), channel_id=1, source_target_pairs={{0,4},{4,0},{1,5},{5,1},{2,6},{6,2},{3,7},{7,3},{8,12},{12,8},{9,1... | collective-permute-start | bytes 3145736 | tf_op jit(solution)/shard_map/ppermute | solution.py:409
  45.9 12.3 %collective-permute-start.5 = (bf16[3,384,256]{2,1,0:T(8,128)(2,1)S(1)}, bf16[3,384,256]{2,1,0:T(8,128)(2,1)S(1)}, u32[]{:S(2)}, u32[]{:S(2)}) collective-permute-start(bf16[3,384,256]{2,1,0:T(8,128)(2,1)S(1)} %get-tuple-element.37.refs_2_), channel_id=1, source_target_pairs={{0,4},{4,0},{1,5},{5,1},{2,6},{6,2},{3,7},{7,3},{8,12},{12,8},{9,1... | collective-permute-start | bytes 1769480 | tf_op jit(solution)/shard_map/ppermute | solution.py:410
  48.3 0.7 copy-start.6
  52.5 18.2 %all-to-all-start.1 = ((bf16[4,64,1792]{2,1,0:T(8,128)(2,1)}), bf16[4,64,1792]{2,1,0:T(8,128)(2,1)S(1)}, u32[]{:S(2)}, u32[]{:S(2)}) async-start(bf16[4,64,1792]{2,1,0:T(8,128)(2,1)} %teacher.1), calls=%async_computation.1 | async-start | bytes 1835008 | tf_op jit(solution)/shard_map/all_to_all | solution.py:435
  58.1 2.2 %copy-start.10 = (bf16[64,768]{1,0:T(8,128)(2,1)S(1)}, bf16[64,768]{1,0:T(8,128)(2,1)}, u32[]{:S(2)}) copy-start(bf16[64,768]{1,0:T(8,128)(2,1)} %copy-done.9) | copy-start | bytes 294916
  60.3 1.4 %copy-start.7 = (bf16[4,256,768]{2,1,0:T(8,128)(2,1)S(1)}, bf16[4,256,768]{2,1,0:T(8,128)(2,1)}, u32[]{:S(2)}) copy-start(bf16[4,256,768]{2,1,0:T(8,128)(2,1)} %projector.1.proj_ref.refs_5_) | copy-start | bytes 4718596
  61.7 8.9 %copy-start.8 = (bf16[4,256,768]{2,1,0:T(8,128)(2,1)S(1)}, bf16[4,256,768]{2,1,0:T(8,128)(2,1)}, u32[]{:S(2)}) copy-start(bf16[4,256,768]{2,1,0:T(8,128)(2,1)} %projector.1.proj_ref.refs_5_) | copy-start | bytes 4718596
  72.4 12.9 %all-to-all-start.2 = ((bf16[4,64,1152]{2,1,0:T(8,128)(2,1)}), bf16[4,64,1152]{2,1,0:T(8,128)(2,1)S(1)}, u32[]{:S(2)}, u32[]{:S(2)}) async-start(bf16[4,64,1152]{2,1,0:T(8,128)(2,1)} %difference.1.refs_2_), calls=%async_computation.2 | async-start | bytes 1179648 | tf_op jit(solution)/shard_map/all_to_all | solution.py:477
  89.8 4.2 %collective-permute-start.6 = (bf16[512,768]{1,0:T(8,128)(2,1)S(1)}, bf16[512,768]{1,0:T(8,128)(2,1)S(1)}, u32[]{:S(2)}, u32[]{:S(2)}) collective-permute-start(bf16[512,768]{1,0:T(8,128)(2,1)S(1)} %get-tuple-element.46), channel_id=1, source_target_pairs={{0,4},{4,0},{1,5},{5,1},{2,6},{6,2},{3,7},{7,3},{8,12},{12,8},{9,1... | collective-permute-start | bytes 2359304 | tf_op jit(solution)/shard_map/ppermute | solution.py:495

commit v12 on v11

--- a/solution.py
+++ b/solution.py
@@ -252,10 +252,10 @@
         out_ref[i, :, features + columns :] = tail
 
 
-def backward_kernel(held, back_ref, feat_ref, *refs):
+def backward_kernel(held, back_ref, feat_ref, weights_ref, *refs):
     sources, (keep_ref, send_ref, loss_ref) = refs[:held], refs[held : held + 3]
     copies = fetch(sources, refs[2 * held + 3 : -1], refs[-1])
-    out_ref, packed_ref, weights_ref, mixed_ref, normed_ref, pick_ref = refs[2 * held + 3 : -1]
+    out_ref, packed_ref, mixed_ref, normed_ref, pick_ref = refs[2 * held + 3 : -1]
     features = out_ref.shape[1]
     heads = out_ref.shape[0] // HEAD
     dfeat = back_ref[:, :features]
@@ -265,8 +265,7 @@
     loss_ref[...] = jnp.sum(jnp.sum(tail, 0, keepdims=True), 1, keepdims=True)
     copies[0].wait()
     dmixed = nt(dfeat, out_ref[...]).astype(BF16)
-    for copy in copies[1:3]:
-        copy.wait()
+    copies[1].wait()
     packed = packed_ref[...]
     pieces = []
     for head in range(heads):
@@ -283,7 +282,7 @@
     used = dpacked.shape[1]
     length = dpacked.shape[0]
     right = jnp.concatenate([dpacked, jnp.zeros((length, features - used), BF16)], 1)
-    for copy in copies[3:]:
+    for copy in copies[2:]:
         copy.wait()
     tailed = features - columns
     mixed = jnp.concatenate([jnp.zeros((length, used - tailed), BF16), mixed_ref[...]], 1)
@@ -476,21 +475,21 @@
     )(sources, teacher_parts, message)
     back = lax.all_to_all(message, "x", 0, 0).reshape(length, features + columns + BLOCK)
 
-    held = (kept_out, packed, weights, mixed, normed_rows, pick)
+    held = (kept_out, packed, mixed, normed_rows, pick)
     keep, send, loss = pl.pallas_call(
         lambda *refs: backward_kernel(len(held), *refs),
         out_shape=(
             shape((picked, features), BF16), shape((picked, features), BF16), shape((1, 1), F32),
             *in_place(held),
         ),
-        in_specs=[VMEM] * 2 + [HBM] * len(held),
+        in_specs=[VMEM] * 3 + [HBM] * len(held),
         out_specs=(VMEM,) * 3 + (HBM,) * len(held),
         scratch_shapes=buffers(held),
-        input_output_aliases={2 + i: 3 + i for i in range(len(held))},
+        input_output_aliases={3 + i: 3 + i for i in range(len(held))},
         compiler_params=PARAMS,
         cost_estimate=cost(4),
         name="student_backward",
-    )(back, feat_extra, *held)[:3]
+    )(back, feat_extra, weights, *held)[:3]
 
     total = add(keep, lax.ppermute(send, "c", SWAP)).astype(BF16)
     chips = shares // 2

time: 131 us -> 131 us (level)
    unnamed x32 -> x34, local copies, waits for them, and re-layouts: 3.41 us -> 3.42 us
where the time goes in v12:
time: 131 us; the launch traced here: 130 us
  starting transfers between devices  42.4 us (32%)
  blocking collectives  35.1 us (27%)
  Pallas kernels  23.2 us (18%)
  waiting for transfers between devices  20.2 us (15%)
  local copies, waits for them, and re-layouts  5.44 us (4%)
  between operations  2.23 us (2%)
  other arithmetic  1.52 us (1%)
    all_to_all x1, blocking collectives, on_device(): lax.all_to_all(total.reshape(chips, total.shape[0] // chips, features), C...  35.1 us
    ppermute x4, starting transfers between devices, from_peers(): lax.ppermute(rows(k), axis, [(i, (i + k) % ways) for i in range(ways)])  14.4 us
    all_to_all x1, starting transfers between devices, on_device(): own_core = lax.all_to_all(shard, ('y', 'z'), 0, 0)  14 us
    all_to_all x1, waiting for transfers between devices, on_device(): teacher_parts = lax.all_to_all(teacher_part, 'x', 0, 0)  8.34 us
    all_to_all x1, waiting for transfers between devices, on_device(): lax.all_to_all(message, 'x', 0, 0)  7.38 us
    pallas_call x1, Pallas kernels, on_device(): pl.pallas_call(lambda *refs: backward_kernel(len(held), *refs), out_shape...  4.43 us
    all_to_all x1, starting transfers between devices, on_device(): teacher_parts = lax.all_to_all(teacher_part, 'x', 0, 0)  4.3 us
    pallas_call x1, Pallas kernels, on_device(): pl.pallas_call(teacher_kernel, out_shape=shape((ways, rows, width + featu...  3.55 us
  transfers between devices with their start and end apart: 10, of which 6 were waited for; matrix products, arithmetic and copies ran while one was open for 1% of the time, Pallas kernels for 12%

profile of v12, /device:TPU:16, one launch (start us, length us, event | category | flops | bytes accessed | tf_op | source)
XLA Modules:
  0.0 130.1 jit_solution(1341298023174681456)
XLA Ops:
  0.6 0.8 pad_maximum_fusion
  1.4 1.1 broadcast_in_dim.2
  2.5 14.0 %all-to-all-start = ((bf16[32,16,1024]{2,1,0:T(8,128)(2,1)}), bf16[32,16,1024]{2,1,0:T(8,128)(2,1)S(1)}, u32[]{:S(2)}, u32[]{:S(2)}) async-start(bf16[32,16,1024]{2,1,0:T(8,128)(2,1)} %broadcast_in_dim.2), calls=%async_computation | async-start | bytes 2097152 | tf_op jit(solution)/shard_map/all_to_all | solution.py:345
  16.5 0.7 constant_dynamic-slice_fusion.1
  17.2 4.9 %collective-permute-start.3 = (bf16[384,256]{1,0:T(8,128)(2,1)}, bf16[384,256]{1,0:T(8,128)(2,1)}, u32[]{:S(2)}, u32[]{:S(2)}) collective-permute-start(bf16[384,256]{1,0:T(8,128)(2,1)} %constant_dynamic-slice_fusion.1), channel_id=1, source_target_pairs={{0,2},{1,3},{2,0},{3,1},{4,6},{5,7},{6,4},{7,5},{8,10},{9,11},{10,... | collective-permute-start | bytes 589832 | tf_op jit(solution)/shard_map/ppermute | solution.py:306
  22.9 3.4 %student_forward.1 = (bf16[64,768]{1,0:T(8,128)(2,1)}, bf16[576,256]{1,0:T(8,128)(2,1)}, bf16[64,768]{1,0:T(8,128)(2,1)S(1)}, bf16[576,256]{1,0:T(8,128)(2,1)S(1...) custom-call(s32[1]{0:T(128)S(6)} %copy.32.count_ref.refs_0_, ...), custom_call_target="tpu_custom_call" | custom-call | flops 4000000000 | bytes 1000000 | tf_op jit(solution)/shard_map/student_forward/pallas_call | solution.py:354
  26.3 2.4 %collective-permute-start.1 = (bf16[64,768]{1,0:T(8,128)(2,1)S(1)}, bf16[64,768]{1,0:T(8,128)(2,1)S(1)}, u32[]{:S(2)}, u32[]{:S(2)}) collective-permute-start(bf16[64,768]{1,0:T(8,128)(2,1)S(1)} %get-tuple-element.29), channel_id=1, source_target_pairs={{0,2},{1,3},{2,0},{3,1},{4,6},{5,7},{6,4},{7,5},{8,10},{9,11},{10,... | collective-permute-start | bytes 294920 | tf_op jit(solution)/shard_map/ppermute | solution.py:306
  28.7 3.4 %collective-permute-start = (bf16[576,256]{1,0:T(8,128)(2,1)}, bf16[576,256]{1,0:T(8,128)(2,1)S(1)}, u32[]{:S(2)}, u32[]{:S(2)}) collective-permute-start(bf16[576,256]{1,0:T(8,128)(2,1)} %get-tuple-element.28), channel_id=1, source_target_pairs={{0,1},{1,2},{2,3},{3,0},{4,5},{5,6},{6,7},{7,4},{8,9},{9,10},{10,1... | collective-permute-start | bytes 884744 | tf_op jit(solution)/shard_map/ppermute | solution.py:306
  32.1 3.7 %collective-permute-start.2 = (bf16[576,256]{1,0:T(8,128)(2,1)S(1)}, bf16[576,256]{1,0:T(8,128)(2,1)S(1)}, u32[]{:S(2)}, u32[]{:S(2)}) collective-permute-start(bf16[576,256]{1,0:T(8,128)(2,1)S(1)} %get-tuple-element.30), channel_id=1, source_target_pairs={{0,3},{1,0},{2,1},{3,2},{4,7},{5,4},{6,5},{7,6},{8,11},{9,8},{10,9... | collective-permute-start | bytes 884744 | tf_op jit(solution)/shard_map/ppermute | solution.py:306
  35.9 1.0 copy-done.12
  36.8 2.6 %student_picks.1 = (bf16[2,512,256]{2,1,0:T(8,128)(2,1)}, bf16[2,512,768]{2,1,0:T(8,128)(2,1)}) custom-call(s32[5]{0:T(128)S(1)} %stack.35.place_ref.refs_0_, bf16[256,768]{1,0:T(8,128)(2,1)S(1)} %copy-done.12, bf16[384,256]{1,0:T(8,128)(2,1)} %collective-permute-done.3.refs_5_.refs_2_), custom_call_target="tpu_custom_call" | custom-call | flops 2000000000 | bytes 1000000 | tf_op jit(solution)/shard_map/student_picks/pallas_call | solution.py:377
  39.4 1.2 collective-permute-done.refs_2_
  40.7 0.7 collective-permute-done.2.refs_4_
  41.4 0.7 copy-done.15
  42.1 1.5 %student_rows.1 = (bf16[64,768]{1,0:T(8,128)(2,1)S(1)}, bf16[3,384,256]{2,1,0:T(8,128)(2,1)S(1)}, bf16[576,256]{1,0:T(8,128)(2,1)}, bf16[64,768]{1,0:T(8,128)(2,...) custom-call(bf16[64,768]{1,0:T(8,128)(2,1)S(1)} %dynamic-slice_bitca, ...), custom_call_target="tpu_custom_call", output_to_operand_aliasing={{2}: (2, {}), {3}: (3, {}), {4}: (4, {}), {5}: (5, {})} | custom-call | flops 1000000000 | bytes 1000000 | tf_op jit(solution)/shard_map/student_rows/pallas_call | solution.py:391
  43.9 1.9 %collective-permute-start.4 = (bf16[32,16,1024]{2,1,0:T(8,128)(2,1)S(1)}, bf16[32,16,1024]{2,1,0:T(8,128)(2,1)S(1)}, u32[]{:S(2)}, u32[]{:S(2)}) collective-permute-start(bf16[32,16,1024]{2,1,0:T(8,128)(2,1)S(1)} %all-to-all-done.own_ref), channel_id=1, source_target_pairs={{0,4},{4,0},{1,5},{5,1},{2,6},{6,2},{3,7},{7,3},{8,12},{12,8},{9,1... | collective-permute-start | bytes 3145736 | tf_op jit(solution)/shard_map/ppermute | solution.py:408
  45.9 2.4 %collective-permute-start.5 = (bf16[3,384,256]{2,1,0:T(8,128)(2,1)S(1)}, bf16[3,384,256]{2,1,0:T(8,128)(2,1)S(1)}, u32[]{:S(2)}, u32[]{:S(2)}) collective-permute-start(bf16[3,384,256]{2,1,0:T(8,128)(2,1)S(1)} %get-tuple-element.37.refs_2_), channel_id=1, source_target_pairs={{0,4},{4,0},{1,5},{5,1},{2,6},{6,2},{3,7},{7,3},{8,12},{12,8},{9,1... | collective-permute-start | bytes 1769480 | tf_op jit(solution)/shard_map/ppermute | solution.py:409
  49.0 3.6 %teacher.1 = bf16[4,64,1792]{2,1,0:T(8,128)(2,1)} custom-call(s32[5]{0:T(128)S(1)} %stack.35.place_ref.refs_0_, s32[2]{0:T(128)S(1)} %bitcast.26, bf16[256,1024]{1,0:T(8,128)(2,1)S(1)} %teacher_norm.1.normed_ref, bf16[32,16,1024]{2,1,0:T(8,128)(2,1)S(1)} %all-to-all-done.own_ref, bf16[32,16,1024]{2,1,0:T(8,128)(2,1)S(1)} %collective-permute-done.4.other_ref, ...), custom_call_target="tpu_custom_call" | custom-call | flops 5000000000 | bytes 1000000 | tf_op jit(solution)/shard_map/teacher/pallas_call | solution.py:420
  52.5 4.3 %all-to-all-start.1 = ((bf16[4,64,1792]{2,1,0:T(8,128)(2,1)}), bf16[4,64,1792]{2,1,0:T(8,128)(2,1)S(1)}, u32[]{:S(2)}, u32[]{:S(2)}) async-start(bf16[4,64,1792]{2,1,0:T(8,128)(2,1)} %teacher.1), calls=%async_computation.1 | async-start | bytes 1835008 | tf_op jit(solution)/shard_map/all_to_all | solution.py:434
  58.2 2.2 %projector.1.proj_ref.refs_5_ = bf16[4,256,768]{2,1,0:T(8,128)(2,1)} custom-call(s32[5]{0:T(128)S(1)} %stack.33.refs_0_.refs_1_, bf16[768,256]{1,0:T(8,128)(2,1)S(1)} %copy-done, bf16[3,384,256]{2,1,0:T(8,128)(2,1)S(1)} %get-tuple-element.37.refs_2_, bf16[3,384,256]{2,1,0:T(8,128)(2,1)S(1)} %collective-permute-done.5.refs_3_), custom_call_target="tpu_custom_call" | custom-call | flops 1000000000 | bytes 1000000 | tf_op jit(solution)/shard_map/projector/pallas_call | solution.py:439
  60.3 1.4 %copy-done.7 = bf16[4,256,768]{2,1,0:T(8,128)(2,1)S(1)} copy-done((bf16[4,256,768]{2,1,0:T(8,128)(2,1)S(1)}, bf16[4,256,768]{2,1,0:T(8,128)(2,1)}, u32[]{:S(2)}) %copy-start.7) | copy-done | bytes 1572888
  61.8 0.6 student_predict.1.refs_4_
  62.3 8.3 %all-to-all-done.1.refs_2_.refs_1_ = bf16[4,64,1792]{2,1,0:T(8,128)(2,1)S(1)} async-done(((bf16[4,64,1792]{2,1,0:T(8,128)(2,1)}), bf16[4,64,1792]{2,1,0:T(8,128)(2,1)S(1)}, u32[]{:S(2)}, u32[]{:S(2)}) %all-to-all-start.1) | async-done | bytes 917536 | tf_op jit(solution)/shard_map/all_to_all | solution.py:434
  70.7 1.8 %difference.1.refs_2_ = bf16[4,64,1152]{2,1,0:T(8,128)(2,1)} custom-call(s32[1]{0:T(128)S(6)} %copy.32.count_ref.refs_0_, s32[5]{0:T(128)S(1)} %stack.33.refs_0_.refs_1_, bf16[4,64,1792]{2,1,0:T(8,128)(2,1)S(1)} %all-to-all-done.1.refs_2_.refs_1_, bf16[64,1024]{1,0:T(8,128)(2,1)S(1)} %dynamic-slice_bitcast_fusion.refs_3_, ...), custom_call_target="tpu_custom_call" | custom-call | flops 2000000000 | bytes 1000000 | tf_op jit(solution)/shard_map/difference/pallas_call | solution.py:458
  72.5 3.5 %all-to-all-start.2 = ((bf16[4,64,1152]{2,1,0:T(8,128)(2,1)}), bf16[4,64,1152]{2,1,0:T(8,128)(2,1)S(1)}, u32[]{:S(2)}, u32[]{:S(2)}) async-start(bf16[4,64,1152]{2,1,0:T(8,128)(2,1)} %difference.1.refs_2_), calls=%async_computation.2 | async-start | bytes 1179648 | tf_op jit(solution)/shard_map/all_to_all | solution.py:476
  76.0 2.0 %student_extra.1.refs_1_ = bf16[2,3,512,256]{3,2,1,0:T(8,128)(2,1)S(1)} custom-call(s32[5]{0:T(128)S(1)} %stack.33.refs_0_.refs_1_, bf16[4,64,1792]{2,1,0:T(8,128)(2,1)S(1)} %all-to-all-done.1.refs_2_.refs_1_, bf16[4,64,1152]{2,1,0:T(8,128)(2,1)} %difference.1.refs_2_), custom_call_target="tpu_custom_call" | custom-call | flops 3000000000 | bytes 1000000 | tf_op jit(solution)/shard_map/student_extra/pallas_call | solution.py:467
  78.0 7.4 %all-to-all-done.2 = bf16[4,64,1152]{2,1,0:T(8,128)(2,1)S(1)} async-done(((bf16[4,64,1152]{2,1,0:T(8,128)(2,1)}), bf16[4,64,1152]{2,1,0:T(8,128)(2,1)S(1)}, u32[]{:S(2)}, u32[]{:S(2)}) %all-to-all-start.2) | async-done | bytes 589856 | tf_op jit(solution)/shard_map/all_to_all | solution.py:476
  85.4 4.4 %student_backward.1 = (bf16[512,768]{1,0:T(8,128)(2,1)S(1)}, bf16[512,768]{1,0:T(8,128)(2,1)S(1)}, f32[1,1]{1,0:T(1,128)}, bf16[192,768]{1,0:T(8,128)(2,1)}, bf1...) custom-call(bf16[256,1152]{1,0:T(8,128)(2,1)S(1)} %bitcast.21, ...), custom_call_target="tpu_custom_call", output_to_operand_aliasing={{3}: (3, {}), {4}: (4, {}), {5}: (5, {}), {6}: (6, {}), {7}... | custom-call | flops 4000000000 | bytes 1000000 | tf_op jit(solution)/shard_map/student_backward/pallas_call | solution.py:479
  89.8 1.9 %collective-permute-start.6 = (bf16[512,768]{1,0:T(8,128)(2,1)S(1)}, bf16[512,768]{1,0:T(8,128)(2,1)S(1)}, u32[]{:S(2)}, u32[]{:S(2)}) collective-permute-start(bf16[512,768]{1,0:T(8,128)(2,1)S(1)} %get-tuple-element.46), channel_id=1, source_target_pairs={{0,4},{4,0},{1,5},{5,1},{2,6},{6,2},{3,7},{7,3},{8,12},{12,8},{9,1... | collective-permute-start | bytes 2359304 | tf_op jit(solution)/shard_map/ppermute | solution.py:494
  91.8 2.3 %collective-permute-done.6 = bf16[512,768]{1,0:T(8,128)(2,1)S(1)} collective-permute-done((bf16[512,768]{1,0:T(8,128)(2,1)S(1)}, bf16[512,768]{1,0:T(8,128)(2,1)S(1)}, u32[]{:S(2)}, u32[]{:S(2)}) %collective-permute-start.6) | collective-permute-done | bytes 786464 | tf_op jit(solution)/shard_map/ppermute | solution.py:494
  94.2 35.1 %all_to_all.20.parts_ref = bf16[64,8,768]{2,1,0:T(8,128)(2,1)S(1)} all-to-all(bf16[64,8,768]{2,1,0:T(8,128)(2,1)S(1)} %fusion), channel_id=1, replica_groups=mesh['g'=2,'y'=4,'z'=8,'c'=2,'x'=4] {'g','y','z'}, dimensions={0} | all-to-all | bytes 1572864 | tf_op jit(solution)/shard_map/all_to_all | solution.py:496
  129.3 0.8 gradient_rows.1
  (43 shorter events, 1.9 us)
Async XLA Ops:
  1.4 15.1 %copy-start = (bf16[768,256]{1,0:T(8,128)(2,1)S(1)}, bf16[768,256]{1,0:T(8,128)(2,1)}, u32[]{:S(2)}) copy-start(bf16[768,256]{1,0:T(8,128)(2,1)} %refs_1_.1) | copy-start | bytes 1179652
  2.5 20.4 %copy-start.2 = (bf16[1,256,768]{2,1,0:T(8,128)(2,1)S(1)}, bf16[1,256,768]{2,1,0:T(8,128)(2,1)}, u32[]{:S(2)}) copy-start(bf16[1,256,768]{2,1,0:T(8,128)(2,1)} %param.14) | copy-start | bytes 1179652
  2.5 20.4 %copy-start.3 = (bf16[768,576]{0,1:T(8,128)(2,1)S(1)}, bf16[768,576]{0,1:T(8,128)(2,1)}, u32[]{:S(2)}) copy-start(bf16[768,576]{0,1:T(8,128)(2,1)} %param.17) | copy-start | bytes 2654212
  2.5 20.4 %copy-start.4 = (bf16[192,768]{1,0:T(8,128)(2,1)S(1)}, bf16[192,768]{1,0:T(8,128)(2,1)}, u32[]{:S(2)}) copy-start(bf16[192,768]{1,0:T(8,128)(2,1)} %out_ref.1) | copy-start | bytes 884740
  2.5 41.4 %all-to-all-start = ((bf16[32,16,1024]{2,1,0:T(8,128)(2,1)}), bf16[32,16,1024]{2,1,0:T(8,128)(2,1)S(1)}, u32[]{:S(2)}, u32[]{:S(2)}) async-start(bf16[32,16,1024]{2,1,0:T(8,128)(2,1)} %broadcast_in_dim.2), calls=%async_computation | async-start | bytes 2097152 | tf_op jit(solution)/shard_map/all_to_all | solution.py:345
  17.2 18.6 %collective-permute-start.3 = (bf16[384,256]{1,0:T(8,128)(2,1)}, bf16[384,256]{1,0:T(8,128)(2,1)}, u32[]{:S(2)}, u32[]{:S(2)}) collective-permute-start(bf16[384,256]{1,0:T(8,128)(2,1)} %constant_dynamic-slice_fusion.1), channel_id=1, source_target_pairs={{0,2},{1,3},{2,0},{3,1},{4,6},{5,7},{6,4},{7,5},{8,10},{9,11},{10,... | collective-permute-start | bytes 589832 | tf_op jit(solution)/shard_map/ppermute | solution.py:306
  26.3 13.1 %collective-permute-start.1 = (bf16[64,768]{1,0:T(8,128)(2,1)S(1)}, bf16[64,768]{1,0:T(8,128)(2,1)S(1)}, u32[]{:S(2)}, u32[]{:S(2)}) collective-permute-start(bf16[64,768]{1,0:T(8,128)(2,1)S(1)} %get-tuple-element.29), channel_id=1, source_target_pairs={{0,2},{1,3},{2,0},{3,1},{4,6},{5,7},{6,4},{7,5},{8,10},{9,11},{10,... | collective-permute-start | bytes 294920 | tf_op jit(solution)/shard_map/ppermute | solution.py:306
  28.7 11.9 %collective-permute-start = (bf16[576,256]{1,0:T(8,128)(2,1)}, bf16[576,256]{1,0:T(8,128)(2,1)S(1)}, u32[]{:S(2)}, u32[]{:S(2)}) collective-permute-start(bf16[576,256]{1,0:T(8,128)(2,1)} %get-tuple-element.28), channel_id=1, source_target_pairs={{0,1},{1,2},{2,3},{3,0},{4,5},{5,6},{6,7},{7,4},{8,9},{9,10},{10,1... | collective-permute-start | bytes 884744 | tf_op jit(solution)/shard_map/ppermute | solution.py:306
  32.1 9.2 %collective-permute-start.2 = (bf16[576,256]{1,0:T(8,128)(2,1)S(1)}, bf16[576,256]{1,0:T(8,128)(2,1)S(1)}, u32[]{:S(2)}, u32[]{:S(2)}) collective-permute-start(bf16[576,256]{1,0:T(8,128)(2,1)S(1)} %get-tuple-element.30), channel_id=1, source_target_pairs={{0,3},{1,0},{2,1},{3,2},{4,7},{5,4},{6,5},{7,6},{8,11},{9,8},{10,9... | collective-permute-start | bytes 884744 | tf_op jit(solution)/shard_map/ppermute | solution.py:306
  35.8 1.0 copy-start.12
  36.8 5.3 %copy-start.11 = (bf16[64,768]{1,0:T(8,128)(2,1)S(1)}, bf16[64,768]{1,0:T(8,128)(2,1)}, u32[]{:S(2)}) copy-start(bf16[64,768]{1,0:T(8,128)(2,1)} %get-tuple-element.27.refs_1_) | copy-start | bytes 294916
  39.4 2.7 %copy-start.16 = (bf16[64,768]{1,0:T(8,128)(2,1)}, bf16[64,768]{1,0:T(8,128)(2,1)S(1)}, u32[]{:S(2)}) copy-start(bf16[64,768]{1,0:T(8,128)(2,1)S(1)} %collective-permute-done.1.refs_3_) | copy-start | bytes 294916
  40.6 0.7 copy-start.14
  41.4 0.7 copy-start.15
  42.1 6.2 %copy-start.1 = (bf16[1,256,1024]{2,1,0:T(8,128)(2,1)S(1)}, bf16[1,256,1024]{2,1,0:T(8,128)(2,1)}, u32[]{:S(2)}) copy-start(bf16[1,256,1024]{2,1,0:T(8,128)(2,1)} %param.10) | copy-start | bytes 1572868
  42.1 6.2 %copy-start.5 = (f32[1024]{0:T(1024)S(1)}, f32[1024]{0:T(1024)}, u32[]{:S(2)}) copy-start(f32[1024]{0:T(1024)} %param.11) | copy-start | bytes 12292
  43.7 5.0 %copy-start.9 = (bf16[64,768]{1,0:T(8,128)(2,1)}, bf16[64,768]{1,0:T(8,128)(2,1)S(1)}, u32[]{:S(2)}) copy-start(bf16[64,768]{1,0:T(8,128)(2,1)S(1)} %get-tuple-element.35.after_ref.feat_ref) | copy-start | bytes 294916
  43.9 4.7 %collective-permute-start.4 = (bf16[32,16,1024]{2,1,0:T(8,128)(2,1)S(1)}, bf16[32,16,1024]{2,1,0:T(8,128)(2,1)S(1)}, u32[]{:S(2)}, u32[]{:S(2)}) collective-permute-start(bf16[32,16,1024]{2,1,0:T(8,128)(2,1)S(1)} %all-to-all-done.own_ref), channel_id=1, source_target_pairs={{0,4},{4,0},{1,5},{5,1},{2,6},{6,2},{3,7},{7,3},{8,12},{12,8},{9,1... | collective-permute-start | bytes 3145736 | tf_op jit(solution)/shard_map/ppermute | solution.py:408
  45.9 12.3 %collective-permute-start.5 = (bf16[3,384,256]{2,1,0:T(8,128)(2,1)S(1)}, bf16[3,384,256]{2,1,0:T(8,128)(2,1)S(1)}, u32[]{:S(2)}, u32[]{:S(2)}) collective-permute-start(bf16[3,384,256]{2,1,0:T(8,128)(2,1)S(1)} %get-tuple-element.37.refs_2_), channel_id=1, source_target_pairs={{0,4},{4,0},{1,5},{5,1},{2,6},{6,2},{3,7},{7,3},{8,12},{12,8},{9,1... | collective-permute-start | bytes 1769480 | tf_op jit(solution)/shard_map/ppermute | solution.py:409
  48.3 0.7 copy-start.6
  52.5 18.2 %all-to-all-start.1 = ((bf16[4,64,1792]{2,1,0:T(8,128)(2,1)}), bf16[4,64,1792]{2,1,0:T(8,128)(2,1)S(1)}, u32[]{:S(2)}, u32[]{:S(2)}) async-start(bf16[4,64,1792]{2,1,0:T(8,128)(2,1)} %teacher.1), calls=%async_computation.1 | async-start | bytes 1835008 | tf_op jit(solution)/shard_map/all_to_all | solution.py:434
  58.2 2.2 %copy-start.10 = (bf16[64,768]{1,0:T(8,128)(2,1)S(1)}, bf16[64,768]{1,0:T(8,128)(2,1)}, u32[]{:S(2)}) copy-start(bf16[64,768]{1,0:T(8,128)(2,1)} %copy-done.9) | copy-start | bytes 294916
  60.3 1.4 %copy-start.7 = (bf16[4,256,768]{2,1,0:T(8,128)(2,1)S(1)}, bf16[4,256,768]{2,1,0:T(8,128)(2,1)}, u32[]{:S(2)}) copy-start(bf16[4,256,768]{2,1,0:T(8,128)(2,1)} %projector.1.proj_ref.refs_5_) | copy-start | bytes 4718596
  61.8 8.9 %copy-start.8 = (bf16[4,256,768]{2,1,0:T(8,128)(2,1)S(1)}, bf16[4,256,768]{2,1,0:T(8,128)(2,1)}, u32[]{:S(2)}) copy-start(bf16[4,256,768]{2,1,0:T(8,128)(2,1)} %projector.1.proj_ref.refs_5_) | copy-start | bytes 4718596
  72.5 12.9 %all-to-all-start.2 = ((bf16[4,64,1152]{2,1,0:T(8,128)(2,1)}), bf16[4,64,1152]{2,1,0:T(8,128)(2,1)S(1)}, u32[]{:S(2)}, u32[]{:S(2)}) async-start(bf16[4,64,1152]{2,1,0:T(8,128)(2,1)} %difference.1.refs_2_), calls=%async_computation.2 | async-start | bytes 1179648 | tf_op jit(solution)/shard_map/all_to_all | solution.py:476
  76.0 9.4 %copy-start.13 = (bf16[3,256,256]{2,1,0:T(8,128)(2,1)S(1)}, bf16[3,256,256]{2,1,0:T(8,128)(2,1)}, u32[]{:S(2)}) copy-start(bf16[3,256,256]{2,1,0:T(8,128)(2,1)} %get-tuple-element.38.refs_2_) | copy-start | bytes 1179652
  89.8 4.2 %collective-permute-start.6 = (bf16[512,768]{1,0:T(8,128)(2,1)S(1)}, bf16[512,768]{1,0:T(8,128)(2,1)S(1)}, u32[]{:S(2)}, u32[]{:S(2)}) collective-permute-start(bf16[512,768]{1,0:T(8,128)(2,1)S(1)} %get-tuple-element.46), channel_id=1, source_target_pairs={{0,4},{4,0},{1,5},{5,1},{2,6},{6,2},{3,7},{7,3},{8,12},{12,8},{9,1... | collective-permute-start | bytes 2359304 | tf_op jit(solution)/shard_map/ppermute | solution.py:494
